TPU v7x, 256 devices: a whole 4x4x8 slice. The times are simulated.
256 devices in a mesh: seq: 64 (over x, z, core), head: 4 (over y).
Axes of the slice: x: 4, y: 4, z: 8, core: 2. Of those that a mesh axis runs over, the one named last changes fastest.
Arguments:
- queries: bfloat16 [8192, 2048], P('seq', 'head'), may hold values from -6 to 6
- keys: bfloat16 [8192, 2048], P('seq', 'head'), may hold values from -6 to 6
- values: bfloat16 [8192, 2048], P('seq', 'head'), may hold values from -6 to 6
- gate_log: float32 [8192, 16], P('seq', 'head'), may hold values from -1 to 0
- beta: float32 [8192, 16], P('seq', 'head'), may hold values from 0.0002 to 1
- stream: bfloat16 [8192, 2048], P('seq'), may hold values from -6 to 6
- w_out: bfloat16 [2048, 2048], P('head'), may hold values from -0.125 to 0.125
- w_qkv: bfloat16 [2048, 6144], P(None, 'head'), may hold values from -0.125 to 0.125
Outputs:
- hidden: bfloat16 [8192, 2048], P('seq', 'head')
- attended: bfloat16 [8192, 2048], P('seq', 'head')
All inputs are finite; a program needn't handle non-finite values.
Results may differ from a plain program's by a relative error of at most 0.015.
Values may be sent and summed in bfloat16 or wider, within the bound.
No kernel may reach another device: no remote copies, remote signals or barrier semaphores. Data moves between devices by JAX's collectives and lax.ppermute only.
A program may use at most 128 MiB of HBM per device.

v0:
```python
import jax
import jax.numpy as jnp
from jax import lax
from jax.sharding import PartitionSpec as P

WINDOW = 1024
STRETCH = 64


score_scale = 10.0


def carried_in(shard, axis, combine, identity):
    length, mine = (lax.axis_size(axis), lax.axis_index(axis))
    everything = jax.tree.map(lambda part: lax.all_gather(part, axis), shard)
    start = jax.tree.map(
        lambda part, zero: jnp.broadcast_to(jnp.asarray(zero, part.dtype), part.shape),
        shard,
        identity,
    )

    def hop(k, before):
        reached = k < mine
        new = combine(before, jax.tree.map(lambda part: part[k], everything))
        return jax.tree.map(lambda a, b: jnp.where(reached, a, b), new, before)

    return lax.fori_loop(0, length, hop, start)


def passed_along(block, axis, distance):
    devices = range(lax.axis_size(axis))
    route = [(i - distance, i) for i in devices if i - distance in devices]
    return lax.ppermute(block, axis, route)


def product(left, right):
    return jnp.einsum("hij,hjk->hik", left, right, precision=lax.Precision.HIGHEST)


def to_unit(vectors):
    return vectors * lax.rsqrt(jnp.sum(vectors * vectors, axis=-1, keepdims=True) + 1e-06)


def lower_inverse(coupling):
    identity = jnp.eye(coupling.shape[-1], dtype=jnp.float32)
    result = identity - coupling
    power = coupling
    span = 2
    while span < coupling.shape[-1]:
        power = product(power, power)
        result = product(result, identity + power)
        span = span * 2
    return result


def stretch_parts(query_rows, key_rows, value_rows, gate_rows, beta_rows):
    length = gate_rows.shape[-1]
    cumulative = jnp.cumsum(gate_rows, axis=-1)
    later = lax.broadcasted_iota(jnp.int32, (length, length), 0)
    sooner = lax.broadcasted_iota(jnp.int32, (length, length), 1)
    causal = later >= sooner
    strict = later > sooner
    spread = cumulative[:, :, None] - cumulative[:, None, :]
    decay = jnp.where(causal, jnp.exp(jnp.where(causal, spread, 0.0)), 0.0)
    key_intersection = jnp.einsum(
        "hcd,hed->hce", key_rows, key_rows, precision=lax.Precision.HIGHEST
    )
    coupling = jnp.where(strict, beta_rows[:, :, None] * decay * key_intersection, 0.0)
    inverse = lower_inverse(coupling)
    writes = product(inverse, beta_rows[:, :, None] * value_rows)
    erasers = product(inverse, (beta_rows * jnp.exp(cumulative))[:, :, None] * key_rows)
    key_end = jnp.swapaxes(jnp.exp(cumulative[:, -1:] - cumulative)[:, :, None] * key_rows, 1, 2)
    identity = jnp.eye(key_rows.shape[-1], dtype=jnp.float32)
    transition = jnp.exp(cumulative[:, -1])[:, None, None] * identity - product(key_end, erasers)
    offset = product(key_end, writes)
    intersection = jnp.einsum("hcd,hed->hce", query_rows, key_rows, precision=lax.Precision.HIGHEST)
    mixing = jnp.where(causal, intersection * decay, 0.0)
    query_decayed = jnp.exp(cumulative)[:, :, None] * query_rows
    return (query_decayed, mixing, writes, erasers, transition, offset)


def compose(earlier, later):
    return (product(later[0], earlier[0]), product(later[0], earlier[1]) + later[1])


def delta_layer(queries, keys, values, gate_log, beta):
    rows = queries.shape[0]
    groups = gate_log.shape[1]
    width = queries.shape[1] // groups
    blocks = rows // STRETCH

    def arrange(matrix):
        return (
            matrix.astype(jnp.float32).reshape(blocks, STRETCH, groups, width).transpose(0, 2, 1, 3)
        )

    query_blocks = to_unit(arrange(queries))
    key_blocks = to_unit(arrange(keys))
    value_blocks = arrange(values)
    gate_blocks = gate_log.reshape(blocks, STRETCH, groups).transpose(0, 2, 1)
    beta_blocks = beta.reshape(blocks, STRETCH, groups).transpose(0, 2, 1)

    def advance(carry, inputs):
        carried, state = carry
        query_decayed, mixing, writes, erasers, transition, offset = stretch_parts(*inputs)
        local = product(query_decayed, state) + product(mixing, writes - product(erasers, state))
        through = product(query_decayed - product(mixing, erasers), carried)
        return (
            (product(transition, carried), product(transition, state) + offset),
            (local, through),
        )

    identity = jnp.broadcast_to(jnp.eye(width, dtype=jnp.float32), (groups, width, width))
    start = (identity, jnp.zeros((groups, width, width), jnp.float32))
    final, outputs = lax.scan(
        advance, start, (query_blocks, key_blocks, value_blocks, gate_blocks, beta_blocks)
    )
    prefix = carried_in((final[0], final[1]), "seq", compose, start)
    incoming = prefix[1]
    result = outputs[0] + jnp.einsum(
        "nhcd,hde->nhce", outputs[1], incoming, precision=lax.Precision.HIGHEST
    )
    return result.transpose(0, 2, 1, 3).reshape(rows, groups, width)


def window_layer(unit_queries, unit_keys, head_values):
    rows, groups, width = unit_queries.shape
    packed = jnp.stack(
        [unit_keys.reshape(rows, groups * width), head_values.reshape(rows, groups * width)]
    )
    earlier = []
    moving = packed
    for count in range(WINDOW // rows):
        moving = passed_along(moving, "seq", 1)
        earlier.insert(0, moving)
    context = jnp.concatenate(earlier + [packed], axis=1).reshape(2, WINDOW + rows, groups, width)
    base = lax.axis_index("seq") * rows
    block = min(512, rows)
    key_block = context[0, 0 : WINDOW + block]
    value_block = context[1, 0 : WINDOW + block]
    scores = score_scale * jnp.einsum(
        "qhd,khd->hqk", unit_queries, key_block, preferred_element_type=jnp.float32
    )
    query_place = base + 0 + jnp.arange(block, dtype=jnp.int32)[:, None]
    key_place = base + 0 - WINDOW + jnp.arange(WINDOW + block, dtype=jnp.int32)[None, :]
    allowed = (key_place <= query_place) & (key_place > query_place - WINDOW) & (key_place >= 0)
    expo = jnp.where(allowed[None], jnp.exp(scores), 0.0)
    totals = jnp.sum(expo, axis=-1)
    mixed = jnp.einsum(
        "hqk,khd->qhd", expo.astype(jnp.bfloat16), value_block, preferred_element_type=jnp.float32
    )
    pieces = (mixed / jnp.transpose(totals)[:, :, None]).astype(jnp.bfloat16)
    return pieces.reshape(rows, groups * width)


def body(queries, keys, values, gate_log, beta, stream, w_out, w_qkv):
    rows = queries.shape[0]
    delta_out = delta_layer(queries, keys, values, gate_log, beta)
    groups = delta_out.shape[1]
    width = delta_out.shape[2]
    head_normed = (
        (delta_out * lax.rsqrt(jnp.mean(delta_out * delta_out, axis=-1, keepdims=True) + 1e-05))
        .astype(jnp.bfloat16)
        .reshape(rows, groups * width)
    )
    term = jnp.dot(head_normed, w_out, preferred_element_type=jnp.float32)
    summed = lax.psum(term, "head")
    hidden_full = (stream.astype(jnp.float32) + summed).astype(jnp.bfloat16)
    share_width = hidden_full.shape[1] // lax.axis_size("head")
    hidden_share = lax.dynamic_slice_in_dim(
        hidden_full, lax.axis_index("head") * share_width, share_width, 1
    )
    full_float = hidden_full.astype(jnp.float32)
    normed = (
        full_float * lax.rsqrt(jnp.mean(full_float * full_float, axis=-1, keepdims=True) + 1e-05)
    ).astype(jnp.bfloat16)
    projected = jnp.dot(normed, w_qkv, preferred_element_type=jnp.float32).reshape(
        rows, groups, 3, width
    )
    unit_queries = to_unit(projected[:, :, 0]).astype(jnp.bfloat16)
    unit_keys = to_unit(projected[:, :, 1]).astype(jnp.bfloat16)
    head_values = projected[:, :, 2].astype(jnp.bfloat16)
    attended = window_layer(unit_queries, unit_keys, head_values)
    return (hidden_share, attended)


def solution(mesh):
    in_specs = (
        P("seq", "head"),
        P("seq", "head"),
        P("seq", "head"),
        P("seq", "head"),
        P("seq", "head"),
        P("seq", None),
        P("head", None),
        P(None, "head"),
    )
    out_specs = (P("seq", "head"), P("seq", "head"))
    return jax.shard_map(body, mesh=mesh, in_specs=in_specs, out_specs=out_specs, check_vma=False)
```

profile of v0, /device:TPU:2, one launch (start us, length us, event | category | flops | bytes accessed | tf_op | source)
XLA Modules:
  0.0 488.9 jit_solution(9378358877307148938)
XLA Ops:
  13.5 23.4 %while.31 = (s32[]{:T(128)}, f32[4,128,128]{2,1,0:T(8,128)S(1)}, f32[4,128,128]{2,1,0:T(8,128)S(1)}, f32[2,4,64,128]{3,2,0,1:T(8,128)}, f32[2,4,64,128]{3,2,0,1:...) while((s32[]{:T(128)}, f32[4,128,128]{2,1,0:T(8,128)S(1)}, ...), condition=%wide.region_4.5_spmd.clone, body=%wide.region_2.4_spmd.clone.sunk | while | flops 730841344 | bytes 12002101 | solution.py:115
  38.6 100.5 %all-gather.5.cloned.1.call-done = f32[256,128,128]{2,1,0:T(8,128)} async-done(((f32[4,128,128]{2,1,0:T(8,128)}), f32[256,128,128]{2,1,0:T(8,128)}) %all-gather.5.cloned.1.call-update) | async-done | bytes 16777232 | tf_op jit(solution)/shard_map/all_gather | solution.py:15
  139.2 99.5 %all-gather.7.cloned.1.call-done = f32[256,128,128]{2,1,0:T(8,128)} async-done(((f32[4,128,128]{2,1,0:T(8,128)}), f32[256,128,128]{2,1,0:T(8,128)}) %all-gather.7.cloned.1.call-update) | async-done | bytes 16777232 | tf_op jit(solution)/shard_map/all_gather | solution.py:15
  238.7 95.0 %while.32 = (s32[]{:T(128)}, f32[4,128,128]{2,1,0:T(8,128)S(1)}, s32[]{:T(128)}, f32[64,4,128,128]{3,2,1,0:T(8,128)}, f32[64,4,128,128]{3,2,1,0:T(8,128)}, /*index=5*/s32[]{:T(128)}, s32[]{:T(128)}) while((s32[]{:T(128)}, f32[4,128,128]{2,1,0:T(8,128)S(1)}, s32[]{:T(128)}, f32[64,4,128,128]{3,2,1,0:T(8,128)}, ...), condition=%wide.region_6.7_spmd.clone, body=%wide.region_5.6_spmd.clone.sunk | while | flops 100925440 | bytes 1837663 | solution.py:27
  238.7 1.5 fusion.260
  336.2 49.4 %all-reduce.2.cloned.1.call-done = f32[128,2048]{1,0:T(8,128)} async-done(((f32[128,2048]{1,0:T(8,128)}), f32[128,2048]{1,0:T(8,128)}) %all-reduce.2.cloned.1.call-update) | async-done | bytes 1048592 | tf_op jit(solution)/shard_map/psum | solution.py:167
  385.5 1.5 fusion.70
  387.0 5.4 %fusion.72 = f32[128,1536]{0,1:T(8,128)S(1)} fusion(bf16[2048,1536]{1,0:T(8,128)(2,1)} %param.19, bf16[128,2048]{1,0:T(8,128)(2,1)S(1)} %get-tuple-element.264, f32[128]{0:T(128)S(1)} %add_rsqrt_fusion.5), kind=kOutput, calls=%fused_computation.96 | convolution fusion | flops 806092800 | bytes 7602688 | tf_op jit(solution)/shard_map/dot_general | solution.py:177
  393.2 1.9 collective-permute-start
  395.1 7.9 %collective-permute-done = bf16[2,128,512]{1,2,0:T(8,128)(2,1)S(1)} collective-permute-done((bf16[2,128,512]{1,2,0:T(8,128)(2,1)S(1)}, bf16[2,128,512]{1,2,0:T(8,128)(2,1)S(1)}, u32[]{:S(2)}, u32[]{:S(2)}) %collective-permute-start) | collective-permute-done | bytes 262176 | tf_op jit(solution)/shard_map/ppermute | solution.py:33
  403.6 1.9 collective-permute-start.1
  405.6 7.9 %collective-permute-done.1 = bf16[2,128,512]{1,2,0:T(8,128)(2,1)S(1)} collective-permute-done((bf16[2,128,512]{1,2,0:T(8,128)(2,1)S(1)}, bf16[2,128,512]{1,2,0:T(8,128)(2,1)S(1)}, u32[]{:S(2)}, u32[]{:S(2)}) %collective-permute-start.1) | collective-permute-done | bytes 262176 | tf_op jit(solution)/shard_map/ppermute | solution.py:33
  414.1 1.9 collective-permute-start.2
  416.0 7.9 %collective-permute-done.2 = bf16[2,128,512]{1,2,0:T(8,128)(2,1)S(1)} collective-permute-done((bf16[2,128,512]{1,2,0:T(8,128)(2,1)S(1)}, bf16[2,128,512]{1,2,0:T(8,128)(2,1)S(1)}, u32[]{:S(2)}, u32[]{:S(2)}) %collective-permute-start.2) | collective-permute-done | bytes 262176 | tf_op jit(solution)/shard_map/ppermute | solution.py:33
  424.6 1.9 collective-permute-start.3
  426.5 8.0 %collective-permute-done.3 = bf16[2,128,512]{1,2,0:T(8,128)(2,1)} collective-permute-done((bf16[2,128,512]{1,2,0:T(8,128)(2,1)S(1)}, bf16[2,128,512]{1,2,0:T(8,128)(2,1)}, u32[]{:S(2)}, u32[]{:S(2)}) %collective-permute-start.3) | collective-permute-done | bytes 262176 | tf_op jit(solution)/shard_map/ppermute | solution.py:33
  434.5 1.9 collective-permute-start.4
  436.4 8.2 %collective-permute-done.4 = bf16[2,128,512]{1,2,0:T(8,128)(2,1)} collective-permute-done((bf16[2,128,512]{1,2,0:T(8,128)(2,1)}, bf16[2,128,512]{1,2,0:T(8,128)(2,1)}, u32[]{:S(2)}, u32[]{:S(2)}) %collective-permute-start.4) | collective-permute-done | bytes 262176 | tf_op jit(solution)/shard_map/ppermute | solution.py:33
  444.6 1.9 collective-permute-start.5
  446.6 8.1 %collective-permute-done.5 = bf16[2,128,512]{1,2,0:T(8,128)(2,1)} collective-permute-done((bf16[2,128,512]{1,2,0:T(8,128)(2,1)}, bf16[2,128,512]{1,2,0:T(8,128)(2,1)}, u32[]{:S(2)}, u32[]{:S(2)}) %collective-permute-start.5) | collective-permute-done | bytes 262176 | tf_op jit(solution)/shard_map/ppermute | solution.py:33
  454.7 1.9 collective-permute-start.6
  457.6 7.3 %collective-permute-done.6 = bf16[2,128,512]{1,2,0:T(8,128)(2,1)} collective-permute-done((bf16[2,128,512]{1,2,0:T(8,128)(2,1)}, bf16[2,128,512]{1,2,0:T(8,128)(2,1)}, u32[]{:S(2)}, u32[]{:S(2)}) %collective-permute-start.6) | collective-permute-done | bytes 262176 | tf_op jit(solution)/shard_map/ppermute | solution.py:33
  464.8 1.9 collective-permute-start.7
  467.4 7.4 %collective-permute-done.7 = bf16[2,128,512]{1,2,0:T(8,128)(2,1)S(1)} collective-permute-done((bf16[2,128,512]{1,2,0:T(8,128)(2,1)}, bf16[2,128,512]{1,2,0:T(8,128)(2,1)S(1)}, u32[]{:S(2)}, u32[]{:S(2)}) %collective-permute-start.7) | collective-permute-done | bytes 262176 | tf_op jit(solution)/shard_map/ppermute | solution.py:33
  (287 shorter events, 136.3 us)
Async XLA Ops:
  7.2 327.5 %copy-start = (bf16[512,2048]{1,0:T(8,128)(2,1)S(1)}, bf16[512,2048]{1,0:T(8,128)(2,1)}, u32[]{:S(2)}) copy-start(bf16[512,2048]{1,0:T(8,128)(2,1)} %param.18) | copy-start | bytes 6291460
  7.2 132.0 %all-gather.5.cloned.1.call-start = ((), (), s32[]{:S(2)}) async-start(), calls=%async_computation.1 | async-start | bytes 17039360 | tf_op jit(solution)/shard_map/all_gather | solution.py:15
  20.0 3.7 copy-start.13
  31.7 3.7 copy-start.13
  36.9 0.7 copy-start.2
  36.9 0.8 copy-start.1
  37.6 201.0 %all-gather.7.cloned.1.call-start = ((), (), s32[]{:S(2)}) async-start(), calls=%async_computation.2 | async-start | bytes 17039360 | tf_op jit(solution)/shard_map/all_gather | solution.py:15
  38.4 347.2 %all-reduce.2.cloned.1.call-start = ((), (), s32[]{:S(2)}) async-start(), calls=%async_computation | async-start | bytes 2097152 | tf_op jit(solution)/shard_map/psum | solution.py:167
  238.7 95.0 %copy-start.12 = (f32[2,4,64,128]{3,2,0,1:T(8,128)S(1)}, f32[2,4,64,128]{3,2,0,1:T(8,128)}, u32[]{:S(2)}) copy-start(f32[2,4,64,128]{3,2,0,1:T(8,128)} %get-tuple-element.151) | copy-start | bytes 786436
  238.7 95.0 %copy-start.15 = (f32[2,4,64,128]{3,2,0,1:T(8,128)S(1)}, f32[2,4,64,128]{3,2,0,1:T(8,128)}, u32[]{:S(2)}) copy-start(f32[2,4,64,128]{3,2,0,1:T(8,128)} %get-tuple-element.155) | copy-start | bytes 786436
  334.7 50.9 %copy-start.5 = (bf16[128,2048]{1,0:T(8,128)(2,1)S(1)}, bf16[128,2048]{1,0:T(8,128)(2,1)}, u32[]{:S(2)}) copy-start(bf16[128,2048]{1,0:T(8,128)(2,1)} %param.17) | copy-start | bytes 1572868
  393.2 9.8 %collective-permute-start = (bf16[2,128,512]{1,2,0:T(8,128)(2,1)S(1)}, bf16[2,128,512]{1,2,0:T(8,128)(2,1)S(1)}, u32[]{:S(2)}, u32[]{:S(2)}) collective-permute-start(bf16[2,128,512]{1,2,0:T(8,128)(2,1)S(1)} %pad_maximum_fusion), channel_id=1, source_target_pairs={{0,4},{4,8},{8,12},{12,16},{16,20},{20,24},{24,28},{28,32},{32,36}... | collective-permute-start | bytes 786440 | tf_op jit(solution)/shard_map/ppermute | solution.py:33
  403.6 9.8 %collective-permute-start.1 = (bf16[2,128,512]{1,2,0:T(8,128)(2,1)S(1)}, bf16[2,128,512]{1,2,0:T(8,128)(2,1)S(1)}, u32[]{:S(2)}, u32[]{:S(2)}) collective-permute-start(bf16[2,128,512]{1,2,0:T(8,128)(2,1)S(1)} %collective-permute-done), channel_id=1, source_target_pairs={{0,4},{4,8},{8,12},{12,16},{16,20},{20,24},{24,28},{28,32},{32,36}... | collective-permute-start | bytes 786440 | tf_op jit(solution)/shard_map/ppermute | solution.py:33
  414.1 9.8 %collective-permute-start.2 = (bf16[2,128,512]{1,2,0:T(8,128)(2,1)S(1)}, bf16[2,128,512]{1,2,0:T(8,128)(2,1)S(1)}, u32[]{:S(2)}, u32[]{:S(2)}) collective-permute-start(bf16[2,128,512]{1,2,0:T(8,128)(2,1)S(1)} %collective-permute-done.1), channel_id=1, source_target_pairs={{0,4},{4,8},{8,12},{12,16},{16,20},{20,24},{24,28},{28,32},{32,36}... | collective-permute-start | bytes 786440 | tf_op jit(solution)/shard_map/ppermute | solution.py:33
  424.6 9.9 %collective-permute-start.3 = (bf16[2,128,512]{1,2,0:T(8,128)(2,1)S(1)}, bf16[2,128,512]{1,2,0:T(8,128)(2,1)}, u32[]{:S(2)}, u32[]{:S(2)}) collective-permute-start(bf16[2,128,512]{1,2,0:T(8,128)(2,1)S(1)} %collective-permute-done.2), channel_id=1, source_target_pairs={{0,4},{4,8},{8,12},{12,16},{16,20},{20,24},{24,28},{28,32},{32,36}... | collective-permute-start | bytes 786440 | tf_op jit(solution)/shard_map/ppermute | solution.py:33
  434.5 10.1 %collective-permute-start.4 = (bf16[2,128,512]{1,2,0:T(8,128)(2,1)}, bf16[2,128,512]{1,2,0:T(8,128)(2,1)}, u32[]{:S(2)}, u32[]{:S(2)}) collective-permute-start(bf16[2,128,512]{1,2,0:T(8,128)(2,1)} %collective-permute-done.3), channel_id=1, source_target_pairs={{0,4},{4,8},{8,12},{12,16},{16,20},{20,24},{24,28},{28,32},{32,36}... | collective-permute-start | bytes 786440 | tf_op jit(solution)/shard_map/ppermute | solution.py:33
  444.6 10.1 %collective-permute-start.5 = (bf16[2,128,512]{1,2,0:T(8,128)(2,1)}, bf16[2,128,512]{1,2,0:T(8,128)(2,1)}, u32[]{:S(2)}, u32[]{:S(2)}) collective-permute-start(bf16[2,128,512]{1,2,0:T(8,128)(2,1)} %collective-permute-done.4), channel_id=1, source_target_pairs={{0,4},{4,8},{8,12},{12,16},{16,20},{20,24},{24,28},{28,32},{32,36}... | collective-permute-start | bytes 786440 | tf_op jit(solution)/shard_map/ppermute | solution.py:33
  454.7 10.1 %collective-permute-start.6 = (bf16[2,128,512]{1,2,0:T(8,128)(2,1)}, bf16[2,128,512]{1,2,0:T(8,128)(2,1)}, u32[]{:S(2)}, u32[]{:S(2)}) collective-permute-start(bf16[2,128,512]{1,2,0:T(8,128)(2,1)} %collective-permute-done.5), channel_id=1, source_target_pairs={{0,4},{4,8},{8,12},{12,16},{16,20},{20,24},{24,28},{28,32},{32,36}... | collective-permute-start | bytes 786440 | tf_op jit(solution)/shard_map/ppermute | solution.py:33
  457.5 21.4 %copy-start.11 = (bf16[2,128,512]{1,2,0:T(8,128)(2,1)S(1)}, bf16[2,128,512]{1,2,0:T(8,128)(2,1)}, u32[]{:S(2)}) copy-start(bf16[2,128,512]{1,2,0:T(8,128)(2,1)} %copy-done.10) | copy-start | bytes 786436
  457.5 21.5 %copy-start.9 = (bf16[2,128,512]{1,2,0:T(8,128)(2,1)S(1)}, bf16[2,128,512]{1,2,0:T(8,128)(2,1)}, u32[]{:S(2)}) copy-start(bf16[2,128,512]{1,2,0:T(8,128)(2,1)} %copy-done.8) | copy-start | bytes 786436
  457.5 21.6 %copy-start.7 = (bf16[2,128,512]{1,2,0:T(8,128)(2,1)S(1)}, bf16[2,128,512]{1,2,0:T(8,128)(2,1)}, u32[]{:S(2)}) copy-start(bf16[2,128,512]{1,2,0:T(8,128)(2,1)} %copy-done.6) | copy-start | bytes 786436
  457.5 21.7 %copy-start.4 = (bf16[128,4,1,128]{0,3,2,1:T(8,128)(2,1)S(1)}, bf16[128,4,1,128]{0,3,2,1:T(8,128)(2,1)}, u32[]{:S(2)}) copy-start(bf16[128,4,1,128]{0,3,2,1:T(8,128)(2,1)} %copy-done.3) | copy-start | bytes 393220
  464.8 10.0 %collective-permute-start.7 = (bf16[2,128,512]{1,2,0:T(8,128)(2,1)}, bf16[2,128,512]{1,2,0:T(8,128)(2,1)S(1)}, u32[]{:S(2)}, u32[]{:S(2)}) collective-permute-start(bf16[2,128,512]{1,2,0:T(8,128)(2,1)} %collective-permute-done.6), channel_id=1, source_target_pairs={{0,4},{4,8},{8,12},{12,16},{16,20},{20,24},{24,28},{28,32},{32,36}... | collective-permute-start | bytes 786440 | tf_op jit(solution)/shard_map/ppermute | solution.py:33
  479.3 0.9 copy-start.16
  (6 other events, 4.1 us)
Sparse Core Ops, SparseCore 0:
  37.8 101.3 all-gather.4
  141.9 96.6 all-gather.6
  336.3 49.1 all-reduce.1
where the time goes:
time: 491 us; the launch traced here: 489 us
  waiting for transfers between devices  313 us (64%)
  matrix products  117 us (24%)
  local copies, waits for them, and re-layouts  21.9 us (4%)
  starting transfers between devices  15.6 us (3%)
  between operations  14.2 us (3%)
    all_gather x2, waiting for transfers between devices, carried_in(): everything = jax.tree.map(lambda part: lax.all_gather(part, axis), shard)  200 us
    dot_general x106, matrix products, product(): jnp.einsum('hij,hjk->hik', left, right, precision=lax.Precision.HIGHEST)  107 us
    ppermute x8, waiting for transfers between devices, passed_along(): return lax.ppermute(block, axis, route)  62.6 us
    psum x1, waiting for transfers between devices, body(): summed = lax.psum(term, 'head')  49.4 us
    ppermute x8, starting transfers between devices, passed_along(): return lax.ppermute(block, axis, route)  15.3 us
  transfers between devices with their start and end apart: 11, of which 11 were waited for; matrix products, arithmetic and copies ran while one was open for 0% of the time, Pallas kernels for 0%

commit v1 on v0

v1 whole, which is shorter than its diff:
```python
import functools

import jax
import jax.numpy as jnp
from jax import lax
from jax.experimental import pallas as pl
from jax.experimental.pallas import tpu as pltpu
from jax.sharding import PartitionSpec as P

WINDOW = 1024
WIDTH = 128
SCORE_SCALE = 10.0
F32 = jnp.float32
BF16 = jnp.bfloat16
HIGHEST = lax.Precision.HIGHEST
VMEM = pltpu.VMEM
SMEM = pltpu.SMEM
LIMIT = 40 * 1024 * 1024


def dot(left, right, contract=(1, 0), precision=None):
    return lax.dot_general(
        left,
        right,
        (((contract[0],), (contract[1],)), ((), ())),
        precision=precision,
        preferred_element_type=F32,
    )


def exact(left, right, contract=(1, 0)):
    return dot(left, right, contract, HIGHEST)


def iotas(rows, columns):
    return (
        lax.broadcasted_iota(jnp.int32, (rows, columns), 0),
        lax.broadcasted_iota(jnp.int32, (rows, columns), 1),
    )


def split_diagonal(matrix):
    row, column = iotas(WIDTH, WIDTH)
    high = matrix.astype(BF16)
    return high, jnp.where(row == column, matrix - high.astype(F32), 0.0)


def compose(left_t, left_o, right_t, right_o):
    left_high, left_rest = split_diagonal(left_t)
    right_high, right_rest = split_diagonal(right_t)
    left_column = jnp.sum(left_rest, axis=1, keepdims=True)
    right_row = jnp.sum(right_rest, axis=0, keepdims=True)
    offset = dot(left_high, right_o.astype(BF16)) + left_column * right_o + left_o
    product = dot(left_high, right_high) + left_column * right_t + left_high.astype(F32) * right_row
    return product, offset


def apply(left_t, left_o, state):
    left_high, left_rest = split_diagonal(left_t)
    left_column = jnp.sum(left_rest, axis=1, keepdims=True)
    return dot(left_high, state.astype(BF16)) + left_column * state + left_o


def store_payload(ref, pairs):
    row, _ = iotas(16, WIDTH)
    for n, (transition, offset) in enumerate(pairs):
        high, rest = split_diagonal(transition)
        ref[n * WIDTH : (n + 1) * WIDTH, 0:WIDTH] = high
        ref[n * WIDTH : (n + 1) * WIDTH, WIDTH : 2 * WIDTH] = offset.astype(BF16)
        line = jnp.sum(rest, axis=0, keepdims=True)
        ref[2 * WIDTH : 2 * WIDTH + 16, n * WIDTH : (n + 1) * WIDTH] = jnp.where(
            row == 0, line, 0.0
        ).astype(BF16)


def load_payload(ref, n):
    row, column = iotas(WIDTH, WIDTH)
    line = ref[2 * WIDTH : 2 * WIDTH + 16, n * WIDTH : (n + 1) * WIDTH].astype(F32)
    line = jnp.sum(line, axis=0, keepdims=True)
    transition = ref[n * WIDTH : (n + 1) * WIDTH, 0:WIDTH].astype(F32)
    transition = transition + jnp.where(row == column, line, 0.0)
    offset = ref[n * WIDTH : (n + 1) * WIDTH, WIDTH : 2 * WIDTH].astype(F32)
    return transition, offset


def to_unit(vectors):
    return vectors * lax.rsqrt(jnp.sum(vectors * vectors, axis=-1, keepdims=True) + 1e-06)


def lower_inverses(couplings):
    rows = couplings[0].shape[0]
    row, column = iotas(rows, rows)
    identity = (row == column).astype(F32)
    inside = (row >> 4) == (column >> 4)
    powers = [jnp.where(inside, c, 0.0) for c in couplings]
    results = [identity - p for p in powers]
    span = 2
    while span < 16:
        powers = [exact(p, p) for p in powers]
        results = [exact(r, identity + p) for r, p in zip(results, powers)]
        span *= 2
    shift = 4
    while (1 << shift) < rows:
        level = ((row >> (shift + 1)) == (column >> (shift + 1))) & ((row >> shift) > (column >> shift))
        crossing = [exact(r, jnp.where(level, c, 0.0)) for r, c in zip(results, couplings)]
        results = [r - exact(x, r) for r, x in zip(results, crossing)]
        shift += 1
    return results


def chunk_kernel(place, q_ref, k_ref, v_ref, g_ref, b_ref, local_ref, through_ref, own_ref, pay_ref, pairs):
    rows, groups = g_ref.shape
    core = place[1]
    row, column = iotas(rows, rows)
    causal = row >= column
    strict = row > column
    gates = g_ref[...]
    betas = b_ref[...]
    summed = exact(causal.astype(F32), gates)
    summed_row = exact(gates, (row <= column).astype(F32), (0, 0))
    keys, mixings, couplings, decayed = [], [], [], []
    for h in range(groups):
        span = slice(h * WIDTH, (h + 1) * WIDTH)
        key = to_unit(k_ref[:, span].astype(F32))
        query = to_unit(q_ref[:, span].astype(F32))
        along = summed[:, h : h + 1]
        spread = along - summed_row[h : h + 1, :]
        decay = jnp.where(causal, jnp.exp(jnp.where(causal, spread, 0.0)), 0.0)
        both = exact(jnp.concatenate([key, query], axis=0), key, (1, 1))
        couplings.append(jnp.where(strict, betas[:, h : h + 1] * decay * both[:rows], 0.0))
        mixings.append(both[rows:] * decay)
        keys.append(key)
        decayed.append(jnp.exp(along) * query)
    inverses = lower_inverses(couplings)
    for h in range(groups):
        span = slice(h * WIDTH, (h + 1) * WIDTH)
        along = summed[:, h : h + 1]
        last = summed[rows - 1 : rows, h : h + 1]
        beta = betas[:, h : h + 1]
        value = v_ref[:, span].astype(F32)
        made = exact(
            inverses[h],
            jnp.concatenate([beta * value, (beta * jnp.exp(along)) * keys[h]], axis=1),
        )
        ended = jnp.exp(last - along) * keys[h]
        effect = exact(ended, made, (0, 0))
        inner = exact(mixings[h], made)
        local_ref[h] = inner[:, :WIDTH]
        through_ref[h] = (decayed[h] - inner[:, WIDTH:]).astype(BF16)
        identity = iotas(WIDTH, WIDTH)
        kept = jnp.where(identity[0] == identity[1], jnp.exp(last), 0.0)
        pairs[h, :, 0:WIDTH] = kept - effect[:, WIDTH:]
        pairs[h, :, WIDTH:] = effect[:, :WIDTH]
    half = groups // 2
    own_ref[...] = pairs[pl.ds(core * half, half)]
    away = pairs[pl.ds((1 - core) * half, half)]
    store_payload(pay_ref, [(away[n, :, :WIDTH], away[n, :, WIDTH:]) for n in range(half)])


def pair_kernel(place, own_ref, recv_ref, now_ref, pay_ref, first_ref):
    core = place[1]
    pairs = []
    for n in range(own_ref.shape[0]):
        own = own_ref[n]
        other = jnp.concatenate(load_payload(recv_ref, n), axis=1)
        later = jnp.where(core == 1, own, other)
        sooner = jnp.where(core == 1, other, own)
        first_ref[n] = sooner
        pair = compose(later[:, :WIDTH], later[:, WIDTH:], sooner[:, :WIDTH], sooner[:, WIDTH:])
        now_ref[n, :, :WIDTH] = pair[0]
        now_ref[n, :, WIDTH:] = pair[1]
        pairs.append(pair)
    store_payload(pay_ref, pairs)


def step_kernel(now_ref, recv_ref, next_ref, pay_ref):
    pairs = []
    for n in range(now_ref.shape[0]):
        now = now_ref[n]
        pair = compose(now[:, :WIDTH], now[:, WIDTH:], *load_payload(recv_ref, n))
        next_ref[n, :, :WIDTH] = pair[0]
        next_ref[n, :, WIDTH:] = pair[1]
        pairs.append(pair)
    store_payload(pay_ref, pairs)


def far_kernel(now_ref, recv_ref, pay_ref, offset_ref):
    pairs = []
    for n in range(now_ref.shape[0]):
        now = now_ref[n]
        pair = compose(now[:, :WIDTH], now[:, WIDTH:], *load_payload(recv_ref, n))
        offset_ref[n * WIDTH : (n + 1) * WIDTH, :] = pair[1].astype(BF16)
        pairs.append(pair)
    store_payload(pay_ref, pairs)


def state_kernel(place, near_ref, far_ref, first_ref, mine_ref, away_ref):
    core = place[1]
    for n in range(first_ref.shape[0]):
        span = slice(n * WIDTH, (n + 1) * WIDTH)
        near = load_payload(near_ref, n)
        zeroth = apply(near[0], near[1], far_ref[span, :].astype(F32))
        first = first_ref[n]
        oneth = apply(first[:, :WIDTH], first[:, WIDTH:], zeroth)
        mine_ref[span, :] = jnp.where(core == 0, zeroth, oneth).astype(BF16)
        away_ref[span, :] = jnp.where(core == 0, oneth, zeroth).astype(BF16)


def out_kernel(place, local_ref, through_ref, mine_ref, recv_ref, w_ref, term_ref, *sent_refs):
    core = place[1]
    me = place[2]
    groups = local_ref.shape[0]
    half = groups // 2
    normed = []
    for h in range(groups):
        span = slice((h % half) * WIDTH, (h % half + 1) * WIDTH)
        state = jnp.where(core == h // half, mine_ref[span, :], recv_ref[span, :])
        result = local_ref[h] + dot(through_ref[h], state)
        normed.append(
            (
                result * lax.rsqrt(jnp.mean(result * result, axis=-1, keepdims=True) + 1e-05)
            ).astype(BF16)
        )
    normed = jnp.concatenate(normed, axis=1)
    width = term_ref.shape[1]
    count = len(sent_refs) + 1
    for r in range(count):
        begin = pl.multiple_of(lax.rem(me + r, count) * width, width)
        term = dot(normed, w_ref[:, pl.ds(begin, width)])
        if r == 0:
            term_ref[...] = term
        else:
            sent_refs[r - 1][...] = term.astype(BF16)


def hidden_kernel(place, stream_ref, term_ref, *refs):
    me = place[2]
    width = term_ref.shape[1]
    begin = pl.multiple_of(me * width, width)
    total = term_ref[...]
    for ref in refs[:-1]:
        total = total + ref[...].astype(F32)
    refs[-1][...] = (stream_ref[:, pl.ds(begin, width)].astype(F32) + total).astype(BF16)


def project_kernel(place, w_ref, *refs):
    me = place[2]
    blocks, (q_ref, kv_ref) = refs[:-2], refs[-2:]
    count = len(blocks)
    rows, width = blocks[0].shape
    values = [ref[...].astype(F32) for ref in blocks]
    squares = sum(jnp.sum(v * v, axis=-1, keepdims=True) for v in values)
    scale = lax.rsqrt(squares / (count * width) + 1e-05)
    total = None
    for r in range(count):
        begin = pl.multiple_of(lax.rem(me + count - r, count) * width, width)
        part = dot((values[r] * scale).astype(BF16), w_ref[pl.ds(begin, width), :])
        total = part if total is None else total + part
    groups = q_ref.shape[1] // WIDTH
    for h in range(groups):
        base = h * 3 * WIDTH
        span = slice(h * WIDTH, (h + 1) * WIDTH)
        q_ref[:, span] = to_unit(total[:, base : base + WIDTH]).astype(BF16)
        kv_ref[:, span] = to_unit(total[:, base + WIDTH : base + 2 * WIDTH]).astype(BF16)
        kv_ref[:, groups * WIDTH + h * WIDTH : groups * WIDTH + (h + 1) * WIDTH] = total[
            :, base + 2 * WIDTH : base + 3 * WIDTH
        ].astype(BF16)


def window_kernel(place, q_ref, *refs):
    seq, core = place[0], place[1]
    blocks, out_ref = refs[:-1], refs[-1]
    rows = q_ref.shape[0]
    groups = q_ref.shape[1] // WIDTH
    row, column = iotas(rows, rows)
    query_place = seq * rows + row
    mixed = [None] * groups
    totals = [None] * groups
    for n, ref in enumerate(blocks):
        owner = seq - 2 * (n // 2) if n % 2 == 0 else seq - 2 * (n // 2) + 1 - 2 * core
        key_place = owner * rows + column
        allowed = (key_place <= query_place) & (key_place > query_place - WINDOW) & (key_place >= 0)
        for h in range(groups):
            span = slice(h * WIDTH, (h + 1) * WIDTH)
            scores = SCORE_SCALE * dot(q_ref[:, span], ref[:, span], (1, 1))
            weights = jnp.where(allowed, jnp.exp(scores), 0.0)
            total = jnp.sum(weights, axis=-1, keepdims=True)
            part = dot(
                weights.astype(BF16),
                ref[:, (groups + h) * WIDTH : (groups + h + 1) * WIDTH],
            )
            mixed[h] = part if mixed[h] is None else mixed[h] + part
            totals[h] = total if totals[h] is None else totals[h] + total
    for h in range(groups):
        out_ref[:, h * WIDTH : (h + 1) * WIDTH] = (mixed[h] / totals[h]).astype(BF16)


def call(kernel, outs, smem=0, scratch=()):
    def run(*args):
        return pl.pallas_call(
            kernel,
            out_shape=[jax.ShapeDtypeStruct(shape, kind) for shape, kind in outs],
            in_specs=[pl.BlockSpec(memory_space=SMEM)] * smem
            + [pl.BlockSpec(memory_space=VMEM)] * (len(args) - smem),
            out_specs=[pl.BlockSpec(memory_space=VMEM)] * len(outs),
            scratch_shapes=list(scratch),
            compiler_params=pltpu.CompilerParams(vmem_limit_bytes=LIMIT),
        )(*args)

    return run


def moved(array, axis, distance):
    size = lax.axis_size(axis)
    return lax.ppermute(array, axis, [(i, i + distance) for i in range(size - distance)])


def turned(array, axis, distance):
    size = lax.axis_size(axis)
    return lax.ppermute(array, axis, [(i, (i + distance) % size) for i in range(size)])


def swapped(array):
    return lax.ppermute(array, "seq", [(i, i ^ 1) for i in range(lax.axis_size("seq"))])


def body(queries, keys, values, gate_log, beta, stream, w_out, w_qkv):
    rows, wide = queries.shape
    groups = gate_log.shape[1]
    half = groups // 2
    seq = lax.axis_index("seq")
    head = lax.axis_index("head")
    heads = lax.axis_size("head")
    length = lax.axis_size("seq")
    place = jnp.stack([seq, seq % 2, head]).astype(jnp.int32)
    pair_shape = ((half, WIDTH, 2 * WIDTH), F32)
    pay_shape = ((half * WIDTH + 16, 2 * WIDTH), BF16)
    state_shape = ((half * WIDTH, WIDTH), BF16)

    local, through, own, pay = call(
        chunk_kernel,
        [((groups, rows, WIDTH), F32), ((groups, rows, WIDTH), BF16), pair_shape, pay_shape],
        1,
        [pltpu.VMEM((groups, WIDTH, 2 * WIDTH), F32)],
    )(place, queries, keys, values, gate_log, beta)
    now, pay, first = call(pair_kernel, [pair_shape, pay_shape, pair_shape], 1)(
        place, own, swapped(pay)
    )
    distance = 2
    while distance * 4 < length:
        now, pay = call(step_kernel, [pair_shape, pay_shape])(now, moved(pay, "seq", distance))
        distance *= 2
    pay, offset = call(far_kernel, [pay_shape, state_shape])(now, moved(pay, "seq", distance))
    near = moved(pay, "seq", 2)
    far = moved(offset, "seq", distance * 2 + 2)
    mine, away = call(state_kernel, [state_shape, state_shape], 1)(place, near, far, first)
    terms = call(
        out_kernel,
        [((rows, wide), F32)] + [((rows, wide), BF16)] * (heads - 1),
        1,
    )(place, local, through, mine, swapped(away), w_out)
    received = [turned(terms[r], "head", r) for r in range(1, heads)]
    (hidden,) = call(hidden_kernel, [((rows, wide), BF16)], 1)(place, stream, terms[0], *received)
    others = [turned(hidden, "head", r) for r in range(1, heads)]
    unit_queries, pack = call(
        project_kernel, [((rows, wide), BF16), ((rows, 2 * wide), BF16)], 1
    )(place, w_qkv, hidden, *others)
    blocks = [pack, swapped(pack)]
    moving = pack
    for _ in range(WINDOW // (2 * rows)):
        moving = moved(moving, "seq", 2)
        blocks += [moving, swapped(moving)]
    (attended,) = call(window_kernel, [((rows, wide), BF16)], 1)(place, unit_queries, *blocks)
    return (hidden, attended)


def solution(mesh):
    in_specs = (
        P("seq", "head"),
        P("seq", "head"),
        P("seq", "head"),
        P("seq", "head"),
        P("seq", "head"),
        P("seq", None),
        P("head", None),
        P(None, "head"),
    )
    out_specs = (P("seq", "head"), P("seq", "head"))
    return jax.shard_map(body, mesh=mesh, in_specs=in_specs, out_specs=out_specs, check_vma=False)
```

time: 491 us -> 151 us (0.31)
  the two profiles are of different devices: /device:TPU:2 before, /device:TPU:7 now
where the time goes in v1:
time: 151 us
  waiting for transfers between devices  82.8 us (55%)
  starting transfers between devices  42.3 us (28%)
  Pallas kernels  16.5 us (11%)
  local copies, waits for them, and re-layouts  8.23 us (5%)
    ppermute x10, waiting for transfers between devices, moved(): lax.ppermute(array, axis, [(i, i + distance) for i in range(size - distan...  66.5 us
    ppermute x10, starting transfers between devices, moved(): lax.ppermute(array, axis, [(i, i + distance) for i in range(size - distan...  19.5 us
    pallas_call x11, Pallas kernels, run(): pl.pallas_call(kernel, out_shape=[jax.ShapeDtypeStruct(shape, kind) for s...  16.5 us
    ppermute x7, starting transfers between devices, swapped(): lax.ppermute(array, 'seq', [(i, i ^ 1) for i in range(lax.axis_size('seq'...  14.8 us
    ppermute x6, waiting for transfers between devices, turned(): lax.ppermute(array, axis, [(i, (i + distance) % size) for i in range(size)])  13.2 us
    unnamed x16, local copies, waits for them, and re-layouts  8.23 us
    ppermute x6, starting transfers between devices, turned(): lax.ppermute(array, axis, [(i, (i + distance) % size) for i in range(size)])  7.95 us
    ppermute x7, waiting for transfers between devices, swapped(): lax.ppermute(array, 'seq', [(i, i ^ 1) for i in range(lax.axis_size('seq'...  3.05 us
  transfers between devices with their start and end apart: 23, of which 17 were waited for; matrix products, arithmetic and copies ran while one was open for 0% of the time, Pallas kernels for 0%

profile of v1, /device:TPU:7, one launch (start us, length us, event | category | flops | bytes accessed | tf_op | source)
XLA Modules:
  0.0 150.7 jit_solution(822798795262191013)
XLA Ops:
  5.4 6.2 %shard_map.95 = (f32[4,128,128]{2,1,0:T(8,128)S(1)}, bf16[4,128,128]{2,1,0:T(8,128)(2,1)S(1)}, f32[2,128,256]{2,1,0:T(8,128)S(1)}, bf16[272,256]{1,0:T(8,128)(2,1)S(1)}) custom-call(s32[3]{0:T(128)S(1)} %pad_add_fusion.place, bf16[128,512]{1,0:T(8,128)(2,1)S(1)} %copy-done.4, bf16[128,512]{1,0:T(8,128)(2,1)S(1)} %copy-done.5, ...), custom_call_target="tpu_custom_call" | custom-call | tf_op jit(solution)/shard_map/pallas_call | solution.py:300
  14.2 3.5 %collective-permute-start.1 = (bf16[272,256]{1,0:T(8,128)(2,1)S(1)}, bf16[272,256]{1,0:T(8,128)(2,1)S(1)}, u32[]{:S(2)}, u32[]{:S(2)}) collective-permute-start(bf16[272,256]{1,0:T(8,128)(2,1)S(1)} %get-tuple-element.30), channel_id=1, source_target_pairs={{0,8},{4,12},{8,16},{12,20},{16,24},{20,28},{24,32},{28,36},{32,40... | collective-permute-start | bytes 417800 | tf_op jit(solution)/shard_map/ppermute | solution.py:315
  17.8 7.9 %collective-permute-done.1.recv_ref = bf16[272,256]{1,0:T(8,128)(2,1)S(1)} collective-permute-done((bf16[272,256]{1,0:T(8,128)(2,1)S(1)}, bf16[272,256]{1,0:T(8,128)(2,1)S(1)}, u32[]{:S(2)}, u32[]{:S(2)}) %collective-permute-start.1) | collective-permute-done | bytes 139296 | tf_op jit(solution)/shard_map/ppermute | solution.py:315
  25.9 1.9 %collective-permute-start.2 = (bf16[272,256]{1,0:T(8,128)(2,1)S(1)}, bf16[272,256]{1,0:T(8,128)(2,1)S(1)}, u32[]{:S(2)}, u32[]{:S(2)}) collective-permute-start(bf16[272,256]{1,0:T(8,128)(2,1)S(1)} %get-tuple-element.32), channel_id=1, source_target_pairs={{0,16},{4,20},{8,24},{12,28},{16,32},{20,36},{24,40},{28,44},{32,4... | collective-permute-start | bytes 417800 | tf_op jit(solution)/shard_map/ppermute | solution.py:315
  27.8 10.1 %collective-permute-done.2.recv_ref = bf16[272,256]{1,0:T(8,128)(2,1)S(1)} collective-permute-done((bf16[272,256]{1,0:T(8,128)(2,1)S(1)}, bf16[272,256]{1,0:T(8,128)(2,1)S(1)}, u32[]{:S(2)}, u32[]{:S(2)}) %collective-permute-start.2) | collective-permute-done | bytes 139296 | tf_op jit(solution)/shard_map/ppermute | solution.py:315
  38.2 1.9 %collective-permute-start.3 = (bf16[272,256]{1,0:T(8,128)(2,1)S(1)}, bf16[272,256]{1,0:T(8,128)(2,1)S(1)}, u32[]{:S(2)}, u32[]{:S(2)}) collective-permute-start(bf16[272,256]{1,0:T(8,128)(2,1)S(1)} %get-tuple-element.34), channel_id=1, source_target_pairs={{0,32},{4,36},{8,40},{12,44},{16,48},{20,52},{24,56},{28,60},{32,6... | collective-permute-start | bytes 417800 | tf_op jit(solution)/shard_map/ppermute | solution.py:315
  40.1 10.5 %collective-permute-done.3.recv_ref = bf16[272,256]{1,0:T(8,128)(2,1)S(1)} collective-permute-done((bf16[272,256]{1,0:T(8,128)(2,1)S(1)}, bf16[272,256]{1,0:T(8,128)(2,1)S(1)}, u32[]{:S(2)}, u32[]{:S(2)}) %collective-permute-start.3) | collective-permute-done | bytes 139296 | tf_op jit(solution)/shard_map/ppermute | solution.py:315
  52.1 4.5 %collective-permute-done.4.recv_ref = bf16[272,256]{1,0:T(8,128)(2,1)S(1)} collective-permute-done((bf16[272,256]{1,0:T(8,128)(2,1)S(1)}, bf16[272,256]{1,0:T(8,128)(2,1)S(1)}, u32[]{:S(2)}, u32[]{:S(2)}) %collective-permute-start.4) | collective-permute-done | bytes 139296 | tf_op jit(solution)/shard_map/ppermute | solution.py:315
  56.9 1.9 %collective-permute-start.5 = (bf16[272,256]{1,0:T(8,128)(2,1)S(1)}, bf16[272,256]{1,0:T(8,128)(2,1)S(1)}, u32[]{:S(2)}, u32[]{:S(2)}) collective-permute-start(bf16[272,256]{1,0:T(8,128)(2,1)S(1)} %get-tuple-element.37), channel_id=1, source_target_pairs={{0,8},{4,12},{8,16},{12,20},{16,24},{20,28},{24,32},{28,36},{32,40... | collective-permute-start | bytes 417800 | tf_op jit(solution)/shard_map/ppermute | solution.py:315
  60.1 7.7 %collective-permute-done.6.far_ref = bf16[256,128]{1,0:T(8,128)(2,1)S(1)} collective-permute-done((bf16[256,128]{1,0:T(8,128)(2,1)S(1)}, bf16[256,128]{1,0:T(8,128)(2,1)S(1)}, u32[]{:S(2)}, u32[]{:S(2)}) %collective-permute-start.6) | collective-permute-done | bytes 65568 | tf_op jit(solution)/shard_map/ppermute | solution.py:315
  68.7 3.5 %collective-permute-start.7 = (bf16[256,128]{1,0:T(8,128)(2,1)S(1)}, bf16[256,128]{1,0:T(8,128)(2,1)S(1)}, u32[]{:S(2)}, u32[]{:S(2)}) collective-permute-start(bf16[256,128]{1,0:T(8,128)(2,1)S(1)} %get-tuple-element.41), channel_id=1, source_target_pairs={{0,4},{4,0},{8,12},{12,8},{16,20},{20,16},{24,28},{28,24},{32,36},... | collective-permute-start | bytes 196616 | tf_op jit(solution)/shard_map/ppermute | solution.py:324
  77.3 2.6 %collective-permute-start.9 = (bf16[128,512]{1,0:T(8,128)(2,1)S(1)}, bf16[128,512]{1,0:T(8,128)(2,1)S(1)}, u32[]{:S(2)}, u32[]{:S(2)}) collective-permute-start(bf16[128,512]{1,0:T(8,128)(2,1)S(1)} %get-tuple-element.44), channel_id=1, source_target_pairs={{0,2},{1,3},{2,0},{3,1},{4,6},{5,7},{6,4},{7,5},{8,10},{9,11},{10,... | collective-permute-start | bytes 393224 | tf_op jit(solution)/shard_map/ppermute | solution.py:320
  82.0 3.9 %collective-permute-done.9.refs_1_ = bf16[128,512]{1,0:T(8,128)(2,1)S(1)} collective-permute-done((bf16[128,512]{1,0:T(8,128)(2,1)S(1)}, bf16[128,512]{1,0:T(8,128)(2,1)S(1)}, u32[]{:S(2)}, u32[]{:S(2)}) %collective-permute-start.9) | collective-permute-done | bytes 131104 | tf_op jit(solution)/shard_map/ppermute | solution.py:320
  88.3 2.0 %collective-permute-start.13 = (bf16[128,512]{1,0:T(8,128)(2,1)}, bf16[128,512]{1,0:T(8,128)(2,1)S(1)}, u32[]{:S(2)}, u32[]{:S(2)}) collective-permute-start(bf16[128,512]{1,0:T(8,128)(2,1)} %shard_map.103.refs_0_), channel_id=1, source_target_pairs={{0,3},{1,0},{2,1},{3,2},{4,7},{5,4},{6,5},{7,6},{8,11},{9,8},{10,9... | collective-permute-start | bytes 393224 | tf_op jit(solution)/shard_map/ppermute | solution.py:320
  91.2 2.6 %collective-permute-done.13.refs_3_ = bf16[128,512]{1,0:T(8,128)(2,1)S(1)} collective-permute-done((bf16[128,512]{1,0:T(8,128)(2,1)}, bf16[128,512]{1,0:T(8,128)(2,1)S(1)}, u32[]{:S(2)}, u32[]{:S(2)}) %collective-permute-start.13) | collective-permute-done | bytes 131104 | tf_op jit(solution)/shard_map/ppermute | solution.py:320
  93.7 2.2 %collective-permute-done.12.refs_2_ = bf16[128,512]{1,0:T(8,128)(2,1)S(1)} collective-permute-done((bf16[128,512]{1,0:T(8,128)(2,1)}, bf16[128,512]{1,0:T(8,128)(2,1)S(1)}, u32[]{:S(2)}, u32[]{:S(2)}) %collective-permute-start.12) | collective-permute-done | bytes 131104 | tf_op jit(solution)/shard_map/ppermute | solution.py:320
  95.9 3.5 %collective-permute-done.11.refs_1_ = bf16[128,512]{1,0:T(8,128)(2,1)S(1)} collective-permute-done((bf16[128,512]{1,0:T(8,128)(2,1)}, bf16[128,512]{1,0:T(8,128)(2,1)S(1)}, u32[]{:S(2)}, u32[]{:S(2)}) %collective-permute-start.11) | collective-permute-done | bytes 131104 | tf_op jit(solution)/shard_map/ppermute | solution.py:320
  104.0 8.5 %collective-permute-done.15.refs_2_ = bf16[128,1024]{1,0:T(8,128)(2,1)S(1)} collective-permute-done((bf16[128,1024]{1,0:T(8,128)(2,1)S(1)}, bf16[128,1024]{1,0:T(8,128)(2,1)S(1)}, u32[]{:S(2)}, u32[]{:S(2)}) %collective-permute-start.15) | collective-permute-done | bytes 262176 | tf_op jit(solution)/shard_map/ppermute | solution.py:315
  114.4 7.6 %collective-permute-done.17.refs_4_ = bf16[128,1024]{1,0:T(8,128)(2,1)S(1)} collective-permute-done((bf16[128,1024]{1,0:T(8,128)(2,1)S(1)}, bf16[128,1024]{1,0:T(8,128)(2,1)S(1)}, u32[]{:S(2)}, u32[]{:S(2)}) %collective-permute-start.17) | collective-permute-done | bytes 262176 | tf_op jit(solution)/shard_map/ppermute | solution.py:315
  124.0 7.3 %collective-permute-done.19.refs_6_ = bf16[128,1024]{1,0:T(8,128)(2,1)S(1)} collective-permute-done((bf16[128,1024]{1,0:T(8,128)(2,1)S(1)}, bf16[128,1024]{1,0:T(8,128)(2,1)S(1)}, u32[]{:S(2)}, u32[]{:S(2)}) %collective-permute-start.19) | collective-permute-done | bytes 262176 | tf_op jit(solution)/shard_map/ppermute | solution.py:315
  133.2 4.4 %collective-permute-start.14 = (bf16[128,1024]{1,0:T(8,128)(2,1)S(1)}, bf16[128,1024]{1,0:T(8,128)(2,1)S(1)}, u32[]{:S(2)}, u32[]{:S(2)}) collective-permute-start(bf16[128,1024]{1,0:T(8,128)(2,1)S(1)} %get-tuple-element.47.refs_0_), channel_id=1, source_target_pairs={{0,4},{4,0},{8,12},{12,8},{16,20},{20,16},{24,28},{28,24},{32,36},... | collective-permute-start | bytes 786440 | tf_op jit(solution)/shard_map/ppermute | solution.py:324
  138.2 2.3 %collective-permute-done.21.refs_8_ = bf16[128,1024]{1,0:T(8,128)(2,1)S(1)} collective-permute-done((bf16[128,1024]{1,0:T(8,128)(2,1)S(1)}, bf16[128,1024]{1,0:T(8,128)(2,1)S(1)}, u32[]{:S(2)}, u32[]{:S(2)}) %collective-permute-start.21) | collective-permute-done | bytes 262176 | tf_op jit(solution)/shard_map/ppermute | solution.py:315
  140.5 5.5 %collective-permute-start.22 = (bf16[128,1024]{1,0:T(8,128)(2,1)S(1)}, bf16[128,1024]{1,0:T(8,128)(2,1)S(1)}, u32[]{:S(2)}, u32[]{:S(2)}) collective-permute-start(bf16[128,1024]{1,0:T(8,128)(2,1)S(1)} %collective-permute-done.21.refs_8_), channel_id=1, source_target_pairs={{0,4},{4,0},{8,12},{12,8},{16,20},{20,16},{24,28},{28,24},{32,36},... | collective-permute-start | bytes 786440 | tf_op jit(solution)/shard_map/ppermute | solution.py:324
  147.1 3.6 %shard_map.105 = bf16[128,512]{1,0:T(8,128)(2,1)} custom-call(s32[3]{0:T(128)S(1)} %pad_add_fusion.place, bf16[128,512]{1,0:T(8,128)(2,1)S(1)} %get-tuple-element.46.q_ref, bf16[128,1024]{1,0:T(8,128)(2,1)S(1)} %get-tuple-element.47.refs_0_, bf16[128,1024]{1,0:T(8,128)(2,1)S(1)} %collective-permute-done.14.refs_1_, ...), custom_call_target="tpu_custom_call" | custom-call | tf_op jit(solution)/shard_map/pallas_call | solution.py:300
  (50 shorter events, 34.1 us)
Async XLA Ops:
  2.2 97.2 %copy-start = (bf16[2048,1536]{1,0:T(8,128)(2,1)S(1)}, bf16[2048,1536]{1,0:T(8,128)(2,1)}, u32[]{:S(2)}) copy-start(bf16[2048,1536]{1,0:T(8,128)(2,1)} %w_ref.3) | copy-start | bytes 18874372
  11.7 1.8 %collective-permute-start = (bf16[272,256]{1,0:T(8,128)(2,1)S(1)}, bf16[272,256]{1,0:T(8,128)(2,1)S(1)}, u32[]{:S(2)}, u32[]{:S(2)}) collective-permute-start(bf16[272,256]{1,0:T(8,128)(2,1)S(1)} %get-tuple-element.28), channel_id=1, source_target_pairs={{0,4},{4,0},{8,12},{12,8},{16,20},{20,16},{24,28},{28,24},{32,36},... | collective-permute-start | bytes 417800 | tf_op jit(solution)/shard_map/ppermute | solution.py:324
  14.2 11.5 %collective-permute-start.1 = (bf16[272,256]{1,0:T(8,128)(2,1)S(1)}, bf16[272,256]{1,0:T(8,128)(2,1)S(1)}, u32[]{:S(2)}, u32[]{:S(2)}) collective-permute-start(bf16[272,256]{1,0:T(8,128)(2,1)S(1)} %get-tuple-element.30), channel_id=1, source_target_pairs={{0,8},{4,12},{8,16},{12,20},{16,24},{20,28},{24,32},{28,36},{32,40... | collective-permute-start | bytes 417800 | tf_op jit(solution)/shard_map/ppermute | solution.py:315
  25.9 12.0 %collective-permute-start.2 = (bf16[272,256]{1,0:T(8,128)(2,1)S(1)}, bf16[272,256]{1,0:T(8,128)(2,1)S(1)}, u32[]{:S(2)}, u32[]{:S(2)}) collective-permute-start(bf16[272,256]{1,0:T(8,128)(2,1)S(1)} %get-tuple-element.32), channel_id=1, source_target_pairs={{0,16},{4,20},{8,24},{12,28},{16,32},{20,36},{24,40},{28,44},{32,4... | collective-permute-start | bytes 417800 | tf_op jit(solution)/shard_map/ppermute | solution.py:315
  38.2 12.4 %collective-permute-start.3 = (bf16[272,256]{1,0:T(8,128)(2,1)S(1)}, bf16[272,256]{1,0:T(8,128)(2,1)S(1)}, u32[]{:S(2)}, u32[]{:S(2)}) collective-permute-start(bf16[272,256]{1,0:T(8,128)(2,1)S(1)} %get-tuple-element.34), channel_id=1, source_target_pairs={{0,32},{4,36},{8,40},{12,44},{16,48},{20,52},{24,56},{28,60},{32,6... | collective-permute-start | bytes 417800 | tf_op jit(solution)/shard_map/ppermute | solution.py:315
  50.8 5.8 %collective-permute-start.4 = (bf16[272,256]{1,0:T(8,128)(2,1)S(1)}, bf16[272,256]{1,0:T(8,128)(2,1)S(1)}, u32[]{:S(2)}, u32[]{:S(2)}) collective-permute-start(bf16[272,256]{1,0:T(8,128)(2,1)S(1)} %get-tuple-element.36), channel_id=1, source_target_pairs={{0,64},{4,68},{8,72},{12,76},{16,80},{20,84},{24,88},{28,92},{32,9... | collective-permute-start | bytes 417800 | tf_op jit(solution)/shard_map/ppermute | solution.py:315
  56.9 11.0 %collective-permute-start.5 = (bf16[272,256]{1,0:T(8,128)(2,1)S(1)}, bf16[272,256]{1,0:T(8,128)(2,1)S(1)}, u32[]{:S(2)}, u32[]{:S(2)}) collective-permute-start(bf16[272,256]{1,0:T(8,128)(2,1)S(1)} %get-tuple-element.37), channel_id=1, source_target_pairs={{0,8},{4,12},{8,16},{12,20},{16,24},{20,28},{24,32},{28,36},{32,40... | collective-permute-start | bytes 417800 | tf_op jit(solution)/shard_map/ppermute | solution.py:315
  58.8 9.0 %collective-permute-start.6 = (bf16[256,128]{1,0:T(8,128)(2,1)S(1)}, bf16[256,128]{1,0:T(8,128)(2,1)S(1)}, u32[]{:S(2)}, u32[]{:S(2)}) collective-permute-start(bf16[256,128]{1,0:T(8,128)(2,1)S(1)} %get-tuple-element.38), channel_id=1, source_target_pairs={{0,136},{4,140},{8,144},{12,148},{16,152},{20,156},{24,160},{28,16... | collective-permute-start | bytes 196616 | tf_op jit(solution)/shard_map/ppermute | solution.py:315
  68.7 4.4 %collective-permute-start.7 = (bf16[256,128]{1,0:T(8,128)(2,1)S(1)}, bf16[256,128]{1,0:T(8,128)(2,1)S(1)}, u32[]{:S(2)}, u32[]{:S(2)}) collective-permute-start(bf16[256,128]{1,0:T(8,128)(2,1)S(1)} %get-tuple-element.41), channel_id=1, source_target_pairs={{0,4},{4,0},{8,12},{12,8},{16,20},{20,16},{24,28},{28,24},{32,36},... | collective-permute-start | bytes 196616 | tf_op jit(solution)/shard_map/ppermute | solution.py:324
  75.9 6.1 %collective-permute-start.8 = (bf16[128,512]{1,0:T(8,128)(2,1)S(1)}, bf16[128,512]{1,0:T(8,128)(2,1)S(1)}, u32[]{:S(2)}, u32[]{:S(2)}) collective-permute-start(bf16[128,512]{1,0:T(8,128)(2,1)S(1)} %get-tuple-element.43), channel_id=1, source_target_pairs={{0,1},{1,2},{2,3},{3,0},{4,5},{5,6},{6,7},{7,4},{8,9},{9,10},{10,1... | collective-permute-start | bytes 393224 | tf_op jit(solution)/shard_map/ppermute | solution.py:320
  77.3 8.7 %collective-permute-start.9 = (bf16[128,512]{1,0:T(8,128)(2,1)S(1)}, bf16[128,512]{1,0:T(8,128)(2,1)S(1)}, u32[]{:S(2)}, u32[]{:S(2)}) collective-permute-start(bf16[128,512]{1,0:T(8,128)(2,1)S(1)} %get-tuple-element.44), channel_id=1, source_target_pairs={{0,2},{1,3},{2,0},{3,1},{4,6},{5,7},{6,4},{7,5},{8,10},{9,11},{10,... | collective-permute-start | bytes 393224 | tf_op jit(solution)/shard_map/ppermute | solution.py:320
  79.9 6.1 %collective-permute-start.10 = (bf16[128,512]{1,0:T(8,128)(2,1)S(1)}, bf16[128,512]{1,0:T(8,128)(2,1)S(1)}, u32[]{:S(2)}, u32[]{:S(2)}) collective-permute-start(bf16[128,512]{1,0:T(8,128)(2,1)S(1)} %get-tuple-element.45), channel_id=1, source_target_pairs={{0,3},{1,0},{2,1},{3,2},{4,7},{5,4},{6,5},{7,6},{8,11},{9,8},{10,9... | collective-permute-start | bytes 393224 | tf_op jit(solution)/shard_map/ppermute | solution.py:320
  88.3 5.5 %collective-permute-start.13 = (bf16[128,512]{1,0:T(8,128)(2,1)}, bf16[128,512]{1,0:T(8,128)(2,1)S(1)}, u32[]{:S(2)}, u32[]{:S(2)}) collective-permute-start(bf16[128,512]{1,0:T(8,128)(2,1)} %shard_map.103.refs_0_), channel_id=1, source_target_pairs={{0,3},{1,0},{2,1},{3,2},{4,7},{5,4},{6,5},{7,6},{8,11},{9,8},{10,9... | collective-permute-start | bytes 393224 | tf_op jit(solution)/shard_map/ppermute | solution.py:320
  90.3 5.6 %collective-permute-start.12 = (bf16[128,512]{1,0:T(8,128)(2,1)}, bf16[128,512]{1,0:T(8,128)(2,1)S(1)}, u32[]{:S(2)}, u32[]{:S(2)}) collective-permute-start(bf16[128,512]{1,0:T(8,128)(2,1)} %shard_map.103.refs_0_), channel_id=1, source_target_pairs={{0,2},{1,3},{2,0},{3,1},{4,6},{5,7},{6,4},{7,5},{8,10},{9,11},{10,... | collective-permute-start | bytes 393224 | tf_op jit(solution)/shard_map/ppermute | solution.py:320
  91.0 8.4 %collective-permute-start.11 = (bf16[128,512]{1,0:T(8,128)(2,1)}, bf16[128,512]{1,0:T(8,128)(2,1)S(1)}, u32[]{:S(2)}, u32[]{:S(2)}) collective-permute-start(bf16[128,512]{1,0:T(8,128)(2,1)} %shard_map.103.refs_0_), channel_id=1, source_target_pairs={{0,1},{1,2},{2,3},{3,0},{4,5},{5,6},{6,7},{7,4},{8,9},{9,10},{10,1... | collective-permute-start | bytes 393224 | tf_op jit(solution)/shard_map/ppermute | solution.py:320
  102.0 10.5 %collective-permute-start.15 = (bf16[128,1024]{1,0:T(8,128)(2,1)S(1)}, bf16[128,1024]{1,0:T(8,128)(2,1)S(1)}, u32[]{:S(2)}, u32[]{:S(2)}) collective-permute-start(bf16[128,1024]{1,0:T(8,128)(2,1)S(1)} %get-tuple-element.47.refs_0_), channel_id=1, source_target_pairs={{0,8},{4,12},{8,16},{12,20},{16,24},{20,28},{24,32},{28,36},{32,40... | collective-permute-start | bytes 786440 | tf_op jit(solution)/shard_map/ppermute | solution.py:315
  112.5 9.5 %collective-permute-start.17 = (bf16[128,1024]{1,0:T(8,128)(2,1)S(1)}, bf16[128,1024]{1,0:T(8,128)(2,1)S(1)}, u32[]{:S(2)}, u32[]{:S(2)}) collective-permute-start(bf16[128,1024]{1,0:T(8,128)(2,1)S(1)} %collective-permute-done.15.refs_2_), channel_id=1, source_target_pairs={{0,8},{4,12},{8,16},{12,20},{16,24},{20,28},{24,32},{28,36},{32,40... | collective-permute-start | bytes 786440 | tf_op jit(solution)/shard_map/ppermute | solution.py:315
  122.0 9.2 %collective-permute-start.19 = (bf16[128,1024]{1,0:T(8,128)(2,1)S(1)}, bf16[128,1024]{1,0:T(8,128)(2,1)S(1)}, u32[]{:S(2)}, u32[]{:S(2)}) collective-permute-start(bf16[128,1024]{1,0:T(8,128)(2,1)S(1)} %collective-permute-done.17.refs_4_), channel_id=1, source_target_pairs={{0,8},{4,12},{8,16},{12,20},{16,24},{20,28},{24,32},{28,36},{32,40... | collective-permute-start | bytes 786440 | tf_op jit(solution)/shard_map/ppermute | solution.py:315
  131.3 9.2 %collective-permute-start.21 = (bf16[128,1024]{1,0:T(8,128)(2,1)S(1)}, bf16[128,1024]{1,0:T(8,128)(2,1)S(1)}, u32[]{:S(2)}, u32[]{:S(2)}) collective-permute-start(bf16[128,1024]{1,0:T(8,128)(2,1)S(1)} %collective-permute-done.19.refs_6_), channel_id=1, source_target_pairs={{0,8},{4,12},{8,16},{12,20},{16,24},{20,28},{24,32},{28,36},{32,40... | collective-permute-start | bytes 786440 | tf_op jit(solution)/shard_map/ppermute | solution.py:315
  133.2 12.8 %collective-permute-start.14 = (bf16[128,1024]{1,0:T(8,128)(2,1)S(1)}, bf16[128,1024]{1,0:T(8,128)(2,1)S(1)}, u32[]{:S(2)}, u32[]{:S(2)}) collective-permute-start(bf16[128,1024]{1,0:T(8,128)(2,1)S(1)} %get-tuple-element.47.refs_0_), channel_id=1, source_target_pairs={{0,4},{4,0},{8,12},{12,8},{16,20},{20,16},{24,28},{28,24},{32,36},... | collective-permute-start | bytes 786440 | tf_op jit(solution)/shard_map/ppermute | solution.py:324
  137.6 8.4 %collective-permute-start.16 = (bf16[128,1024]{1,0:T(8,128)(2,1)S(1)}, bf16[128,1024]{1,0:T(8,128)(2,1)S(1)}, u32[]{:S(2)}, u32[]{:S(2)}) collective-permute-start(bf16[128,1024]{1,0:T(8,128)(2,1)S(1)} %collective-permute-done.15.refs_2_), channel_id=1, source_target_pairs={{0,4},{4,0},{8,12},{12,8},{16,20},{20,16},{24,28},{28,24},{32,36},... | collective-permute-start | bytes 786440 | tf_op jit(solution)/shard_map/ppermute | solution.py:324
  137.7 8.3 %collective-permute-start.18 = (bf16[128,1024]{1,0:T(8,128)(2,1)S(1)}, bf16[128,1024]{1,0:T(8,128)(2,1)S(1)}, u32[]{:S(2)}, u32[]{:S(2)}) collective-permute-start(bf16[128,1024]{1,0:T(8,128)(2,1)S(1)} %collective-permute-done.17.refs_4_), channel_id=1, source_target_pairs={{0,4},{4,0},{8,12},{12,8},{16,20},{20,16},{24,28},{28,24},{32,36},... | collective-permute-start | bytes 786440 | tf_op jit(solution)/shard_map/ppermute | solution.py:324
  138.1 7.9 %collective-permute-start.20 = (bf16[128,1024]{1,0:T(8,128)(2,1)S(1)}, bf16[128,1024]{1,0:T(8,128)(2,1)S(1)}, u32[]{:S(2)}, u32[]{:S(2)}) collective-permute-start(bf16[128,1024]{1,0:T(8,128)(2,1)S(1)} %collective-permute-done.19.refs_6_), channel_id=1, source_target_pairs={{0,4},{4,0},{8,12},{12,8},{16,20},{20,16},{24,28},{28,24},{32,36},... | collective-permute-start | bytes 786440 | tf_op jit(solution)/shard_map/ppermute | solution.py:324
  140.5 6.6 %collective-permute-start.22 = (bf16[128,1024]{1,0:T(8,128)(2,1)S(1)}, bf16[128,1024]{1,0:T(8,128)(2,1)S(1)}, u32[]{:S(2)}, u32[]{:S(2)}) collective-permute-start(bf16[128,1024]{1,0:T(8,128)(2,1)S(1)} %collective-permute-done.21.refs_8_), channel_id=1, source_target_pairs={{0,4},{4,0},{8,12},{12,8},{16,20},{20,16},{24,28},{28,24},{32,36},... | collective-permute-start | bytes 786440 | tf_op jit(solution)/shard_map/ppermute | solution.py:324
  (6 other events, 6.7 us)

commit v2 on v1

v2 whole, which is shorter than its diff:
```python
import functools

import jax
import jax.numpy as jnp
from jax import lax
from jax.experimental import pallas as pl
from jax.experimental.pallas import tpu as pltpu
from jax.sharding import PartitionSpec as P

WINDOW = 1024
WIDTH = 128
SCORE_SCALE = 10.0
F32 = jnp.float32
BF16 = jnp.bfloat16
HIGHEST = lax.Precision.HIGHEST
VMEM = pltpu.VMEM
SMEM = pltpu.SMEM
LIMIT = 16 * 1024 * 1024
CHUNK_LIMIT = 54579 * 1024


def dot(left, right, contract=(1, 0), precision=None):
    return lax.dot_general(
        left,
        right,
        (((contract[0],), (contract[1],)), ((), ())),
        precision=precision,
        preferred_element_type=F32,
    )


def exact(left, right, contract=(1, 0)):
    return dot(left, right, contract, HIGHEST)


def iotas(rows, columns):
    return (
        lax.broadcasted_iota(jnp.int32, (rows, columns), 0),
        lax.broadcasted_iota(jnp.int32, (rows, columns), 1),
    )


def fine(left, right, contract=(1, 0)):
    left_high = left.astype(BF16)
    right_high = right.astype(BF16)
    left_low = (left - left_high.astype(F32)).astype(BF16)
    right_low = (right - right_high.astype(F32)).astype(BF16)
    return (
        dot(left_high, right_high, contract)
        + dot(left_high, right_low, contract)
        + dot(left_low, right_high, contract)
    )


def split_diagonal(matrix):
    row, column = iotas(WIDTH, WIDTH)
    high = matrix.astype(BF16)
    return high, jnp.where(row == column, matrix - high.astype(F32), 0.0)


def compose(left, right):
    left_t, left_o = left
    right_t, right_o = right
    left_high, left_rest = split_diagonal(left_t)
    right_high, right_rest = split_diagonal(right_t)
    left_column = jnp.sum(left_rest, axis=1, keepdims=True)
    right_row = jnp.sum(right_rest, axis=0, keepdims=True)
    offset = dot(left_high, right_o.astype(BF16)) + left_column * right_o + left_o
    product = dot(left_high, right_high) + left_column * right_t + left_high.astype(F32) * right_row
    return product, offset


def apply(left, state):
    left_t, left_o = left
    left_high, left_rest = split_diagonal(left_t)
    left_column = jnp.sum(left_rest, axis=1, keepdims=True)
    return dot(left_high, state.astype(BF16)) + left_column * state + left_o


def store_payload(ref, pair):
    row, _ = iotas(16, 2 * WIDTH)
    transition, offset = pair
    high, rest = split_diagonal(transition)
    ref[0:WIDTH, 0:WIDTH] = high
    ref[0:WIDTH, WIDTH : 2 * WIDTH] = offset.astype(BF16)
    line = jnp.sum(rest, axis=0, keepdims=True)
    line = jnp.concatenate([line, jnp.zeros_like(line)], axis=1)
    ref[WIDTH : WIDTH + 16, :] = jnp.where(row == 0, line, 0.0).astype(BF16)


def load_payload(ref):
    row, column = iotas(WIDTH, WIDTH)
    line = ref[WIDTH : WIDTH + 16, 0:WIDTH].astype(F32)
    line = jnp.sum(line, axis=0, keepdims=True)
    transition = ref[0:WIDTH, 0:WIDTH].astype(F32)
    transition = transition + jnp.where(row == column, line, 0.0)
    return transition, ref[0:WIDTH, WIDTH : 2 * WIDTH].astype(F32)


def joined(pair):
    return jnp.concatenate(pair, axis=1)


def parted(array):
    return array[:, :WIDTH], array[:, WIDTH:]


def to_unit(vectors):
    return vectors * lax.rsqrt(jnp.sum(vectors * vectors, axis=-1, keepdims=True) + 1e-06)


def lower_inverses(couplings):
    rows = couplings[0].shape[0]
    row, column = iotas(rows, rows)
    identity = (row == column).astype(F32)
    inside = (row >> 3) == (column >> 3)
    powers = [jnp.where(inside, c, 0.0) for c in couplings]
    results = [identity - p for p in powers]
    span = 2
    while span < 8:
        powers = [fine(p, p) for p in powers]
        results = [fine(r, identity + p) for r, p in zip(results, powers)]
        span *= 2
    shift = 3
    while (1 << shift) < rows:
        level = ((row >> (shift + 1)) == (column >> (shift + 1))) & ((row >> shift) > (column >> shift))
        crossing = [fine(r, jnp.where(level, c, 0.0)) for r, c in zip(results, couplings)]
        results = [r - fine(x, r) for r, x in zip(results, crossing)]
        shift += 1
    return results


def chunk_kernel(
    place,
    g_ref,
    b_ref,
    q_hbm,
    k_hbm,
    v_hbm,
    local_ref,
    through_ref,
    own_ref,
    pay1_ref,
    pay2_ref,
    pay3_ref,
    q_ref,
    k_ref,
    v_ref,
    pairs,
    sems,
):
    part = place[1]
    groups, rows = g_ref.shape
    loads = [
        pltpu.make_async_copy(src, dst, sems.at[n])
        for n, (src, dst) in enumerate(
            [
                (k_hbm, k_ref),
                (q_hbm, q_ref),
                (v_hbm, v_ref),
            ]
        )
    ]
    for load in loads:
        load.start()
    row, column = iotas(rows, rows)
    causal = row >= column
    strict = row > column
    gates = g_ref[...]
    summed = exact(causal.astype(F32), gates, (1, 1))
    summed_row = exact(gates, (row <= column).astype(F32))
    betas = exact((row == column).astype(F32), b_ref[...], (1, 1))
    loads[0].wait()
    loads[1].wait()
    keys, mixings, couplings, decayed = [], [], [], []
    for h in range(groups):
        span = slice(h * WIDTH, (h + 1) * WIDTH)
        key = to_unit(k_ref[:, span].astype(F32)).astype(BF16)
        query = to_unit(q_ref[:, span].astype(F32)).astype(BF16)
        along = summed[:, h : h + 1]
        spread = along - summed_row[h : h + 1, :]
        decay = jnp.where(causal, jnp.exp(jnp.where(causal, spread, 0.0)), 0.0)
        both = dot(jnp.concatenate([key, query], axis=0), key, (1, 1))
        couplings.append(jnp.where(strict, betas[:, h : h + 1] * decay * both[:rows], 0.0))
        mixings.append((both[rows:] * decay).astype(BF16))
        keys.append(key.astype(F32))
        decayed.append(jnp.exp(along) * query.astype(F32))
    inverses = lower_inverses(couplings)
    loads[2].wait()
    for h in range(groups):
        span = slice(h * WIDTH, (h + 1) * WIDTH)
        along = summed[:, h : h + 1]
        last = summed[rows - 1 : rows, h : h + 1]
        beta = betas[:, h : h + 1]
        value = v_ref[:, span].astype(F32)
        made = fine(
            inverses[h],
            jnp.concatenate([beta * value, (beta * jnp.exp(along)) * keys[h]], axis=1),
        ).astype(BF16)
        ended = (jnp.exp(last - along) * keys[h]).astype(BF16)
        effect = dot(ended, made, (0, 0))
        inner = dot(mixings[h], made)
        local_ref[h] = inner[:, :WIDTH].astype(BF16)
        through_ref[h] = (decayed[h] - inner[:, WIDTH:]).astype(BF16)
        identity = iotas(WIDTH, WIDTH)
        kept = jnp.where(identity[0] == identity[1], jnp.exp(last), 0.0)
        pairs[h, :, 0:WIDTH] = kept - effect[:, WIDTH:]
        pairs[h, :, WIDTH:] = effect[:, :WIDTH]
    own_ref[...] = pairs[part]
    for r, ref in ((1, pay1_ref), (2, pay2_ref), (3, pay3_ref)):
        store_payload(ref, parted(pairs[part ^ r]))


def group_kernel(place, own_ref, recv1_ref, recv2_ref, recv3_ref, before_ref, all_ref, pay_ref, pairs):
    part = place[1]
    pairs[part] = own_ref[...]
    for r, ref in ((1, recv1_ref), (2, recv2_ref), (3, recv3_ref)):
        pairs[part ^ r] = joined(load_payload(ref))
    blocks = [parted(pairs[n]) for n in range(4)]
    total = blocks[0]
    for n in range(1, 4):
        before_ref[n - 1] = joined(total)
        total = compose(blocks[n], total)
    all_ref[...] = joined(total)
    store_payload(pay_ref, total)


def fetch_kernel(place, all_ref, wout_ref, wqkv_ref, stream_ref, wout_out, wqkv_out, stream_out, all_out, sems):
    width = stream_out.shape[1]
    begin = pl.multiple_of(place[2] * width, width)
    loads = [
        pltpu.make_async_copy(src, dst, sems.at[n])
        for n, (src, dst) in enumerate(
            [
                (wout_ref, wout_out),
                (wqkv_ref, wqkv_out),
                (stream_ref.at[:, pl.ds(begin, width)], stream_out),
            ]
        )
    ]
    for load in loads:
        load.start()
    all_out[...] = all_ref[...]
    for load in loads:
        load.wait()


def row_kernel(place, all_ref, recv1_ref, recv2_ref, recv3_ref, before_ref, pay_ref, pairs, starts):
    group = place[3]
    pairs[group] = all_ref[...]
    for d, ref in ((1, recv1_ref), (2, recv2_ref), (3, recv3_ref)):
        pairs[(group + 4 - d) & 3] = joined(load_payload(ref))
    row, column = iotas(WIDTH, 2 * WIDTH)
    starts[0] = (row == column).astype(F32)
    total = parted(pairs[0])
    for n in range(1, 4):
        starts[n] = joined(total)
        total = compose(parted(pairs[n]), total)
    before_ref[...] = starts[group]
    store_payload(pay_ref, total)


def state_kernel(
    place, row1_ref, row2_ref, row3_ref, before_row_ref, before_ref, mine_ref, out1_ref, out2_ref, out3_ref, states
):
    part = place[1]
    state = load_payload(row3_ref)[1]
    state = apply(load_payload(row2_ref), state)
    state = apply(load_payload(row1_ref), state)
    state = apply(parted(before_row_ref[...]), state)
    states[0] = state.astype(BF16)
    for n in range(3):
        states[n + 1] = apply(parted(before_ref[n]), state).astype(BF16)
    mine_ref[...] = states[part]
    for r, ref in ((1, out1_ref), (2, out2_ref), (3, out3_ref)):
        ref[...] = states[part ^ r]


def out_kernel(
    place, local_ref, through_ref, mine_ref, recv1_ref, recv2_ref, recv3_ref, w_ref, term_ref, *refs
):
    part = place[1]
    me = place[2]
    sent_refs, states = refs[:-1], refs[-1]
    groups = local_ref.shape[0]
    states[part] = mine_ref[...]
    for r, ref in ((1, recv1_ref), (2, recv2_ref), (3, recv3_ref)):
        states[part ^ r] = ref[...]
    normed = []
    for h in range(groups):
        result = local_ref[h].astype(F32) + dot(through_ref[h], states[h])
        normed.append(
            (
                result * lax.rsqrt(jnp.mean(result * result, axis=-1, keepdims=True) + 1e-05)
            ).astype(BF16)
        )
    normed = jnp.concatenate(normed, axis=1)
    width = term_ref.shape[1]
    count = len(sent_refs) + 1
    for r in range(count):
        begin = pl.multiple_of(lax.rem(me + r, count) * width, width)
        term = dot(normed, w_ref[:, pl.ds(begin, width)])
        if r == 0:
            term_ref[...] = term
        else:
            sent_refs[r - 1][...] = term.astype(BF16)


def hidden_kernel(stream_ref, term_ref, *refs):
    total = term_ref[...]
    for ref in refs[:-1]:
        total = total + ref[...].astype(F32)
    refs[-1][...] = (stream_ref[...].astype(F32) + total).astype(BF16)


def project_kernel(place, w_ref, *refs):
    me = place[2]
    blocks, (q_ref, kv_ref) = refs[:-2], refs[-2:]
    count = len(blocks)
    rows, width = blocks[0].shape
    values = [ref[...].astype(F32) for ref in blocks]
    squares = sum(jnp.sum(v * v, axis=-1, keepdims=True) for v in values)
    scale = lax.rsqrt(squares / (count * width) + 1e-05)
    total = None
    for r in range(count):
        begin = pl.multiple_of(lax.rem(me + count - r, count) * width, width)
        part = dot((values[r] * scale).astype(BF16), w_ref[pl.ds(begin, width), :])
        total = part if total is None else total + part
    groups = q_ref.shape[1] // WIDTH
    for h in range(groups):
        base = h * 3 * WIDTH
        span = slice(h * WIDTH, (h + 1) * WIDTH)
        q_ref[:, span] = to_unit(total[:, base : base + WIDTH]).astype(BF16)
        kv_ref[:, span] = to_unit(total[:, base + WIDTH : base + 2 * WIDTH]).astype(BF16)
        kv_ref[:, groups * WIDTH + h * WIDTH : groups * WIDTH + (h + 1) * WIDTH] = total[
            :, base + 2 * WIDTH : base + 3 * WIDTH
        ].astype(BF16)


def window_parts(place, q_ref, blocks, first, mixed, totals):
    seq = place[0]
    core = seq & 1
    rows = q_ref.shape[0]
    groups = q_ref.shape[1] // WIDTH
    row, column = iotas(rows, rows)
    query_place = seq * rows + row
    for n, ref in enumerate(blocks):
        owner = seq - 2 * (first + n // 2)
        if n % 2 == 1:
            owner = owner + 1 - 2 * core
        key_place = owner * rows + column
        allowed = (key_place <= query_place) & (key_place > query_place - WINDOW) & (key_place >= 0)
        for h in range(groups):
            span = slice(h * WIDTH, (h + 1) * WIDTH)
            scores = SCORE_SCALE * dot(q_ref[:, span], ref[:, span], (1, 1))
            weights = jnp.where(allowed, jnp.exp(scores), 0.0)
            total = jnp.sum(weights, axis=-1, keepdims=True)
            part = dot(
                weights.astype(BF16),
                ref[:, (groups + h) * WIDTH : (groups + h + 1) * WIDTH],
            )
            mixed[h] = part if mixed[h] is None else mixed[h] + part
            totals[h] = total if totals[h] is None else totals[h] + total


def near_kernel(place, hidden_ref, q_ref, *refs):
    blocks, (mixed_ref, total_ref, keep_ref) = refs[:-3], refs[-3:]
    keep_ref[...] = hidden_ref[...]
    groups = q_ref.shape[1] // WIDTH
    mixed, totals = [None] * groups, [None] * groups
    window_parts(place, q_ref, blocks, 0, mixed, totals)
    for h in range(groups):
        span = slice(h * WIDTH, (h + 1) * WIDTH)
        mixed_ref[:, span] = mixed[h]
        total_ref[:, span] = jnp.broadcast_to(totals[h], mixed[h].shape)


def third_kernel(place, q_ref, mixed_ref, total_ref, own_ref, other_ref, mixed_out, total_out):
    groups = q_ref.shape[1] // WIDTH
    rows = q_ref.shape[0]
    spans = [slice(h * WIDTH, (h + 1) * WIDTH) for h in range(groups)]
    mixed = [mixed_ref[:, span] for span in spans]
    totals = [total_ref[:, span] for span in spans]
    window_parts(place, q_ref, [own_ref, other_ref], WINDOW // (2 * rows) - 1, mixed, totals)
    for h, span in enumerate(spans):
        mixed_out[:, span] = mixed[h]
        total_out[:, span] = totals[h]


def last_kernel(place, q_ref, mixed_ref, total_ref, own_ref, other_ref, out_ref):
    groups = q_ref.shape[1] // WIDTH
    rows = q_ref.shape[0]
    spans = [slice(h * WIDTH, (h + 1) * WIDTH) for h in range(groups)]
    mixed = [mixed_ref[:, span] for span in spans]
    totals = [total_ref[:, span] for span in spans]
    window_parts(place, q_ref, [own_ref, other_ref], WINDOW // (2 * rows), mixed, totals)
    for h, span in enumerate(spans):
        out_ref[:, span] = (mixed[h] / totals[h]).astype(BF16)


def call(kernel, outs, smem=0, scratch=(), spaces=None, limit=LIMIT):
    def run(*args):
        places = [SMEM] * smem + (spaces or [VMEM] * (len(args) - smem))
        return pl.pallas_call(
            kernel,
            out_shape=[jax.ShapeDtypeStruct(shape, kind) for shape, kind in outs],
            in_specs=[pl.BlockSpec(memory_space=place) for place in places],
            out_specs=[pl.BlockSpec(memory_space=VMEM)] * len(outs),
            scratch_shapes=list(scratch),
            compiler_params=pltpu.CompilerParams(vmem_limit_bytes=limit),
        )(*args)

    return run


def moved(array, axis, distance):
    size = lax.axis_size(axis)
    return lax.ppermute(array, axis, [(i, i + distance) for i in range(size - distance)])


def turned(array, axis, distance):
    size = lax.axis_size(axis)
    return lax.ppermute(array, axis, [(i, (i + distance) % size) for i in range(size)])


def crossed(array, mask):
    return lax.ppermute(array, "seq", [(i, i ^ mask) for i in range(lax.axis_size("seq"))])


def rotated(array, distance):
    return lax.ppermute(
        array,
        "seq",
        [(i, (i & -16) + ((i + 4 * distance) & 15)) for i in range(lax.axis_size("seq"))],
    )


def body(queries, keys, values, gate_log, beta, stream, w_out, w_qkv):
    rows, wide = queries.shape
    groups = gate_log.shape[1]
    seq = lax.axis_index("seq")
    head = lax.axis_index("head")
    heads = lax.axis_size("head")
    place = jnp.stack([seq, seq & 3, head, (seq >> 2) & 3]).astype(jnp.int32)
    pair_shape = ((WIDTH, 2 * WIDTH), F32)
    pay_shape = ((WIDTH + 16, 2 * WIDTH), BF16)
    state_shape = ((WIDTH, WIDTH), BF16)
    row_shape = ((rows, wide), BF16)
    four_pairs = pltpu.VMEM((4, WIDTH, 2 * WIDTH), F32)
    four_states = pltpu.VMEM((4, WIDTH, WIDTH), BF16)

    local, through, own, pay1, pay2, pay3 = call(
        chunk_kernel,
        [((groups, rows, WIDTH), BF16)] * 2 + [pair_shape]
        + [pay_shape] * 3,
        1,
        [pltpu.VMEM((rows, wide), BF16)] * 3 + [four_pairs, pltpu.SemaphoreType.DMA((3,))],
        [VMEM, VMEM] + [pltpu.HBM] * 3,
        CHUNK_LIMIT,
    )(place, gate_log.T, beta.T, queries, keys, values)
    before, everything, pay = call(
        group_kernel, [((3, WIDTH, 2 * WIDTH), F32), pair_shape, pay_shape], 1, [four_pairs]
    )(place, own, crossed(pay1, 1), crossed(pay2, 2), crossed(pay3, 3))
    rowed = [rotated(pay, d) for d in (1, 2, 3)]
    everything, w_out, w_qkv, stream = lax.optimization_barrier((everything, w_out, w_qkv, stream))
    w_out, w_qkv, stream, everything = call(
        fetch_kernel,
        [(w_out.shape, BF16), (w_qkv.shape, BF16), row_shape, pair_shape],
        1,
        [pltpu.SemaphoreType.DMA((3,))],
        [VMEM] + [pl.ANY] * 3,
    )(place, everything, w_out, w_qkv, stream)
    before_row, pay = call(row_kernel, [pair_shape, pay_shape], 1, [four_pairs] * 2)(
        place, everything, *rowed
    )
    mine, out1, out2, out3 = call(state_kernel, [state_shape] * 4, 1, [four_states])(
        place, *[moved(pay, "seq", 16 * d) for d in (1, 2, 3)], before_row, before
    )
    terms = call(
        out_kernel,
        [((rows, wide), F32)] + [row_shape] * (heads - 1),
        1,
        [four_states],
    )(
        place,
        local,
        through,
        mine,
        crossed(out1, 1),
        crossed(out2, 2),
        crossed(out3, 3),
        w_out,
    )
    received = [turned(terms[r], "head", r) for r in range(1, heads)]
    (hidden,) = call(hidden_kernel, [row_shape])(stream, terms[0], *received)
    others = [turned(hidden, "head", r) for r in range(1, heads)]
    unit_queries, pack = call(project_kernel, [row_shape, ((rows, 2 * wide), BF16)], 1)(
        place, w_qkv, hidden, *others
    )
    hops = [pack]
    for _ in range(WINDOW // (2 * rows) - 1):
        hops.append(moved(hops[-1], "seq", 2))
    blocks = [block for hop in hops[:-1] for block in (hop, crossed(hop, 1))]
    sums = [((rows, wide), F32)] * 2
    mixed, totals, kept = call(near_kernel, sums + [row_shape], 1)(
        place, hidden, unit_queries, *blocks
    )
    third, mixed, totals = lax.optimization_barrier((hops[-1], mixed, totals))
    fourth = moved(third, "seq", 2)
    mixed, totals = call(third_kernel, sums, 1)(
        place, unit_queries, mixed, totals, third, crossed(third, 1)
    )
    (attended,) = call(last_kernel, [row_shape], 1)(
        place, unit_queries, mixed, totals, fourth, crossed(fourth, 1)
    )
    return (kept, attended)


def solution(mesh):
    in_specs = (
        P("seq", "head"),
        P("seq", "head"),
        P("seq", "head"),
        P("seq", "head"),
        P("seq", "head"),
        P("seq", None),
        P("head", None),
        P(None, "head"),
    )
    out_specs = (P("seq", "head"), P("seq", "head"))
    return jax.shard_map(body, mesh=mesh, in_specs=in_specs, out_specs=out_specs, check_vma=False)
```

time: 151 us -> 127 us (0.84)
  the two profiles are of different devices: /device:TPU:7 before, /device:TPU:3 now
where the time goes in v2:
time: 127 us
  waiting for transfers between devices  51.3 us (40%)
  starting transfers between devices  47.4 us (37%)
  Pallas kernels  20.2 us (16%)
  local copies, waits for them, and re-layouts  6.78 us (5%)
    ppermute x7, waiting for transfers between devices, moved(): lax.ppermute(array, axis, [(i, i + distance) for i in range(size - distan...  31.8 us
    pallas_call x11, Pallas kernels, run(): pl.pallas_call(kernel, out_shape=[jax.ShapeDtypeStruct(shape, kind) for s...  20.2 us
    ppermute x7, starting transfers between devices, moved(): lax.ppermute(array, axis, [(i, i + distance) for i in range(size - distan...  15.3 us
    ppermute x11, starting transfers between devices, crossed(): lax.ppermute(array, 'seq', [(i, i ^ mask) for i in range(lax.axis_size('s...  15 us
    ppermute x6, waiting for transfers between devices, turned(): lax.ppermute(array, axis, [(i, (i + distance) % size) for i in range(size)])  13 us
    ppermute x3, starting transfers between devices, rotated(): lax.ppermute(array, 'seq', [(i, (i & -16) + (i + 4 * distance & 15)) for...  9.05 us
    ppermute x6, starting transfers between devices, turned(): lax.ppermute(array, axis, [(i, (i + distance) % size) for i in range(size)])  8.03 us
    unnamed x10, local copies, waits for them, and re-layouts  6.78 us
  transfers between devices with their start and end apart: 27, of which 14 were waited for; matrix products, arithmetic and copies ran while one was open for 0% of the time, Pallas kernels for 5%

profile of v2, /device:TPU:3, one launch (start us, length us, event | category | flops | bytes accessed | tf_op | source)
XLA Modules:
  0.0 126.6 jit_solution(4187101255479241210)
XLA Ops:
  2.1 5.5 %shard_map.95 = (bf16[4,128,128]{2,1,0:T(8,128)(2,1)S(1)}, bf16[4,128,128]{2,1,0:T(8,128)(2,1)S(1)}, f32[128,256]{1,0:T(8,128)S(1)}, bf16[144,256]{1,0:T(8,128)(...) custom-call(s32[4]{0:T(128)S(1)} %pad_add_fusion.place, f32[4,128]{1,0:T(4,128)S(1)} %bitcast.6, ...), custom_call_target="tpu_custom_call" | custom-call | tf_op jit(solution)/shard_map/pallas_call | solution.py:404
  10.1 2.4 %collective-permute-done.1.recv2_ref = bf16[144,256]{1,0:T(8,128)(2,1)S(1)} collective-permute-done((bf16[144,256]{1,0:T(8,128)(2,1)S(1)}, bf16[144,256]{1,0:T(8,128)(2,1)S(1)}, u32[]{:S(2)}, u32[]{:S(2)}) %collective-permute-start.1) | collective-permute-done | bytes 73760 | tf_op jit(solution)/shard_map/ppermute | solution.py:427
  15.3 5.8 %collective-permute-start.5 = (bf16[144,256]{1,0:T(8,128)(2,1)S(1)}, bf16[144,256]{1,0:T(8,128)(2,1)S(1)}, u32[]{:S(2)}, u32[]{:S(2)}) collective-permute-start(bf16[144,256]{1,0:T(8,128)(2,1)S(1)} %get-tuple-element.52), channel_id=1, source_target_pairs={{0,48},{4,52},{8,56},{12,60},{16,0},{20,4},{24,8},{28,12},{32,16},... | collective-permute-start | bytes 221192 | tf_op jit(solution)/shard_map/ppermute | solution.py:431
  22.1 2.3 %collective-permute-start.3 = (bf16[144,256]{1,0:T(8,128)(2,1)S(1)}, bf16[144,256]{1,0:T(8,128)(2,1)S(1)}, u32[]{:S(2)}, u32[]{:S(2)}) collective-permute-start(bf16[144,256]{1,0:T(8,128)(2,1)S(1)} %get-tuple-element.52), channel_id=1, source_target_pairs={{0,16},{4,20},{8,24},{12,28},{16,32},{20,36},{24,40},{28,44},{32,4... | collective-permute-start | bytes 221192 | tf_op jit(solution)/shard_map/ppermute | solution.py:431
  24.4 2.8 %copy-done = bf16[2048,1536]{1,0:T(8,128)(2,1)S(1)} copy-done((bf16[2048,1536]{1,0:T(8,128)(2,1)S(1)}, bf16[2048,1536]{1,0:T(8,128)(2,1)}, u32[]{:S(2)}) %copy-start) | copy-done | bytes 6291480
  32.8 4.4 %collective-permute-start.7 = (bf16[144,256]{1,0:T(8,128)(2,1)S(1)}, bf16[144,256]{1,0:T(8,128)(2,1)S(1)}, u32[]{:S(2)}, u32[]{:S(2)}) collective-permute-start(bf16[144,256]{1,0:T(8,128)(2,1)S(1)} %get-tuple-element.53), channel_id=1, source_target_pairs={{0,128},{4,132},{8,136},{12,140},{16,144},{20,148},{24,152},{28,15... | collective-permute-start | bytes 221192 | tf_op jit(solution)/shard_map/ppermute | solution.py:418
  39.1 3.1 %collective-permute-done.6.row1_ref = bf16[144,256]{1,0:T(8,128)(2,1)S(1)} collective-permute-done((bf16[144,256]{1,0:T(8,128)(2,1)S(1)}, bf16[144,256]{1,0:T(8,128)(2,1)S(1)}, u32[]{:S(2)}, u32[]{:S(2)}) %collective-permute-start.6) | collective-permute-done | bytes 73760 | tf_op jit(solution)/shard_map/ppermute | solution.py:418
  43.4 2.6 %collective-permute-start.9 = (bf16[128,128]{1,0:T(8,128)(2,1)S(1)}, bf16[128,128]{1,0:T(8,128)(2,1)S(1)}, u32[]{:S(2)}, u32[]{:S(2)}) collective-permute-start(bf16[128,128]{1,0:T(8,128)(2,1)S(1)} %get-tuple-element.57), channel_id=1, source_target_pairs={{0,4},{4,0},{8,12},{12,8},{16,20},{20,16},{24,28},{28,24},{32,36},... | collective-permute-start | bytes 98312 | tf_op jit(solution)/shard_map/ppermute | solution.py:427
  52.7 2.6 %collective-permute-start.13 = (bf16[128,512]{1,0:T(8,128)(2,1)S(1)}, bf16[128,512]{1,0:T(8,128)(2,1)S(1)}, u32[]{:S(2)}, u32[]{:S(2)}) collective-permute-start(bf16[128,512]{1,0:T(8,128)(2,1)S(1)} %get-tuple-element.63), channel_id=1, source_target_pairs={{0,2},{1,3},{2,0},{3,1},{4,6},{5,7},{6,4},{7,5},{8,10},{9,11},{10,... | collective-permute-start | bytes 393224 | tf_op jit(solution)/shard_map/ppermute | solution.py:423
  57.5 3.9 %collective-permute-done.13.refs_1_ = bf16[128,512]{1,0:T(8,128)(2,1)S(1)} collective-permute-done((bf16[128,512]{1,0:T(8,128)(2,1)S(1)}, bf16[128,512]{1,0:T(8,128)(2,1)S(1)}, u32[]{:S(2)}, u32[]{:S(2)}) %collective-permute-start.13) | collective-permute-done | bytes 131104 | tf_op jit(solution)/shard_map/ppermute | solution.py:423
  61.5 2.1 %collective-permute-start.17 = (bf16[128,512]{1,0:T(8,128)(2,1)S(1)}, bf16[128,512]{1,0:T(8,128)(2,1)S(1)}, u32[]{:S(2)}, u32[]{:S(2)}) collective-permute-start(bf16[128,512]{1,0:T(8,128)(2,1)S(1)} %shard_map.101.refs_0_.hidden_ref), channel_id=1, source_target_pairs={{0,3},{1,0},{2,1},{3,2},{4,7},{5,4},{6,5},{7,6},{8,11},{9,8},{10,9... | collective-permute-start | bytes 393224 | tf_op jit(solution)/shard_map/ppermute | solution.py:423
  64.5 2.3 %collective-permute-done.17.refs_3_ = bf16[128,512]{1,0:T(8,128)(2,1)S(1)} collective-permute-done((bf16[128,512]{1,0:T(8,128)(2,1)S(1)}, bf16[128,512]{1,0:T(8,128)(2,1)S(1)}, u32[]{:S(2)}, u32[]{:S(2)}) %collective-permute-start.17) | collective-permute-done | bytes 131104 | tf_op jit(solution)/shard_map/ppermute | solution.py:423
  66.7 2.2 %collective-permute-done.16.refs_2_ = bf16[128,512]{1,0:T(8,128)(2,1)S(1)} collective-permute-done((bf16[128,512]{1,0:T(8,128)(2,1)S(1)}, bf16[128,512]{1,0:T(8,128)(2,1)S(1)}, u32[]{:S(2)}, u32[]{:S(2)}) %collective-permute-start.16) | collective-permute-done | bytes 131104 | tf_op jit(solution)/shard_map/ppermute | solution.py:423
  69.0 3.5 %collective-permute-done.15.refs_1_ = bf16[128,512]{1,0:T(8,128)(2,1)S(1)} collective-permute-done((bf16[128,512]{1,0:T(8,128)(2,1)S(1)}, bf16[128,512]{1,0:T(8,128)(2,1)S(1)}, u32[]{:S(2)}, u32[]{:S(2)}) %collective-permute-start.15) | collective-permute-done | bytes 131104 | tf_op jit(solution)/shard_map/ppermute | solution.py:423
  74.2 2.7 %collective-permute-start.19 = (bf16[128,1024]{1,0:T(8,128)(2,1)S(1)}, bf16[128,1024]{1,0:T(8,128)(2,1)S(1)}, u32[]{:S(2)}, u32[]{:S(2)}) collective-permute-start(bf16[128,1024]{1,0:T(8,128)(2,1)S(1)} %get-tuple-element.67.refs_0_), channel_id=1, source_target_pairs={{0,8},{4,12},{8,16},{12,20},{16,24},{20,28},{24,32},{28,36},{32,40... | collective-permute-start | bytes 786440 | tf_op jit(solution)/shard_map/ppermute | solution.py:418
  76.9 7.8 %collective-permute-done.19.refs_2_ = bf16[128,1024]{1,0:T(8,128)(2,1)S(1)} collective-permute-done((bf16[128,1024]{1,0:T(8,128)(2,1)S(1)}, bf16[128,1024]{1,0:T(8,128)(2,1)S(1)}, u32[]{:S(2)}, u32[]{:S(2)}) %collective-permute-start.19) | collective-permute-done | bytes 262176 | tf_op jit(solution)/shard_map/ppermute | solution.py:418
  86.6 2.3 %collective-permute-start.18 = (bf16[128,1024]{1,0:T(8,128)(2,1)S(1)}, bf16[128,1024]{1,0:T(8,128)(2,1)S(1)}, u32[]{:S(2)}, u32[]{:S(2)}) collective-permute-start(bf16[128,1024]{1,0:T(8,128)(2,1)S(1)} %get-tuple-element.67.refs_0_), channel_id=1, source_target_pairs={{0,4},{4,0},{8,12},{12,8},{16,20},{20,16},{24,28},{28,24},{32,36},... | collective-permute-start | bytes 786440 | tf_op jit(solution)/shard_map/ppermute | solution.py:427
  89.0 5.2 %collective-permute-done.21.refs_4_ = bf16[128,1024]{1,0:T(8,128)(2,1)S(1)} collective-permute-done((bf16[128,1024]{1,0:T(8,128)(2,1)S(1)}, bf16[128,1024]{1,0:T(8,128)(2,1)S(1)}, u32[]{:S(2)}, u32[]{:S(2)}) %collective-permute-start.21) | collective-permute-done | bytes 262176 | tf_op jit(solution)/shard_map/ppermute | solution.py:418
  94.2 3.2 %collective-permute-start.22 = (bf16[128,1024]{1,0:T(8,128)(2,1)S(1)}, bf16[128,1024]{1,0:T(8,128)(2,1)S(1)}, u32[]{:S(2)}, u32[]{:S(2)}) collective-permute-start(bf16[128,1024]{1,0:T(8,128)(2,1)S(1)} %collective-permute-done.21.refs_4_), channel_id=1, source_target_pairs={{0,4},{4,0},{8,12},{12,8},{16,20},{20,16},{24,28},{28,24},{32,36},... | collective-permute-start | bytes 786440 | tf_op jit(solution)/shard_map/ppermute | solution.py:427
  99.3 2.6 %shard_map.103 = (f32[128,512]{1,0:T(8,128)S(1)}, f32[128,512]{1,0:T(8,128)S(1)}, bf16[128,512]{1,0:T(8,128)(2,1)}) custom-call(s32[4]{0:T(128)S(1)} %pad_add_fusion.place, bf16[128,512]{1,0:T(8,128)(2,1)S(1)} %shard_map.101.refs_0_.hidden_ref, bf16[128,512]{1,0:T(8,128)(2,1)S(1)} %get-tuple-element.66.q_ref, ...), custom_call_target="tpu_custom_call" | custom-call | tf_op jit(solution)/shard_map/pallas_call | solution.py:404
  101.9 7.4 %collective-permute-done.23.own_ref = bf16[128,1024]{1,0:T(8,128)(2,1)S(1)} collective-permute-done((bf16[128,1024]{1,0:T(8,128)(2,1)S(1)}, bf16[128,1024]{1,0:T(8,128)(2,1)S(1)}, u32[]{:S(2)}, u32[]{:S(2)}) %collective-permute-start.23) | collective-permute-done | bytes 262176 | tf_op jit(solution)/shard_map/ppermute | solution.py:418
  112.1 8.3 %collective-permute-done.25.own_ref = bf16[128,1024]{1,0:T(8,128)(2,1)S(1)} collective-permute-done((bf16[128,1024]{1,0:T(8,128)(2,1)S(1)}, bf16[128,1024]{1,0:T(8,128)(2,1)S(1)}, u32[]{:S(2)}, u32[]{:S(2)}) %collective-permute-start.25) | collective-permute-done | bytes 262176 | tf_op jit(solution)/shard_map/ppermute | solution.py:418
  122.0 2.0 %shard_map.104 = (f32[128,512]{1,0:T(8,128)S(1)}, f32[128,512]{1,0:T(8,128)S(1)}) custom-call(s32[4]{0:T(128)S(1)} %pad_add_fusion.place, bf16[128,512]{1,0:T(8,128)(2,1)S(1)} %get-tuple-element.66.q_ref, f32[128,512]{1,0:T(8,128)S(1)} %get-tuple-element.71.mixed_ref, f32[128,512]{1,0:T(8,128)S(1)} %get-tuple-element.72.total_ref, ...), custom_call_target="tpu_custom_call" | custom-call | tf_op jit(solution)/shard_map/pallas_call | solution.py:404
  124.0 2.6 %shard_map.105 = bf16[128,512]{1,0:T(8,128)(2,1)} custom-call(s32[4]{0:T(128)S(1)} %pad_add_fusion.place, bf16[128,512]{1,0:T(8,128)(2,1)S(1)} %get-tuple-element.66.q_ref, f32[128,512]{1,0:T(8,128)S(1)} %get-tuple-element.74.mixed_ref, f32[128,512]{1,0:T(8,128)S(1)} %get-tuple-element.75.total_ref, bf16[128,1024]{1,0:T(8,128)(2,1)S(1)} %collective-permute-done.25.own_ref, ...), custom_call_target="tpu_custom_call" | custom-call | tf_op jit(solution)/shard_map/pallas_call | solution.py:404
  (52 shorter events, 36.3 us)
Async XLA Ops:
  8.4 4.2 %collective-permute-start.1 = (bf16[144,256]{1,0:T(8,128)(2,1)S(1)}, bf16[144,256]{1,0:T(8,128)(2,1)S(1)}, u32[]{:S(2)}, u32[]{:S(2)}) collective-permute-start(bf16[144,256]{1,0:T(8,128)(2,1)S(1)} %get-tuple-element.41), channel_id=1, source_target_pairs={{0,8},{4,12},{8,0},{12,4},{16,24},{20,28},{24,16},{28,20},{32,40},... | collective-permute-start | bytes 221192 | tf_op jit(solution)/shard_map/ppermute | solution.py:427
  10.0 4.2 %collective-permute-start.2 = (bf16[144,256]{1,0:T(8,128)(2,1)S(1)}, bf16[144,256]{1,0:T(8,128)(2,1)S(1)}, u32[]{:S(2)}, u32[]{:S(2)}) collective-permute-start(bf16[144,256]{1,0:T(8,128)(2,1)S(1)} %get-tuple-element.42), channel_id=1, source_target_pairs={{0,12},{4,8},{8,4},{12,0},{16,28},{20,24},{24,20},{28,16},{32,44},... | collective-permute-start | bytes 221192 | tf_op jit(solution)/shard_map/ppermute | solution.py:427
  15.3 15.6 %collective-permute-start.5 = (bf16[144,256]{1,0:T(8,128)(2,1)S(1)}, bf16[144,256]{1,0:T(8,128)(2,1)S(1)}, u32[]{:S(2)}, u32[]{:S(2)}) collective-permute-start(bf16[144,256]{1,0:T(8,128)(2,1)S(1)} %get-tuple-element.52), channel_id=1, source_target_pairs={{0,48},{4,52},{8,56},{12,60},{16,0},{20,4},{24,8},{28,12},{32,16},... | collective-permute-start | bytes 221192 | tf_op jit(solution)/shard_map/ppermute | solution.py:431
  21.1 9.9 %collective-permute-start.4 = (bf16[144,256]{1,0:T(8,128)(2,1)S(1)}, bf16[144,256]{1,0:T(8,128)(2,1)S(1)}, u32[]{:S(2)}, u32[]{:S(2)}) collective-permute-start(bf16[144,256]{1,0:T(8,128)(2,1)S(1)} %get-tuple-element.52), channel_id=1, source_target_pairs={{0,32},{4,36},{8,40},{12,44},{16,48},{20,52},{24,56},{28,60},{32,0... | collective-permute-start | bytes 221192 | tf_op jit(solution)/shard_map/ppermute | solution.py:431
  22.1 8.9 %collective-permute-start.3 = (bf16[144,256]{1,0:T(8,128)(2,1)S(1)}, bf16[144,256]{1,0:T(8,128)(2,1)S(1)}, u32[]{:S(2)}, u32[]{:S(2)}) collective-permute-start(bf16[144,256]{1,0:T(8,128)(2,1)S(1)} %get-tuple-element.52), channel_id=1, source_target_pairs={{0,16},{4,20},{8,24},{12,28},{16,32},{20,36},{24,40},{28,44},{32,4... | collective-permute-start | bytes 221192 | tf_op jit(solution)/shard_map/ppermute | solution.py:431
  32.1 7.0 %collective-permute-start.8 = (bf16[144,256]{1,0:T(8,128)(2,1)S(1)}, bf16[144,256]{1,0:T(8,128)(2,1)S(1)}, u32[]{:S(2)}, u32[]{:S(2)}) collective-permute-start(bf16[144,256]{1,0:T(8,128)(2,1)S(1)} %get-tuple-element.53), channel_id=1, source_target_pairs={{0,192},{4,196},{8,200},{12,204},{16,208},{20,212},{24,216},{28,22... | collective-permute-start | bytes 221192 | tf_op jit(solution)/shard_map/ppermute | solution.py:418
  32.8 6.3 %collective-permute-start.7 = (bf16[144,256]{1,0:T(8,128)(2,1)S(1)}, bf16[144,256]{1,0:T(8,128)(2,1)S(1)}, u32[]{:S(2)}, u32[]{:S(2)}) collective-permute-start(bf16[144,256]{1,0:T(8,128)(2,1)S(1)} %get-tuple-element.53), channel_id=1, source_target_pairs={{0,128},{4,132},{8,136},{12,140},{16,144},{20,148},{24,152},{28,15... | collective-permute-start | bytes 221192 | tf_op jit(solution)/shard_map/ppermute | solution.py:418
  37.2 5.1 %collective-permute-start.6 = (bf16[144,256]{1,0:T(8,128)(2,1)S(1)}, bf16[144,256]{1,0:T(8,128)(2,1)S(1)}, u32[]{:S(2)}, u32[]{:S(2)}) collective-permute-start(bf16[144,256]{1,0:T(8,128)(2,1)S(1)} %get-tuple-element.53), channel_id=1, source_target_pairs={{0,64},{4,68},{8,72},{12,76},{16,80},{20,84},{24,88},{28,92},{32,9... | collective-permute-start | bytes 221192 | tf_op jit(solution)/shard_map/ppermute | solution.py:418
  43.4 4.3 %collective-permute-start.9 = (bf16[128,128]{1,0:T(8,128)(2,1)S(1)}, bf16[128,128]{1,0:T(8,128)(2,1)S(1)}, u32[]{:S(2)}, u32[]{:S(2)}) collective-permute-start(bf16[128,128]{1,0:T(8,128)(2,1)S(1)} %get-tuple-element.57), channel_id=1, source_target_pairs={{0,4},{4,0},{8,12},{12,8},{16,20},{20,16},{24,28},{28,24},{32,36},... | collective-permute-start | bytes 98312 | tf_op jit(solution)/shard_map/ppermute | solution.py:427
  51.3 6.1 %collective-permute-start.12 = (bf16[128,512]{1,0:T(8,128)(2,1)S(1)}, bf16[128,512]{1,0:T(8,128)(2,1)S(1)}, u32[]{:S(2)}, u32[]{:S(2)}) collective-permute-start(bf16[128,512]{1,0:T(8,128)(2,1)S(1)} %get-tuple-element.62), channel_id=1, source_target_pairs={{0,1},{1,2},{2,3},{3,0},{4,5},{5,6},{6,7},{7,4},{8,9},{9,10},{10,1... | collective-permute-start | bytes 393224 | tf_op jit(solution)/shard_map/ppermute | solution.py:423
  52.7 8.7 %collective-permute-start.13 = (bf16[128,512]{1,0:T(8,128)(2,1)S(1)}, bf16[128,512]{1,0:T(8,128)(2,1)S(1)}, u32[]{:S(2)}, u32[]{:S(2)}) collective-permute-start(bf16[128,512]{1,0:T(8,128)(2,1)S(1)} %get-tuple-element.63), channel_id=1, source_target_pairs={{0,2},{1,3},{2,0},{3,1},{4,6},{5,7},{6,4},{7,5},{8,10},{9,11},{10,... | collective-permute-start | bytes 393224 | tf_op jit(solution)/shard_map/ppermute | solution.py:423
  55.3 6.1 %collective-permute-start.14 = (bf16[128,512]{1,0:T(8,128)(2,1)S(1)}, bf16[128,512]{1,0:T(8,128)(2,1)S(1)}, u32[]{:S(2)}, u32[]{:S(2)}) collective-permute-start(bf16[128,512]{1,0:T(8,128)(2,1)S(1)} %get-tuple-element.64), channel_id=1, source_target_pairs={{0,3},{1,0},{2,1},{3,2},{4,7},{5,4},{6,5},{7,6},{8,11},{9,8},{10,9... | collective-permute-start | bytes 393224 | tf_op jit(solution)/shard_map/ppermute | solution.py:423
  61.5 5.3 %collective-permute-start.17 = (bf16[128,512]{1,0:T(8,128)(2,1)S(1)}, bf16[128,512]{1,0:T(8,128)(2,1)S(1)}, u32[]{:S(2)}, u32[]{:S(2)}) collective-permute-start(bf16[128,512]{1,0:T(8,128)(2,1)S(1)} %shard_map.101.refs_0_.hidden_ref), channel_id=1, source_target_pairs={{0,3},{1,0},{2,1},{3,2},{4,7},{5,4},{6,5},{7,6},{8,11},{9,8},{10,9... | collective-permute-start | bytes 393224 | tf_op jit(solution)/shard_map/ppermute | solution.py:423
  63.6 5.4 %collective-permute-start.16 = (bf16[128,512]{1,0:T(8,128)(2,1)S(1)}, bf16[128,512]{1,0:T(8,128)(2,1)S(1)}, u32[]{:S(2)}, u32[]{:S(2)}) collective-permute-start(bf16[128,512]{1,0:T(8,128)(2,1)S(1)} %shard_map.101.refs_0_.hidden_ref), channel_id=1, source_target_pairs={{0,2},{1,3},{2,0},{3,1},{4,6},{5,7},{6,4},{7,5},{8,10},{9,11},{10,... | collective-permute-start | bytes 393224 | tf_op jit(solution)/shard_map/ppermute | solution.py:423
  64.3 8.2 %collective-permute-start.15 = (bf16[128,512]{1,0:T(8,128)(2,1)S(1)}, bf16[128,512]{1,0:T(8,128)(2,1)S(1)}, u32[]{:S(2)}, u32[]{:S(2)}) collective-permute-start(bf16[128,512]{1,0:T(8,128)(2,1)S(1)} %shard_map.101.refs_0_.hidden_ref), channel_id=1, source_target_pairs={{0,1},{1,2},{2,3},{3,0},{4,5},{5,6},{6,7},{7,4},{8,9},{9,10},{10,1... | collective-permute-start | bytes 393224 | tf_op jit(solution)/shard_map/ppermute | solution.py:423
  74.2 10.5 %collective-permute-start.19 = (bf16[128,1024]{1,0:T(8,128)(2,1)S(1)}, bf16[128,1024]{1,0:T(8,128)(2,1)S(1)}, u32[]{:S(2)}, u32[]{:S(2)}) collective-permute-start(bf16[128,1024]{1,0:T(8,128)(2,1)S(1)} %get-tuple-element.67.refs_0_), channel_id=1, source_target_pairs={{0,8},{4,12},{8,16},{12,20},{16,24},{20,28},{24,32},{28,36},{32,40... | collective-permute-start | bytes 786440 | tf_op jit(solution)/shard_map/ppermute | solution.py:418
  84.7 9.5 %collective-permute-start.21 = (bf16[128,1024]{1,0:T(8,128)(2,1)S(1)}, bf16[128,1024]{1,0:T(8,128)(2,1)S(1)}, u32[]{:S(2)}, u32[]{:S(2)}) collective-permute-start(bf16[128,1024]{1,0:T(8,128)(2,1)S(1)} %collective-permute-done.19.refs_2_), channel_id=1, source_target_pairs={{0,8},{4,12},{8,16},{12,20},{16,24},{20,28},{24,32},{28,36},{32,40... | collective-permute-start | bytes 786440 | tf_op jit(solution)/shard_map/ppermute | solution.py:418
  86.6 12.7 %collective-permute-start.18 = (bf16[128,1024]{1,0:T(8,128)(2,1)S(1)}, bf16[128,1024]{1,0:T(8,128)(2,1)S(1)}, u32[]{:S(2)}, u32[]{:S(2)}) collective-permute-start(bf16[128,1024]{1,0:T(8,128)(2,1)S(1)} %get-tuple-element.67.refs_0_), channel_id=1, source_target_pairs={{0,4},{4,0},{8,12},{12,8},{16,20},{20,16},{24,28},{28,24},{32,36},... | collective-permute-start | bytes 786440 | tf_op jit(solution)/shard_map/ppermute | solution.py:427
  88.9 10.4 %collective-permute-start.20 = (bf16[128,1024]{1,0:T(8,128)(2,1)S(1)}, bf16[128,1024]{1,0:T(8,128)(2,1)S(1)}, u32[]{:S(2)}, u32[]{:S(2)}) collective-permute-start(bf16[128,1024]{1,0:T(8,128)(2,1)S(1)} %collective-permute-done.19.refs_2_), channel_id=1, source_target_pairs={{0,4},{4,0},{8,12},{12,8},{16,20},{20,16},{24,28},{28,24},{32,36},... | collective-permute-start | bytes 786440 | tf_op jit(solution)/shard_map/ppermute | solution.py:427
  94.2 5.1 %collective-permute-start.22 = (bf16[128,1024]{1,0:T(8,128)(2,1)S(1)}, bf16[128,1024]{1,0:T(8,128)(2,1)S(1)}, u32[]{:S(2)}, u32[]{:S(2)}) collective-permute-start(bf16[128,1024]{1,0:T(8,128)(2,1)S(1)} %collective-permute-done.21.refs_4_), channel_id=1, source_target_pairs={{0,4},{4,0},{8,12},{12,8},{16,20},{20,16},{24,28},{28,24},{32,36},... | collective-permute-start | bytes 786440 | tf_op jit(solution)/shard_map/ppermute | solution.py:427
  97.4 11.9 %collective-permute-start.23 = (bf16[128,1024]{1,0:T(8,128)(2,1)S(1)}, bf16[128,1024]{1,0:T(8,128)(2,1)S(1)}, u32[]{:S(2)}, u32[]{:S(2)}) collective-permute-start(bf16[128,1024]{1,0:T(8,128)(2,1)S(1)} %collective-permute-done.21.refs_4_), channel_id=1, source_target_pairs={{0,8},{4,12},{8,16},{12,20},{16,24},{20,28},{24,32},{28,36},{32,40... | collective-permute-start | bytes 786440 | tf_op jit(solution)/shard_map/ppermute | solution.py:418
  109.3 11.0 %collective-permute-start.25 = (bf16[128,1024]{1,0:T(8,128)(2,1)S(1)}, bf16[128,1024]{1,0:T(8,128)(2,1)S(1)}, u32[]{:S(2)}, u32[]{:S(2)}) collective-permute-start(bf16[128,1024]{1,0:T(8,128)(2,1)S(1)} %collective-permute-done.23.own_ref), channel_id=1, source_target_pairs={{0,8},{4,12},{8,16},{12,20},{16,24},{20,28},{24,32},{28,36},{32,40... | collective-permute-start | bytes 786440 | tf_op jit(solution)/shard_map/ppermute | solution.py:418
  111.2 10.8 %collective-permute-start.24 = (bf16[128,1024]{1,0:T(8,128)(2,1)S(1)}, bf16[128,1024]{1,0:T(8,128)(2,1)S(1)}, u32[]{:S(2)}, u32[]{:S(2)}) collective-permute-start(bf16[128,1024]{1,0:T(8,128)(2,1)S(1)} %collective-permute-done.23.own_ref), channel_id=1, source_target_pairs={{0,4},{4,0},{8,12},{12,8},{16,20},{20,16},{24,28},{28,24},{32,36},... | collective-permute-start | bytes 786440 | tf_op jit(solution)/shard_map/ppermute | solution.py:427
  120.3 3.6 %collective-permute-start.26 = (bf16[128,1024]{1,0:T(8,128)(2,1)S(1)}, bf16[128,1024]{1,0:T(8,128)(2,1)S(1)}, u32[]{:S(2)}, u32[]{:S(2)}) collective-permute-start(bf16[128,1024]{1,0:T(8,128)(2,1)S(1)} %collective-permute-done.25.own_ref), channel_id=1, source_target_pairs={{0,4},{4,0},{8,12},{12,8},{16,20},{20,16},{24,28},{28,24},{32,36},... | collective-permute-start | bytes 786440 | tf_op jit(solution)/shard_map/ppermute | solution.py:427
  (8 other events, 15.4 us)

commit v3 on v2

--- a/solution.py
+++ b/solution.py
@@ -16,6 +16,7 @@
 VMEM = pltpu.VMEM
 SMEM = pltpu.SMEM
 LIMIT = 16 * 1024 * 1024
+FETCH_LIMIT = 44 * 1024 * 1024
 CHUNK_LIMIT = 54579 * 1024
 
 
@@ -225,22 +226,23 @@
     store_payload(pay_ref, total)
 
 
-def fetch_kernel(place, all_ref, wout_ref, wqkv_ref, stream_ref, wout_out, wqkv_out, stream_out, all_out, sems):
+def fetch_wide_kernel(token_ref, source_ref, fetched_ref, token_out, sem):
+    load = pltpu.make_async_copy(source_ref, fetched_ref, sem)
+    load.start()
+    token_out[...] = token_ref[...]
+    load.wait()
+
+
+def fetch_kernel(place, token_ref, weight_ref, stream_ref, weight_out, stream_out, token_out, sems):
     width = stream_out.shape[1]
     begin = pl.multiple_of(place[2] * width, width)
     loads = [
-        pltpu.make_async_copy(src, dst, sems.at[n])
-        for n, (src, dst) in enumerate(
-            [
-                (wout_ref, wout_out),
-                (wqkv_ref, wqkv_out),
-                (stream_ref.at[:, pl.ds(begin, width)], stream_out),
-            ]
-        )
+        pltpu.make_async_copy(weight_ref, weight_out, sems.at[0]),
+        pltpu.make_async_copy(stream_ref.at[:, pl.ds(begin, width)], stream_out, sems.at[1]),
     ]
     for load in loads:
         load.start()
-    all_out[...] = all_ref[...]
+    token_out[...] = token_ref[...]
     for load in loads:
         load.wait()
 
@@ -337,65 +339,80 @@
         ].astype(BF16)
 
 
-def window_parts(place, q_ref, blocks, first, mixed, totals):
-    seq = place[0]
-    core = seq & 1
+def window_part(query_place, key_chip, core, q_ref, own_ref, other_ref, sums):
     rows = q_ref.shape[0]
     groups = q_ref.shape[1] // WIDTH
-    row, column = iotas(rows, rows)
-    query_place = seq * rows + row
-    for n, ref in enumerate(blocks):
-        owner = seq - 2 * (first + n // 2)
-        if n % 2 == 1:
-            owner = owner + 1 - 2 * core
-        key_place = owner * rows + column
-        allowed = (key_place <= query_place) & (key_place > query_place - WINDOW) & (key_place >= 0)
-        for h in range(groups):
-            span = slice(h * WIDTH, (h + 1) * WIDTH)
-            scores = SCORE_SCALE * dot(q_ref[:, span], ref[:, span], (1, 1))
-            weights = jnp.where(allowed, jnp.exp(scores), 0.0)
-            total = jnp.sum(weights, axis=-1, keepdims=True)
-            part = dot(
-                weights.astype(BF16),
-                ref[:, (groups + h) * WIDTH : (groups + h + 1) * WIDTH],
-            )
-            mixed[h] = part if mixed[h] is None else mixed[h] + part
-            totals[h] = total if totals[h] is None else totals[h] + total
-
-
-def near_kernel(place, hidden_ref, q_ref, *refs):
-    blocks, (mixed_ref, total_ref, keep_ref) = refs[:-3], refs[-3:]
+    row, column = iotas(rows, 2 * rows)
+    query_place = query_place * rows + row
+    own_place = (2 * key_chip + core) * rows + column
+    other_place = (2 * key_chip + 1 - core) * rows + column - rows
+    key_place = jnp.where(column < rows, own_place, other_place)
+    allowed = (key_place <= query_place) & (key_place > query_place - WINDOW) & (key_place >= 0)
+    ones = jnp.ones((2 * rows, WIDTH), BF16)
+    for h in range(groups):
+        span = slice(h * WIDTH, (h + 1) * WIDTH)
+        value_span = slice((groups + h) * WIDTH, (groups + h + 1) * WIDTH)
+        keys = jnp.concatenate([own_ref[:, span], other_ref[:, span]], axis=0)
+        values = jnp.concatenate([own_ref[:, value_span], other_ref[:, value_span]], axis=0)
+        scores = SCORE_SCALE * dot(q_ref[:, span], keys, (1, 1))
+        weights = jnp.where(allowed, jnp.exp(scores), 0.0).astype(BF16)
+        part = dot(weights, jnp.concatenate([values, ones], axis=1))
+        sums[h] = part if sums[h] is None else sums[h] + part
+
+
+def sum_spans(groups):
+    return [slice(2 * h * WIDTH, 2 * (h + 1) * WIDTH) for h in range(groups)]
+
+
+def away_kernel(place, hidden_ref, q_ref, own_ref, other_ref, sums_ref, keep_ref):
     keep_ref[...] = hidden_ref[...]
+    seq = place[0]
     groups = q_ref.shape[1] // WIDTH
-    mixed, totals = [None] * groups, [None] * groups
-    window_parts(place, q_ref, blocks, 0, mixed, totals)
-    for h in range(groups):
+    sums = [None] * groups
+    window_part(seq + 4, (seq >> 1) - 1, seq & 1, q_ref, own_ref, other_ref, sums)
+    for h, span in enumerate(sum_spans(groups)):
+        sums_ref[:, span] = sums[h]
+
+
+def back_kernel(place, q_ref, sums_ref, own_ref, other_ref, back_ref):
+    seq = place[0]
+    rows = q_ref.shape[0]
+    groups = q_ref.shape[1] // WIDTH
+    sums = [sums_ref[:, span] for span in sum_spans(groups)]
+    window_part(seq + 4, (seq >> 1) - 2, seq & 1, q_ref, own_ref, other_ref, sums)
+    _, column = iotas(rows, WIDTH)
+    totals = jnp.zeros((rows, WIDTH), BF16)
+    for h in range(groups):
+        back_ref[:, h * WIDTH : (h + 1) * WIDTH] = sums[h][:, :WIDTH].astype(BF16)
+        total = sums[h][:, WIDTH:]
+        high = total.astype(BF16)
+        low = (total - high.astype(F32)).astype(BF16)
+        totals = jnp.where(column == 2 * h, high, jnp.where(column == 2 * h + 1, low, totals))
+    back_ref[:, groups * WIDTH :] = totals
+
+
+def home_kernel(place, q_ref, *refs):
+    blocks, sums_ref = refs[:-1], refs[-1]
+    seq = place[0]
+    groups = q_ref.shape[1] // WIDTH
+    sums = [None] * groups
+    for n in range(len(blocks) // 2):
+        window_part(
+            seq, (seq >> 1) - n, seq & 1, q_ref, blocks[2 * n], blocks[2 * n + 1], sums
+        )
+    for h, span in enumerate(sum_spans(groups)):
+        sums_ref[:, span] = sums[h]
+
+
+def last_kernel(sums_ref, back_ref, out_ref):
+    groups = out_ref.shape[1] // WIDTH
+    totals = back_ref[:, groups * WIDTH :].astype(F32)
+    for h in range(groups):
+        far = totals[:, 2 * h : 2 * h + 1] + totals[:, 2 * h + 1 : 2 * h + 2]
         span = slice(h * WIDTH, (h + 1) * WIDTH)
-        mixed_ref[:, span] = mixed[h]
-        total_ref[:, span] = jnp.broadcast_to(totals[h], mixed[h].shape)
-
-
-def third_kernel(place, q_ref, mixed_ref, total_ref, own_ref, other_ref, mixed_out, total_out):
-    groups = q_ref.shape[1] // WIDTH
-    rows = q_ref.shape[0]
-    spans = [slice(h * WIDTH, (h + 1) * WIDTH) for h in range(groups)]
-    mixed = [mixed_ref[:, span] for span in spans]
-    totals = [total_ref[:, span] for span in spans]
-    window_parts(place, q_ref, [own_ref, other_ref], WINDOW // (2 * rows) - 1, mixed, totals)
-    for h, span in enumerate(spans):
-        mixed_out[:, span] = mixed[h]
-        total_out[:, span] = totals[h]
-
-
-def last_kernel(place, q_ref, mixed_ref, total_ref, own_ref, other_ref, out_ref):
-    groups = q_ref.shape[1] // WIDTH
-    rows = q_ref.shape[0]
-    spans = [slice(h * WIDTH, (h + 1) * WIDTH) for h in range(groups)]
-    mixed = [mixed_ref[:, span] for span in spans]
-    totals = [total_ref[:, span] for span in spans]
-    window_parts(place, q_ref, [own_ref, other_ref], WINDOW // (2 * rows), mixed, totals)
-    for h, span in enumerate(spans):
-        out_ref[:, span] = (mixed[h] / totals[h]).astype(BF16)
+        mixed = sums_ref[:, 2 * h * WIDTH : (2 * h + 1) * WIDTH] + back_ref[:, span].astype(F32)
+        total = sums_ref[:, (2 * h + 1) * WIDTH : (2 * h + 2) * WIDTH] + far
+        out_ref[:, span] = (mixed / total).astype(BF16)
 
 
 def call(kernel, outs, smem=0, scratch=(), spaces=None, limit=LIMIT):
@@ -415,7 +432,9 @@
 
 def moved(array, axis, distance):
     size = lax.axis_size(axis)
-    return lax.ppermute(array, axis, [(i, i + distance) for i in range(size - distance)])
+    return lax.ppermute(
+        array, axis, [(i, i + distance) for i in range(size) if 0 <= i + distance < size]
+    )
 
 
 def turned(array, axis, distance):
@@ -462,19 +481,30 @@
         group_kernel, [((3, WIDTH, 2 * WIDTH), F32), pair_shape, pay_shape], 1, [four_pairs]
     )(place, own, crossed(pay1, 1), crossed(pay2, 2), crossed(pay3, 3))
     rowed = [rotated(pay, d) for d in (1, 2, 3)]
-    everything, w_out, w_qkv, stream = lax.optimization_barrier((everything, w_out, w_qkv, stream))
-    w_out, w_qkv, stream, everything = call(
-        fetch_kernel,
-        [(w_out.shape, BF16), (w_qkv.shape, BF16), row_shape, pair_shape],
-        1,
-        [pltpu.SemaphoreType.DMA((3,))],
-        [VMEM] + [pl.ANY] * 3,
-    )(place, everything, w_out, w_qkv, stream)
+    everything, w_qkv = lax.optimization_barrier((everything, w_qkv))
+    w_qkv, everything = call(
+        fetch_wide_kernel,
+        [(w_qkv.shape, BF16), pair_shape],
+        0,
+        [pltpu.SemaphoreType.DMA],
+        [VMEM, pltpu.HBM],
+        FETCH_LIMIT,
+    )(everything, w_qkv)
     before_row, pay = call(row_kernel, [pair_shape, pay_shape], 1, [four_pairs] * 2)(
         place, everything, *rowed
     )
+    earlier = [moved(pay, "seq", 16 * d) for d in (1, 2, 3)]
+    before_row, w_out, stream = lax.optimization_barrier((before_row, w_out, stream))
+    w_out, stream, before_row = call(
+        fetch_kernel,
+        [(w_out.shape, BF16), row_shape, pair_shape],
+        1,
+        [pltpu.SemaphoreType.DMA((2,))],
+        [VMEM, pltpu.HBM, pltpu.HBM],
+        FETCH_LIMIT,
+    )(place, before_row, w_out, stream)
     mine, out1, out2, out3 = call(state_kernel, [state_shape] * 4, 1, [four_states])(
-        place, *[moved(pay, "seq", 16 * d) for d in (1, 2, 3)], before_row, before
+        place, *earlier, before_row, before
     )
     terms = call(
         out_kernel,
@@ -497,22 +527,22 @@
     unit_queries, pack = call(project_kernel, [row_shape, ((rows, 2 * wide), BF16)], 1)(
         place, w_qkv, hidden, *others
     )
-    hops = [pack]
-    for _ in range(WINDOW // (2 * rows) - 1):
-        hops.append(moved(hops[-1], "seq", 2))
-    blocks = [block for hop in hops[:-1] for block in (hop, crossed(hop, 1))]
-    sums = [((rows, wide), F32)] * 2
-    mixed, totals, kept = call(near_kernel, sums + [row_shape], 1)(
-        place, hidden, unit_queries, *blocks
-    )
-    third, mixed, totals = lax.optimization_barrier((hops[-1], mixed, totals))
-    fourth = moved(third, "seq", 2)
-    mixed, totals = call(third_kernel, sums, 1)(
-        place, unit_queries, mixed, totals, third, crossed(third, 1)
-    )
-    (attended,) = call(last_kernel, [row_shape], 1)(
-        place, unit_queries, mixed, totals, fourth, crossed(fourth, 1)
-    )
+    first, visitors = lax.optimization_barrier(
+        (moved(pack, "seq", 2), moved(unit_queries, "seq", -4))
+    )
+    home = [pack, crossed(pack, 1), first, crossed(first, 1)]
+    sums_shape = ((rows, 2 * wide), F32)
+    away, kept = call(away_kernel, [sums_shape, row_shape], 1)(
+        place, hidden, visitors, home[2], home[3]
+    )
+    second, away = lax.optimization_barrier((moved(first, "seq", 2), away))
+    home += [second, crossed(second, 1)]
+    (back,) = call(back_kernel, [((rows, wide + WIDTH), BF16)], 1)(
+        place, visitors, away, home[4], home[5]
+    )
+    returned = moved(back, "seq", 4)
+    (sums,) = call(home_kernel, [sums_shape], 1)(place, unit_queries, *home)
+    (attended,) = call(last_kernel, [row_shape])(sums, returned)
     return (kept, attended)
 
 

time: 127 us -> 119 us (0.937)
  local copies, waits for them, and re-layouts: 6.78 us -> 1.52 us
  waiting for transfers between devices: 51.3 us -> 46.6 us
  starting transfers between devices: 47.4 us -> 49 us
    ppermute x7, waiting for transfers between devices: 31.8 us -> 23.8 us  [moved(): lax.ppermute(array, axis, [(i, i + distance) for i in range(size) if 0 <=...]
    ppermute x7, starting transfers between devices: 15.3 us -> 21.1 us  [moved(): lax.ppermute(array, axis, [(i, i + distance) for i in range(size) if 0 <=...]
    unnamed x10 -> x8, local copies, waits for them, and re-layouts: 6.78 us -> 1.52 us
    ppermute x11 -> x9, starting transfers between devices: 15 us -> 10.9 us  [crossed(): lax.ppermute(array, 'seq', [(i, i ^ mask) for i in range(lax.axis_size('s...]
    ppermute x3, waiting for transfers between devices: 0.01 us -> 2.19 us  [rotated(): lax.ppermute(array, 'seq', [(i, (i & -16) + (i + 4 * distance & 15)) for...]
    ppermute x11 -> x9, waiting for transfers between devices: 6.57 us -> 7.61 us  [crossed(): lax.ppermute(array, 'seq', [(i, i ^ mask) for i in range(lax.axis_size('s...]
    pallas_call x11 -> x13, Pallas kernels: 20.2 us -> 20.3 us  [run(): pl.pallas_call(kernel, out_shape=[jax.ShapeDtypeStruct(shape, kind) for s...]
  transfers between devices with their start and end apart: 27 -> 25, of which waited for: 14 -> 18; matrix products, arithmetic and copies ran while one was open for 0% -> 0% of each run, Pallas kernels for 5% -> 6%
where the time goes in v3:
time: 119 us; the launch traced here: 118 us
  starting transfers between devices  49 us (41%)
  waiting for transfers between devices  46.6 us (39%)
  Pallas kernels  20.3 us (17%)
  local copies, waits for them, and re-layouts  1.52 us (1%)
    ppermute x7, waiting for transfers between devices, moved(): lax.ppermute(array, axis, [(i, i + distance) for i in range(size) if 0 <=...  23.8 us
    ppermute x7, starting transfers between devices, moved(): lax.ppermute(array, axis, [(i, i + distance) for i in range(size) if 0 <=...  21.1 us
    pallas_call x13, Pallas kernels, run(): pl.pallas_call(kernel, out_shape=[jax.ShapeDtypeStruct(shape, kind) for s...  20.3 us
    ppermute x6, waiting for transfers between devices, turned(): lax.ppermute(array, axis, [(i, (i + distance) % size) for i in range(size)])  13 us
    ppermute x9, starting transfers between devices, crossed(): lax.ppermute(array, 'seq', [(i, i ^ mask) for i in range(lax.axis_size('s...  10.9 us
    ppermute x3, starting transfers between devices, rotated(): lax.ppermute(array, 'seq', [(i, (i & -16) + (i + 4 * distance & 15)) for...  9.05 us
    ppermute x6, starting transfers between devices, turned(): lax.ppermute(array, axis, [(i, (i + distance) % size) for i in range(size)])  8.04 us
    ppermute x9, waiting for transfers between devices, crossed(): lax.ppermute(array, 'seq', [(i, i ^ mask) for i in range(lax.axis_size('s...  7.61 us
  transfers between devices with their start and end apart: 25, of which 18 were waited for; matrix products, arithmetic and copies ran while one was open for 0% of the time, Pallas kernels for 6%

profile of v3, /device:TPU:3, one launch (start us, length us, event | category | flops | bytes accessed | tf_op | source)
XLA Modules:
  0.0 118.3 jit_solution(1443655118924415508)
XLA Ops:
  2.2 5.5 %shard_map.95 = (bf16[4,128,128]{2,1,0:T(8,128)(2,1)S(1)}, bf16[4,128,128]{2,1,0:T(8,128)(2,1)S(1)}, f32[128,256]{1,0:T(8,128)S(1)}, bf16[144,256]{1,0:T(8,128)(...) custom-call(s32[4]{0:T(128)S(1)} %pad_add_fusion.place, f32[4,128]{1,0:T(4,128)S(1)} %bitcast.6, ...), custom_call_target="tpu_custom_call" | custom-call | tf_op jit(solution)/shard_map/pallas_call | solution.py:421
  10.3 2.4 %collective-permute-done.1.recv2_ref = bf16[144,256]{1,0:T(8,128)(2,1)S(1)} collective-permute-done((bf16[144,256]{1,0:T(8,128)(2,1)S(1)}, bf16[144,256]{1,0:T(8,128)(2,1)S(1)}, u32[]{:S(2)}, u32[]{:S(2)}) %collective-permute-start.1) | collective-permute-done | bytes 73760 | tf_op jit(solution)/shard_map/ppermute | solution.py:446
  12.7 1.7 %collective-permute-done.2.recv3_ref = bf16[144,256]{1,0:T(8,128)(2,1)S(1)} collective-permute-done((bf16[144,256]{1,0:T(8,128)(2,1)S(1)}, bf16[144,256]{1,0:T(8,128)(2,1)S(1)}, u32[]{:S(2)}, u32[]{:S(2)}) %collective-permute-start.2) | collective-permute-done | bytes 73760 | tf_op jit(solution)/shard_map/ppermute | solution.py:446
  15.5 5.8 %collective-permute-start.5 = (bf16[144,256]{1,0:T(8,128)(2,1)S(1)}, bf16[144,256]{1,0:T(8,128)(2,1)S(1)}, u32[]{:S(2)}, u32[]{:S(2)}) collective-permute-start(bf16[144,256]{1,0:T(8,128)(2,1)S(1)} %get-tuple-element.47), channel_id=1, source_target_pairs={{0,48},{4,52},{8,56},{12,60},{16,0},{20,4},{24,8},{28,12},{32,16},... | collective-permute-start | bytes 221192 | tf_op jit(solution)/shard_map/ppermute | solution.py:450
  22.3 2.3 %collective-permute-start.3 = (bf16[144,256]{1,0:T(8,128)(2,1)S(1)}, bf16[144,256]{1,0:T(8,128)(2,1)S(1)}, u32[]{:S(2)}, u32[]{:S(2)}) collective-permute-start(bf16[144,256]{1,0:T(8,128)(2,1)S(1)} %get-tuple-element.47), channel_id=1, source_target_pairs={{0,16},{4,20},{8,24},{12,28},{16,32},{20,36},{24,40},{28,44},{32,4... | collective-permute-start | bytes 221192 | tf_op jit(solution)/shard_map/ppermute | solution.py:450
  24.6 2.8 %shard_map.97 = (bf16[2048,1536]{1,0:T(8,128)(2,1)S(1)}, f32[128,256]{1,0:T(8,128)S(1)}) custom-call(f32[128,256]{1,0:T(8,128)S(1)} %get-tuple-element.44.token_ref, bf16[2048,1536]{1,0:T(8,128)(2,1)} %source_ref), custom_call_target="tpu_custom_call" | custom-call | tf_op jit(solution)/shard_map/pallas_call | solution.py:421
  31.3 4.4 %collective-permute-start.7 = (bf16[144,256]{1,0:T(8,128)(2,1)S(1)}, bf16[144,256]{1,0:T(8,128)(2,1)S(1)}, u32[]{:S(2)}, u32[]{:S(2)}) collective-permute-start(bf16[144,256]{1,0:T(8,128)(2,1)S(1)} %get-tuple-element.55), channel_id=1, source_target_pairs={{0,128},{4,132},{8,136},{12,140},{16,144},{20,148},{24,152},{28,15... | collective-permute-start | bytes 221192 | tf_op jit(solution)/shard_map/ppermute | solution.py:435
  35.8 1.9 %collective-permute-start.6 = (bf16[144,256]{1,0:T(8,128)(2,1)S(1)}, bf16[144,256]{1,0:T(8,128)(2,1)S(1)}, u32[]{:S(2)}, u32[]{:S(2)}) collective-permute-start(bf16[144,256]{1,0:T(8,128)(2,1)S(1)} %get-tuple-element.55), channel_id=1, source_target_pairs={{0,64},{4,68},{8,72},{12,76},{16,80},{20,84},{24,88},{28,92},{32,9... | collective-permute-start | bytes 221192 | tf_op jit(solution)/shard_map/ppermute | solution.py:435
  38.5 2.7 %collective-permute-done.6.row1_ref = bf16[144,256]{1,0:T(8,128)(2,1)S(1)} collective-permute-done((bf16[144,256]{1,0:T(8,128)(2,1)S(1)}, bf16[144,256]{1,0:T(8,128)(2,1)S(1)}, u32[]{:S(2)}, u32[]{:S(2)}) %collective-permute-start.6) | collective-permute-done | bytes 73760 | tf_op jit(solution)/shard_map/ppermute | solution.py:435
  42.3 3.8 %collective-permute-start.9 = (bf16[128,128]{1,0:T(8,128)(2,1)S(1)}, bf16[128,128]{1,0:T(8,128)(2,1)S(1)}, u32[]{:S(2)}, u32[]{:S(2)}) collective-permute-start(bf16[128,128]{1,0:T(8,128)(2,1)S(1)} %get-tuple-element.59), channel_id=1, source_target_pairs={{0,4},{4,0},{8,12},{12,8},{16,20},{20,16},{24,28},{28,24},{32,36},... | collective-permute-start | bytes 98312 | tf_op jit(solution)/shard_map/ppermute | solution.py:446
  52.7 2.6 %collective-permute-start.13 = (bf16[128,512]{1,0:T(8,128)(2,1)S(1)}, bf16[128,512]{1,0:T(8,128)(2,1)S(1)}, u32[]{:S(2)}, u32[]{:S(2)}) collective-permute-start(bf16[128,512]{1,0:T(8,128)(2,1)S(1)} %get-tuple-element.65), channel_id=1, source_target_pairs={{0,2},{1,3},{2,0},{3,1},{4,6},{5,7},{6,4},{7,5},{8,10},{9,11},{10,... | collective-permute-start | bytes 393224 | tf_op jit(solution)/shard_map/ppermute | solution.py:442
  57.5 3.9 %collective-permute-done.13.refs_1_ = bf16[128,512]{1,0:T(8,128)(2,1)S(1)} collective-permute-done((bf16[128,512]{1,0:T(8,128)(2,1)S(1)}, bf16[128,512]{1,0:T(8,128)(2,1)S(1)}, u32[]{:S(2)}, u32[]{:S(2)}) %collective-permute-start.13) | collective-permute-done | bytes 131104 | tf_op jit(solution)/shard_map/ppermute | solution.py:442
  61.5 2.1 %collective-permute-start.17 = (bf16[128,512]{1,0:T(8,128)(2,1)S(1)}, bf16[128,512]{1,0:T(8,128)(2,1)S(1)}, u32[]{:S(2)}, u32[]{:S(2)}) collective-permute-start(bf16[128,512]{1,0:T(8,128)(2,1)S(1)} %shard_map.102.refs_0_.hidden_ref), channel_id=1, source_target_pairs={{0,3},{1,0},{2,1},{3,2},{4,7},{5,4},{6,5},{7,6},{8,11},{9,8},{10,9... | collective-permute-start | bytes 393224 | tf_op jit(solution)/shard_map/ppermute | solution.py:442
  64.5 2.4 %collective-permute-done.17.refs_3_ = bf16[128,512]{1,0:T(8,128)(2,1)S(1)} collective-permute-done((bf16[128,512]{1,0:T(8,128)(2,1)S(1)}, bf16[128,512]{1,0:T(8,128)(2,1)S(1)}, u32[]{:S(2)}, u32[]{:S(2)}) %collective-permute-start.17) | collective-permute-done | bytes 131104 | tf_op jit(solution)/shard_map/ppermute | solution.py:442
  66.8 2.2 %collective-permute-done.16.refs_2_ = bf16[128,512]{1,0:T(8,128)(2,1)S(1)} collective-permute-done((bf16[128,512]{1,0:T(8,128)(2,1)S(1)}, bf16[128,512]{1,0:T(8,128)(2,1)S(1)}, u32[]{:S(2)}, u32[]{:S(2)}) %collective-permute-start.16) | collective-permute-done | bytes 131104 | tf_op jit(solution)/shard_map/ppermute | solution.py:442
  69.0 3.5 %collective-permute-done.15.refs_1_ = bf16[128,512]{1,0:T(8,128)(2,1)S(1)} collective-permute-done((bf16[128,512]{1,0:T(8,128)(2,1)S(1)}, bf16[128,512]{1,0:T(8,128)(2,1)S(1)}, u32[]{:S(2)}, u32[]{:S(2)}) %collective-permute-start.15) | collective-permute-done | bytes 131104 | tf_op jit(solution)/shard_map/ppermute | solution.py:442
  74.2 2.7 %collective-permute-start.18 = (bf16[128,1024]{1,0:T(8,128)(2,1)S(1)}, bf16[128,1024]{1,0:T(8,128)(2,1)S(1)}, u32[]{:S(2)}, u32[]{:S(2)}) collective-permute-start(bf16[128,1024]{1,0:T(8,128)(2,1)S(1)} %get-tuple-element.68.refs_0_), channel_id=1, source_target_pairs={{0,8},{4,12},{8,16},{12,20},{16,24},{20,28},{24,32},{28,36},{32,40... | collective-permute-start | bytes 786440 | tf_op jit(solution)/shard_map/ppermute | solution.py:435
  76.9 3.6 %collective-permute-start.19 = (bf16[128,512]{1,0:T(8,128)(2,1)S(1)}, bf16[128,512]{1,0:T(8,128)(2,1)S(1)}, u32[]{:S(2)}, u32[]{:S(2)}) collective-permute-start(bf16[128,512]{1,0:T(8,128)(2,1)S(1)} %get-tuple-element.69.q_ref), channel_id=1, source_target_pairs={{16,0},{20,4},{24,8},{28,12},{32,16},{36,20},{40,24},{44,28},{48,3... | collective-permute-start | bytes 393224 | tf_op jit(solution)/shard_map/ppermute | solution.py:435
  80.5 3.3 %collective-permute-done.19.q_ref = bf16[128,512]{1,0:T(8,128)(2,1)S(1)} collective-permute-done((bf16[128,512]{1,0:T(8,128)(2,1)S(1)}, bf16[128,512]{1,0:T(8,128)(2,1)S(1)}, u32[]{:S(2)}, u32[]{:S(2)}) %collective-permute-start.19) | collective-permute-done | bytes 131104 | tf_op jit(solution)/shard_map/ppermute | solution.py:435
  84.7 2.3 %collective-permute-start.20 = (bf16[128,1024]{1,0:T(8,128)(2,1)S(1)}, bf16[128,1024]{1,0:T(8,128)(2,1)S(1)}, u32[]{:S(2)}, u32[]{:S(2)}) collective-permute-start(bf16[128,1024]{1,0:T(8,128)(2,1)S(1)} %collective-permute-done.18.own_ref.refs_2_), channel_id=1, source_target_pairs={{0,4},{4,0},{8,12},{12,8},{16,20},{20,16},{24,28},{28,24},{32,36},... | collective-permute-start | bytes 786440 | tf_op jit(solution)/shard_map/ppermute | solution.py:446
  86.9 5.1 %collective-permute-start.22 = (bf16[128,1024]{1,0:T(8,128)(2,1)S(1)}, bf16[128,1024]{1,0:T(8,128)(2,1)S(1)}, u32[]{:S(2)}, u32[]{:S(2)}) collective-permute-start(bf16[128,1024]{1,0:T(8,128)(2,1)S(1)} %collective-permute-done.18.own_ref.refs_2_), channel_id=1, source_target_pairs={{0,8},{4,12},{8,16},{12,20},{16,24},{20,28},{24,32},{28,36},{32,40... | collective-permute-start | bytes 786440 | tf_op jit(solution)/shard_map/ppermute | solution.py:435
  93.5 7.0 %collective-permute-done.22.refs_4_.own_ref = bf16[128,1024]{1,0:T(8,128)(2,1)S(1)} collective-permute-done((bf16[128,1024]{1,0:T(8,128)(2,1)S(1)}, bf16[128,1024]{1,0:T(8,128)(2,1)S(1)}, u32[]{:S(2)}, u32[]{:S(2)}) %collective-permute-start.22) | collective-permute-done | bytes 262176 | tf_op jit(solution)/shard_map/ppermute | solution.py:435
  103.2 2.7 %collective-permute-start.24 = (bf16[128,640]{1,0:T(8,128)(2,1)S(1)}, bf16[128,640]{1,0:T(8,128)(2,1)S(1)}, u32[]{:S(2)}, u32[]{:S(2)}) collective-permute-start(bf16[128,640]{1,0:T(8,128)(2,1)S(1)} %shard_map.106), channel_id=1, source_target_pairs={{0,16},{4,20},{8,24},{12,28},{16,32},{20,36},{24,40},{28,44},{32,4... | collective-permute-start | bytes 491528 | tf_op jit(solution)/shard_map/ppermute | solution.py:435
  107.4 10.0 %collective-permute-done.24.back_ref = bf16[128,640]{1,0:T(8,128)(2,1)S(1)} collective-permute-done((bf16[128,640]{1,0:T(8,128)(2,1)S(1)}, bf16[128,640]{1,0:T(8,128)(2,1)S(1)}, u32[]{:S(2)}, u32[]{:S(2)}) %collective-permute-start.24) | collective-permute-done | bytes 163872 | tf_op jit(solution)/shard_map/ppermute | solution.py:435
  (48 shorter events, 30.9 us)
Async XLA Ops:
  7.8 2.5 %collective-permute-start = (bf16[144,256]{1,0:T(8,128)(2,1)S(1)}, bf16[144,256]{1,0:T(8,128)(2,1)S(1)}, u32[]{:S(2)}, u32[]{:S(2)}) collective-permute-start(bf16[144,256]{1,0:T(8,128)(2,1)S(1)} %get-tuple-element.40), channel_id=1, source_target_pairs={{0,4},{4,0},{8,12},{12,8},{16,20},{20,16},{24,28},{28,24},{32,36},... | collective-permute-start | bytes 221192 | tf_op jit(solution)/shard_map/ppermute | solution.py:446
  8.6 4.1 %collective-permute-start.1 = (bf16[144,256]{1,0:T(8,128)(2,1)S(1)}, bf16[144,256]{1,0:T(8,128)(2,1)S(1)}, u32[]{:S(2)}, u32[]{:S(2)}) collective-permute-start(bf16[144,256]{1,0:T(8,128)(2,1)S(1)} %get-tuple-element.41), channel_id=1, source_target_pairs={{0,8},{4,12},{8,0},{12,4},{16,24},{20,28},{24,16},{28,20},{32,40},... | collective-permute-start | bytes 221192 | tf_op jit(solution)/shard_map/ppermute | solution.py:446
  10.2 4.2 %collective-permute-start.2 = (bf16[144,256]{1,0:T(8,128)(2,1)S(1)}, bf16[144,256]{1,0:T(8,128)(2,1)S(1)}, u32[]{:S(2)}, u32[]{:S(2)}) collective-permute-start(bf16[144,256]{1,0:T(8,128)(2,1)S(1)} %get-tuple-element.42), channel_id=1, source_target_pairs={{0,12},{4,8},{8,4},{12,0},{16,28},{20,24},{24,20},{28,16},{32,44},... | collective-permute-start | bytes 221192 | tf_op jit(solution)/shard_map/ppermute | solution.py:446
  15.5 11.9 %collective-permute-start.5 = (bf16[144,256]{1,0:T(8,128)(2,1)S(1)}, bf16[144,256]{1,0:T(8,128)(2,1)S(1)}, u32[]{:S(2)}, u32[]{:S(2)}) collective-permute-start(bf16[144,256]{1,0:T(8,128)(2,1)S(1)} %get-tuple-element.47), channel_id=1, source_target_pairs={{0,48},{4,52},{8,56},{12,60},{16,0},{20,4},{24,8},{28,12},{32,16},... | collective-permute-start | bytes 221192 | tf_op jit(solution)/shard_map/ppermute | solution.py:450
  21.3 7.3 %collective-permute-start.4 = (bf16[144,256]{1,0:T(8,128)(2,1)S(1)}, bf16[144,256]{1,0:T(8,128)(2,1)S(1)}, u32[]{:S(2)}, u32[]{:S(2)}) collective-permute-start(bf16[144,256]{1,0:T(8,128)(2,1)S(1)} %get-tuple-element.47), channel_id=1, source_target_pairs={{0,32},{4,36},{8,40},{12,44},{16,48},{20,52},{24,56},{28,60},{32,0... | collective-permute-start | bytes 221192 | tf_op jit(solution)/shard_map/ppermute | solution.py:450
  22.3 7.3 %collective-permute-start.3 = (bf16[144,256]{1,0:T(8,128)(2,1)S(1)}, bf16[144,256]{1,0:T(8,128)(2,1)S(1)}, u32[]{:S(2)}, u32[]{:S(2)}) collective-permute-start(bf16[144,256]{1,0:T(8,128)(2,1)S(1)} %get-tuple-element.47), channel_id=1, source_target_pairs={{0,16},{4,20},{8,24},{12,28},{16,32},{20,36},{24,40},{28,44},{32,4... | collective-permute-start | bytes 221192 | tf_op jit(solution)/shard_map/ppermute | solution.py:450
  30.7 7.8 %collective-permute-start.8 = (bf16[144,256]{1,0:T(8,128)(2,1)S(1)}, bf16[144,256]{1,0:T(8,128)(2,1)S(1)}, u32[]{:S(2)}, u32[]{:S(2)}) collective-permute-start(bf16[144,256]{1,0:T(8,128)(2,1)S(1)} %get-tuple-element.55), channel_id=1, source_target_pairs={{0,192},{4,196},{8,200},{12,204},{16,208},{20,212},{24,216},{28,22... | collective-permute-start | bytes 221192 | tf_op jit(solution)/shard_map/ppermute | solution.py:435
  31.3 7.2 %collective-permute-start.7 = (bf16[144,256]{1,0:T(8,128)(2,1)S(1)}, bf16[144,256]{1,0:T(8,128)(2,1)S(1)}, u32[]{:S(2)}, u32[]{:S(2)}) collective-permute-start(bf16[144,256]{1,0:T(8,128)(2,1)S(1)} %get-tuple-element.55), channel_id=1, source_target_pairs={{0,128},{4,132},{8,136},{12,140},{16,144},{20,148},{24,152},{28,15... | collective-permute-start | bytes 221192 | tf_op jit(solution)/shard_map/ppermute | solution.py:435
  35.8 5.4 %collective-permute-start.6 = (bf16[144,256]{1,0:T(8,128)(2,1)S(1)}, bf16[144,256]{1,0:T(8,128)(2,1)S(1)}, u32[]{:S(2)}, u32[]{:S(2)}) collective-permute-start(bf16[144,256]{1,0:T(8,128)(2,1)S(1)} %get-tuple-element.55), channel_id=1, source_target_pairs={{0,64},{4,68},{8,72},{12,76},{16,80},{20,84},{24,88},{28,92},{32,9... | collective-permute-start | bytes 221192 | tf_op jit(solution)/shard_map/ppermute | solution.py:435
  42.3 5.5 %collective-permute-start.9 = (bf16[128,128]{1,0:T(8,128)(2,1)S(1)}, bf16[128,128]{1,0:T(8,128)(2,1)S(1)}, u32[]{:S(2)}, u32[]{:S(2)}) collective-permute-start(bf16[128,128]{1,0:T(8,128)(2,1)S(1)} %get-tuple-element.59), channel_id=1, source_target_pairs={{0,4},{4,0},{8,12},{12,8},{16,20},{20,16},{24,28},{28,24},{32,36},... | collective-permute-start | bytes 98312 | tf_op jit(solution)/shard_map/ppermute | solution.py:446
  46.1 2.8 %collective-permute-start.10 = (bf16[128,128]{1,0:T(8,128)(2,1)S(1)}, bf16[128,128]{1,0:T(8,128)(2,1)S(1)}, u32[]{:S(2)}, u32[]{:S(2)}) collective-permute-start(bf16[128,128]{1,0:T(8,128)(2,1)S(1)} %get-tuple-element.60), channel_id=1, source_target_pairs={{0,8},{4,12},{8,0},{12,4},{16,24},{20,28},{24,16},{28,20},{32,40},... | collective-permute-start | bytes 98312 | tf_op jit(solution)/shard_map/ppermute | solution.py:446
  46.7 3.4 %collective-permute-start.11 = (bf16[128,128]{1,0:T(8,128)(2,1)S(1)}, bf16[128,128]{1,0:T(8,128)(2,1)S(1)}, u32[]{:S(2)}, u32[]{:S(2)}) collective-permute-start(bf16[128,128]{1,0:T(8,128)(2,1)S(1)} %get-tuple-element.61), channel_id=1, source_target_pairs={{0,12},{4,8},{8,4},{12,0},{16,28},{20,24},{24,20},{28,16},{32,44},... | collective-permute-start | bytes 98312 | tf_op jit(solution)/shard_map/ppermute | solution.py:446
  51.3 6.1 %collective-permute-start.12 = (bf16[128,512]{1,0:T(8,128)(2,1)S(1)}, bf16[128,512]{1,0:T(8,128)(2,1)S(1)}, u32[]{:S(2)}, u32[]{:S(2)}) collective-permute-start(bf16[128,512]{1,0:T(8,128)(2,1)S(1)} %get-tuple-element.64), channel_id=1, source_target_pairs={{0,1},{1,2},{2,3},{3,0},{4,5},{5,6},{6,7},{7,4},{8,9},{9,10},{10,1... | collective-permute-start | bytes 393224 | tf_op jit(solution)/shard_map/ppermute | solution.py:442
  52.7 8.7 %collective-permute-start.13 = (bf16[128,512]{1,0:T(8,128)(2,1)S(1)}, bf16[128,512]{1,0:T(8,128)(2,1)S(1)}, u32[]{:S(2)}, u32[]{:S(2)}) collective-permute-start(bf16[128,512]{1,0:T(8,128)(2,1)S(1)} %get-tuple-element.65), channel_id=1, source_target_pairs={{0,2},{1,3},{2,0},{3,1},{4,6},{5,7},{6,4},{7,5},{8,10},{9,11},{10,... | collective-permute-start | bytes 393224 | tf_op jit(solution)/shard_map/ppermute | solution.py:442
  55.3 6.0 %collective-permute-start.14 = (bf16[128,512]{1,0:T(8,128)(2,1)S(1)}, bf16[128,512]{1,0:T(8,128)(2,1)S(1)}, u32[]{:S(2)}, u32[]{:S(2)}) collective-permute-start(bf16[128,512]{1,0:T(8,128)(2,1)S(1)} %get-tuple-element.66), channel_id=1, source_target_pairs={{0,3},{1,0},{2,1},{3,2},{4,7},{5,4},{6,5},{7,6},{8,11},{9,8},{10,9... | collective-permute-start | bytes 393224 | tf_op jit(solution)/shard_map/ppermute | solution.py:442
  61.5 5.4 %collective-permute-start.17 = (bf16[128,512]{1,0:T(8,128)(2,1)S(1)}, bf16[128,512]{1,0:T(8,128)(2,1)S(1)}, u32[]{:S(2)}, u32[]{:S(2)}) collective-permute-start(bf16[128,512]{1,0:T(8,128)(2,1)S(1)} %shard_map.102.refs_0_.hidden_ref), channel_id=1, source_target_pairs={{0,3},{1,0},{2,1},{3,2},{4,7},{5,4},{6,5},{7,6},{8,11},{9,8},{10,9... | collective-permute-start | bytes 393224 | tf_op jit(solution)/shard_map/ppermute | solution.py:442
  63.6 5.4 %collective-permute-start.16 = (bf16[128,512]{1,0:T(8,128)(2,1)S(1)}, bf16[128,512]{1,0:T(8,128)(2,1)S(1)}, u32[]{:S(2)}, u32[]{:S(2)}) collective-permute-start(bf16[128,512]{1,0:T(8,128)(2,1)S(1)} %shard_map.102.refs_0_.hidden_ref), channel_id=1, source_target_pairs={{0,2},{1,3},{2,0},{3,1},{4,6},{5,7},{6,4},{7,5},{8,10},{9,11},{10,... | collective-permute-start | bytes 393224 | tf_op jit(solution)/shard_map/ppermute | solution.py:442
  64.3 8.1 %collective-permute-start.15 = (bf16[128,512]{1,0:T(8,128)(2,1)S(1)}, bf16[128,512]{1,0:T(8,128)(2,1)S(1)}, u32[]{:S(2)}, u32[]{:S(2)}) collective-permute-start(bf16[128,512]{1,0:T(8,128)(2,1)S(1)} %shard_map.102.refs_0_.hidden_ref), channel_id=1, source_target_pairs={{0,1},{1,2},{2,3},{3,0},{4,5},{5,6},{6,7},{7,4},{8,9},{9,10},{10,1... | collective-permute-start | bytes 393224 | tf_op jit(solution)/shard_map/ppermute | solution.py:442
  74.2 10.5 %collective-permute-start.18 = (bf16[128,1024]{1,0:T(8,128)(2,1)S(1)}, bf16[128,1024]{1,0:T(8,128)(2,1)S(1)}, u32[]{:S(2)}, u32[]{:S(2)}) collective-permute-start(bf16[128,1024]{1,0:T(8,128)(2,1)S(1)} %get-tuple-element.68.refs_0_), channel_id=1, source_target_pairs={{0,8},{4,12},{8,16},{12,20},{16,24},{20,28},{24,32},{28,36},{32,40... | collective-permute-start | bytes 786440 | tf_op jit(solution)/shard_map/ppermute | solution.py:435
  76.9 6.9 %collective-permute-start.19 = (bf16[128,512]{1,0:T(8,128)(2,1)S(1)}, bf16[128,512]{1,0:T(8,128)(2,1)S(1)}, u32[]{:S(2)}, u32[]{:S(2)}) collective-permute-start(bf16[128,512]{1,0:T(8,128)(2,1)S(1)} %get-tuple-element.69.q_ref), channel_id=1, source_target_pairs={{16,0},{20,4},{24,8},{28,12},{32,16},{36,20},{40,24},{44,28},{48,3... | collective-permute-start | bytes 393224 | tf_op jit(solution)/shard_map/ppermute | solution.py:435
  84.7 7.3 %collective-permute-start.20 = (bf16[128,1024]{1,0:T(8,128)(2,1)S(1)}, bf16[128,1024]{1,0:T(8,128)(2,1)S(1)}, u32[]{:S(2)}, u32[]{:S(2)}) collective-permute-start(bf16[128,1024]{1,0:T(8,128)(2,1)S(1)} %collective-permute-done.18.own_ref.refs_2_), channel_id=1, source_target_pairs={{0,4},{4,0},{8,12},{12,8},{16,20},{20,16},{24,28},{28,24},{32,36},... | collective-permute-start | bytes 786440 | tf_op jit(solution)/shard_map/ppermute | solution.py:446
  86.9 13.6 %collective-permute-start.22 = (bf16[128,1024]{1,0:T(8,128)(2,1)S(1)}, bf16[128,1024]{1,0:T(8,128)(2,1)S(1)}, u32[]{:S(2)}, u32[]{:S(2)}) collective-permute-start(bf16[128,1024]{1,0:T(8,128)(2,1)S(1)} %collective-permute-done.18.own_ref.refs_2_), channel_id=1, source_target_pairs={{0,8},{4,12},{8,16},{12,20},{16,24},{20,28},{24,32},{28,36},{32,40... | collective-permute-start | bytes 786440 | tf_op jit(solution)/shard_map/ppermute | solution.py:435
  101.1 4.8 %collective-permute-start.21 = (bf16[128,1024]{1,0:T(8,128)(2,1)S(1)}, bf16[128,1024]{1,0:T(8,128)(2,1)S(1)}, u32[]{:S(2)}, u32[]{:S(2)}) collective-permute-start(bf16[128,1024]{1,0:T(8,128)(2,1)S(1)} %get-tuple-element.68.refs_0_), channel_id=1, source_target_pairs={{0,4},{4,0},{8,12},{12,8},{16,20},{20,16},{24,28},{28,24},{32,36},... | collective-permute-start | bytes 786440 | tf_op jit(solution)/shard_map/ppermute | solution.py:446
  103.2 14.3 %collective-permute-start.24 = (bf16[128,640]{1,0:T(8,128)(2,1)S(1)}, bf16[128,640]{1,0:T(8,128)(2,1)S(1)}, u32[]{:S(2)}, u32[]{:S(2)}) collective-permute-start(bf16[128,640]{1,0:T(8,128)(2,1)S(1)} %shard_map.106), channel_id=1, source_target_pairs={{0,16},{4,20},{8,24},{12,28},{16,32},{20,36},{24,40},{28,44},{32,4... | collective-permute-start | bytes 491528 | tf_op jit(solution)/shard_map/ppermute | solution.py:435
  (5 other events, 77.4 us)

commit v4 on v3

--- a/solution.py
+++ b/solution.py
@@ -17,7 +17,7 @@
 SMEM = pltpu.SMEM
 LIMIT = 16 * 1024 * 1024
 FETCH_LIMIT = 44 * 1024 * 1024
-CHUNK_LIMIT = 54579 * 1024
+CHUNK_LIMIT = 54448 * 1024
 
 
 def dot(left, right, contract=(1, 0), precision=None):
@@ -131,63 +131,44 @@
     return results
 
 
-def chunk_kernel(
-    place,
-    g_ref,
-    b_ref,
-    q_hbm,
-    k_hbm,
-    v_hbm,
-    local_ref,
-    through_ref,
-    own_ref,
-    pay1_ref,
-    pay2_ref,
-    pay3_ref,
-    q_ref,
-    k_ref,
-    v_ref,
-    pairs,
-    sems,
+def decays(g_ref):
+    groups, rows = g_ref.shape
+    row, column = iotas(rows, rows)
+    gates = g_ref[...]
+    causal = row >= column
+    summed = exact(causal.astype(F32), gates, (1, 1))
+    summed_row = exact(gates, (row <= column).astype(F32))
+    spreads = [summed[:, h : h + 1] - summed_row[h : h + 1, :] for h in range(groups)]
+    return summed, [
+        jnp.where(causal, jnp.exp(jnp.where(causal, spread, 0.0)), 0.0) for spread in spreads
+    ]
+
+
+def map_kernel(
+    place, g_ref, b_ref, k_hbm, v_hbm, keys_ref, writes_ref, erasers_ref, own_ref, pay1_ref, pay2_ref, pay3_ref, k_ref, v_ref, pairs, sems
 ):
     part = place[1]
     groups, rows = g_ref.shape
     loads = [
-        pltpu.make_async_copy(src, dst, sems.at[n])
-        for n, (src, dst) in enumerate(
-            [
-                (k_hbm, k_ref),
-                (q_hbm, q_ref),
-                (v_hbm, v_ref),
-            ]
-        )
+        pltpu.make_async_copy(k_hbm, k_ref, sems.at[0]),
+        pltpu.make_async_copy(v_hbm, v_ref, sems.at[1]),
     ]
     for load in loads:
         load.start()
     row, column = iotas(rows, rows)
-    causal = row >= column
-    strict = row > column
-    gates = g_ref[...]
-    summed = exact(causal.astype(F32), gates, (1, 1))
-    summed_row = exact(gates, (row <= column).astype(F32))
+    summed, decay = decays(g_ref)
     betas = exact((row == column).astype(F32), b_ref[...], (1, 1))
     loads[0].wait()
-    loads[1].wait()
-    keys, mixings, couplings, decayed = [], [], [], []
+    keys, couplings = [], []
     for h in range(groups):
         span = slice(h * WIDTH, (h + 1) * WIDTH)
         key = to_unit(k_ref[:, span].astype(F32)).astype(BF16)
-        query = to_unit(q_ref[:, span].astype(F32)).astype(BF16)
-        along = summed[:, h : h + 1]
-        spread = along - summed_row[h : h + 1, :]
-        decay = jnp.where(causal, jnp.exp(jnp.where(causal, spread, 0.0)), 0.0)
-        both = dot(jnp.concatenate([key, query], axis=0), key, (1, 1))
-        couplings.append(jnp.where(strict, betas[:, h : h + 1] * decay * both[:rows], 0.0))
-        mixings.append((both[rows:] * decay).astype(BF16))
+        keys_ref[:, span] = key
+        both = dot(key, key, (1, 1))
+        couplings.append(jnp.where(row > column, betas[:, h : h + 1] * decay[h] * both, 0.0))
         keys.append(key.astype(F32))
-        decayed.append(jnp.exp(along) * query.astype(F32))
     inverses = lower_inverses(couplings)
-    loads[2].wait()
+    loads[1].wait()
     for h in range(groups):
         span = slice(h * WIDTH, (h + 1) * WIDTH)
         along = summed[:, h : h + 1]
@@ -198,11 +179,9 @@
             inverses[h],
             jnp.concatenate([beta * value, (beta * jnp.exp(along)) * keys[h]], axis=1),
         ).astype(BF16)
+        writes_ref[h], erasers_ref[h] = parted(made)
         ended = (jnp.exp(last - along) * keys[h]).astype(BF16)
         effect = dot(ended, made, (0, 0))
-        inner = dot(mixings[h], made)
-        local_ref[h] = inner[:, :WIDTH].astype(BF16)
-        through_ref[h] = (decayed[h] - inner[:, WIDTH:]).astype(BF16)
         identity = iotas(WIDTH, WIDTH)
         kept = jnp.where(identity[0] == identity[1], jnp.exp(last), 0.0)
         pairs[h, :, 0:WIDTH] = kept - effect[:, WIDTH:]
@@ -212,18 +191,35 @@
         store_payload(ref, parted(pairs[part ^ r]))
 
 
-def group_kernel(place, own_ref, recv1_ref, recv2_ref, recv3_ref, before_ref, all_ref, pay_ref, pairs):
+def query_kernel(g_ref, q_ref, keys_ref, writes_ref, erasers_ref, local_ref, through_ref):
+    groups = g_ref.shape[0]
+    summed, decay = decays(g_ref)
+    for h in range(groups):
+        span = slice(h * WIDTH, (h + 1) * WIDTH)
+        query = to_unit(q_ref[:, span].astype(F32)).astype(BF16)
+        mixing = (dot(query, keys_ref[:, span], (1, 1)) * decay[h]).astype(BF16)
+        inner = dot(mixing, joined((writes_ref[h], erasers_ref[h])))
+        local_ref[h] = inner[:, :WIDTH].astype(BF16)
+        decayed = jnp.exp(summed[:, h : h + 1]) * query.astype(F32)
+        through_ref[h] = (decayed - inner[:, WIDTH:]).astype(BF16)
+
+
+def prefixes(blocks):
+    two = compose(blocks[1], blocks[0])
+    return two, compose(blocks[2], two), compose(compose(blocks[3], blocks[2]), two)
+
+
+def group_kernel(place, own_ref, recv2_ref, recv3_ref, recv1_ref, before_ref, all_ref, pay_ref, pairs):
     part = place[1]
     pairs[part] = own_ref[...]
     for r, ref in ((1, recv1_ref), (2, recv2_ref), (3, recv3_ref)):
         pairs[part ^ r] = joined(load_payload(ref))
-    blocks = [parted(pairs[n]) for n in range(4)]
-    total = blocks[0]
-    for n in range(1, 4):
-        before_ref[n - 1] = joined(total)
-        total = compose(blocks[n], total)
+    two, three, total = prefixes([parted(pairs[n]) for n in range(4)])
+    store_payload(pay_ref, total)
     all_ref[...] = joined(total)
-    store_payload(pay_ref, total)
+    before_ref[0] = pairs[0]
+    before_ref[1] = joined(two)
+    before_ref[2] = joined(three)
 
 
 def fetch_wide_kernel(token_ref, source_ref, fetched_ref, token_out, sem):
@@ -233,7 +229,9 @@
     load.wait()
 
 
-def fetch_kernel(place, token_ref, weight_ref, stream_ref, weight_out, stream_out, token_out, sems):
+def fetch_kernel(
+    place, before_row_ref, before_ref, weight_ref, stream_ref, weight_out, stream_out, maps_ref, sems
+):
     width = stream_out.shape[1]
     begin = pl.multiple_of(place[2] * width, width)
     loads = [
@@ -242,44 +240,42 @@
     ]
     for load in loads:
         load.start()
-    token_out[...] = token_ref[...]
+    maps_ref[0] = before_row_ref[...]
+    for n in range(3):
+        maps_ref[n + 1] = joined(compose(parted(before_ref[n]), parted(before_row_ref[...])))
     for load in loads:
         load.wait()
 
 
-def row_kernel(place, all_ref, recv1_ref, recv2_ref, recv3_ref, before_ref, pay_ref, pairs, starts):
+def row_kernel(place, all_ref, recv2_ref, recv1_ref, recv3_ref, before_ref, pay_ref, pairs, starts):
     group = place[3]
     pairs[group] = all_ref[...]
     for d, ref in ((1, recv1_ref), (2, recv2_ref), (3, recv3_ref)):
         pairs[(group + 4 - d) & 3] = joined(load_payload(ref))
+    two, three, total = prefixes([parted(pairs[n]) for n in range(4)])
+    store_payload(pay_ref, total)
     row, column = iotas(WIDTH, 2 * WIDTH)
     starts[0] = (row == column).astype(F32)
-    total = parted(pairs[0])
-    for n in range(1, 4):
-        starts[n] = joined(total)
-        total = compose(parted(pairs[n]), total)
+    starts[1] = pairs[0]
+    starts[2] = joined(two)
+    starts[3] = joined(three)
     before_ref[...] = starts[group]
-    store_payload(pay_ref, total)
-
-
-def state_kernel(
-    place, row1_ref, row2_ref, row3_ref, before_row_ref, before_ref, mine_ref, out1_ref, out2_ref, out3_ref, states
-):
+
+
+def state_kernel(place, row2_ref, row1_ref, row3_ref, maps_ref, mine_ref, out1_ref, out2_ref, out3_ref, states):
     part = place[1]
     state = load_payload(row3_ref)[1]
     state = apply(load_payload(row2_ref), state)
     state = apply(load_payload(row1_ref), state)
-    state = apply(parted(before_row_ref[...]), state)
-    states[0] = state.astype(BF16)
-    for n in range(3):
-        states[n + 1] = apply(parted(before_ref[n]), state).astype(BF16)
+    for n in range(4):
+        states[n] = apply(parted(maps_ref[n]), state).astype(BF16)
     mine_ref[...] = states[part]
     for r, ref in ((1, out1_ref), (2, out2_ref), (3, out3_ref)):
         ref[...] = states[part ^ r]
 
 
 def out_kernel(
-    place, local_ref, through_ref, mine_ref, recv1_ref, recv2_ref, recv3_ref, w_ref, term_ref, *refs
+    place, local_ref, through_ref, mine_ref, recv2_ref, recv3_ref, recv1_ref, w_ref, term_ref, *refs
 ):
     part = place[1]
     me = place[2]
@@ -324,9 +320,9 @@
     squares = sum(jnp.sum(v * v, axis=-1, keepdims=True) for v in values)
     scale = lax.rsqrt(squares / (count * width) + 1e-05)
     total = None
-    for r in range(count):
+    for n, r in enumerate((0, 2, 1, 3)):
         begin = pl.multiple_of(lax.rem(me + count - r, count) * width, width)
-        part = dot((values[r] * scale).astype(BF16), w_ref[pl.ds(begin, width), :])
+        part = dot((values[n] * scale).astype(BF16), w_ref[pl.ds(begin, width), :])
         total = part if total is None else total + part
     groups = q_ref.shape[1] // WIDTH
     for h in range(groups):
@@ -364,22 +360,16 @@
     return [slice(2 * h * WIDTH, 2 * (h + 1) * WIDTH) for h in range(groups)]
 
 
-def away_kernel(place, hidden_ref, q_ref, own_ref, other_ref, sums_ref, keep_ref):
-    keep_ref[...] = hidden_ref[...]
-    seq = place[0]
-    groups = q_ref.shape[1] // WIDTH
-    sums = [None] * groups
-    window_part(seq + 4, (seq >> 1) - 1, seq & 1, q_ref, own_ref, other_ref, sums)
-    for h, span in enumerate(sum_spans(groups)):
-        sums_ref[:, span] = sums[h]
-
-
-def back_kernel(place, q_ref, sums_ref, own_ref, other_ref, back_ref):
+def back_kernel(place, hidden_ref, q_ref, *refs):
+    blocks, (back_ref, keep_ref) = refs[:-2], refs[-2:]
     seq = place[0]
     rows = q_ref.shape[0]
     groups = q_ref.shape[1] // WIDTH
-    sums = [sums_ref[:, span] for span in sum_spans(groups)]
-    window_part(seq + 4, (seq >> 1) - 2, seq & 1, q_ref, own_ref, other_ref, sums)
+    sums = [None] * groups
+    for n in range(len(blocks) // 2):
+        window_part(
+            seq + 4, (seq >> 1) - 1 - n, seq & 1, q_ref, blocks[2 * n], blocks[2 * n + 1], sums
+        )
     _, column = iotas(rows, WIDTH)
     totals = jnp.zeros((rows, WIDTH), BF16)
     for h in range(groups):
@@ -389,6 +379,7 @@
         low = (total - high.astype(F32)).astype(BF16)
         totals = jnp.where(column == 2 * h, high, jnp.where(column == 2 * h + 1, low, totals))
     back_ref[:, groups * WIDTH :] = totals
+    keep_ref[...] = hidden_ref[...]
 
 
 def home_kernel(place, q_ref, *refs):
@@ -468,19 +459,24 @@
     four_pairs = pltpu.VMEM((4, WIDTH, 2 * WIDTH), F32)
     four_states = pltpu.VMEM((4, WIDTH, WIDTH), BF16)
 
-    local, through, own, pay1, pay2, pay3 = call(
-        chunk_kernel,
-        [((groups, rows, WIDTH), BF16)] * 2 + [pair_shape]
-        + [pay_shape] * 3,
+    gates = gate_log.T
+    unit_keys, writes, erasers, own, pay1, pay2, pay3 = call(
+        map_kernel,
+        [row_shape] + [((groups, rows, WIDTH), BF16)] * 2 + [pair_shape] + [pay_shape] * 3,
         1,
-        [pltpu.VMEM((rows, wide), BF16)] * 3 + [four_pairs, pltpu.SemaphoreType.DMA((3,))],
-        [VMEM, VMEM] + [pltpu.HBM] * 3,
+        [pltpu.VMEM((rows, wide), BF16)] * 2 + [four_pairs, pltpu.SemaphoreType.DMA((2,))],
+        [VMEM, VMEM] + [pltpu.HBM] * 2,
         CHUNK_LIMIT,
-    )(place, gate_log.T, beta.T, queries, keys, values)
+    )(place, gates, beta.T, keys, values)
+    pay2, pay3, pay1 = crossed(pay2, 2), crossed(pay3, 3), crossed(pay1, 1)
+    local, through = call(query_kernel, [((groups, rows, WIDTH), BF16)] * 2)(
+        gates, queries, unit_keys, writes, erasers
+    )
+    own, local, through = lax.optimization_barrier((own, local, through))
     before, everything, pay = call(
         group_kernel, [((3, WIDTH, 2 * WIDTH), F32), pair_shape, pay_shape], 1, [four_pairs]
-    )(place, own, crossed(pay1, 1), crossed(pay2, 2), crossed(pay3, 3))
-    rowed = [rotated(pay, d) for d in (1, 2, 3)]
+    )(place, own, pay2, pay3, pay1)
+    row2, row1, row3 = [rotated(pay, d) for d in (2, 1, 3)]
     everything, w_qkv = lax.optimization_barrier((everything, w_qkv))
     w_qkv, everything = call(
         fetch_wide_kernel,
@@ -491,20 +487,20 @@
         FETCH_LIMIT,
     )(everything, w_qkv)
     before_row, pay = call(row_kernel, [pair_shape, pay_shape], 1, [four_pairs] * 2)(
-        place, everything, *rowed
-    )
-    earlier = [moved(pay, "seq", 16 * d) for d in (1, 2, 3)]
+        place, everything, row2, row1, row3
+    )
+    row2, row1, row3 = [moved(pay, "seq", 16 * d) for d in (2, 1, 3)]
     before_row, w_out, stream = lax.optimization_barrier((before_row, w_out, stream))
-    w_out, stream, before_row = call(
+    w_out, stream, maps = call(
         fetch_kernel,
-        [(w_out.shape, BF16), row_shape, pair_shape],
+        [(w_out.shape, BF16), row_shape, ((4, WIDTH, 2 * WIDTH), F32)],
         1,
         [pltpu.SemaphoreType.DMA((2,))],
-        [VMEM, pltpu.HBM, pltpu.HBM],
+        [VMEM, VMEM, pltpu.HBM, pltpu.HBM],
         FETCH_LIMIT,
-    )(place, before_row, w_out, stream)
+    )(place, before_row, before, w_out, stream)
     mine, out1, out2, out3 = call(state_kernel, [state_shape] * 4, 1, [four_states])(
-        place, *earlier, before_row, before
+        place, row2, row1, row3, maps
     )
     terms = call(
         out_kernel,
@@ -516,32 +512,31 @@
         local,
         through,
         mine,
-        crossed(out1, 1),
         crossed(out2, 2),
         crossed(out3, 3),
+        crossed(out1, 1),
         w_out,
     )
-    received = [turned(terms[r], "head", r) for r in range(1, heads)]
+    received = [turned(terms[r], "head", r) for r in (2, 1, 3)]
     (hidden,) = call(hidden_kernel, [row_shape])(stream, terms[0], *received)
-    others = [turned(hidden, "head", r) for r in range(1, heads)]
+    other2, other1, other3 = [turned(hidden, "head", r) for r in (2, 1, 3)]
     unit_queries, pack = call(project_kernel, [row_shape, ((rows, 2 * wide), BF16)], 1)(
-        place, w_qkv, hidden, *others
+        place, w_qkv, hidden, other2, other1, other3
     )
     first, visitors = lax.optimization_barrier(
-        (moved(pack, "seq", 2), moved(unit_queries, "seq", -4))
-    )
-    home = [pack, crossed(pack, 1), first, crossed(first, 1)]
-    sums_shape = ((rows, 2 * wide), F32)
-    away, kept = call(away_kernel, [sums_shape, row_shape], 1)(
-        place, hidden, visitors, home[2], home[3]
-    )
-    second, away = lax.optimization_barrier((moved(first, "seq", 2), away))
-    home += [second, crossed(second, 1)]
-    (back,) = call(back_kernel, [((rows, wide + WIDTH), BF16)], 1)(
-        place, visitors, away, home[4], home[5]
+        (moved(pack, "seq", 2), moved(unit_queries, "seq", -2))
+    )
+    second, visitors = lax.optimization_barrier(
+        (moved(first, "seq", 2), moved(visitors, "seq", -2))
+    )
+    home = [
+        pack, crossed(pack, 1), first, crossed(first, 1), second, crossed(second, 1)
+    ]
+    back, kept = call(back_kernel, [((rows, wide + WIDTH), BF16), row_shape], 1)(
+        place, hidden, visitors, *home[2:]
     )
     returned = moved(back, "seq", 4)
-    (sums,) = call(home_kernel, [sums_shape], 1)(place, unit_queries, *home)
+    (sums,) = call(home_kernel, [((rows, 2 * wide), F32)], 1)(place, unit_queries, *home)
     (attended,) = call(last_kernel, [row_shape])(sums, returned)
     return (kept, attended)
 

time: 119 us -> 111 us (0.933)
  the two profiles are of different devices: /device:TPU:3 before, /device:TPU:6 now
where the time goes in v4:
time: 111 us; the launch traced here: 110 us
  starting transfers between devices  51.9 us (47%)
  waiting for transfers between devices  34.7 us (31%)
  Pallas kernels  20.3 us (18%)
  local copies, waits for them, and re-layouts  2.43 us (2%)
    ppermute x8, starting transfers between devices, moved(): lax.ppermute(array, axis, [(i, i + distance) for i in range(size) if 0 <=...  24.7 us
    pallas_call x13, Pallas kernels, run(): pl.pallas_call(kernel, out_shape=[jax.ShapeDtypeStruct(shape, kind) for s...  20.3 us
    ppermute x8, waiting for transfers between devices, moved(): lax.ppermute(array, axis, [(i, i + distance) for i in range(size) if 0 <=...  20.2 us
    ppermute x6, starting transfers between devices, turned(): lax.ppermute(array, axis, [(i, (i + distance) % size) for i in range(size)])  11.6 us
    ppermute x3, starting transfers between devices, rotated(): lax.ppermute(array, 'seq', [(i, (i & -16) + (i + 4 * distance & 15)) for...  10.7 us
    ppermute x6, waiting for transfers between devices, turned(): lax.ppermute(array, axis, [(i, (i + distance) % size) for i in range(size)])  7.05 us
    ppermute x9, waiting for transfers between devices, crossed(): lax.ppermute(array, 'seq', [(i, i ^ mask) for i in range(lax.axis_size('s...  6.3 us
    ppermute x9, starting transfers between devices, crossed(): lax.ppermute(array, 'seq', [(i, i ^ mask) for i in range(lax.axis_size('s...  5.05 us
  transfers between devices with their start and end apart: 26, of which 17 were waited for; matrix products, arithmetic and copies ran while one was open for 0% of the time, Pallas kernels for 7%

profile of v4, /device:TPU:6, one launch (start us, length us, event | category | flops | bytes accessed | tf_op | source)
XLA Modules:
  0.0 110.2 jit_solution(17674077012138547355)
XLA Ops:
  2.2 5.2 %shard_map.95 = (bf16[128,512]{1,0:T(8,128)(2,1)S(1)}, bf16[4,128,128]{2,1,0:T(8,128)(2,1)S(1)}, bf16[4,128,128]{2,1,0:T(8,128)(2,1)S(1)}, f32[128,256]{1,0:T(8,...) custom-call(s32[4]{0:T(128)S(1)} %pad_add_fusion.place, ...), custom_call_target="tpu_custom_call" | custom-call | tf_op jit(solution)/shard_map/pallas_call | solution.py:412
  7.4 2.0 %collective-permute-start = (bf16[144,256]{1,0:T(8,128)(2,1)S(1)}, bf16[144,256]{1,0:T(8,128)(2,1)S(1)}, u32[]{:S(2)}, u32[]{:S(2)}) collective-permute-start(bf16[144,256]{1,0:T(8,128)(2,1)S(1)} %get-tuple-element.52), channel_id=1, source_target_pairs={{0,8},{4,12},{8,0},{12,4},{16,24},{20,28},{24,16},{28,20},{32,40},... | collective-permute-start | bytes 221192 | tf_op jit(solution)/shard_map/ppermute | solution.py:437
  11.9 1.9 %collective-permute-done.1.recv3_ref = bf16[144,256]{1,0:T(8,128)(2,1)S(1)} collective-permute-done((bf16[144,256]{1,0:T(8,128)(2,1)S(1)}, bf16[144,256]{1,0:T(8,128)(2,1)S(1)}, u32[]{:S(2)}, u32[]{:S(2)}) %collective-permute-start.1) | collective-permute-done | bytes 73760 | tf_op jit(solution)/shard_map/ppermute | solution.py:437
  14.8 6.5 %collective-permute-start.3 = (bf16[144,256]{1,0:T(8,128)(2,1)S(1)}, bf16[144,256]{1,0:T(8,128)(2,1)S(1)}, u32[]{:S(2)}, u32[]{:S(2)}) collective-permute-start(bf16[144,256]{1,0:T(8,128)(2,1)S(1)} %get-tuple-element.59), channel_id=1, source_target_pairs={{0,32},{4,36},{8,40},{12,44},{16,48},{20,52},{24,56},{28,60},{32,0... | collective-permute-start | bytes 221192 | tf_op jit(solution)/shard_map/ppermute | solution.py:441
  22.8 2.6 %collective-permute-start.5 = (bf16[144,256]{1,0:T(8,128)(2,1)S(1)}, bf16[144,256]{1,0:T(8,128)(2,1)S(1)}, u32[]{:S(2)}, u32[]{:S(2)}) collective-permute-start(bf16[144,256]{1,0:T(8,128)(2,1)S(1)} %get-tuple-element.59), channel_id=1, source_target_pairs={{0,48},{4,52},{8,56},{12,60},{16,0},{20,4},{24,8},{28,12},{32,16},... | collective-permute-start | bytes 221192 | tf_op jit(solution)/shard_map/ppermute | solution.py:441
  25.5 2.8 %shard_map.98 = (bf16[2048,1536]{1,0:T(8,128)(2,1)S(1)}, f32[128,256]{1,0:T(8,128)S(1)}) custom-call(f32[128,256]{1,0:T(8,128)S(1)} %get-tuple-element.56.token_ref, bf16[2048,1536]{1,0:T(8,128)(2,1)} %source_ref), custom_call_target="tpu_custom_call" | custom-call | tf_op jit(solution)/shard_map/pallas_call | solution.py:412
  35.3 2.9 %collective-permute-done.6.row2_ref = bf16[144,256]{1,0:T(8,128)(2,1)S(1)} collective-permute-done((bf16[144,256]{1,0:T(8,128)(2,1)S(1)}, bf16[144,256]{1,0:T(8,128)(2,1)S(1)}, u32[]{:S(2)}, u32[]{:S(2)}) %collective-permute-start.6) | collective-permute-done | bytes 73760 | tf_op jit(solution)/shard_map/ppermute | solution.py:426
  38.2 3.8 %collective-permute-done.8.row3_ref = bf16[144,256]{1,0:T(8,128)(2,1)S(1)} collective-permute-done((bf16[144,256]{1,0:T(8,128)(2,1)S(1)}, bf16[144,256]{1,0:T(8,128)(2,1)S(1)}, u32[]{:S(2)}, u32[]{:S(2)}) %collective-permute-start.8) | collective-permute-done | bytes 73760 | tf_op jit(solution)/shard_map/ppermute | solution.py:426
  46.5 1.8 %collective-permute-done.9.recv2_ref = bf16[128,128]{1,0:T(8,128)(2,1)S(1)} collective-permute-done((bf16[128,128]{1,0:T(8,128)(2,1)S(1)}, bf16[128,128]{1,0:T(8,128)(2,1)S(1)}, u32[]{:S(2)}, u32[]{:S(2)}) %collective-permute-start.9) | collective-permute-done | bytes 32800 | tf_op jit(solution)/shard_map/ppermute | solution.py:437
  49.5 3.3 %collective-permute-start.12 = (bf16[128,512]{1,0:T(8,128)(2,1)S(1)}, bf16[128,512]{1,0:T(8,128)(2,1)S(1)}, u32[]{:S(2)}, u32[]{:S(2)}) collective-permute-start(bf16[128,512]{1,0:T(8,128)(2,1)S(1)} %get-tuple-element.76), channel_id=1, source_target_pairs={{0,2},{1,3},{2,0},{3,1},{4,6},{5,7},{6,4},{7,5},{8,10},{9,11},{10,... | collective-permute-start | bytes 393224 | tf_op jit(solution)/shard_map/ppermute | solution.py:433
  53.5 2.6 %collective-permute-start.14 = (bf16[128,512]{1,0:T(8,128)(2,1)S(1)}, bf16[128,512]{1,0:T(8,128)(2,1)S(1)}, u32[]{:S(2)}, u32[]{:S(2)}) collective-permute-start(bf16[128,512]{1,0:T(8,128)(2,1)S(1)} %get-tuple-element.78), channel_id=1, source_target_pairs={{0,3},{1,0},{2,1},{3,2},{4,7},{5,4},{6,5},{7,6},{8,11},{9,8},{10,9... | collective-permute-start | bytes 393224 | tf_op jit(solution)/shard_map/ppermute | solution.py:433
  57.4 1.8 %collective-permute-done.13.refs_1_ = bf16[128,512]{1,0:T(8,128)(2,1)S(1)} collective-permute-done((bf16[128,512]{1,0:T(8,128)(2,1)S(1)}, bf16[128,512]{1,0:T(8,128)(2,1)S(1)}, u32[]{:S(2)}, u32[]{:S(2)}) %collective-permute-start.13) | collective-permute-done | bytes 131104 | tf_op jit(solution)/shard_map/ppermute | solution.py:433
  59.2 1.8 %collective-permute-start.15 = (bf16[128,512]{1,0:T(8,128)(2,1)S(1)}, bf16[128,512]{1,0:T(8,128)(2,1)S(1)}, u32[]{:S(2)}, u32[]{:S(2)}) collective-permute-start(bf16[128,512]{1,0:T(8,128)(2,1)S(1)} %shard_map.103.refs_0_.hidden_ref), channel_id=1, source_target_pairs={{0,2},{1,3},{2,0},{3,1},{4,6},{5,7},{6,4},{7,5},{8,10},{9,11},{10,... | collective-permute-start | bytes 393224 | tf_op jit(solution)/shard_map/ppermute | solution.py:433
  61.0 2.2 %collective-permute-start.16 = (bf16[128,512]{1,0:T(8,128)(2,1)S(1)}, bf16[128,512]{1,0:T(8,128)(2,1)S(1)}, u32[]{:S(2)}, u32[]{:S(2)}) collective-permute-start(bf16[128,512]{1,0:T(8,128)(2,1)S(1)} %shard_map.103.refs_0_.hidden_ref), channel_id=1, source_target_pairs={{0,1},{1,2},{2,3},{3,0},{4,5},{5,6},{6,7},{7,4},{8,9},{9,10},{10,1... | collective-permute-start | bytes 393224 | tf_op jit(solution)/shard_map/ppermute | solution.py:433
  64.3 2.2 %collective-permute-done.15.refs_1_ = bf16[128,512]{1,0:T(8,128)(2,1)S(1)} collective-permute-done((bf16[128,512]{1,0:T(8,128)(2,1)S(1)}, bf16[128,512]{1,0:T(8,128)(2,1)S(1)}, u32[]{:S(2)}, u32[]{:S(2)}) %collective-permute-start.15) | collective-permute-done | bytes 131104 | tf_op jit(solution)/shard_map/ppermute | solution.py:433
  70.0 2.8 %collective-permute-start.18 = (bf16[128,1024]{1,0:T(8,128)(2,1)S(1)}, bf16[128,1024]{1,0:T(8,128)(2,1)S(1)}, u32[]{:S(2)}, u32[]{:S(2)}) collective-permute-start(bf16[128,1024]{1,0:T(8,128)(2,1)S(1)} %get-tuple-element.80.refs_0_), channel_id=1, source_target_pairs={{0,8},{4,12},{8,16},{12,20},{16,24},{20,28},{24,32},{28,36},{32,40... | collective-permute-start | bytes 786440 | tf_op jit(solution)/shard_map/ppermute | solution.py:426
  72.8 5.2 %collective-permute-start.19 = (bf16[128,512]{1,0:T(8,128)(2,1)S(1)}, bf16[128,512]{1,0:T(8,128)(2,1)S(1)}, u32[]{:S(2)}, u32[]{:S(2)}) collective-permute-start(bf16[128,512]{1,0:T(8,128)(2,1)S(1)} %get-tuple-element.81.q_ref), channel_id=1, source_target_pairs={{8,0},{12,4},{16,8},{20,12},{24,16},{28,20},{32,24},{36,28},{40,32... | collective-permute-start | bytes 393224 | tf_op jit(solution)/shard_map/ppermute | solution.py:426
  77.9 2.5 %collective-permute-done.19 = bf16[128,512]{1,0:T(8,128)(2,1)S(1)} collective-permute-done((bf16[128,512]{1,0:T(8,128)(2,1)S(1)}, bf16[128,512]{1,0:T(8,128)(2,1)S(1)}, u32[]{:S(2)}, u32[]{:S(2)}) %collective-permute-start.19) | collective-permute-done | bytes 131104 | tf_op jit(solution)/shard_map/ppermute | solution.py:426
  80.4 2.8 %collective-permute-start.20 = (bf16[128,1024]{1,0:T(8,128)(2,1)S(1)}, bf16[128,1024]{1,0:T(8,128)(2,1)S(1)}, u32[]{:S(2)}, u32[]{:S(2)}) collective-permute-start(bf16[128,1024]{1,0:T(8,128)(2,1)S(1)} %collective-permute-done.18.refs_0_.refs_2_), channel_id=1, source_target_pairs={{0,8},{4,12},{8,16},{12,20},{16,24},{20,28},{24,32},{28,36},{32,40... | collective-permute-start | bytes 786440 | tf_op jit(solution)/shard_map/ppermute | solution.py:426
  83.2 5.6 %collective-permute-start.21 = (bf16[128,512]{1,0:T(8,128)(2,1)S(1)}, bf16[128,512]{1,0:T(8,128)(2,1)S(1)}, u32[]{:S(2)}, u32[]{:S(2)}) collective-permute-start(bf16[128,512]{1,0:T(8,128)(2,1)S(1)} %collective-permute-done.19), channel_id=1, source_target_pairs={{8,0},{12,4},{16,8},{20,12},{24,16},{28,20},{32,24},{36,28},{40,32... | collective-permute-start | bytes 393224 | tf_op jit(solution)/shard_map/ppermute | solution.py:426
  88.9 2.4 %collective-permute-done.21.q_ref = bf16[128,512]{1,0:T(8,128)(2,1)S(1)} collective-permute-done((bf16[128,512]{1,0:T(8,128)(2,1)S(1)}, bf16[128,512]{1,0:T(8,128)(2,1)S(1)}, u32[]{:S(2)}, u32[]{:S(2)}) %collective-permute-start.21) | collective-permute-done | bytes 131104 | tf_op jit(solution)/shard_map/ppermute | solution.py:426
  92.9 1.8 %shard_map.105 = (bf16[128,640]{1,0:T(8,128)(2,1)S(1)}, bf16[128,512]{1,0:T(8,128)(2,1)}) custom-call(s32[4]{0:T(128)S(1)} %pad_add_fusion.place, bf16[128,512]{1,0:T(8,128)(2,1)S(1)} %shard_map.103.refs_0_.hidden_ref, bf16[128,512]{1,0:T(8,128)(2,1)S(1)} %collective-permute-done.21.q_ref, bf16[128,1024]{1,0:T(8,128)(2,1)S(1)} %collective-permute-done.18.refs_0_.refs_2_, ...), custom_call_target="tpu_custom_call" | custom-call | tf_op jit(solution)/shard_map/pallas_call | solution.py:412
  94.7 4.5 %collective-permute-start.25 = (bf16[128,640]{1,0:T(8,128)(2,1)S(1)}, bf16[128,640]{1,0:T(8,128)(2,1)S(1)}, u32[]{:S(2)}, u32[]{:S(2)}) collective-permute-start(bf16[128,640]{1,0:T(8,128)(2,1)S(1)} %get-tuple-element.87), channel_id=1, source_target_pairs={{0,16},{4,20},{8,24},{12,28},{16,32},{20,36},{24,40},{28,44},{32,4... | collective-permute-start | bytes 491528 | tf_op jit(solution)/shard_map/ppermute | solution.py:426
  100.7 8.6 %collective-permute-done.25.back_ref = bf16[128,640]{1,0:T(8,128)(2,1)S(1)} collective-permute-done((bf16[128,640]{1,0:T(8,128)(2,1)S(1)}, bf16[128,640]{1,0:T(8,128)(2,1)S(1)}, u32[]{:S(2)}, u32[]{:S(2)}) %collective-permute-start.25) | collective-permute-done | bytes 163872 | tf_op jit(solution)/shard_map/ppermute | solution.py:426
  (52 shorter events, 29.9 us)
Async XLA Ops:
  7.4 4.4 %collective-permute-start = (bf16[144,256]{1,0:T(8,128)(2,1)S(1)}, bf16[144,256]{1,0:T(8,128)(2,1)S(1)}, u32[]{:S(2)}, u32[]{:S(2)}) collective-permute-start(bf16[144,256]{1,0:T(8,128)(2,1)S(1)} %get-tuple-element.52), channel_id=1, source_target_pairs={{0,8},{4,12},{8,0},{12,4},{16,24},{20,28},{24,16},{28,20},{32,40},... | collective-permute-start | bytes 221192 | tf_op jit(solution)/shard_map/ppermute | solution.py:437
  9.4 4.3 %collective-permute-start.1 = (bf16[144,256]{1,0:T(8,128)(2,1)S(1)}, bf16[144,256]{1,0:T(8,128)(2,1)S(1)}, u32[]{:S(2)}, u32[]{:S(2)}) collective-permute-start(bf16[144,256]{1,0:T(8,128)(2,1)S(1)} %get-tuple-element.53), channel_id=1, source_target_pairs={{0,12},{4,8},{8,4},{12,0},{16,28},{20,24},{24,20},{28,16},{32,44},... | collective-permute-start | bytes 221192 | tf_op jit(solution)/shard_map/ppermute | solution.py:437
  9.4 4.3 %collective-permute-start.2 = (bf16[144,256]{1,0:T(8,128)(2,1)S(1)}, bf16[144,256]{1,0:T(8,128)(2,1)S(1)}, u32[]{:S(2)}, u32[]{:S(2)}) collective-permute-start(bf16[144,256]{1,0:T(8,128)(2,1)S(1)} %get-tuple-element.54), channel_id=1, source_target_pairs={{0,4},{4,0},{8,12},{12,8},{16,20},{20,16},{24,28},{28,24},{32,36},... | collective-permute-start | bytes 221192 | tf_op jit(solution)/shard_map/ppermute | solution.py:437
  14.8 13.5 %collective-permute-start.3 = (bf16[144,256]{1,0:T(8,128)(2,1)S(1)}, bf16[144,256]{1,0:T(8,128)(2,1)S(1)}, u32[]{:S(2)}, u32[]{:S(2)}) collective-permute-start(bf16[144,256]{1,0:T(8,128)(2,1)S(1)} %get-tuple-element.59), channel_id=1, source_target_pairs={{0,32},{4,36},{8,40},{12,44},{16,48},{20,52},{24,56},{28,60},{32,0... | collective-permute-start | bytes 221192 | tf_op jit(solution)/shard_map/ppermute | solution.py:441
  21.4 7.1 %collective-permute-start.4 = (bf16[144,256]{1,0:T(8,128)(2,1)S(1)}, bf16[144,256]{1,0:T(8,128)(2,1)S(1)}, u32[]{:S(2)}, u32[]{:S(2)}) collective-permute-start(bf16[144,256]{1,0:T(8,128)(2,1)S(1)} %get-tuple-element.59), channel_id=1, source_target_pairs={{0,16},{4,20},{8,24},{12,28},{16,32},{20,36},{24,40},{28,44},{32,4... | collective-permute-start | bytes 221192 | tf_op jit(solution)/shard_map/ppermute | solution.py:441
  22.8 6.5 %collective-permute-start.5 = (bf16[144,256]{1,0:T(8,128)(2,1)S(1)}, bf16[144,256]{1,0:T(8,128)(2,1)S(1)}, u32[]{:S(2)}, u32[]{:S(2)}) collective-permute-start(bf16[144,256]{1,0:T(8,128)(2,1)S(1)} %get-tuple-element.59), channel_id=1, source_target_pairs={{0,48},{4,52},{8,56},{12,60},{16,0},{20,4},{24,8},{28,12},{32,16},... | collective-permute-start | bytes 221192 | tf_op jit(solution)/shard_map/ppermute | solution.py:441
  30.5 7.8 %collective-permute-start.6 = (bf16[144,256]{1,0:T(8,128)(2,1)S(1)}, bf16[144,256]{1,0:T(8,128)(2,1)S(1)}, u32[]{:S(2)}, u32[]{:S(2)}) collective-permute-start(bf16[144,256]{1,0:T(8,128)(2,1)S(1)} %get-tuple-element.68), channel_id=1, source_target_pairs={{0,128},{4,132},{8,136},{12,140},{16,144},{20,148},{24,152},{28,15... | collective-permute-start | bytes 221192 | tf_op jit(solution)/shard_map/ppermute | solution.py:426
  31.8 6.5 %collective-permute-start.7 = (bf16[144,256]{1,0:T(8,128)(2,1)S(1)}, bf16[144,256]{1,0:T(8,128)(2,1)S(1)}, u32[]{:S(2)}, u32[]{:S(2)}) collective-permute-start(bf16[144,256]{1,0:T(8,128)(2,1)S(1)} %get-tuple-element.68), channel_id=1, source_target_pairs={{0,64},{4,68},{8,72},{12,76},{16,80},{20,84},{24,88},{28,92},{32,9... | collective-permute-start | bytes 221192 | tf_op jit(solution)/shard_map/ppermute | solution.py:426
  33.1 8.9 %collective-permute-start.8 = (bf16[144,256]{1,0:T(8,128)(2,1)S(1)}, bf16[144,256]{1,0:T(8,128)(2,1)S(1)}, u32[]{:S(2)}, u32[]{:S(2)}) collective-permute-start(bf16[144,256]{1,0:T(8,128)(2,1)S(1)} %get-tuple-element.68), channel_id=1, source_target_pairs={{0,192},{4,196},{8,200},{12,204},{16,208},{20,212},{24,216},{28,22... | collective-permute-start | bytes 221192 | tf_op jit(solution)/shard_map/ppermute | solution.py:426
  43.0 3.5 %collective-permute-start.10 = (bf16[128,128]{1,0:T(8,128)(2,1)S(1)}, bf16[128,128]{1,0:T(8,128)(2,1)S(1)}, u32[]{:S(2)}, u32[]{:S(2)}) collective-permute-start(bf16[128,128]{1,0:T(8,128)(2,1)S(1)} %get-tuple-element.72), channel_id=1, source_target_pairs={{0,12},{4,8},{8,4},{12,0},{16,28},{20,24},{24,20},{28,16},{32,44},... | collective-permute-start | bytes 98312 | tf_op jit(solution)/shard_map/ppermute | solution.py:437
  43.1 3.4 %collective-permute-start.11 = (bf16[128,128]{1,0:T(8,128)(2,1)S(1)}, bf16[128,128]{1,0:T(8,128)(2,1)S(1)}, u32[]{:S(2)}, u32[]{:S(2)}) collective-permute-start(bf16[128,128]{1,0:T(8,128)(2,1)S(1)} %get-tuple-element.73), channel_id=1, source_target_pairs={{0,4},{4,0},{8,12},{12,8},{16,20},{20,16},{24,28},{28,24},{32,36},... | collective-permute-start | bytes 98312 | tf_op jit(solution)/shard_map/ppermute | solution.py:437
  44.4 3.9 %collective-permute-start.9 = (bf16[128,128]{1,0:T(8,128)(2,1)S(1)}, bf16[128,128]{1,0:T(8,128)(2,1)S(1)}, u32[]{:S(2)}, u32[]{:S(2)}) collective-permute-start(bf16[128,128]{1,0:T(8,128)(2,1)S(1)} %get-tuple-element.71), channel_id=1, source_target_pairs={{0,8},{4,12},{8,0},{12,4},{16,24},{20,28},{24,16},{28,20},{32,40},... | collective-permute-start | bytes 98312 | tf_op jit(solution)/shard_map/ppermute | solution.py:437
  49.5 7.8 %collective-permute-start.12 = (bf16[128,512]{1,0:T(8,128)(2,1)S(1)}, bf16[128,512]{1,0:T(8,128)(2,1)S(1)}, u32[]{:S(2)}, u32[]{:S(2)}) collective-permute-start(bf16[128,512]{1,0:T(8,128)(2,1)S(1)} %get-tuple-element.76), channel_id=1, source_target_pairs={{0,2},{1,3},{2,0},{3,1},{4,6},{5,7},{6,4},{7,5},{8,10},{9,11},{10,... | collective-permute-start | bytes 393224 | tf_op jit(solution)/shard_map/ppermute | solution.py:433
  52.8 6.3 %collective-permute-start.13 = (bf16[128,512]{1,0:T(8,128)(2,1)S(1)}, bf16[128,512]{1,0:T(8,128)(2,1)S(1)}, u32[]{:S(2)}, u32[]{:S(2)}) collective-permute-start(bf16[128,512]{1,0:T(8,128)(2,1)S(1)} %get-tuple-element.77), channel_id=1, source_target_pairs={{0,1},{1,2},{2,3},{3,0},{4,5},{5,6},{6,7},{7,4},{8,9},{9,10},{10,1... | collective-permute-start | bytes 393224 | tf_op jit(solution)/shard_map/ppermute | solution.py:433
  53.5 5.7 %collective-permute-start.14 = (bf16[128,512]{1,0:T(8,128)(2,1)S(1)}, bf16[128,512]{1,0:T(8,128)(2,1)S(1)}, u32[]{:S(2)}, u32[]{:S(2)}) collective-permute-start(bf16[128,512]{1,0:T(8,128)(2,1)S(1)} %get-tuple-element.78), channel_id=1, source_target_pairs={{0,3},{1,0},{2,1},{3,2},{4,7},{5,4},{6,5},{7,6},{8,11},{9,8},{10,9... | collective-permute-start | bytes 393224 | tf_op jit(solution)/shard_map/ppermute | solution.py:433
  59.2 7.3 %collective-permute-start.15 = (bf16[128,512]{1,0:T(8,128)(2,1)S(1)}, bf16[128,512]{1,0:T(8,128)(2,1)S(1)}, u32[]{:S(2)}, u32[]{:S(2)}) collective-permute-start(bf16[128,512]{1,0:T(8,128)(2,1)S(1)} %shard_map.103.refs_0_.hidden_ref), channel_id=1, source_target_pairs={{0,2},{1,3},{2,0},{3,1},{4,6},{5,7},{6,4},{7,5},{8,10},{9,11},{10,... | collective-permute-start | bytes 393224 | tf_op jit(solution)/shard_map/ppermute | solution.py:433
  61.0 6.8 %collective-permute-start.16 = (bf16[128,512]{1,0:T(8,128)(2,1)S(1)}, bf16[128,512]{1,0:T(8,128)(2,1)S(1)}, u32[]{:S(2)}, u32[]{:S(2)}) collective-permute-start(bf16[128,512]{1,0:T(8,128)(2,1)S(1)} %shard_map.103.refs_0_.hidden_ref), channel_id=1, source_target_pairs={{0,1},{1,2},{2,3},{3,0},{4,5},{5,6},{6,7},{7,4},{8,9},{9,10},{10,1... | collective-permute-start | bytes 393224 | tf_op jit(solution)/shard_map/ppermute | solution.py:433
  63.2 5.0 %collective-permute-start.17 = (bf16[128,512]{1,0:T(8,128)(2,1)S(1)}, bf16[128,512]{1,0:T(8,128)(2,1)S(1)}, u32[]{:S(2)}, u32[]{:S(2)}) collective-permute-start(bf16[128,512]{1,0:T(8,128)(2,1)S(1)} %shard_map.103.refs_0_.hidden_ref), channel_id=1, source_target_pairs={{0,3},{1,0},{2,1},{3,2},{4,7},{5,4},{6,5},{7,6},{8,11},{9,8},{10,9... | collective-permute-start | bytes 393224 | tf_op jit(solution)/shard_map/ppermute | solution.py:433
  70.0 10.5 %collective-permute-start.18 = (bf16[128,1024]{1,0:T(8,128)(2,1)S(1)}, bf16[128,1024]{1,0:T(8,128)(2,1)S(1)}, u32[]{:S(2)}, u32[]{:S(2)}) collective-permute-start(bf16[128,1024]{1,0:T(8,128)(2,1)S(1)} %get-tuple-element.80.refs_0_), channel_id=1, source_target_pairs={{0,8},{4,12},{8,16},{12,20},{16,24},{20,28},{24,32},{28,36},{32,40... | collective-permute-start | bytes 786440 | tf_op jit(solution)/shard_map/ppermute | solution.py:426
  72.8 7.7 %collective-permute-start.19 = (bf16[128,512]{1,0:T(8,128)(2,1)S(1)}, bf16[128,512]{1,0:T(8,128)(2,1)S(1)}, u32[]{:S(2)}, u32[]{:S(2)}) collective-permute-start(bf16[128,512]{1,0:T(8,128)(2,1)S(1)} %get-tuple-element.81.q_ref), channel_id=1, source_target_pairs={{8,0},{12,4},{16,8},{20,12},{24,16},{28,20},{32,24},{36,28},{40,32... | collective-permute-start | bytes 393224 | tf_op jit(solution)/shard_map/ppermute | solution.py:426
  80.4 10.9 %collective-permute-start.20 = (bf16[128,1024]{1,0:T(8,128)(2,1)S(1)}, bf16[128,1024]{1,0:T(8,128)(2,1)S(1)}, u32[]{:S(2)}, u32[]{:S(2)}) collective-permute-start(bf16[128,1024]{1,0:T(8,128)(2,1)S(1)} %collective-permute-done.18.refs_0_.refs_2_), channel_id=1, source_target_pairs={{0,8},{4,12},{8,16},{12,20},{16,24},{20,28},{24,32},{28,36},{32,40... | collective-permute-start | bytes 786440 | tf_op jit(solution)/shard_map/ppermute | solution.py:426
  83.2 8.1 %collective-permute-start.21 = (bf16[128,512]{1,0:T(8,128)(2,1)S(1)}, bf16[128,512]{1,0:T(8,128)(2,1)S(1)}, u32[]{:S(2)}, u32[]{:S(2)}) collective-permute-start(bf16[128,512]{1,0:T(8,128)(2,1)S(1)} %collective-permute-done.19), channel_id=1, source_target_pairs={{8,0},{12,4},{16,8},{20,12},{24,16},{28,20},{32,24},{36,28},{40,32... | collective-permute-start | bytes 393224 | tf_op jit(solution)/shard_map/ppermute | solution.py:426
  91.3 7.8 %collective-permute-start.24 = (bf16[128,1024]{1,0:T(8,128)(2,1)S(1)}, bf16[128,1024]{1,0:T(8,128)(2,1)S(1)}, u32[]{:S(2)}, u32[]{:S(2)}) collective-permute-start(bf16[128,1024]{1,0:T(8,128)(2,1)S(1)} %get-tuple-element.80.refs_0_), channel_id=1, source_target_pairs={{0,4},{4,0},{8,12},{12,8},{16,20},{20,16},{24,28},{28,24},{32,36},... | collective-permute-start | bytes 786440 | tf_op jit(solution)/shard_map/ppermute | solution.py:437
  94.7 14.7 %collective-permute-start.25 = (bf16[128,640]{1,0:T(8,128)(2,1)S(1)}, bf16[128,640]{1,0:T(8,128)(2,1)S(1)}, u32[]{:S(2)}, u32[]{:S(2)}) collective-permute-start(bf16[128,640]{1,0:T(8,128)(2,1)S(1)} %get-tuple-element.87), channel_id=1, source_target_pairs={{0,16},{4,20},{8,24},{12,28},{16,32},{20,36},{24,40},{28,44},{32,4... | collective-permute-start | bytes 491528 | tf_op jit(solution)/shard_map/ppermute | solution.py:426
  (7 other events, 74.5 us)

commit v5 on v4

--- a/solution.py
+++ b/solution.py
@@ -131,10 +131,11 @@
     return results
 
 
-def decays(g_ref):
-    groups, rows = g_ref.shape
+def decays(gb_ref):
+    rows = gb_ref.shape[1]
+    groups = gb_ref.shape[0] // 2
     row, column = iotas(rows, rows)
-    gates = g_ref[...]
+    gates = gb_ref[0:groups, :]
     causal = row >= column
     summed = exact(causal.astype(F32), gates, (1, 1))
     summed_row = exact(gates, (row <= column).astype(F32))
@@ -145,10 +146,11 @@
 
 
 def map_kernel(
-    place, g_ref, b_ref, k_hbm, v_hbm, keys_ref, writes_ref, erasers_ref, own_ref, pay1_ref, pay2_ref, pay3_ref, k_ref, v_ref, pairs, sems
+    place, gb_ref, k_hbm, v_hbm, keys_ref, writes_ref, erasers_ref, own_ref, pay1_ref, pay2_ref, pay3_ref, k_ref, v_ref, pairs, sems
 ):
     part = place[1]
-    groups, rows = g_ref.shape
+    rows = gb_ref.shape[1]
+    groups = gb_ref.shape[0] // 2
     loads = [
         pltpu.make_async_copy(k_hbm, k_ref, sems.at[0]),
         pltpu.make_async_copy(v_hbm, v_ref, sems.at[1]),
@@ -156,8 +158,8 @@
     for load in loads:
         load.start()
     row, column = iotas(rows, rows)
-    summed, decay = decays(g_ref)
-    betas = exact((row == column).astype(F32), b_ref[...], (1, 1))
+    summed, decay = decays(gb_ref)
+    betas = exact((row == column).astype(F32), gb_ref[groups:, :], (1, 1))
     loads[0].wait()
     keys, couplings = [], []
     for h in range(groups):
@@ -191,9 +193,9 @@
         store_payload(ref, parted(pairs[part ^ r]))
 
 
-def query_kernel(g_ref, q_ref, keys_ref, writes_ref, erasers_ref, local_ref, through_ref):
-    groups = g_ref.shape[0]
-    summed, decay = decays(g_ref)
+def query_kernel(gb_ref, q_ref, keys_ref, writes_ref, erasers_ref, local_ref, through_ref):
+    groups = gb_ref.shape[0] // 2
+    summed, decay = decays(gb_ref)
     for h in range(groups):
         span = slice(h * WIDTH, (h + 1) * WIDTH)
         query = to_unit(q_ref[:, span].astype(F32)).astype(BF16)
@@ -251,7 +253,7 @@
     group = place[3]
     pairs[group] = all_ref[...]
     for d, ref in ((1, recv1_ref), (2, recv2_ref), (3, recv3_ref)):
-        pairs[(group + 4 - d) & 3] = joined(load_payload(ref))
+        pairs[group ^ d] = joined(load_payload(ref))
     two, three, total = prefixes([parted(pairs[n]) for n in range(4)])
     store_payload(pay_ref, total)
     row, column = iotas(WIDTH, 2 * WIDTH)
@@ -262,11 +264,16 @@
     before_ref[...] = starts[group]
 
 
-def state_kernel(place, row2_ref, row1_ref, row3_ref, maps_ref, mine_ref, out1_ref, out2_ref, out3_ref, states):
-    part = place[1]
-    state = load_payload(row3_ref)[1]
-    state = apply(load_payload(row2_ref), state)
-    state = apply(load_payload(row1_ref), state)
+def state_kernel(
+    place, recv2_ref, recv1_ref, recv3_ref, maps_ref, mine_ref, out1_ref, out2_ref, out3_ref, rows, states
+):
+    part, line = place[1], place[4]
+    rows[line] = jnp.zeros(rows.shape[1:], F32)
+    for r, ref in ((1, recv1_ref), (2, recv2_ref), (3, recv3_ref)):
+        rows[line ^ r] = joined(load_payload(ref))
+    state = jnp.where(line > 0, rows[0][:, WIDTH:], 0.0)
+    for n in (1, 2):
+        state = jnp.where(line > n, apply(parted(rows[n]), state), state)
     for n in range(4):
         states[n] = apply(parted(maps_ref[n]), state).astype(BF16)
     mine_ref[...] = states[part]
@@ -296,7 +303,7 @@
     width = term_ref.shape[1]
     count = len(sent_refs) + 1
     for r in range(count):
-        begin = pl.multiple_of(lax.rem(me + r, count) * width, width)
+        begin = pl.multiple_of((me ^ r) * width, width)
         term = dot(normed, w_ref[:, pl.ds(begin, width)])
         if r == 0:
             term_ref[...] = term
@@ -321,7 +328,7 @@
     scale = lax.rsqrt(squares / (count * width) + 1e-05)
     total = None
     for n, r in enumerate((0, 2, 1, 3)):
-        begin = pl.multiple_of(lax.rem(me + count - r, count) * width, width)
+        begin = pl.multiple_of((me ^ r) * width, width)
         part = dot((values[n] * scale).astype(BF16), w_ref[pl.ds(begin, width), :])
         total = part if total is None else total + part
     groups = q_ref.shape[1] // WIDTH
@@ -428,21 +435,8 @@
     )
 
 
-def turned(array, axis, distance):
-    size = lax.axis_size(axis)
-    return lax.ppermute(array, axis, [(i, (i + distance) % size) for i in range(size)])
-
-
-def crossed(array, mask):
-    return lax.ppermute(array, "seq", [(i, i ^ mask) for i in range(lax.axis_size("seq"))])
-
-
-def rotated(array, distance):
-    return lax.ppermute(
-        array,
-        "seq",
-        [(i, (i & -16) + ((i + 4 * distance) & 15)) for i in range(lax.axis_size("seq"))],
-    )
+def crossed(array, mask, axis="seq"):
+    return lax.ppermute(array, axis, [(i, i ^ mask) for i in range(lax.axis_size(axis))])
 
 
 def body(queries, keys, values, gate_log, beta, stream, w_out, w_qkv):
@@ -451,7 +445,7 @@
     seq = lax.axis_index("seq")
     head = lax.axis_index("head")
     heads = lax.axis_size("head")
-    place = jnp.stack([seq, seq & 3, head, (seq >> 2) & 3]).astype(jnp.int32)
+    place = jnp.stack([seq, seq & 3, head, (seq >> 2) & 3, seq >> 4]).astype(jnp.int32)
     pair_shape = ((WIDTH, 2 * WIDTH), F32)
     pay_shape = ((WIDTH + 16, 2 * WIDTH), BF16)
     state_shape = ((WIDTH, WIDTH), BF16)
@@ -459,15 +453,15 @@
     four_pairs = pltpu.VMEM((4, WIDTH, 2 * WIDTH), F32)
     four_states = pltpu.VMEM((4, WIDTH, WIDTH), BF16)
 
-    gates = gate_log.T
+    gates = jnp.concatenate([gate_log.T, beta.T], axis=0)
     unit_keys, writes, erasers, own, pay1, pay2, pay3 = call(
         map_kernel,
         [row_shape] + [((groups, rows, WIDTH), BF16)] * 2 + [pair_shape] + [pay_shape] * 3,
         1,
         [pltpu.VMEM((rows, wide), BF16)] * 2 + [four_pairs, pltpu.SemaphoreType.DMA((2,))],
-        [VMEM, VMEM] + [pltpu.HBM] * 2,
+        [VMEM] + [pltpu.HBM] * 2,
         CHUNK_LIMIT,
-    )(place, gates, beta.T, keys, values)
+    )(place, gates, keys, values)
     pay2, pay3, pay1 = crossed(pay2, 2), crossed(pay3, 3), crossed(pay1, 1)
     local, through = call(query_kernel, [((groups, rows, WIDTH), BF16)] * 2)(
         gates, queries, unit_keys, writes, erasers
@@ -476,7 +470,7 @@
     before, everything, pay = call(
         group_kernel, [((3, WIDTH, 2 * WIDTH), F32), pair_shape, pay_shape], 1, [four_pairs]
     )(place, own, pay2, pay3, pay1)
-    row2, row1, row3 = [rotated(pay, d) for d in (2, 1, 3)]
+    row2, row1, row3 = [crossed(pay, 4 * d) for d in (2, 1, 3)]
     everything, w_qkv = lax.optimization_barrier((everything, w_qkv))
     w_qkv, everything = call(
         fetch_wide_kernel,
@@ -489,7 +483,7 @@
     before_row, pay = call(row_kernel, [pair_shape, pay_shape], 1, [four_pairs] * 2)(
         place, everything, row2, row1, row3
     )
-    row2, row1, row3 = [moved(pay, "seq", 16 * d) for d in (2, 1, 3)]
+    row2, row1, row3 = [crossed(pay, 16 * d) for d in (2, 1, 3)]
     before_row, w_out, stream = lax.optimization_barrier((before_row, w_out, stream))
     w_out, stream, maps = call(
         fetch_kernel,
@@ -499,7 +493,7 @@
         [VMEM, VMEM, pltpu.HBM, pltpu.HBM],
         FETCH_LIMIT,
     )(place, before_row, before, w_out, stream)
-    mine, out1, out2, out3 = call(state_kernel, [state_shape] * 4, 1, [four_states])(
+    mine, out1, out2, out3 = call(state_kernel, [state_shape] * 4, 1, [four_pairs, four_states])(
         place, row2, row1, row3, maps
     )
     terms = call(
@@ -517,9 +511,9 @@
         crossed(out1, 1),
         w_out,
     )
-    received = [turned(terms[r], "head", r) for r in (2, 1, 3)]
+    received = [crossed(terms[r], r, "head") for r in (2, 1, 3)]
     (hidden,) = call(hidden_kernel, [row_shape])(stream, terms[0], *received)
-    other2, other1, other3 = [turned(hidden, "head", r) for r in (2, 1, 3)]
+    other2, other1, other3 = [crossed(hidden, r, "head") for r in (2, 1, 3)]
     unit_queries, pack = call(project_kernel, [row_shape, ((rows, 2 * wide), BF16)], 1)(
         place, w_qkv, hidden, other2, other1, other3
     )

time: 111 us -> 107 us (0.964)
  the two profiles are of different devices: /device:TPU:6 before, /device:TPU:34 now
where the time goes in v5:
time: 107 us
  starting transfers between devices  43.2 us (40%)
  waiting for transfers between devices  40.6 us (38%)
  Pallas kernels  20.3 us (19%)
    ppermute x21, starting transfers between devices, crossed(): lax.ppermute(array, axis, [(i, i ^ mask) for i in range(lax.axis_size(axi...  26.5 us
    ppermute x21, waiting for transfers between devices, crossed(): lax.ppermute(array, axis, [(i, i ^ mask) for i in range(lax.axis_size(axi...  22.7 us
    pallas_call x13, Pallas kernels, run(): pl.pallas_call(kernel, out_shape=[jax.ShapeDtypeStruct(shape, kind) for s...  20.3 us
    ppermute x5, waiting for transfers between devices, moved(): lax.ppermute(array, axis, [(i, i + distance) for i in range(size) if 0 <=...  17.9 us
    ppermute x5, starting transfers between devices, moved(): lax.ppermute(array, axis, [(i, i + distance) for i in range(size) if 0 <=...  16.8 us
  transfers between devices with their start and end apart: 26, of which 18 were waited for; matrix products, arithmetic and copies ran while one was open for 0% of the time, Pallas kernels for 8%

profile of v5, /device:TPU:34, one launch (start us, length us, event | category | flops | bytes accessed | tf_op | source)
XLA Modules:
  0.0 106.8 jit_solution(5537085715034860827)
XLA Ops:
  1.6 5.2 %shard_map.95 = (bf16[128,512]{1,0:T(8,128)(2,1)S(1)}, bf16[4,128,128]{2,1,0:T(8,128)(2,1)S(1)}, bf16[4,128,128]{2,1,0:T(8,128)(2,1)S(1)}, f32[128,256]{1,0:T(8,...) custom-call(s32[5]{0:T(128)S(1)} %stack.23.place, ...), custom_call_target="tpu_custom_call" | custom-call | tf_op jit(solution)/shard_map/pallas_call | solution.py:419
  12.7 7.1 %collective-permute-start.3 = (bf16[144,256]{1,0:T(8,128)(2,1)S(1)}, bf16[144,256]{1,0:T(8,128)(2,1)S(1)}, u32[]{:S(2)}, u32[]{:S(2)}) collective-permute-start(bf16[144,256]{1,0:T(8,128)(2,1)S(1)} %get-tuple-element.59), channel_id=1, source_target_pairs={{0,32},{4,36},{8,40},{12,44},{16,48},{20,52},{24,56},{28,60},{32,0... | collective-permute-start | bytes 221192 | tf_op jit(solution)/shard_map/ppermute | solution.py:439
  19.8 1.5 %collective-permute-start.4 = (bf16[144,256]{1,0:T(8,128)(2,1)S(1)}, bf16[144,256]{1,0:T(8,128)(2,1)S(1)}, u32[]{:S(2)}, u32[]{:S(2)}) collective-permute-start(bf16[144,256]{1,0:T(8,128)(2,1)S(1)} %get-tuple-element.59), channel_id=1, source_target_pairs={{0,16},{4,20},{8,24},{12,28},{16,0},{20,4},{24,8},{28,12},{32,48},... | collective-permute-start | bytes 221192 | tf_op jit(solution)/shard_map/ppermute | solution.py:439
  21.3 2.8 %shard_map.98 = (bf16[2048,1536]{1,0:T(8,128)(2,1)S(1)}, f32[128,256]{1,0:T(8,128)S(1)}) custom-call(f32[128,256]{1,0:T(8,128)S(1)} %get-tuple-element.56.token_ref, bf16[2048,1536]{1,0:T(8,128)(2,1)} %source_ref), custom_call_target="tpu_custom_call" | custom-call | tf_op jit(solution)/shard_map/pallas_call | solution.py:419
  24.1 2.5 %collective-permute-done.4.recv1_ref = bf16[144,256]{1,0:T(8,128)(2,1)S(1)} collective-permute-done((bf16[144,256]{1,0:T(8,128)(2,1)S(1)}, bf16[144,256]{1,0:T(8,128)(2,1)S(1)}, u32[]{:S(2)}, u32[]{:S(2)}) %collective-permute-start.4) | collective-permute-done | bytes 73760 | tf_op jit(solution)/shard_map/ppermute | solution.py:439
  26.5 2.3 %collective-permute-done.5.recv3_ref = bf16[144,256]{1,0:T(8,128)(2,1)S(1)} collective-permute-done((bf16[144,256]{1,0:T(8,128)(2,1)S(1)}, bf16[144,256]{1,0:T(8,128)(2,1)S(1)}, u32[]{:S(2)}, u32[]{:S(2)}) %collective-permute-start.5) | collective-permute-done | bytes 73760 | tf_op jit(solution)/shard_map/ppermute | solution.py:439
  29.9 2.2 %collective-permute-start.6 = (bf16[144,256]{1,0:T(8,128)(2,1)S(1)}, bf16[144,256]{1,0:T(8,128)(2,1)S(1)}, u32[]{:S(2)}, u32[]{:S(2)}) collective-permute-start(bf16[144,256]{1,0:T(8,128)(2,1)S(1)} %get-tuple-element.68), channel_id=1, source_target_pairs={{0,128},{4,132},{8,136},{12,140},{16,144},{20,148},{24,152},{28,15... | collective-permute-start | bytes 221192 | tf_op jit(solution)/shard_map/ppermute | solution.py:439
  39.2 2.0 %collective-permute-start.9 = (bf16[128,128]{1,0:T(8,128)(2,1)S(1)}, bf16[128,128]{1,0:T(8,128)(2,1)S(1)}, u32[]{:S(2)}, u32[]{:S(2)}) collective-permute-start(bf16[128,128]{1,0:T(8,128)(2,1)S(1)} %get-tuple-element.71), channel_id=1, source_target_pairs={{0,8},{4,12},{8,0},{12,4},{16,24},{20,28},{24,16},{28,20},{32,40},... | collective-permute-start | bytes 98312 | tf_op jit(solution)/shard_map/ppermute | solution.py:439
  44.4 3.5 %collective-permute-start.12 = (bf16[128,512]{1,0:T(8,128)(2,1)S(1)}, bf16[128,512]{1,0:T(8,128)(2,1)S(1)}, u32[]{:S(2)}, u32[]{:S(2)}) collective-permute-start(bf16[128,512]{1,0:T(8,128)(2,1)S(1)} %get-tuple-element.76), channel_id=1, source_target_pairs={{0,2},{1,3},{2,0},{3,1},{4,6},{5,7},{6,4},{7,5},{8,10},{9,11},{10,... | collective-permute-start | bytes 393224 | tf_op jit(solution)/shard_map/ppermute | solution.py:439
  48.9 3.3 %collective-permute-done.12.refs_0_ = bf16[128,512]{1,0:T(8,128)(2,1)S(1)} collective-permute-done((bf16[128,512]{1,0:T(8,128)(2,1)S(1)}, bf16[128,512]{1,0:T(8,128)(2,1)S(1)}, u32[]{:S(2)}, u32[]{:S(2)}) %collective-permute-start.12) | collective-permute-done | bytes 131104 | tf_op jit(solution)/shard_map/ppermute | solution.py:439
  52.2 1.9 %collective-permute-done.13.refs_1_ = bf16[128,512]{1,0:T(8,128)(2,1)S(1)} collective-permute-done((bf16[128,512]{1,0:T(8,128)(2,1)S(1)}, bf16[128,512]{1,0:T(8,128)(2,1)S(1)}, u32[]{:S(2)}, u32[]{:S(2)}) %collective-permute-start.13) | collective-permute-done | bytes 131104 | tf_op jit(solution)/shard_map/ppermute | solution.py:439
  54.8 2.4 %collective-permute-start.15 = (bf16[128,512]{1,0:T(8,128)(2,1)S(1)}, bf16[128,512]{1,0:T(8,128)(2,1)S(1)}, u32[]{:S(2)}, u32[]{:S(2)}) collective-permute-start(bf16[128,512]{1,0:T(8,128)(2,1)S(1)} %shard_map.103.refs_0_.hidden_ref), channel_id=1, source_target_pairs={{0,2},{1,3},{2,0},{3,1},{4,6},{5,7},{6,4},{7,5},{8,10},{9,11},{10,... | collective-permute-start | bytes 393224 | tf_op jit(solution)/shard_map/ppermute | solution.py:439
  59.0 3.0 %collective-permute-done.15.refs_1_ = bf16[128,512]{1,0:T(8,128)(2,1)S(1)} collective-permute-done((bf16[128,512]{1,0:T(8,128)(2,1)S(1)}, bf16[128,512]{1,0:T(8,128)(2,1)S(1)}, u32[]{:S(2)}, u32[]{:S(2)}) %collective-permute-start.15) | collective-permute-done | bytes 131104 | tf_op jit(solution)/shard_map/ppermute | solution.py:439
  64.4 1.7 %shard_map.104 = (bf16[128,512]{1,0:T(8,128)(2,1)S(1)}, bf16[128,1024]{1,0:T(8,128)(2,1)S(1)}) custom-call(s32[5]{0:T(128)S(1)} %stack.23.place, bf16[2048,1536]{1,0:T(8,128)(2,1)S(1)} %get-tuple-element.79.w_ref, bf16[128,512]{1,0:T(8,128)(2,1)S(1)} %shard_map.103.refs_0_.hidden_ref, bf16[128,512]{1,0:T(8,128)(2,1)S(1)} %collective-permute-done.15.refs_1_, ...), custom_call_target="tpu_custom_call" | custom-call | tf_op jit(solution)/shard_map/pallas_call | solution.py:419
  66.1 2.7 %collective-permute-start.18 = (bf16[128,1024]{1,0:T(8,128)(2,1)S(1)}, bf16[128,1024]{1,0:T(8,128)(2,1)S(1)}, u32[]{:S(2)}, u32[]{:S(2)}) collective-permute-start(bf16[128,1024]{1,0:T(8,128)(2,1)S(1)} %get-tuple-element.80.refs_0_), channel_id=1, source_target_pairs={{0,8},{4,12},{8,16},{12,20},{16,24},{20,28},{24,32},{28,36},{32,40... | collective-permute-start | bytes 786440 | tf_op jit(solution)/shard_map/ppermute | solution.py:433
  68.9 3.1 %collective-permute-start.19 = (bf16[128,512]{1,0:T(8,128)(2,1)S(1)}, bf16[128,512]{1,0:T(8,128)(2,1)S(1)}, u32[]{:S(2)}, u32[]{:S(2)}) collective-permute-start(bf16[128,512]{1,0:T(8,128)(2,1)S(1)} %get-tuple-element.81.q_ref), channel_id=1, source_target_pairs={{8,0},{12,4},{16,8},{20,12},{24,16},{28,20},{32,24},{36,28},{40,32... | collective-permute-start | bytes 393224 | tf_op jit(solution)/shard_map/ppermute | solution.py:433
  72.0 3.7 %collective-permute-done.19 = bf16[128,512]{1,0:T(8,128)(2,1)S(1)} collective-permute-done((bf16[128,512]{1,0:T(8,128)(2,1)S(1)}, bf16[128,512]{1,0:T(8,128)(2,1)S(1)}, u32[]{:S(2)}, u32[]{:S(2)}) %collective-permute-start.19) | collective-permute-done | bytes 131104 | tf_op jit(solution)/shard_map/ppermute | solution.py:433
  75.7 3.4 %collective-permute-start.20 = (bf16[128,1024]{1,0:T(8,128)(2,1)S(1)}, bf16[128,1024]{1,0:T(8,128)(2,1)S(1)}, u32[]{:S(2)}, u32[]{:S(2)}) collective-permute-start(bf16[128,1024]{1,0:T(8,128)(2,1)S(1)} %collective-permute-done.18.refs_0_.refs_2_), channel_id=1, source_target_pairs={{0,8},{4,12},{8,16},{12,20},{16,24},{20,28},{24,32},{28,36},{32,40... | collective-permute-start | bytes 786440 | tf_op jit(solution)/shard_map/ppermute | solution.py:433
  79.1 2.9 %collective-permute-start.21 = (bf16[128,512]{1,0:T(8,128)(2,1)S(1)}, bf16[128,512]{1,0:T(8,128)(2,1)S(1)}, u32[]{:S(2)}, u32[]{:S(2)}) collective-permute-start(bf16[128,512]{1,0:T(8,128)(2,1)S(1)} %collective-permute-done.19), channel_id=1, source_target_pairs={{8,0},{12,4},{16,8},{20,12},{24,16},{28,20},{32,24},{36,28},{40,32... | collective-permute-start | bytes 393224 | tf_op jit(solution)/shard_map/ppermute | solution.py:433
  82.2 5.1 %collective-permute-done.21.q_ref = bf16[128,512]{1,0:T(8,128)(2,1)S(1)} collective-permute-done((bf16[128,512]{1,0:T(8,128)(2,1)S(1)}, bf16[128,512]{1,0:T(8,128)(2,1)S(1)}, u32[]{:S(2)}, u32[]{:S(2)}) %collective-permute-start.21) | collective-permute-done | bytes 131104 | tf_op jit(solution)/shard_map/ppermute | solution.py:433
  88.8 1.8 %shard_map.105 = (bf16[128,640]{1,0:T(8,128)(2,1)S(1)}, bf16[128,512]{1,0:T(8,128)(2,1)}) custom-call(s32[5]{0:T(128)S(1)} %stack.23.place, bf16[128,512]{1,0:T(8,128)(2,1)S(1)} %shard_map.103.refs_0_.hidden_ref, bf16[128,512]{1,0:T(8,128)(2,1)S(1)} %collective-permute-done.21.q_ref, bf16[128,1024]{1,0:T(8,128)(2,1)S(1)} %collective-permute-done.18.refs_0_.refs_2_, ...), custom_call_target="tpu_custom_call" | custom-call | tf_op jit(solution)/shard_map/pallas_call | solution.py:419
  90.6 4.6 %collective-permute-start.25 = (bf16[128,640]{1,0:T(8,128)(2,1)S(1)}, bf16[128,640]{1,0:T(8,128)(2,1)S(1)}, u32[]{:S(2)}, u32[]{:S(2)}) collective-permute-start(bf16[128,640]{1,0:T(8,128)(2,1)S(1)} %get-tuple-element.87), channel_id=1, source_target_pairs={{0,16},{4,20},{8,24},{12,28},{16,32},{20,36},{24,40},{28,44},{32,4... | collective-permute-start | bytes 491528 | tf_op jit(solution)/shard_map/ppermute | solution.py:433
  95.2 1.6 %shard_map.106.sums_ref = f32[128,1024]{1,0:T(8,128)S(1)} custom-call(s32[5]{0:T(128)S(1)} %stack.23.place, bf16[128,512]{1,0:T(8,128)(2,1)S(1)} %get-tuple-element.81.q_ref, bf16[128,1024]{1,0:T(8,128)(2,1)S(1)} %get-tuple-element.80.refs_0_, bf16[128,1024]{1,0:T(8,128)(2,1)S(1)} %collective-permute-done.24.refs_1_, ...), custom_call_target="tpu_custom_call" | custom-call | tf_op jit(solution)/shard_map/pallas_call | solution.py:419
  96.8 9.1 %collective-permute-done.25.back_ref = bf16[128,640]{1,0:T(8,128)(2,1)S(1)} collective-permute-done((bf16[128,640]{1,0:T(8,128)(2,1)S(1)}, bf16[128,640]{1,0:T(8,128)(2,1)S(1)}, u32[]{:S(2)}, u32[]{:S(2)}) %collective-permute-start.25) | collective-permute-done | bytes 163872 | tf_op jit(solution)/shard_map/ppermute | solution.py:433
  (49 shorter events, 26.6 us)
Async XLA Ops:
  6.8 4.9 %collective-permute-start = (bf16[144,256]{1,0:T(8,128)(2,1)S(1)}, bf16[144,256]{1,0:T(8,128)(2,1)S(1)}, u32[]{:S(2)}, u32[]{:S(2)}) collective-permute-start(bf16[144,256]{1,0:T(8,128)(2,1)S(1)} %get-tuple-element.52), channel_id=1, source_target_pairs={{0,8},{4,12},{8,0},{12,4},{16,24},{20,28},{24,16},{28,20},{32,40},... | collective-permute-start | bytes 221192 | tf_op jit(solution)/shard_map/ppermute | solution.py:439
  7.0 4.7 %collective-permute-start.1 = (bf16[144,256]{1,0:T(8,128)(2,1)S(1)}, bf16[144,256]{1,0:T(8,128)(2,1)S(1)}, u32[]{:S(2)}, u32[]{:S(2)}) collective-permute-start(bf16[144,256]{1,0:T(8,128)(2,1)S(1)} %get-tuple-element.53), channel_id=1, source_target_pairs={{0,12},{4,8},{8,4},{12,0},{16,28},{20,24},{24,20},{28,16},{32,44},... | collective-permute-start | bytes 221192 | tf_op jit(solution)/shard_map/ppermute | solution.py:439
  8.0 3.6 %collective-permute-start.2 = (bf16[144,256]{1,0:T(8,128)(2,1)S(1)}, bf16[144,256]{1,0:T(8,128)(2,1)S(1)}, u32[]{:S(2)}, u32[]{:S(2)}) collective-permute-start(bf16[144,256]{1,0:T(8,128)(2,1)S(1)} %get-tuple-element.54), channel_id=1, source_target_pairs={{0,4},{4,0},{8,12},{12,8},{16,20},{20,16},{24,28},{28,24},{32,36},... | collective-permute-start | bytes 221192 | tf_op jit(solution)/shard_map/ppermute | solution.py:439
  12.7 11.3 %collective-permute-start.3 = (bf16[144,256]{1,0:T(8,128)(2,1)S(1)}, bf16[144,256]{1,0:T(8,128)(2,1)S(1)}, u32[]{:S(2)}, u32[]{:S(2)}) collective-permute-start(bf16[144,256]{1,0:T(8,128)(2,1)S(1)} %get-tuple-element.59), channel_id=1, source_target_pairs={{0,32},{4,36},{8,40},{12,44},{16,48},{20,52},{24,56},{28,60},{32,0... | collective-permute-start | bytes 221192 | tf_op jit(solution)/shard_map/ppermute | solution.py:439
  19.8 6.7 %collective-permute-start.4 = (bf16[144,256]{1,0:T(8,128)(2,1)S(1)}, bf16[144,256]{1,0:T(8,128)(2,1)S(1)}, u32[]{:S(2)}, u32[]{:S(2)}) collective-permute-start(bf16[144,256]{1,0:T(8,128)(2,1)S(1)} %get-tuple-element.59), channel_id=1, source_target_pairs={{0,16},{4,20},{8,24},{12,28},{16,0},{20,4},{24,8},{28,12},{32,48},... | collective-permute-start | bytes 221192 | tf_op jit(solution)/shard_map/ppermute | solution.py:439
  21.3 7.6 %collective-permute-start.5 = (bf16[144,256]{1,0:T(8,128)(2,1)S(1)}, bf16[144,256]{1,0:T(8,128)(2,1)S(1)}, u32[]{:S(2)}, u32[]{:S(2)}) collective-permute-start(bf16[144,256]{1,0:T(8,128)(2,1)S(1)} %get-tuple-element.59), channel_id=1, source_target_pairs={{0,48},{4,52},{8,56},{12,60},{16,32},{20,36},{24,40},{28,44},{32,1... | collective-permute-start | bytes 221192 | tf_op jit(solution)/shard_map/ppermute | solution.py:439
  29.9 5.9 %collective-permute-start.6 = (bf16[144,256]{1,0:T(8,128)(2,1)S(1)}, bf16[144,256]{1,0:T(8,128)(2,1)S(1)}, u32[]{:S(2)}, u32[]{:S(2)}) collective-permute-start(bf16[144,256]{1,0:T(8,128)(2,1)S(1)} %get-tuple-element.68), channel_id=1, source_target_pairs={{0,128},{4,132},{8,136},{12,140},{16,144},{20,148},{24,152},{28,15... | collective-permute-start | bytes 221192 | tf_op jit(solution)/shard_map/ppermute | solution.py:439
  32.2 4.5 %collective-permute-start.7 = (bf16[144,256]{1,0:T(8,128)(2,1)S(1)}, bf16[144,256]{1,0:T(8,128)(2,1)S(1)}, u32[]{:S(2)}, u32[]{:S(2)}) collective-permute-start(bf16[144,256]{1,0:T(8,128)(2,1)S(1)} %get-tuple-element.68), channel_id=1, source_target_pairs={{0,64},{4,68},{8,72},{12,76},{16,80},{20,84},{24,88},{28,92},{32,9... | collective-permute-start | bytes 221192 | tf_op jit(solution)/shard_map/ppermute | solution.py:439
  33.6 4.4 %collective-permute-start.8 = (bf16[144,256]{1,0:T(8,128)(2,1)S(1)}, bf16[144,256]{1,0:T(8,128)(2,1)S(1)}, u32[]{:S(2)}, u32[]{:S(2)}) collective-permute-start(bf16[144,256]{1,0:T(8,128)(2,1)S(1)} %get-tuple-element.68), channel_id=1, source_target_pairs={{0,192},{4,196},{8,200},{12,204},{16,208},{20,212},{24,216},{28,22... | collective-permute-start | bytes 221192 | tf_op jit(solution)/shard_map/ppermute | solution.py:439
  39.0 3.4 %collective-permute-start.10 = (bf16[128,128]{1,0:T(8,128)(2,1)S(1)}, bf16[128,128]{1,0:T(8,128)(2,1)S(1)}, u32[]{:S(2)}, u32[]{:S(2)}) collective-permute-start(bf16[128,128]{1,0:T(8,128)(2,1)S(1)} %get-tuple-element.72), channel_id=1, source_target_pairs={{0,12},{4,8},{8,4},{12,0},{16,28},{20,24},{24,20},{28,16},{32,44},... | collective-permute-start | bytes 98312 | tf_op jit(solution)/shard_map/ppermute | solution.py:439
  39.2 4.0 %collective-permute-start.9 = (bf16[128,128]{1,0:T(8,128)(2,1)S(1)}, bf16[128,128]{1,0:T(8,128)(2,1)S(1)}, u32[]{:S(2)}, u32[]{:S(2)}) collective-permute-start(bf16[128,128]{1,0:T(8,128)(2,1)S(1)} %get-tuple-element.71), channel_id=1, source_target_pairs={{0,8},{4,12},{8,0},{12,4},{16,24},{20,28},{24,16},{28,20},{32,40},... | collective-permute-start | bytes 98312 | tf_op jit(solution)/shard_map/ppermute | solution.py:439
  44.4 7.8 %collective-permute-start.12 = (bf16[128,512]{1,0:T(8,128)(2,1)S(1)}, bf16[128,512]{1,0:T(8,128)(2,1)S(1)}, u32[]{:S(2)}, u32[]{:S(2)}) collective-permute-start(bf16[128,512]{1,0:T(8,128)(2,1)S(1)} %get-tuple-element.76), channel_id=1, source_target_pairs={{0,2},{1,3},{2,0},{3,1},{4,6},{5,7},{6,4},{7,5},{8,10},{9,11},{10,... | collective-permute-start | bytes 393224 | tf_op jit(solution)/shard_map/ppermute | solution.py:439
  47.9 6.2 %collective-permute-start.13 = (bf16[128,512]{1,0:T(8,128)(2,1)S(1)}, bf16[128,512]{1,0:T(8,128)(2,1)S(1)}, u32[]{:S(2)}, u32[]{:S(2)}) collective-permute-start(bf16[128,512]{1,0:T(8,128)(2,1)S(1)} %get-tuple-element.77), channel_id=1, source_target_pairs={{0,1},{1,0},{2,3},{3,2},{4,5},{5,4},{6,7},{7,6},{8,9},{9,8},{10,11... | collective-permute-start | bytes 393224 | tf_op jit(solution)/shard_map/ppermute | solution.py:439
  48.5 6.2 %collective-permute-start.14 = (bf16[128,512]{1,0:T(8,128)(2,1)S(1)}, bf16[128,512]{1,0:T(8,128)(2,1)S(1)}, u32[]{:S(2)}, u32[]{:S(2)}) collective-permute-start(bf16[128,512]{1,0:T(8,128)(2,1)S(1)} %get-tuple-element.78), channel_id=1, source_target_pairs={{0,3},{1,2},{2,1},{3,0},{4,7},{5,6},{6,5},{7,4},{8,11},{9,10},{10,... | collective-permute-start | bytes 393224 | tf_op jit(solution)/shard_map/ppermute | solution.py:439
  54.8 7.2 %collective-permute-start.15 = (bf16[128,512]{1,0:T(8,128)(2,1)S(1)}, bf16[128,512]{1,0:T(8,128)(2,1)S(1)}, u32[]{:S(2)}, u32[]{:S(2)}) collective-permute-start(bf16[128,512]{1,0:T(8,128)(2,1)S(1)} %shard_map.103.refs_0_.hidden_ref), channel_id=1, source_target_pairs={{0,2},{1,3},{2,0},{3,1},{4,6},{5,7},{6,4},{7,5},{8,10},{9,11},{10,... | collective-permute-start | bytes 393224 | tf_op jit(solution)/shard_map/ppermute | solution.py:439
  57.2 6.2 %collective-permute-start.16 = (bf16[128,512]{1,0:T(8,128)(2,1)S(1)}, bf16[128,512]{1,0:T(8,128)(2,1)S(1)}, u32[]{:S(2)}, u32[]{:S(2)}) collective-permute-start(bf16[128,512]{1,0:T(8,128)(2,1)S(1)} %shard_map.103.refs_0_.hidden_ref), channel_id=1, source_target_pairs={{0,1},{1,0},{2,3},{3,2},{4,5},{5,4},{6,7},{7,6},{8,9},{9,8},{10,11... | collective-permute-start | bytes 393224 | tf_op jit(solution)/shard_map/ppermute | solution.py:439
  57.8 6.6 %collective-permute-start.17 = (bf16[128,512]{1,0:T(8,128)(2,1)S(1)}, bf16[128,512]{1,0:T(8,128)(2,1)S(1)}, u32[]{:S(2)}, u32[]{:S(2)}) collective-permute-start(bf16[128,512]{1,0:T(8,128)(2,1)S(1)} %shard_map.103.refs_0_.hidden_ref), channel_id=1, source_target_pairs={{0,3},{1,2},{2,1},{3,0},{4,7},{5,6},{6,5},{7,4},{8,11},{9,10},{10,... | collective-permute-start | bytes 393224 | tf_op jit(solution)/shard_map/ppermute | solution.py:439
  66.1 9.6 %collective-permute-start.18 = (bf16[128,1024]{1,0:T(8,128)(2,1)S(1)}, bf16[128,1024]{1,0:T(8,128)(2,1)S(1)}, u32[]{:S(2)}, u32[]{:S(2)}) collective-permute-start(bf16[128,1024]{1,0:T(8,128)(2,1)S(1)} %get-tuple-element.80.refs_0_), channel_id=1, source_target_pairs={{0,8},{4,12},{8,16},{12,20},{16,24},{20,28},{24,32},{28,36},{32,40... | collective-permute-start | bytes 786440 | tf_op jit(solution)/shard_map/ppermute | solution.py:433
  68.9 6.9 %collective-permute-start.19 = (bf16[128,512]{1,0:T(8,128)(2,1)S(1)}, bf16[128,512]{1,0:T(8,128)(2,1)S(1)}, u32[]{:S(2)}, u32[]{:S(2)}) collective-permute-start(bf16[128,512]{1,0:T(8,128)(2,1)S(1)} %get-tuple-element.81.q_ref), channel_id=1, source_target_pairs={{8,0},{12,4},{16,8},{20,12},{24,16},{28,20},{32,24},{36,28},{40,32... | collective-permute-start | bytes 393224 | tf_op jit(solution)/shard_map/ppermute | solution.py:433
  75.7 11.5 %collective-permute-start.20 = (bf16[128,1024]{1,0:T(8,128)(2,1)S(1)}, bf16[128,1024]{1,0:T(8,128)(2,1)S(1)}, u32[]{:S(2)}, u32[]{:S(2)}) collective-permute-start(bf16[128,1024]{1,0:T(8,128)(2,1)S(1)} %collective-permute-done.18.refs_0_.refs_2_), channel_id=1, source_target_pairs={{0,8},{4,12},{8,16},{12,20},{16,24},{20,28},{24,32},{28,36},{32,40... | collective-permute-start | bytes 786440 | tf_op jit(solution)/shard_map/ppermute | solution.py:433
  79.1 8.1 %collective-permute-start.21 = (bf16[128,512]{1,0:T(8,128)(2,1)S(1)}, bf16[128,512]{1,0:T(8,128)(2,1)S(1)}, u32[]{:S(2)}, u32[]{:S(2)}) collective-permute-start(bf16[128,512]{1,0:T(8,128)(2,1)S(1)} %collective-permute-done.19), channel_id=1, source_target_pairs={{8,0},{12,4},{16,8},{20,12},{24,16},{28,20},{32,24},{36,28},{40,32... | collective-permute-start | bytes 393224 | tf_op jit(solution)/shard_map/ppermute | solution.py:433
  82.1 5.7 %collective-permute-start.22 = (bf16[128,1024]{1,0:T(8,128)(2,1)S(1)}, bf16[128,1024]{1,0:T(8,128)(2,1)S(1)}, u32[]{:S(2)}, u32[]{:S(2)}) collective-permute-start(bf16[128,1024]{1,0:T(8,128)(2,1)S(1)} %collective-permute-done.18.refs_0_.refs_2_), channel_id=1, source_target_pairs={{0,4},{4,0},{8,12},{12,8},{16,20},{20,16},{24,28},{28,24},{32,36},... | collective-permute-start | bytes 786440 | tf_op jit(solution)/shard_map/ppermute | solution.py:439
  87.2 8.0 %collective-permute-start.24 = (bf16[128,1024]{1,0:T(8,128)(2,1)S(1)}, bf16[128,1024]{1,0:T(8,128)(2,1)S(1)}, u32[]{:S(2)}, u32[]{:S(2)}) collective-permute-start(bf16[128,1024]{1,0:T(8,128)(2,1)S(1)} %get-tuple-element.80.refs_0_), channel_id=1, source_target_pairs={{0,4},{4,0},{8,12},{12,8},{16,20},{20,16},{24,28},{28,24},{32,36},... | collective-permute-start | bytes 786440 | tf_op jit(solution)/shard_map/ppermute | solution.py:439
  90.6 15.4 %collective-permute-start.25 = (bf16[128,640]{1,0:T(8,128)(2,1)S(1)}, bf16[128,640]{1,0:T(8,128)(2,1)S(1)}, u32[]{:S(2)}, u32[]{:S(2)}) collective-permute-start(bf16[128,640]{1,0:T(8,128)(2,1)S(1)} %get-tuple-element.87), channel_id=1, source_target_pairs={{0,16},{4,20},{8,24},{12,28},{16,32},{20,36},{24,40},{28,44},{32,4... | collective-permute-start | bytes 491528 | tf_op jit(solution)/shard_map/ppermute | solution.py:433
  (5 other events, 72.8 us)

commit v6 on v5

--- a/solution.py
+++ b/solution.py
@@ -41,16 +41,14 @@
     )
 
 
-def fine(left, right, contract=(1, 0)):
+def fine(left, right):
     left_high = left.astype(BF16)
     right_high = right.astype(BF16)
     left_low = (left - left_high.astype(F32)).astype(BF16)
     right_low = (right - right_high.astype(F32)).astype(BF16)
-    return (
-        dot(left_high, right_high, contract)
-        + dot(left_high, right_low, contract)
-        + dot(left_low, right_high, contract)
-    )
+    wide = right.shape[1]
+    both = dot(left_high, jnp.concatenate([right_high, right_low], axis=1))
+    return both[:, :wide] + both[:, wide:] + dot(left_low, right_high)
 
 
 def split_diagonal(matrix):
@@ -135,12 +133,18 @@
     rows = gb_ref.shape[1]
     groups = gb_ref.shape[0] // 2
     row, column = iotas(rows, rows)
-    gates = gb_ref[0:groups, :]
+    both = gb_ref[...]
+    high = both.astype(BF16)
+    rest = both - high.astype(F32)
+    middle = rest.astype(BF16)
+    low = (rest - middle.astype(F32)).astype(BF16)
+    sums = dot(jnp.concatenate([high, middle, low], axis=0), (row <= column).astype(BF16))
+    count = 2 * groups
+    summed_row = sums[:count] + sums[count : 2 * count] + sums[2 * count :]
+    columns = jnp.concatenate([summed_row[:groups], both[groups:]], axis=0).T
     causal = row >= column
-    summed = exact(causal.astype(F32), gates, (1, 1))
-    summed_row = exact(gates, (row <= column).astype(F32))
-    spreads = [summed[:, h : h + 1] - summed_row[h : h + 1, :] for h in range(groups)]
-    return summed, [
+    spreads = [columns[:, h : h + 1] - summed_row[h : h + 1, :] for h in range(groups)]
+    return columns, [
         jnp.where(causal, jnp.exp(jnp.where(causal, spread, 0.0)), 0.0) for spread in spreads
     ]
 
@@ -159,7 +163,7 @@
         load.start()
     row, column = iotas(rows, rows)
     summed, decay = decays(gb_ref)
-    betas = exact((row == column).astype(F32), gb_ref[groups:, :], (1, 1))
+    betas = summed[:, groups:]
     loads[0].wait()
     keys, couplings = [], []
     for h in range(groups):
@@ -249,7 +253,7 @@
         load.wait()
 
 
-def row_kernel(place, all_ref, recv2_ref, recv1_ref, recv3_ref, before_ref, pay_ref, pairs, starts):
+def row_kernel(place, all_ref, recv1_ref, recv3_ref, recv2_ref, before_ref, pay_ref, pairs, starts):
     group = place[3]
     pairs[group] = all_ref[...]
     for d, ref in ((1, recv1_ref), (2, recv2_ref), (3, recv3_ref)):
@@ -367,16 +371,22 @@
     return [slice(2 * h * WIDTH, 2 * (h + 1) * WIDTH) for h in range(groups)]
 
 
-def back_kernel(place, hidden_ref, q_ref, *refs):
-    blocks, (back_ref, keep_ref) = refs[:-2], refs[-2:]
+def away_kernel(place, hidden_ref, q_ref, own_ref, other_ref, sums_ref, keep_ref):
+    seq = place[0]
+    groups = q_ref.shape[1] // WIDTH
+    sums = [None] * groups
+    window_part(seq + 4, (seq >> 1) - 1, seq & 1, q_ref, own_ref, other_ref, sums)
+    for h, span in enumerate(sum_spans(groups)):
+        sums_ref[:, span] = sums[h]
+    keep_ref[...] = hidden_ref[...]
+
+
+def back_kernel(place, q_ref, sums_ref, own_ref, other_ref, back_ref):
     seq = place[0]
     rows = q_ref.shape[0]
     groups = q_ref.shape[1] // WIDTH
-    sums = [None] * groups
-    for n in range(len(blocks) // 2):
-        window_part(
-            seq + 4, (seq >> 1) - 1 - n, seq & 1, q_ref, blocks[2 * n], blocks[2 * n + 1], sums
-        )
+    sums = [sums_ref[:, span] for span in sum_spans(groups)]
+    window_part(seq + 4, (seq >> 1) - 2, seq & 1, q_ref, own_ref, other_ref, sums)
     _, column = iotas(rows, WIDTH)
     totals = jnp.zeros((rows, WIDTH), BF16)
     for h in range(groups):
@@ -386,7 +396,6 @@
         low = (total - high.astype(F32)).astype(BF16)
         totals = jnp.where(column == 2 * h, high, jnp.where(column == 2 * h + 1, low, totals))
     back_ref[:, groups * WIDTH :] = totals
-    keep_ref[...] = hidden_ref[...]
 
 
 def home_kernel(place, q_ref, *refs):
@@ -470,7 +479,7 @@
     before, everything, pay = call(
         group_kernel, [((3, WIDTH, 2 * WIDTH), F32), pair_shape, pay_shape], 1, [four_pairs]
     )(place, own, pay2, pay3, pay1)
-    row2, row1, row3 = [crossed(pay, 4 * d) for d in (2, 1, 3)]
+    row1, row3, row2 = [crossed(pay, 4 * d) for d in (1, 3, 2)]
     everything, w_qkv = lax.optimization_barrier((everything, w_qkv))
     w_qkv, everything = call(
         fetch_wide_kernel,
@@ -481,7 +490,7 @@
         FETCH_LIMIT,
     )(everything, w_qkv)
     before_row, pay = call(row_kernel, [pair_shape, pay_shape], 1, [four_pairs] * 2)(
-        place, everything, row2, row1, row3
+        place, everything, row1, row3, row2
     )
     row2, row1, row3 = [crossed(pay, 16 * d) for d in (2, 1, 3)]
     before_row, w_out, stream = lax.optimization_barrier((before_row, w_out, stream))
@@ -526,8 +535,12 @@
     home = [
         pack, crossed(pack, 1), first, crossed(first, 1), second, crossed(second, 1)
     ]
-    back, kept = call(back_kernel, [((rows, wide + WIDTH), BF16), row_shape], 1)(
-        place, hidden, visitors, *home[2:]
+    sums_shape = ((rows, 2 * wide), F32)
+    away, kept = call(away_kernel, [sums_shape, row_shape], 1)(
+        place, hidden, visitors, home[2], home[3]
+    )
+    (back,) = call(back_kernel, [((rows, wide + WIDTH), BF16)], 1)(
+        place, visitors, away, home[4], home[5]
     )
     returned = moved(back, "seq", 4)
     (sums,) = call(home_kernel, [((rows, 2 * wide), F32)], 1)(place, unit_queries, *home)

time: 107 us -> 107 us (level)
    pallas_call x13 -> x14, Pallas kernels: 20.3 us -> 20.7 us  [run(): pl.pallas_call(kernel, out_shape=[jax.ShapeDtypeStruct(shape, kind) for s...]
  transfers between devices with their start and end apart: 26 -> 26, of which waited for: 18 -> 17; matrix products, arithmetic and copies ran while one was open for 0% -> 0% of each run, Pallas kernels for 8% -> 8%
where the time goes in v6:
time: 107 us
  starting transfers between devices  43 us (40%)
  waiting for transfers between devices  40.8 us (38%)
  Pallas kernels  20.7 us (19%)
    ppermute x21, starting transfers between devices, crossed(): lax.ppermute(array, axis, [(i, i ^ mask) for i in range(lax.axis_size(axi...  26.4 us
    ppermute x21, waiting for transfers between devices, crossed(): lax.ppermute(array, axis, [(i, i ^ mask) for i in range(lax.axis_size(axi...  22.8 us
    pallas_call x14, Pallas kernels, run(): pl.pallas_call(kernel, out_shape=[jax.ShapeDtypeStruct(shape, kind) for s...  20.7 us
    ppermute x5, waiting for transfers between devices, moved(): lax.ppermute(array, axis, [(i, i + distance) for i in range(size) if 0 <=...  18 us
    ppermute x5, starting transfers between devices, moved(): lax.ppermute(array, axis, [(i, i + distance) for i in range(size) if 0 <=...  16.6 us
  transfers between devices with their start and end apart: 26, of which 17 were waited for; matrix products, arithmetic and copies ran while one was open for 0% of the time, Pallas kernels for 8%

profile of v6, /device:TPU:34, one launch (start us, length us, event | category | flops | bytes accessed | tf_op | source)
XLA Modules:
  0.0 107.2 jit_solution(12303551487710378339)
XLA Ops:
  1.6 4.9 %shard_map.95 = (bf16[128,512]{1,0:T(8,128)(2,1)S(1)}, bf16[4,128,128]{2,1,0:T(8,128)(2,1)S(1)}, bf16[4,128,128]{2,1,0:T(8,128)(2,1)S(1)}, f32[128,256]{1,0:T(8,...) custom-call(s32[5]{0:T(128)S(1)} %stack.23.place, ...), custom_call_target="tpu_custom_call" | custom-call | tf_op jit(solution)/shard_map/pallas_call | solution.py:428
  12.5 3.4 %collective-permute-start.3 = (bf16[144,256]{1,0:T(8,128)(2,1)S(1)}, bf16[144,256]{1,0:T(8,128)(2,1)S(1)}, u32[]{:S(2)}, u32[]{:S(2)}) collective-permute-start(bf16[144,256]{1,0:T(8,128)(2,1)S(1)} %get-tuple-element.59), channel_id=1, source_target_pairs={{0,16},{4,20},{8,24},{12,28},{16,0},{20,4},{24,8},{28,12},{32,48},... | collective-permute-start | bytes 221192 | tf_op jit(solution)/shard_map/ppermute | solution.py:448
  15.8 4.3 %collective-permute-start.4 = (bf16[144,256]{1,0:T(8,128)(2,1)S(1)}, bf16[144,256]{1,0:T(8,128)(2,1)S(1)}, u32[]{:S(2)}, u32[]{:S(2)}) collective-permute-start(bf16[144,256]{1,0:T(8,128)(2,1)S(1)} %get-tuple-element.59), channel_id=1, source_target_pairs={{0,48},{4,52},{8,56},{12,60},{16,32},{20,36},{24,40},{28,44},{32,1... | collective-permute-start | bytes 221192 | tf_op jit(solution)/shard_map/ppermute | solution.py:448
  21.0 2.8 %shard_map.98 = (bf16[2048,1536]{1,0:T(8,128)(2,1)S(1)}, f32[128,256]{1,0:T(8,128)S(1)}) custom-call(f32[128,256]{1,0:T(8,128)S(1)} %get-tuple-element.56.token_ref, bf16[2048,1536]{1,0:T(8,128)(2,1)} %source_ref), custom_call_target="tpu_custom_call" | custom-call | tf_op jit(solution)/shard_map/pallas_call | solution.py:428
  24.1 5.6 %collective-permute-done.5.recv2_ref = bf16[144,256]{1,0:T(8,128)(2,1)S(1)} collective-permute-done((bf16[144,256]{1,0:T(8,128)(2,1)S(1)}, bf16[144,256]{1,0:T(8,128)(2,1)S(1)}, u32[]{:S(2)}, u32[]{:S(2)}) %collective-permute-start.5) | collective-permute-done | bytes 73760 | tf_op jit(solution)/shard_map/ppermute | solution.py:448
  30.8 2.2 %collective-permute-start.6 = (bf16[144,256]{1,0:T(8,128)(2,1)S(1)}, bf16[144,256]{1,0:T(8,128)(2,1)S(1)}, u32[]{:S(2)}, u32[]{:S(2)}) collective-permute-start(bf16[144,256]{1,0:T(8,128)(2,1)S(1)} %get-tuple-element.68), channel_id=1, source_target_pairs={{0,128},{4,132},{8,136},{12,140},{16,144},{20,148},{24,152},{28,15... | collective-permute-start | bytes 221192 | tf_op jit(solution)/shard_map/ppermute | solution.py:448
  33.0 1.4 %collective-permute-start.7 = (bf16[144,256]{1,0:T(8,128)(2,1)S(1)}, bf16[144,256]{1,0:T(8,128)(2,1)S(1)}, u32[]{:S(2)}, u32[]{:S(2)}) collective-permute-start(bf16[144,256]{1,0:T(8,128)(2,1)S(1)} %get-tuple-element.68), channel_id=1, source_target_pairs={{0,64},{4,68},{8,72},{12,76},{16,80},{20,84},{24,88},{28,92},{32,9... | collective-permute-start | bytes 221192 | tf_op jit(solution)/shard_map/ppermute | solution.py:448
  40.1 2.0 %collective-permute-start.9 = (bf16[128,128]{1,0:T(8,128)(2,1)S(1)}, bf16[128,128]{1,0:T(8,128)(2,1)S(1)}, u32[]{:S(2)}, u32[]{:S(2)}) collective-permute-start(bf16[128,128]{1,0:T(8,128)(2,1)S(1)} %get-tuple-element.71), channel_id=1, source_target_pairs={{0,8},{4,12},{8,0},{12,4},{16,24},{20,28},{24,16},{28,20},{32,40},... | collective-permute-start | bytes 98312 | tf_op jit(solution)/shard_map/ppermute | solution.py:448
  45.3 3.5 %collective-permute-start.12 = (bf16[128,512]{1,0:T(8,128)(2,1)S(1)}, bf16[128,512]{1,0:T(8,128)(2,1)S(1)}, u32[]{:S(2)}, u32[]{:S(2)}) collective-permute-start(bf16[128,512]{1,0:T(8,128)(2,1)S(1)} %get-tuple-element.76), channel_id=1, source_target_pairs={{0,2},{1,3},{2,0},{3,1},{4,6},{5,7},{6,4},{7,5},{8,10},{9,11},{10,... | collective-permute-start | bytes 393224 | tf_op jit(solution)/shard_map/ppermute | solution.py:448
  49.8 3.3 %collective-permute-done.12.refs_0_ = bf16[128,512]{1,0:T(8,128)(2,1)S(1)} collective-permute-done((bf16[128,512]{1,0:T(8,128)(2,1)S(1)}, bf16[128,512]{1,0:T(8,128)(2,1)S(1)}, u32[]{:S(2)}, u32[]{:S(2)}) %collective-permute-start.12) | collective-permute-done | bytes 131104 | tf_op jit(solution)/shard_map/ppermute | solution.py:448
  53.1 1.9 %collective-permute-done.13.refs_1_ = bf16[128,512]{1,0:T(8,128)(2,1)S(1)} collective-permute-done((bf16[128,512]{1,0:T(8,128)(2,1)S(1)}, bf16[128,512]{1,0:T(8,128)(2,1)S(1)}, u32[]{:S(2)}, u32[]{:S(2)}) %collective-permute-start.13) | collective-permute-done | bytes 131104 | tf_op jit(solution)/shard_map/ppermute | solution.py:448
  55.7 2.4 %collective-permute-start.15 = (bf16[128,512]{1,0:T(8,128)(2,1)S(1)}, bf16[128,512]{1,0:T(8,128)(2,1)S(1)}, u32[]{:S(2)}, u32[]{:S(2)}) collective-permute-start(bf16[128,512]{1,0:T(8,128)(2,1)S(1)} %shard_map.103.refs_0_.hidden_ref), channel_id=1, source_target_pairs={{0,2},{1,3},{2,0},{3,1},{4,6},{5,7},{6,4},{7,5},{8,10},{9,11},{10,... | collective-permute-start | bytes 393224 | tf_op jit(solution)/shard_map/ppermute | solution.py:448
  59.8 3.0 %collective-permute-done.15.refs_1_ = bf16[128,512]{1,0:T(8,128)(2,1)S(1)} collective-permute-done((bf16[128,512]{1,0:T(8,128)(2,1)S(1)}, bf16[128,512]{1,0:T(8,128)(2,1)S(1)}, u32[]{:S(2)}, u32[]{:S(2)}) %collective-permute-start.15) | collective-permute-done | bytes 131104 | tf_op jit(solution)/shard_map/ppermute | solution.py:448
  65.3 1.7 %shard_map.104 = (bf16[128,512]{1,0:T(8,128)(2,1)S(1)}, bf16[128,1024]{1,0:T(8,128)(2,1)S(1)}) custom-call(s32[5]{0:T(128)S(1)} %stack.23.place, bf16[2048,1536]{1,0:T(8,128)(2,1)S(1)} %get-tuple-element.79.w_ref, bf16[128,512]{1,0:T(8,128)(2,1)S(1)} %shard_map.103.refs_0_.hidden_ref, bf16[128,512]{1,0:T(8,128)(2,1)S(1)} %collective-permute-done.15.refs_1_, ...), custom_call_target="tpu_custom_call" | custom-call | tf_op jit(solution)/shard_map/pallas_call | solution.py:428
  67.0 2.9 %collective-permute-start.18 = (bf16[128,1024]{1,0:T(8,128)(2,1)S(1)}, bf16[128,1024]{1,0:T(8,128)(2,1)S(1)}, u32[]{:S(2)}, u32[]{:S(2)}) collective-permute-start(bf16[128,1024]{1,0:T(8,128)(2,1)S(1)} %get-tuple-element.80.refs_0_), channel_id=1, source_target_pairs={{0,8},{4,12},{8,16},{12,20},{16,24},{20,28},{24,32},{28,36},{32,40... | collective-permute-start | bytes 786440 | tf_op jit(solution)/shard_map/ppermute | solution.py:442
  69.9 2.9 %collective-permute-start.19 = (bf16[128,512]{1,0:T(8,128)(2,1)S(1)}, bf16[128,512]{1,0:T(8,128)(2,1)S(1)}, u32[]{:S(2)}, u32[]{:S(2)}) collective-permute-start(bf16[128,512]{1,0:T(8,128)(2,1)S(1)} %get-tuple-element.81.q_ref), channel_id=1, source_target_pairs={{8,0},{12,4},{16,8},{20,12},{24,16},{28,20},{32,24},{36,28},{40,32... | collective-permute-start | bytes 393224 | tf_op jit(solution)/shard_map/ppermute | solution.py:442
  72.9 3.9 %collective-permute-done.19 = bf16[128,512]{1,0:T(8,128)(2,1)S(1)} collective-permute-done((bf16[128,512]{1,0:T(8,128)(2,1)S(1)}, bf16[128,512]{1,0:T(8,128)(2,1)S(1)}, u32[]{:S(2)}, u32[]{:S(2)}) %collective-permute-start.19) | collective-permute-done | bytes 131104 | tf_op jit(solution)/shard_map/ppermute | solution.py:442
  76.8 3.0 %collective-permute-start.20 = (bf16[128,1024]{1,0:T(8,128)(2,1)S(1)}, bf16[128,1024]{1,0:T(8,128)(2,1)S(1)}, u32[]{:S(2)}, u32[]{:S(2)}) collective-permute-start(bf16[128,1024]{1,0:T(8,128)(2,1)S(1)} %collective-permute-done.18.own_ref.refs_2_), channel_id=1, source_target_pairs={{0,8},{4,12},{8,16},{12,20},{16,24},{20,28},{24,32},{28,36},{32,40... | collective-permute-start | bytes 786440 | tf_op jit(solution)/shard_map/ppermute | solution.py:442
  79.8 3.1 %collective-permute-start.21 = (bf16[128,512]{1,0:T(8,128)(2,1)S(1)}, bf16[128,512]{1,0:T(8,128)(2,1)S(1)}, u32[]{:S(2)}, u32[]{:S(2)}) collective-permute-start(bf16[128,512]{1,0:T(8,128)(2,1)S(1)} %collective-permute-done.19), channel_id=1, source_target_pairs={{8,0},{12,4},{16,8},{20,12},{24,16},{28,20},{32,24},{36,28},{40,32... | collective-permute-start | bytes 393224 | tf_op jit(solution)/shard_map/ppermute | solution.py:442
  83.0 3.8 %collective-permute-done.21.q_ref = bf16[128,512]{1,0:T(8,128)(2,1)S(1)} collective-permute-done((bf16[128,512]{1,0:T(8,128)(2,1)S(1)}, bf16[128,512]{1,0:T(8,128)(2,1)S(1)}, u32[]{:S(2)}, u32[]{:S(2)}) %collective-permute-start.21) | collective-permute-done | bytes 131104 | tf_op jit(solution)/shard_map/ppermute | solution.py:442
  87.3 1.5 %shard_map.105 = (f32[128,1024]{1,0:T(8,128)S(1)}, bf16[128,512]{1,0:T(8,128)(2,1)}) custom-call(s32[5]{0:T(128)S(1)} %stack.23.place, bf16[128,512]{1,0:T(8,128)(2,1)S(1)} %shard_map.103.refs_0_.hidden_ref, bf16[128,512]{1,0:T(8,128)(2,1)S(1)} %collective-permute-done.21.q_ref, bf16[128,1024]{1,0:T(8,128)(2,1)S(1)} %collective-permute-done.18.own_ref.refs_2_, ...), custom_call_target="tpu_custom_call" | custom-call | tf_op jit(solution)/shard_map/pallas_call | solution.py:428
  89.8 4.6 %collective-permute-start.25 = (bf16[128,640]{1,0:T(8,128)(2,1)S(1)}, bf16[128,640]{1,0:T(8,128)(2,1)S(1)}, u32[]{:S(2)}, u32[]{:S(2)}) collective-permute-start(bf16[128,640]{1,0:T(8,128)(2,1)S(1)} %shard_map.107), channel_id=1, source_target_pairs={{0,16},{4,20},{8,24},{12,28},{16,32},{20,36},{24,40},{28,44},{32,4... | collective-permute-start | bytes 491528 | tf_op jit(solution)/shard_map/ppermute | solution.py:442
  94.4 1.6 %shard_map.106.sums_ref = f32[128,1024]{1,0:T(8,128)S(1)} custom-call(s32[5]{0:T(128)S(1)} %stack.23.place, bf16[128,512]{1,0:T(8,128)(2,1)S(1)} %get-tuple-element.81.q_ref, bf16[128,1024]{1,0:T(8,128)(2,1)S(1)} %get-tuple-element.80.refs_0_, bf16[128,1024]{1,0:T(8,128)(2,1)S(1)} %collective-permute-done.23.refs_1_, ...), custom_call_target="tpu_custom_call" | custom-call | tf_op jit(solution)/shard_map/pallas_call | solution.py:428
  96.0 10.3 %collective-permute-done.25.back_ref = bf16[128,640]{1,0:T(8,128)(2,1)S(1)} collective-permute-done((bf16[128,640]{1,0:T(8,128)(2,1)S(1)}, bf16[128,640]{1,0:T(8,128)(2,1)S(1)}, u32[]{:S(2)}, u32[]{:S(2)}) %collective-permute-start.25) | collective-permute-done | bytes 163872 | tf_op jit(solution)/shard_map/ppermute | solution.py:442
  (50 shorter events, 26.3 us)
Async XLA Ops:
  6.5 4.9 %collective-permute-start = (bf16[144,256]{1,0:T(8,128)(2,1)S(1)}, bf16[144,256]{1,0:T(8,128)(2,1)S(1)}, u32[]{:S(2)}, u32[]{:S(2)}) collective-permute-start(bf16[144,256]{1,0:T(8,128)(2,1)S(1)} %get-tuple-element.52), channel_id=1, source_target_pairs={{0,8},{4,12},{8,0},{12,4},{16,24},{20,28},{24,16},{28,20},{32,40},... | collective-permute-start | bytes 221192 | tf_op jit(solution)/shard_map/ppermute | solution.py:448
  6.7 4.7 %collective-permute-start.1 = (bf16[144,256]{1,0:T(8,128)(2,1)S(1)}, bf16[144,256]{1,0:T(8,128)(2,1)S(1)}, u32[]{:S(2)}, u32[]{:S(2)}) collective-permute-start(bf16[144,256]{1,0:T(8,128)(2,1)S(1)} %get-tuple-element.53), channel_id=1, source_target_pairs={{0,12},{4,8},{8,4},{12,0},{16,28},{20,24},{24,20},{28,16},{32,44},... | collective-permute-start | bytes 221192 | tf_op jit(solution)/shard_map/ppermute | solution.py:448
  7.8 3.6 %collective-permute-start.2 = (bf16[144,256]{1,0:T(8,128)(2,1)S(1)}, bf16[144,256]{1,0:T(8,128)(2,1)S(1)}, u32[]{:S(2)}, u32[]{:S(2)}) collective-permute-start(bf16[144,256]{1,0:T(8,128)(2,1)S(1)} %get-tuple-element.54), channel_id=1, source_target_pairs={{0,4},{4,0},{8,12},{12,8},{16,20},{20,16},{24,28},{28,24},{32,36},... | collective-permute-start | bytes 221192 | tf_op jit(solution)/shard_map/ppermute | solution.py:448
  12.5 11.3 %collective-permute-start.3 = (bf16[144,256]{1,0:T(8,128)(2,1)S(1)}, bf16[144,256]{1,0:T(8,128)(2,1)S(1)}, u32[]{:S(2)}, u32[]{:S(2)}) collective-permute-start(bf16[144,256]{1,0:T(8,128)(2,1)S(1)} %get-tuple-element.59), channel_id=1, source_target_pairs={{0,16},{4,20},{8,24},{12,28},{16,0},{20,4},{24,8},{28,12},{32,48},... | collective-permute-start | bytes 221192 | tf_op jit(solution)/shard_map/ppermute | solution.py:448
  15.8 8.3 %collective-permute-start.4 = (bf16[144,256]{1,0:T(8,128)(2,1)S(1)}, bf16[144,256]{1,0:T(8,128)(2,1)S(1)}, u32[]{:S(2)}, u32[]{:S(2)}) collective-permute-start(bf16[144,256]{1,0:T(8,128)(2,1)S(1)} %get-tuple-element.59), channel_id=1, source_target_pairs={{0,48},{4,52},{8,56},{12,60},{16,32},{20,36},{24,40},{28,44},{32,1... | collective-permute-start | bytes 221192 | tf_op jit(solution)/shard_map/ppermute | solution.py:448
  20.1 9.7 %collective-permute-start.5 = (bf16[144,256]{1,0:T(8,128)(2,1)S(1)}, bf16[144,256]{1,0:T(8,128)(2,1)S(1)}, u32[]{:S(2)}, u32[]{:S(2)}) collective-permute-start(bf16[144,256]{1,0:T(8,128)(2,1)S(1)} %get-tuple-element.59), channel_id=1, source_target_pairs={{0,32},{4,36},{8,40},{12,44},{16,48},{20,52},{24,56},{28,60},{32,0... | collective-permute-start | bytes 221192 | tf_op jit(solution)/shard_map/ppermute | solution.py:448
  30.8 5.9 %collective-permute-start.6 = (bf16[144,256]{1,0:T(8,128)(2,1)S(1)}, bf16[144,256]{1,0:T(8,128)(2,1)S(1)}, u32[]{:S(2)}, u32[]{:S(2)}) collective-permute-start(bf16[144,256]{1,0:T(8,128)(2,1)S(1)} %get-tuple-element.68), channel_id=1, source_target_pairs={{0,128},{4,132},{8,136},{12,140},{16,144},{20,148},{24,152},{28,15... | collective-permute-start | bytes 221192 | tf_op jit(solution)/shard_map/ppermute | solution.py:448
  33.0 4.6 %collective-permute-start.7 = (bf16[144,256]{1,0:T(8,128)(2,1)S(1)}, bf16[144,256]{1,0:T(8,128)(2,1)S(1)}, u32[]{:S(2)}, u32[]{:S(2)}) collective-permute-start(bf16[144,256]{1,0:T(8,128)(2,1)S(1)} %get-tuple-element.68), channel_id=1, source_target_pairs={{0,64},{4,68},{8,72},{12,76},{16,80},{20,84},{24,88},{28,92},{32,9... | collective-permute-start | bytes 221192 | tf_op jit(solution)/shard_map/ppermute | solution.py:448
  34.5 4.4 %collective-permute-start.8 = (bf16[144,256]{1,0:T(8,128)(2,1)S(1)}, bf16[144,256]{1,0:T(8,128)(2,1)S(1)}, u32[]{:S(2)}, u32[]{:S(2)}) collective-permute-start(bf16[144,256]{1,0:T(8,128)(2,1)S(1)} %get-tuple-element.68), channel_id=1, source_target_pairs={{0,192},{4,196},{8,200},{12,204},{16,208},{20,212},{24,216},{28,22... | collective-permute-start | bytes 221192 | tf_op jit(solution)/shard_map/ppermute | solution.py:448
  39.9 3.4 %collective-permute-start.10 = (bf16[128,128]{1,0:T(8,128)(2,1)S(1)}, bf16[128,128]{1,0:T(8,128)(2,1)S(1)}, u32[]{:S(2)}, u32[]{:S(2)}) collective-permute-start(bf16[128,128]{1,0:T(8,128)(2,1)S(1)} %get-tuple-element.72), channel_id=1, source_target_pairs={{0,12},{4,8},{8,4},{12,0},{16,28},{20,24},{24,20},{28,16},{32,44},... | collective-permute-start | bytes 98312 | tf_op jit(solution)/shard_map/ppermute | solution.py:448
  40.1 4.0 %collective-permute-start.9 = (bf16[128,128]{1,0:T(8,128)(2,1)S(1)}, bf16[128,128]{1,0:T(8,128)(2,1)S(1)}, u32[]{:S(2)}, u32[]{:S(2)}) collective-permute-start(bf16[128,128]{1,0:T(8,128)(2,1)S(1)} %get-tuple-element.71), channel_id=1, source_target_pairs={{0,8},{4,12},{8,0},{12,4},{16,24},{20,28},{24,16},{28,20},{32,40},... | collective-permute-start | bytes 98312 | tf_op jit(solution)/shard_map/ppermute | solution.py:448
  45.3 7.8 %collective-permute-start.12 = (bf16[128,512]{1,0:T(8,128)(2,1)S(1)}, bf16[128,512]{1,0:T(8,128)(2,1)S(1)}, u32[]{:S(2)}, u32[]{:S(2)}) collective-permute-start(bf16[128,512]{1,0:T(8,128)(2,1)S(1)} %get-tuple-element.76), channel_id=1, source_target_pairs={{0,2},{1,3},{2,0},{3,1},{4,6},{5,7},{6,4},{7,5},{8,10},{9,11},{10,... | collective-permute-start | bytes 393224 | tf_op jit(solution)/shard_map/ppermute | solution.py:448
  48.7 6.2 %collective-permute-start.13 = (bf16[128,512]{1,0:T(8,128)(2,1)S(1)}, bf16[128,512]{1,0:T(8,128)(2,1)S(1)}, u32[]{:S(2)}, u32[]{:S(2)}) collective-permute-start(bf16[128,512]{1,0:T(8,128)(2,1)S(1)} %get-tuple-element.77), channel_id=1, source_target_pairs={{0,1},{1,0},{2,3},{3,2},{4,5},{5,4},{6,7},{7,6},{8,9},{9,8},{10,11... | collective-permute-start | bytes 393224 | tf_op jit(solution)/shard_map/ppermute | solution.py:448
  49.4 6.2 %collective-permute-start.14 = (bf16[128,512]{1,0:T(8,128)(2,1)S(1)}, bf16[128,512]{1,0:T(8,128)(2,1)S(1)}, u32[]{:S(2)}, u32[]{:S(2)}) collective-permute-start(bf16[128,512]{1,0:T(8,128)(2,1)S(1)} %get-tuple-element.78), channel_id=1, source_target_pairs={{0,3},{1,2},{2,1},{3,0},{4,7},{5,6},{6,5},{7,4},{8,11},{9,10},{10,... | collective-permute-start | bytes 393224 | tf_op jit(solution)/shard_map/ppermute | solution.py:448
  55.7 7.2 %collective-permute-start.15 = (bf16[128,512]{1,0:T(8,128)(2,1)S(1)}, bf16[128,512]{1,0:T(8,128)(2,1)S(1)}, u32[]{:S(2)}, u32[]{:S(2)}) collective-permute-start(bf16[128,512]{1,0:T(8,128)(2,1)S(1)} %shard_map.103.refs_0_.hidden_ref), channel_id=1, source_target_pairs={{0,2},{1,3},{2,0},{3,1},{4,6},{5,7},{6,4},{7,5},{8,10},{9,11},{10,... | collective-permute-start | bytes 393224 | tf_op jit(solution)/shard_map/ppermute | solution.py:448
  58.0 6.2 %collective-permute-start.16 = (bf16[128,512]{1,0:T(8,128)(2,1)S(1)}, bf16[128,512]{1,0:T(8,128)(2,1)S(1)}, u32[]{:S(2)}, u32[]{:S(2)}) collective-permute-start(bf16[128,512]{1,0:T(8,128)(2,1)S(1)} %shard_map.103.refs_0_.hidden_ref), channel_id=1, source_target_pairs={{0,1},{1,0},{2,3},{3,2},{4,5},{5,4},{6,7},{7,6},{8,9},{9,8},{10,11... | collective-permute-start | bytes 393224 | tf_op jit(solution)/shard_map/ppermute | solution.py:448
  58.7 6.6 %collective-permute-start.17 = (bf16[128,512]{1,0:T(8,128)(2,1)S(1)}, bf16[128,512]{1,0:T(8,128)(2,1)S(1)}, u32[]{:S(2)}, u32[]{:S(2)}) collective-permute-start(bf16[128,512]{1,0:T(8,128)(2,1)S(1)} %shard_map.103.refs_0_.hidden_ref), channel_id=1, source_target_pairs={{0,3},{1,2},{2,1},{3,0},{4,7},{5,6},{6,5},{7,4},{8,11},{9,10},{10,... | collective-permute-start | bytes 393224 | tf_op jit(solution)/shard_map/ppermute | solution.py:448
  67.0 9.8 %collective-permute-start.18 = (bf16[128,1024]{1,0:T(8,128)(2,1)S(1)}, bf16[128,1024]{1,0:T(8,128)(2,1)S(1)}, u32[]{:S(2)}, u32[]{:S(2)}) collective-permute-start(bf16[128,1024]{1,0:T(8,128)(2,1)S(1)} %get-tuple-element.80.refs_0_), channel_id=1, source_target_pairs={{0,8},{4,12},{8,16},{12,20},{16,24},{20,28},{24,32},{28,36},{32,40... | collective-permute-start | bytes 786440 | tf_op jit(solution)/shard_map/ppermute | solution.py:442
  69.9 6.9 %collective-permute-start.19 = (bf16[128,512]{1,0:T(8,128)(2,1)S(1)}, bf16[128,512]{1,0:T(8,128)(2,1)S(1)}, u32[]{:S(2)}, u32[]{:S(2)}) collective-permute-start(bf16[128,512]{1,0:T(8,128)(2,1)S(1)} %get-tuple-element.81.q_ref), channel_id=1, source_target_pairs={{8,0},{12,4},{16,8},{20,12},{24,16},{28,20},{32,24},{36,28},{40,32... | collective-permute-start | bytes 393224 | tf_op jit(solution)/shard_map/ppermute | solution.py:442
  76.8 10.0 %collective-permute-start.20 = (bf16[128,1024]{1,0:T(8,128)(2,1)S(1)}, bf16[128,1024]{1,0:T(8,128)(2,1)S(1)}, u32[]{:S(2)}, u32[]{:S(2)}) collective-permute-start(bf16[128,1024]{1,0:T(8,128)(2,1)S(1)} %collective-permute-done.18.own_ref.refs_2_), channel_id=1, source_target_pairs={{0,8},{4,12},{8,16},{12,20},{16,24},{20,28},{24,32},{28,36},{32,40... | collective-permute-start | bytes 786440 | tf_op jit(solution)/shard_map/ppermute | solution.py:442
  79.8 7.0 %collective-permute-start.21 = (bf16[128,512]{1,0:T(8,128)(2,1)S(1)}, bf16[128,512]{1,0:T(8,128)(2,1)S(1)}, u32[]{:S(2)}, u32[]{:S(2)}) collective-permute-start(bf16[128,512]{1,0:T(8,128)(2,1)S(1)} %collective-permute-done.19), channel_id=1, source_target_pairs={{8,0},{12,4},{16,8},{20,12},{24,16},{28,20},{32,24},{36,28},{40,32... | collective-permute-start | bytes 393224 | tf_op jit(solution)/shard_map/ppermute | solution.py:442
  82.9 4.4 %collective-permute-start.22 = (bf16[128,1024]{1,0:T(8,128)(2,1)S(1)}, bf16[128,1024]{1,0:T(8,128)(2,1)S(1)}, u32[]{:S(2)}, u32[]{:S(2)}) collective-permute-start(bf16[128,1024]{1,0:T(8,128)(2,1)S(1)} %collective-permute-done.18.own_ref.refs_2_), channel_id=1, source_target_pairs={{0,4},{4,0},{8,12},{12,8},{16,20},{20,16},{24,28},{28,24},{32,36},... | collective-permute-start | bytes 786440 | tf_op jit(solution)/shard_map/ppermute | solution.py:448
  86.8 7.6 %collective-permute-start.23 = (bf16[128,1024]{1,0:T(8,128)(2,1)S(1)}, bf16[128,1024]{1,0:T(8,128)(2,1)S(1)}, u32[]{:S(2)}, u32[]{:S(2)}) collective-permute-start(bf16[128,1024]{1,0:T(8,128)(2,1)S(1)} %get-tuple-element.80.refs_0_), channel_id=1, source_target_pairs={{0,4},{4,0},{8,12},{12,8},{16,20},{20,16},{24,28},{28,24},{32,36},... | collective-permute-start | bytes 786440 | tf_op jit(solution)/shard_map/ppermute | solution.py:448
  89.8 16.5 %collective-permute-start.25 = (bf16[128,640]{1,0:T(8,128)(2,1)S(1)}, bf16[128,640]{1,0:T(8,128)(2,1)S(1)}, u32[]{:S(2)}, u32[]{:S(2)}) collective-permute-start(bf16[128,640]{1,0:T(8,128)(2,1)S(1)} %shard_map.107), channel_id=1, source_target_pairs={{0,16},{4,20},{8,24},{12,28},{16,32},{20,36},{24,40},{28,44},{32,4... | collective-permute-start | bytes 491528 | tf_op jit(solution)/shard_map/ppermute | solution.py:442
  (5 other events, 75.0 us)

commit v7 on v6

--- a/solution.py
+++ b/solution.py
@@ -322,28 +322,47 @@
     refs[-1][...] = (stream_ref[...].astype(F32) + total).astype(BF16)
 
 
-def project_kernel(place, w_ref, *refs):
+def own_kernel(place, hidden_ref, w_ref, part_ref):
+    width = hidden_ref.shape[1]
+    begin = pl.multiple_of(place[2] * width, width)
+    part_ref[...] = dot(hidden_ref[...], w_ref[pl.ds(begin, width), :])
+
+
+def product_of(place, w_ref, blocks, first, size):
     me = place[2]
-    blocks, (q_ref, kv_ref) = refs[:-2], refs[-2:]
-    count = len(blocks)
-    rows, width = blocks[0].shape
-    values = [ref[...].astype(F32) for ref in blocks]
-    squares = sum(jnp.sum(v * v, axis=-1, keepdims=True) for v in values)
-    scale = lax.rsqrt(squares / (count * width) + 1e-05)
+    width = blocks[0].shape[1]
     total = None
-    for n, r in enumerate((0, 2, 1, 3)):
+    for block, r in zip(blocks, (2, 1, 3)):
         begin = pl.multiple_of((me ^ r) * width, width)
-        part = dot((values[n] * scale).astype(BF16), w_ref[pl.ds(begin, width), :])
+        part = dot(block[...], w_ref[pl.ds(begin, width), first : first + size])
         total = part if total is None else total + part
-    groups = q_ref.shape[1] // WIDTH
-    for h in range(groups):
-        base = h * 3 * WIDTH
-        span = slice(h * WIDTH, (h + 1) * WIDTH)
-        q_ref[:, span] = to_unit(total[:, base : base + WIDTH]).astype(BF16)
-        kv_ref[:, span] = to_unit(total[:, base + WIDTH : base + 2 * WIDTH]).astype(BF16)
-        kv_ref[:, groups * WIDTH + h * WIDTH : groups * WIDTH + (h + 1) * WIDTH] = total[
-            :, base + 2 * WIDTH : base + 3 * WIDTH
-        ].astype(BF16)
+    return total
+
+
+def pair_kernel(place, w_ref, part_ref, hidden_ref, block2_ref, block1_ref, block3_ref, kv_ref, scale_ref):
+    blocks = [block2_ref, block1_ref, block3_ref]
+    squares = 0.0
+    for ref in [hidden_ref] + blocks:
+        value = ref[...].astype(F32)
+        squares = squares + jnp.sum(value * value, axis=-1, keepdims=True)
+    rows, width = hidden_ref.shape
+    scale = lax.rsqrt(squares / (4 * width) + 1e-05)
+    scale_ref[...] = jnp.broadcast_to(scale, scale_ref.shape)
+    groups = width // WIDTH
+    for h in range(groups):
+        begin = (3 * h + 1) * WIDTH
+        total = part_ref[:, begin : begin + 2 * WIDTH] + product_of(place, w_ref, blocks, begin, 2 * WIDTH)
+        total = total * scale
+        kv_ref[:, h * WIDTH : (h + 1) * WIDTH] = to_unit(total[:, :WIDTH]).astype(BF16)
+        kv_ref[:, (groups + h) * WIDTH : (groups + h + 1) * WIDTH] = total[:, WIDTH:].astype(BF16)
+
+
+def unit_kernel(place, w_ref, part_ref, scale_ref, block2_ref, block1_ref, block3_ref, q_ref):
+    blocks = [block2_ref, block1_ref, block3_ref]
+    for h in range(q_ref.shape[1] // WIDTH):
+        begin = 3 * h * WIDTH
+        total = part_ref[:, begin : begin + WIDTH] + product_of(place, w_ref, blocks, begin, WIDTH)
+        q_ref[:, h * WIDTH : (h + 1) * WIDTH] = to_unit(total * scale_ref[...]).astype(BF16)
 
 
 def window_part(query_place, key_chip, core, q_ref, own_ref, other_ref, sums):
@@ -387,15 +406,15 @@
     groups = q_ref.shape[1] // WIDTH
     sums = [sums_ref[:, span] for span in sum_spans(groups)]
     window_part(seq + 4, (seq >> 1) - 2, seq & 1, q_ref, own_ref, other_ref, sums)
-    _, column = iotas(rows, WIDTH)
-    totals = jnp.zeros((rows, WIDTH), BF16)
-    for h in range(groups):
-        back_ref[:, h * WIDTH : (h + 1) * WIDTH] = sums[h][:, :WIDTH].astype(BF16)
-        total = sums[h][:, WIDTH:]
-        high = total.astype(BF16)
-        low = (total - high.astype(F32)).astype(BF16)
-        totals = jnp.where(column == 2 * h, high, jnp.where(column == 2 * h + 1, low, totals))
-    back_ref[:, groups * WIDTH :] = totals
+    row, column = iotas(rows, WIDTH)
+    line, _ = iotas(16, WIDTH)
+    for h in range(groups):
+        span = slice(h * WIDTH, (h + 1) * WIDTH)
+        back_ref[0:rows, span] = sums[h][:, :WIDTH].astype(BF16)
+        total = jnp.sum(jnp.where(row == column, sums[h][:, WIDTH:], 0.0), axis=0, keepdims=True)
+        high = total.astype(BF16).astype(F32)
+        totals = jnp.where(line == 0, high, jnp.where(line == 1, total - high, 0.0))
+        back_ref[rows : rows + 16, span] = totals.astype(BF16)
 
 
 def home_kernel(place, q_ref, *refs):
@@ -413,11 +432,13 @@
 
 def last_kernel(sums_ref, back_ref, out_ref):
     groups = out_ref.shape[1] // WIDTH
-    totals = back_ref[:, groups * WIDTH :].astype(F32)
-    for h in range(groups):
-        far = totals[:, 2 * h : 2 * h + 1] + totals[:, 2 * h + 1 : 2 * h + 2]
+    rows = out_ref.shape[0]
+    row, column = iotas(rows, WIDTH)
+    for h in range(groups):
         span = slice(h * WIDTH, (h + 1) * WIDTH)
-        mixed = sums_ref[:, 2 * h * WIDTH : (2 * h + 1) * WIDTH] + back_ref[:, span].astype(F32)
+        line = jnp.sum(back_ref[rows : rows + 16, span].astype(F32), axis=0, keepdims=True)
+        far = jnp.sum(jnp.where(row == column, line, 0.0), axis=1, keepdims=True)
+        mixed = sums_ref[:, 2 * h * WIDTH : (2 * h + 1) * WIDTH] + back_ref[0:rows, span].astype(F32)
         total = sums_ref[:, (2 * h + 1) * WIDTH : (2 * h + 2) * WIDTH] + far
         out_ref[:, span] = (mixed / total).astype(BF16)
 
@@ -523,9 +544,12 @@
     received = [crossed(terms[r], r, "head") for r in (2, 1, 3)]
     (hidden,) = call(hidden_kernel, [row_shape])(stream, terms[0], *received)
     other2, other1, other3 = [crossed(hidden, r, "head") for r in (2, 1, 3)]
-    unit_queries, pack = call(project_kernel, [row_shape, ((rows, 2 * wide), BF16)], 1)(
-        place, w_qkv, hidden, other2, other1, other3
-    )
+    (part,) = call(own_kernel, [((rows, w_qkv.shape[1]), F32)], 1)(place, hidden, w_qkv)
+    others = (other2, other1, other3)
+    pack, scale = call(pair_kernel, [((rows, 2 * wide), BF16), ((rows, WIDTH), F32)], 1)(
+        place, w_qkv, part, hidden, *others
+    )
+    (unit_queries,) = call(unit_kernel, [row_shape], 1)(place, w_qkv, part, scale, *others)
     first, visitors = lax.optimization_barrier(
         (moved(pack, "seq", 2), moved(unit_queries, "seq", -2))
     )
@@ -539,7 +563,7 @@
     away, kept = call(away_kernel, [sums_shape, row_shape], 1)(
         place, hidden, visitors, home[2], home[3]
     )
-    (back,) = call(back_kernel, [((rows, wide + WIDTH), BF16)], 1)(
+    (back,) = call(back_kernel, [((rows + 16, wide), BF16)], 1)(
         place, visitors, away, home[4], home[5]
     )
     returned = moved(back, "seq", 4)

time: 107 us -> 107 us (level)
  Pallas kernels: 20.7 us -> 22.3 us
  waiting for transfers between devices: 40.8 us -> 39.4 us
    pallas_call x14 -> x16, Pallas kernels: 20.7 us -> 22.3 us  [run(): pl.pallas_call(kernel, out_shape=[jax.ShapeDtypeStruct(shape, kind) for s...]
  transfers between devices with their start and end apart: 26 -> 26, of which waited for: 17 -> 17; matrix products, arithmetic and copies ran while one was open for 0% -> 0% of each run, Pallas kernels for 8% -> 10%
where the time goes in v7:
time: 107 us
  starting transfers between devices  42.7 us (40%)
  waiting for transfers between devices  39.4 us (37%)
  Pallas kernels  22.3 us (21%)
    ppermute x21, starting transfers between devices, crossed(): lax.ppermute(array, axis, [(i, i ^ mask) for i in range(lax.axis_size(axi...  26.4 us
    pallas_call x16, Pallas kernels, run(): pl.pallas_call(kernel, out_shape=[jax.ShapeDtypeStruct(shape, kind) for s...  22.3 us
    ppermute x21, waiting for transfers between devices, crossed(): lax.ppermute(array, axis, [(i, i ^ mask) for i in range(lax.axis_size(axi...  21.9 us
    ppermute x5, waiting for transfers between devices, moved(): lax.ppermute(array, axis, [(i, i + distance) for i in range(size) if 0 <=...  17.6 us
    ppermute x5, starting transfers between devices, moved(): lax.ppermute(array, axis, [(i, i + distance) for i in range(size) if 0 <=...  16.3 us
  transfers between devices with their start and end apart: 26, of which 17 were waited for; matrix products, arithmetic and copies ran while one was open for 0% of the time, Pallas kernels for 10%

profile of v7, /device:TPU:34, one launch (start us, length us, event | category | flops | bytes accessed | tf_op | source)
XLA Modules:
  0.0 107.1 jit_solution(13199858513559222164)
XLA Ops:
  1.6 4.9 %shard_map.95 = (bf16[128,512]{1,0:T(8,128)(2,1)S(1)}, bf16[4,128,128]{2,1,0:T(8,128)(2,1)S(1)}, bf16[4,128,128]{2,1,0:T(8,128)(2,1)S(1)}, f32[128,256]{1,0:T(8,...) custom-call(s32[5]{0:T(128)S(1)} %stack.23.place, ...), custom_call_target="tpu_custom_call" | custom-call | tf_op jit(solution)/shard_map/pallas_call | solution.py:449
  12.5 3.4 %collective-permute-start.3 = (bf16[144,256]{1,0:T(8,128)(2,1)S(1)}, bf16[144,256]{1,0:T(8,128)(2,1)S(1)}, u32[]{:S(2)}, u32[]{:S(2)}) collective-permute-start(bf16[144,256]{1,0:T(8,128)(2,1)S(1)} %get-tuple-element.59), channel_id=1, source_target_pairs={{0,16},{4,20},{8,24},{12,28},{16,0},{20,4},{24,8},{28,12},{32,48},... | collective-permute-start | bytes 221192 | tf_op jit(solution)/shard_map/ppermute | solution.py:469
  15.8 4.3 %collective-permute-start.4 = (bf16[144,256]{1,0:T(8,128)(2,1)S(1)}, bf16[144,256]{1,0:T(8,128)(2,1)S(1)}, u32[]{:S(2)}, u32[]{:S(2)}) collective-permute-start(bf16[144,256]{1,0:T(8,128)(2,1)S(1)} %get-tuple-element.59), channel_id=1, source_target_pairs={{0,48},{4,52},{8,56},{12,60},{16,32},{20,36},{24,40},{28,44},{32,1... | collective-permute-start | bytes 221192 | tf_op jit(solution)/shard_map/ppermute | solution.py:469
  21.0 2.8 %shard_map.98 = (bf16[2048,1536]{1,0:T(8,128)(2,1)S(1)}, f32[128,256]{1,0:T(8,128)S(1)}) custom-call(f32[128,256]{1,0:T(8,128)S(1)} %get-tuple-element.56.token_ref, bf16[2048,1536]{1,0:T(8,128)(2,1)} %source_ref), custom_call_target="tpu_custom_call" | custom-call | tf_op jit(solution)/shard_map/pallas_call | solution.py:449
  24.1 5.6 %collective-permute-done.5.recv2_ref = bf16[144,256]{1,0:T(8,128)(2,1)S(1)} collective-permute-done((bf16[144,256]{1,0:T(8,128)(2,1)S(1)}, bf16[144,256]{1,0:T(8,128)(2,1)S(1)}, u32[]{:S(2)}, u32[]{:S(2)}) %collective-permute-start.5) | collective-permute-done | bytes 73760 | tf_op jit(solution)/shard_map/ppermute | solution.py:469
  30.8 2.2 %collective-permute-start.6 = (bf16[144,256]{1,0:T(8,128)(2,1)S(1)}, bf16[144,256]{1,0:T(8,128)(2,1)S(1)}, u32[]{:S(2)}, u32[]{:S(2)}) collective-permute-start(bf16[144,256]{1,0:T(8,128)(2,1)S(1)} %get-tuple-element.68), channel_id=1, source_target_pairs={{0,128},{4,132},{8,136},{12,140},{16,144},{20,148},{24,152},{28,15... | collective-permute-start | bytes 221192 | tf_op jit(solution)/shard_map/ppermute | solution.py:469
  33.0 1.4 %collective-permute-start.7 = (bf16[144,256]{1,0:T(8,128)(2,1)S(1)}, bf16[144,256]{1,0:T(8,128)(2,1)S(1)}, u32[]{:S(2)}, u32[]{:S(2)}) collective-permute-start(bf16[144,256]{1,0:T(8,128)(2,1)S(1)} %get-tuple-element.68), channel_id=1, source_target_pairs={{0,64},{4,68},{8,72},{12,76},{16,80},{20,84},{24,88},{28,92},{32,9... | collective-permute-start | bytes 221192 | tf_op jit(solution)/shard_map/ppermute | solution.py:469
  40.1 2.0 %collective-permute-start.9 = (bf16[128,128]{1,0:T(8,128)(2,1)S(1)}, bf16[128,128]{1,0:T(8,128)(2,1)S(1)}, u32[]{:S(2)}, u32[]{:S(2)}) collective-permute-start(bf16[128,128]{1,0:T(8,128)(2,1)S(1)} %get-tuple-element.71), channel_id=1, source_target_pairs={{0,8},{4,12},{8,0},{12,4},{16,24},{20,28},{24,16},{28,20},{32,40},... | collective-permute-start | bytes 98312 | tf_op jit(solution)/shard_map/ppermute | solution.py:469
  45.3 3.5 %collective-permute-start.12 = (bf16[128,512]{1,0:T(8,128)(2,1)S(1)}, bf16[128,512]{1,0:T(8,128)(2,1)S(1)}, u32[]{:S(2)}, u32[]{:S(2)}) collective-permute-start(bf16[128,512]{1,0:T(8,128)(2,1)S(1)} %get-tuple-element.76), channel_id=1, source_target_pairs={{0,2},{1,3},{2,0},{3,1},{4,6},{5,7},{6,4},{7,5},{8,10},{9,11},{10,... | collective-permute-start | bytes 393224 | tf_op jit(solution)/shard_map/ppermute | solution.py:469
  49.8 3.3 %collective-permute-done.12.refs_0_ = bf16[128,512]{1,0:T(8,128)(2,1)S(1)} collective-permute-done((bf16[128,512]{1,0:T(8,128)(2,1)S(1)}, bf16[128,512]{1,0:T(8,128)(2,1)S(1)}, u32[]{:S(2)}, u32[]{:S(2)}) %collective-permute-start.12) | collective-permute-done | bytes 131104 | tf_op jit(solution)/shard_map/ppermute | solution.py:469
  53.1 1.9 %collective-permute-done.13.refs_1_ = bf16[128,512]{1,0:T(8,128)(2,1)S(1)} collective-permute-done((bf16[128,512]{1,0:T(8,128)(2,1)S(1)}, bf16[128,512]{1,0:T(8,128)(2,1)S(1)}, u32[]{:S(2)}, u32[]{:S(2)}) %collective-permute-start.13) | collective-permute-done | bytes 131104 | tf_op jit(solution)/shard_map/ppermute | solution.py:469
  55.7 2.4 %collective-permute-start.15 = (bf16[128,512]{1,0:T(8,128)(2,1)S(1)}, bf16[128,512]{1,0:T(8,128)(2,1)S(1)}, u32[]{:S(2)}, u32[]{:S(2)}) collective-permute-start(bf16[128,512]{1,0:T(8,128)(2,1)S(1)} %shard_map.103.hidden_ref), channel_id=1, source_target_pairs={{0,2},{1,3},{2,0},{3,1},{4,6},{5,7},{6,4},{7,5},{8,10},{9,11},{10,... | collective-permute-start | bytes 393224 | tf_op jit(solution)/shard_map/ppermute | solution.py:469
  60.8 2.1 %collective-permute-done.15.block2_ref = bf16[128,512]{1,0:T(8,128)(2,1)S(1)} collective-permute-done((bf16[128,512]{1,0:T(8,128)(2,1)S(1)}, bf16[128,512]{1,0:T(8,128)(2,1)S(1)}, u32[]{:S(2)}, u32[]{:S(2)}) %collective-permute-start.15) | collective-permute-done | bytes 131104 | tf_op jit(solution)/shard_map/ppermute | solution.py:469
  62.9 1.4 %collective-permute-done.16.block1_ref = bf16[128,512]{1,0:T(8,128)(2,1)S(1)} collective-permute-done((bf16[128,512]{1,0:T(8,128)(2,1)S(1)}, bf16[128,512]{1,0:T(8,128)(2,1)S(1)}, u32[]{:S(2)}, u32[]{:S(2)}) %collective-permute-start.16) | collective-permute-done | bytes 131104 | tf_op jit(solution)/shard_map/ppermute | solution.py:469
  66.5 2.9 %collective-permute-start.18 = (bf16[128,1024]{1,0:T(8,128)(2,1)S(1)}, bf16[128,1024]{1,0:T(8,128)(2,1)S(1)}, u32[]{:S(2)}, u32[]{:S(2)}) collective-permute-start(bf16[128,1024]{1,0:T(8,128)(2,1)S(1)} %get-tuple-element.80.refs_0_), channel_id=1, source_target_pairs={{0,8},{4,12},{8,16},{12,20},{16,24},{20,28},{24,32},{28,36},{32,40... | collective-permute-start | bytes 786440 | tf_op jit(solution)/shard_map/ppermute | solution.py:463
  70.7 2.9 %collective-permute-start.19 = (bf16[128,512]{1,0:T(8,128)(2,1)S(1)}, bf16[128,512]{1,0:T(8,128)(2,1)S(1)}, u32[]{:S(2)}, u32[]{:S(2)}) collective-permute-start(bf16[128,512]{1,0:T(8,128)(2,1)S(1)} %shard_map.106.q_ref), channel_id=1, source_target_pairs={{8,0},{12,4},{16,8},{20,12},{24,16},{28,20},{32,24},{36,28},{40,32... | collective-permute-start | bytes 393224 | tf_op jit(solution)/shard_map/ppermute | solution.py:463
  73.6 3.9 %collective-permute-done.19 = bf16[128,512]{1,0:T(8,128)(2,1)S(1)} collective-permute-done((bf16[128,512]{1,0:T(8,128)(2,1)S(1)}, bf16[128,512]{1,0:T(8,128)(2,1)S(1)}, u32[]{:S(2)}, u32[]{:S(2)}) %collective-permute-start.19) | collective-permute-done | bytes 131104 | tf_op jit(solution)/shard_map/ppermute | solution.py:463
  77.6 3.0 %collective-permute-start.20 = (bf16[128,1024]{1,0:T(8,128)(2,1)S(1)}, bf16[128,1024]{1,0:T(8,128)(2,1)S(1)}, u32[]{:S(2)}, u32[]{:S(2)}) collective-permute-start(bf16[128,1024]{1,0:T(8,128)(2,1)S(1)} %collective-permute-done.18.own_ref.refs_2_), channel_id=1, source_target_pairs={{0,8},{4,12},{8,16},{12,20},{16,24},{20,28},{24,32},{28,36},{32,40... | collective-permute-start | bytes 786440 | tf_op jit(solution)/shard_map/ppermute | solution.py:463
  80.6 2.8 %collective-permute-start.21 = (bf16[128,512]{1,0:T(8,128)(2,1)S(1)}, bf16[128,512]{1,0:T(8,128)(2,1)S(1)}, u32[]{:S(2)}, u32[]{:S(2)}) collective-permute-start(bf16[128,512]{1,0:T(8,128)(2,1)S(1)} %collective-permute-done.19), channel_id=1, source_target_pairs={{8,0},{12,4},{16,8},{20,12},{24,16},{28,20},{32,24},{36,28},{40,32... | collective-permute-start | bytes 393224 | tf_op jit(solution)/shard_map/ppermute | solution.py:463
  83.5 4.0 %collective-permute-done.21.q_ref = bf16[128,512]{1,0:T(8,128)(2,1)S(1)} collective-permute-done((bf16[128,512]{1,0:T(8,128)(2,1)S(1)}, bf16[128,512]{1,0:T(8,128)(2,1)S(1)}, u32[]{:S(2)}, u32[]{:S(2)}) %collective-permute-start.21) | collective-permute-done | bytes 131104 | tf_op jit(solution)/shard_map/ppermute | solution.py:463
  88.1 1.5 %shard_map.107 = (f32[128,1024]{1,0:T(8,128)S(1)}, bf16[128,512]{1,0:T(8,128)(2,1)}) custom-call(s32[5]{0:T(128)S(1)} %stack.23.place, bf16[128,512]{1,0:T(8,128)(2,1)S(1)} %shard_map.103.hidden_ref, bf16[128,512]{1,0:T(8,128)(2,1)S(1)} %collective-permute-done.21.q_ref, bf16[128,1024]{1,0:T(8,128)(2,1)S(1)} %collective-permute-done.18.own_ref.refs_2_, ...), custom_call_target="tpu_custom_call" | custom-call | tf_op jit(solution)/shard_map/pallas_call | solution.py:449
  90.5 4.6 %collective-permute-start.25 = (bf16[144,512]{1,0:T(8,128)(2,1)S(1)}, bf16[144,512]{1,0:T(8,128)(2,1)S(1)}, u32[]{:S(2)}, u32[]{:S(2)}) collective-permute-start(bf16[144,512]{1,0:T(8,128)(2,1)S(1)} %shard_map.109), channel_id=1, source_target_pairs={{0,16},{4,20},{8,24},{12,28},{16,32},{20,36},{24,40},{28,44},{32,4... | collective-permute-start | bytes 442376 | tf_op jit(solution)/shard_map/ppermute | solution.py:463
  95.1 1.6 %shard_map.108.sums_ref = f32[128,1024]{1,0:T(8,128)S(1)} custom-call(s32[5]{0:T(128)S(1)} %stack.23.place, bf16[128,512]{1,0:T(8,128)(2,1)S(1)} %shard_map.106.q_ref, bf16[128,1024]{1,0:T(8,128)(2,1)S(1)} %get-tuple-element.80.refs_0_, bf16[128,1024]{1,0:T(8,128)(2,1)S(1)} %collective-permute-done.23.refs_1_, ...), custom_call_target="tpu_custom_call" | custom-call | tf_op jit(solution)/shard_map/pallas_call | solution.py:449
  96.7 9.6 %collective-permute-done.25.back_ref = bf16[144,512]{1,0:T(8,128)(2,1)S(1)} collective-permute-done((bf16[144,512]{1,0:T(8,128)(2,1)S(1)}, bf16[144,512]{1,0:T(8,128)(2,1)S(1)}, u32[]{:S(2)}, u32[]{:S(2)}) %collective-permute-start.25) | collective-permute-done | bytes 147488 | tf_op jit(solution)/shard_map/ppermute | solution.py:463
  (52 shorter events, 28.3 us)
Async XLA Ops:
  6.5 4.9 %collective-permute-start = (bf16[144,256]{1,0:T(8,128)(2,1)S(1)}, bf16[144,256]{1,0:T(8,128)(2,1)S(1)}, u32[]{:S(2)}, u32[]{:S(2)}) collective-permute-start(bf16[144,256]{1,0:T(8,128)(2,1)S(1)} %get-tuple-element.52), channel_id=1, source_target_pairs={{0,8},{4,12},{8,0},{12,4},{16,24},{20,28},{24,16},{28,20},{32,40},... | collective-permute-start | bytes 221192 | tf_op jit(solution)/shard_map/ppermute | solution.py:469
  6.7 4.7 %collective-permute-start.1 = (bf16[144,256]{1,0:T(8,128)(2,1)S(1)}, bf16[144,256]{1,0:T(8,128)(2,1)S(1)}, u32[]{:S(2)}, u32[]{:S(2)}) collective-permute-start(bf16[144,256]{1,0:T(8,128)(2,1)S(1)} %get-tuple-element.53), channel_id=1, source_target_pairs={{0,12},{4,8},{8,4},{12,0},{16,28},{20,24},{24,20},{28,16},{32,44},... | collective-permute-start | bytes 221192 | tf_op jit(solution)/shard_map/ppermute | solution.py:469
  7.8 3.6 %collective-permute-start.2 = (bf16[144,256]{1,0:T(8,128)(2,1)S(1)}, bf16[144,256]{1,0:T(8,128)(2,1)S(1)}, u32[]{:S(2)}, u32[]{:S(2)}) collective-permute-start(bf16[144,256]{1,0:T(8,128)(2,1)S(1)} %get-tuple-element.54), channel_id=1, source_target_pairs={{0,4},{4,0},{8,12},{12,8},{16,20},{20,16},{24,28},{28,24},{32,36},... | collective-permute-start | bytes 221192 | tf_op jit(solution)/shard_map/ppermute | solution.py:469
  12.5 11.3 %collective-permute-start.3 = (bf16[144,256]{1,0:T(8,128)(2,1)S(1)}, bf16[144,256]{1,0:T(8,128)(2,1)S(1)}, u32[]{:S(2)}, u32[]{:S(2)}) collective-permute-start(bf16[144,256]{1,0:T(8,128)(2,1)S(1)} %get-tuple-element.59), channel_id=1, source_target_pairs={{0,16},{4,20},{8,24},{12,28},{16,0},{20,4},{24,8},{28,12},{32,48},... | collective-permute-start | bytes 221192 | tf_op jit(solution)/shard_map/ppermute | solution.py:469
  15.8 8.3 %collective-permute-start.4 = (bf16[144,256]{1,0:T(8,128)(2,1)S(1)}, bf16[144,256]{1,0:T(8,128)(2,1)S(1)}, u32[]{:S(2)}, u32[]{:S(2)}) collective-permute-start(bf16[144,256]{1,0:T(8,128)(2,1)S(1)} %get-tuple-element.59), channel_id=1, source_target_pairs={{0,48},{4,52},{8,56},{12,60},{16,32},{20,36},{24,40},{28,44},{32,1... | collective-permute-start | bytes 221192 | tf_op jit(solution)/shard_map/ppermute | solution.py:469
  20.1 9.7 %collective-permute-start.5 = (bf16[144,256]{1,0:T(8,128)(2,1)S(1)}, bf16[144,256]{1,0:T(8,128)(2,1)S(1)}, u32[]{:S(2)}, u32[]{:S(2)}) collective-permute-start(bf16[144,256]{1,0:T(8,128)(2,1)S(1)} %get-tuple-element.59), channel_id=1, source_target_pairs={{0,32},{4,36},{8,40},{12,44},{16,48},{20,52},{24,56},{28,60},{32,0... | collective-permute-start | bytes 221192 | tf_op jit(solution)/shard_map/ppermute | solution.py:469
  30.8 5.9 %collective-permute-start.6 = (bf16[144,256]{1,0:T(8,128)(2,1)S(1)}, bf16[144,256]{1,0:T(8,128)(2,1)S(1)}, u32[]{:S(2)}, u32[]{:S(2)}) collective-permute-start(bf16[144,256]{1,0:T(8,128)(2,1)S(1)} %get-tuple-element.68), channel_id=1, source_target_pairs={{0,128},{4,132},{8,136},{12,140},{16,144},{20,148},{24,152},{28,15... | collective-permute-start | bytes 221192 | tf_op jit(solution)/shard_map/ppermute | solution.py:469
  33.0 4.6 %collective-permute-start.7 = (bf16[144,256]{1,0:T(8,128)(2,1)S(1)}, bf16[144,256]{1,0:T(8,128)(2,1)S(1)}, u32[]{:S(2)}, u32[]{:S(2)}) collective-permute-start(bf16[144,256]{1,0:T(8,128)(2,1)S(1)} %get-tuple-element.68), channel_id=1, source_target_pairs={{0,64},{4,68},{8,72},{12,76},{16,80},{20,84},{24,88},{28,92},{32,9... | collective-permute-start | bytes 221192 | tf_op jit(solution)/shard_map/ppermute | solution.py:469
  34.5 4.4 %collective-permute-start.8 = (bf16[144,256]{1,0:T(8,128)(2,1)S(1)}, bf16[144,256]{1,0:T(8,128)(2,1)S(1)}, u32[]{:S(2)}, u32[]{:S(2)}) collective-permute-start(bf16[144,256]{1,0:T(8,128)(2,1)S(1)} %get-tuple-element.68), channel_id=1, source_target_pairs={{0,192},{4,196},{8,200},{12,204},{16,208},{20,212},{24,216},{28,22... | collective-permute-start | bytes 221192 | tf_op jit(solution)/shard_map/ppermute | solution.py:469
  39.9 3.4 %collective-permute-start.10 = (bf16[128,128]{1,0:T(8,128)(2,1)S(1)}, bf16[128,128]{1,0:T(8,128)(2,1)S(1)}, u32[]{:S(2)}, u32[]{:S(2)}) collective-permute-start(bf16[128,128]{1,0:T(8,128)(2,1)S(1)} %get-tuple-element.72), channel_id=1, source_target_pairs={{0,12},{4,8},{8,4},{12,0},{16,28},{20,24},{24,20},{28,16},{32,44},... | collective-permute-start | bytes 98312 | tf_op jit(solution)/shard_map/ppermute | solution.py:469
  40.1 4.0 %collective-permute-start.9 = (bf16[128,128]{1,0:T(8,128)(2,1)S(1)}, bf16[128,128]{1,0:T(8,128)(2,1)S(1)}, u32[]{:S(2)}, u32[]{:S(2)}) collective-permute-start(bf16[128,128]{1,0:T(8,128)(2,1)S(1)} %get-tuple-element.71), channel_id=1, source_target_pairs={{0,8},{4,12},{8,0},{12,4},{16,24},{20,28},{24,16},{28,20},{32,40},... | collective-permute-start | bytes 98312 | tf_op jit(solution)/shard_map/ppermute | solution.py:469
  45.3 7.8 %collective-permute-start.12 = (bf16[128,512]{1,0:T(8,128)(2,1)S(1)}, bf16[128,512]{1,0:T(8,128)(2,1)S(1)}, u32[]{:S(2)}, u32[]{:S(2)}) collective-permute-start(bf16[128,512]{1,0:T(8,128)(2,1)S(1)} %get-tuple-element.76), channel_id=1, source_target_pairs={{0,2},{1,3},{2,0},{3,1},{4,6},{5,7},{6,4},{7,5},{8,10},{9,11},{10,... | collective-permute-start | bytes 393224 | tf_op jit(solution)/shard_map/ppermute | solution.py:469
  48.7 6.2 %collective-permute-start.13 = (bf16[128,512]{1,0:T(8,128)(2,1)S(1)}, bf16[128,512]{1,0:T(8,128)(2,1)S(1)}, u32[]{:S(2)}, u32[]{:S(2)}) collective-permute-start(bf16[128,512]{1,0:T(8,128)(2,1)S(1)} %get-tuple-element.77), channel_id=1, source_target_pairs={{0,1},{1,0},{2,3},{3,2},{4,5},{5,4},{6,7},{7,6},{8,9},{9,8},{10,11... | collective-permute-start | bytes 393224 | tf_op jit(solution)/shard_map/ppermute | solution.py:469
  49.4 6.2 %collective-permute-start.14 = (bf16[128,512]{1,0:T(8,128)(2,1)S(1)}, bf16[128,512]{1,0:T(8,128)(2,1)S(1)}, u32[]{:S(2)}, u32[]{:S(2)}) collective-permute-start(bf16[128,512]{1,0:T(8,128)(2,1)S(1)} %get-tuple-element.78), channel_id=1, source_target_pairs={{0,3},{1,2},{2,1},{3,0},{4,7},{5,6},{6,5},{7,4},{8,11},{9,10},{10,... | collective-permute-start | bytes 393224 | tf_op jit(solution)/shard_map/ppermute | solution.py:469
  55.7 7.2 %collective-permute-start.15 = (bf16[128,512]{1,0:T(8,128)(2,1)S(1)}, bf16[128,512]{1,0:T(8,128)(2,1)S(1)}, u32[]{:S(2)}, u32[]{:S(2)}) collective-permute-start(bf16[128,512]{1,0:T(8,128)(2,1)S(1)} %shard_map.103.hidden_ref), channel_id=1, source_target_pairs={{0,2},{1,3},{2,0},{3,1},{4,6},{5,7},{6,4},{7,5},{8,10},{9,11},{10,... | collective-permute-start | bytes 393224 | tf_op jit(solution)/shard_map/ppermute | solution.py:469
  58.0 6.2 %collective-permute-start.16 = (bf16[128,512]{1,0:T(8,128)(2,1)S(1)}, bf16[128,512]{1,0:T(8,128)(2,1)S(1)}, u32[]{:S(2)}, u32[]{:S(2)}) collective-permute-start(bf16[128,512]{1,0:T(8,128)(2,1)S(1)} %shard_map.103.hidden_ref), channel_id=1, source_target_pairs={{0,1},{1,0},{2,3},{3,2},{4,5},{5,4},{6,7},{7,6},{8,9},{9,8},{10,11... | collective-permute-start | bytes 393224 | tf_op jit(solution)/shard_map/ppermute | solution.py:469
  58.7 6.6 %collective-permute-start.17 = (bf16[128,512]{1,0:T(8,128)(2,1)S(1)}, bf16[128,512]{1,0:T(8,128)(2,1)S(1)}, u32[]{:S(2)}, u32[]{:S(2)}) collective-permute-start(bf16[128,512]{1,0:T(8,128)(2,1)S(1)} %shard_map.103.hidden_ref), channel_id=1, source_target_pairs={{0,3},{1,2},{2,1},{3,0},{4,7},{5,6},{6,5},{7,4},{8,11},{9,10},{10,... | collective-permute-start | bytes 393224 | tf_op jit(solution)/shard_map/ppermute | solution.py:469
  66.5 11.0 %collective-permute-start.18 = (bf16[128,1024]{1,0:T(8,128)(2,1)S(1)}, bf16[128,1024]{1,0:T(8,128)(2,1)S(1)}, u32[]{:S(2)}, u32[]{:S(2)}) collective-permute-start(bf16[128,1024]{1,0:T(8,128)(2,1)S(1)} %get-tuple-element.80.refs_0_), channel_id=1, source_target_pairs={{0,8},{4,12},{8,16},{12,20},{16,24},{20,28},{24,32},{28,36},{32,40... | collective-permute-start | bytes 786440 | tf_op jit(solution)/shard_map/ppermute | solution.py:463
  70.7 6.9 %collective-permute-start.19 = (bf16[128,512]{1,0:T(8,128)(2,1)S(1)}, bf16[128,512]{1,0:T(8,128)(2,1)S(1)}, u32[]{:S(2)}, u32[]{:S(2)}) collective-permute-start(bf16[128,512]{1,0:T(8,128)(2,1)S(1)} %shard_map.106.q_ref), channel_id=1, source_target_pairs={{8,0},{12,4},{16,8},{20,12},{24,16},{28,20},{32,24},{36,28},{40,32... | collective-permute-start | bytes 393224 | tf_op jit(solution)/shard_map/ppermute | solution.py:463
  77.6 10.0 %collective-permute-start.20 = (bf16[128,1024]{1,0:T(8,128)(2,1)S(1)}, bf16[128,1024]{1,0:T(8,128)(2,1)S(1)}, u32[]{:S(2)}, u32[]{:S(2)}) collective-permute-start(bf16[128,1024]{1,0:T(8,128)(2,1)S(1)} %collective-permute-done.18.own_ref.refs_2_), channel_id=1, source_target_pairs={{0,8},{4,12},{8,16},{12,20},{16,24},{20,28},{24,32},{28,36},{32,40... | collective-permute-start | bytes 786440 | tf_op jit(solution)/shard_map/ppermute | solution.py:463
  80.6 7.0 %collective-permute-start.21 = (bf16[128,512]{1,0:T(8,128)(2,1)S(1)}, bf16[128,512]{1,0:T(8,128)(2,1)S(1)}, u32[]{:S(2)}, u32[]{:S(2)}) collective-permute-start(bf16[128,512]{1,0:T(8,128)(2,1)S(1)} %collective-permute-done.19), channel_id=1, source_target_pairs={{8,0},{12,4},{16,8},{20,12},{24,16},{28,20},{32,24},{36,28},{40,32... | collective-permute-start | bytes 393224 | tf_op jit(solution)/shard_map/ppermute | solution.py:463
  83.4 4.7 %collective-permute-start.22 = (bf16[128,1024]{1,0:T(8,128)(2,1)S(1)}, bf16[128,1024]{1,0:T(8,128)(2,1)S(1)}, u32[]{:S(2)}, u32[]{:S(2)}) collective-permute-start(bf16[128,1024]{1,0:T(8,128)(2,1)S(1)} %collective-permute-done.18.own_ref.refs_2_), channel_id=1, source_target_pairs={{0,4},{4,0},{8,12},{12,8},{16,20},{20,16},{24,28},{28,24},{32,36},... | collective-permute-start | bytes 786440 | tf_op jit(solution)/shard_map/ppermute | solution.py:469
  87.5 7.6 %collective-permute-start.23 = (bf16[128,1024]{1,0:T(8,128)(2,1)S(1)}, bf16[128,1024]{1,0:T(8,128)(2,1)S(1)}, u32[]{:S(2)}, u32[]{:S(2)}) collective-permute-start(bf16[128,1024]{1,0:T(8,128)(2,1)S(1)} %get-tuple-element.80.refs_0_), channel_id=1, source_target_pairs={{0,4},{4,0},{8,12},{12,8},{16,20},{20,16},{24,28},{28,24},{32,36},... | collective-permute-start | bytes 786440 | tf_op jit(solution)/shard_map/ppermute | solution.py:469
  90.5 15.8 %collective-permute-start.25 = (bf16[144,512]{1,0:T(8,128)(2,1)S(1)}, bf16[144,512]{1,0:T(8,128)(2,1)S(1)}, u32[]{:S(2)}, u32[]{:S(2)}) collective-permute-start(bf16[144,512]{1,0:T(8,128)(2,1)S(1)} %shard_map.109), channel_id=1, source_target_pairs={{0,16},{4,20},{8,24},{12,28},{16,32},{20,36},{24,40},{28,44},{32,4... | collective-permute-start | bytes 442376 | tf_op jit(solution)/shard_map/ppermute | solution.py:463
  (5 other events, 75.0 us)

commit v8 on v7

--- a/solution.py
+++ b/solution.py
@@ -253,7 +253,7 @@
         load.wait()
 
 
-def row_kernel(place, all_ref, recv1_ref, recv3_ref, recv2_ref, before_ref, pay_ref, pairs, starts):
+def row_kernel(place, all_ref, recv2_ref, recv1_ref, recv3_ref, before_ref, pay_ref, pairs, starts):
     group = place[3]
     pairs[group] = all_ref[...]
     for d, ref in ((1, recv1_ref), (2, recv2_ref), (3, recv3_ref)):
@@ -328,41 +328,28 @@
     part_ref[...] = dot(hidden_ref[...], w_ref[pl.ds(begin, width), :])
 
 
-def product_of(place, w_ref, blocks, first, size):
+def project_kernel(place, w_ref, part_ref, hidden_ref, block2_ref, block1_ref, block3_ref, q_ref, kv_ref):
     me = place[2]
-    width = blocks[0].shape[1]
-    total = None
+    blocks = [block2_ref, block1_ref, block3_ref]
+    rows, width = hidden_ref.shape
+    total = part_ref[...]
     for block, r in zip(blocks, (2, 1, 3)):
         begin = pl.multiple_of((me ^ r) * width, width)
-        part = dot(block[...], w_ref[pl.ds(begin, width), first : first + size])
-        total = part if total is None else total + part
-    return total
-
-
-def pair_kernel(place, w_ref, part_ref, hidden_ref, block2_ref, block1_ref, block3_ref, kv_ref, scale_ref):
-    blocks = [block2_ref, block1_ref, block3_ref]
+        total = total + dot(block[...], w_ref[pl.ds(begin, width), :])
     squares = 0.0
     for ref in [hidden_ref] + blocks:
         value = ref[...].astype(F32)
         squares = squares + jnp.sum(value * value, axis=-1, keepdims=True)
-    rows, width = hidden_ref.shape
-    scale = lax.rsqrt(squares / (4 * width) + 1e-05)
-    scale_ref[...] = jnp.broadcast_to(scale, scale_ref.shape)
+    total = total * lax.rsqrt(squares / (4 * width) + 1e-05)
     groups = width // WIDTH
     for h in range(groups):
-        begin = (3 * h + 1) * WIDTH
-        total = part_ref[:, begin : begin + 2 * WIDTH] + product_of(place, w_ref, blocks, begin, 2 * WIDTH)
-        total = total * scale
-        kv_ref[:, h * WIDTH : (h + 1) * WIDTH] = to_unit(total[:, :WIDTH]).astype(BF16)
-        kv_ref[:, (groups + h) * WIDTH : (groups + h + 1) * WIDTH] = total[:, WIDTH:].astype(BF16)
-
-
-def unit_kernel(place, w_ref, part_ref, scale_ref, block2_ref, block1_ref, block3_ref, q_ref):
-    blocks = [block2_ref, block1_ref, block3_ref]
-    for h in range(q_ref.shape[1] // WIDTH):
-        begin = 3 * h * WIDTH
-        total = part_ref[:, begin : begin + WIDTH] + product_of(place, w_ref, blocks, begin, WIDTH)
-        q_ref[:, h * WIDTH : (h + 1) * WIDTH] = to_unit(total * scale_ref[...]).astype(BF16)
+        base = h * 3 * WIDTH
+        span = slice(h * WIDTH, (h + 1) * WIDTH)
+        q_ref[:, span] = to_unit(total[:, base : base + WIDTH]).astype(BF16)
+        kv_ref[:, span] = to_unit(total[:, base + WIDTH : base + 2 * WIDTH]).astype(BF16)
+        kv_ref[:, (groups + h) * WIDTH : (groups + h + 1) * WIDTH] = total[
+            :, base + 2 * WIDTH : base + 3 * WIDTH
+        ].astype(BF16)
 
 
 def window_part(query_place, key_chip, core, q_ref, own_ref, other_ref, sums):
@@ -500,7 +487,7 @@
     before, everything, pay = call(
         group_kernel, [((3, WIDTH, 2 * WIDTH), F32), pair_shape, pay_shape], 1, [four_pairs]
     )(place, own, pay2, pay3, pay1)
-    row1, row3, row2 = [crossed(pay, 4 * d) for d in (1, 3, 2)]
+    row2, row1, row3 = [crossed(pay, 4 * d) for d in (2, 1, 3)]
     everything, w_qkv = lax.optimization_barrier((everything, w_qkv))
     w_qkv, everything = call(
         fetch_wide_kernel,
@@ -511,7 +498,7 @@
         FETCH_LIMIT,
     )(everything, w_qkv)
     before_row, pay = call(row_kernel, [pair_shape, pay_shape], 1, [four_pairs] * 2)(
-        place, everything, row1, row3, row2
+        place, everything, row2, row1, row3
     )
     row2, row1, row3 = [crossed(pay, 16 * d) for d in (2, 1, 3)]
     before_row, w_out, stream = lax.optimization_barrier((before_row, w_out, stream))
@@ -545,11 +532,9 @@
     (hidden,) = call(hidden_kernel, [row_shape])(stream, terms[0], *received)
     other2, other1, other3 = [crossed(hidden, r, "head") for r in (2, 1, 3)]
     (part,) = call(own_kernel, [((rows, w_qkv.shape[1]), F32)], 1)(place, hidden, w_qkv)
-    others = (other2, other1, other3)
-    pack, scale = call(pair_kernel, [((rows, 2 * wide), BF16), ((rows, WIDTH), F32)], 1)(
-        place, w_qkv, part, hidden, *others
-    )
-    (unit_queries,) = call(unit_kernel, [row_shape], 1)(place, w_qkv, part, scale, *others)
+    unit_queries, pack = call(project_kernel, [row_shape, ((rows, 2 * wide), BF16)], 1)(
+        place, w_qkv, part, hidden, other2, other1, other3
+    )
     first, visitors = lax.optimization_barrier(
         (moved(pack, "seq", 2), moved(unit_queries, "seq", -2))
     )

time: 107 us -> 105 us (0.981)
  waiting for transfers between devices: 39.4 us -> 37.8 us
  Pallas kernels: 22.3 us -> 21.2 us
    ppermute x21, waiting for transfers between devices: 21.9 us -> 20.7 us  [crossed(): lax.ppermute(array, axis, [(i, i ^ mask) for i in range(lax.axis_size(axi...]
    pallas_call x16 -> x15, Pallas kernels: 22.3 us -> 21.2 us  [run(): pl.pallas_call(kernel, out_shape=[jax.ShapeDtypeStruct(shape, kind) for s...]
  transfers between devices with their start and end apart: 26 -> 26, of which waited for: 17 -> 17; matrix products, arithmetic and copies ran while one was open for 0% -> 0% of each run, Pallas kernels for 10% -> 9%
where the time goes in v8:
time: 105 us
  starting transfers between devices  43.2 us (41%)
  waiting for transfers between devices  37.8 us (36%)
  Pallas kernels  21.2 us (20%)
    ppermute x21, starting transfers between devices, crossed(): lax.ppermute(array, axis, [(i, i ^ mask) for i in range(lax.axis_size(axi...  26.5 us
    pallas_call x15, Pallas kernels, run(): pl.pallas_call(kernel, out_shape=[jax.ShapeDtypeStruct(shape, kind) for s...  21.2 us
    ppermute x21, waiting for transfers between devices, crossed(): lax.ppermute(array, axis, [(i, i ^ mask) for i in range(lax.axis_size(axi...  20.7 us
    ppermute x5, waiting for transfers between devices, moved(): lax.ppermute(array, axis, [(i, i + distance) for i in range(size) if 0 <=...  17.1 us
    ppermute x5, starting transfers between devices, moved(): lax.ppermute(array, axis, [(i, i + distance) for i in range(size) if 0 <=...  16.8 us
  transfers between devices with their start and end apart: 26, of which 17 were waited for; matrix products, arithmetic and copies ran while one was open for 0% of the time, Pallas kernels for 9%

profile of v8, /device:TPU:34, one launch (start us, length us, event | category | flops | bytes accessed | tf_op | source)
XLA Modules:
  0.0 105.0 jit_solution(12723308430581269549)
XLA Ops:
  1.6 4.9 %shard_map.95 = (bf16[128,512]{1,0:T(8,128)(2,1)S(1)}, bf16[4,128,128]{2,1,0:T(8,128)(2,1)S(1)}, bf16[4,128,128]{2,1,0:T(8,128)(2,1)S(1)}, f32[128,256]{1,0:T(8,...) custom-call(s32[5]{0:T(128)S(1)} %stack.23.place, ...), custom_call_target="tpu_custom_call" | custom-call | tf_op jit(solution)/shard_map/pallas_call | solution.py:436
  12.5 7.1 %collective-permute-start.3 = (bf16[144,256]{1,0:T(8,128)(2,1)S(1)}, bf16[144,256]{1,0:T(8,128)(2,1)S(1)}, u32[]{:S(2)}, u32[]{:S(2)}) collective-permute-start(bf16[144,256]{1,0:T(8,128)(2,1)S(1)} %get-tuple-element.59), channel_id=1, source_target_pairs={{0,32},{4,36},{8,40},{12,44},{16,48},{20,52},{24,56},{28,60},{32,0... | collective-permute-start | bytes 221192 | tf_op jit(solution)/shard_map/ppermute | solution.py:456
  19.5 1.5 %collective-permute-start.4 = (bf16[144,256]{1,0:T(8,128)(2,1)S(1)}, bf16[144,256]{1,0:T(8,128)(2,1)S(1)}, u32[]{:S(2)}, u32[]{:S(2)}) collective-permute-start(bf16[144,256]{1,0:T(8,128)(2,1)S(1)} %get-tuple-element.59), channel_id=1, source_target_pairs={{0,16},{4,20},{8,24},{12,28},{16,0},{20,4},{24,8},{28,12},{32,48},... | collective-permute-start | bytes 221192 | tf_op jit(solution)/shard_map/ppermute | solution.py:456
  21.0 2.8 %shard_map.98 = (bf16[2048,1536]{1,0:T(8,128)(2,1)S(1)}, f32[128,256]{1,0:T(8,128)S(1)}) custom-call(f32[128,256]{1,0:T(8,128)S(1)} %get-tuple-element.56.token_ref, bf16[2048,1536]{1,0:T(8,128)(2,1)} %source_ref), custom_call_target="tpu_custom_call" | custom-call | tf_op jit(solution)/shard_map/pallas_call | solution.py:436
  23.8 2.5 %collective-permute-done.4.recv1_ref = bf16[144,256]{1,0:T(8,128)(2,1)S(1)} collective-permute-done((bf16[144,256]{1,0:T(8,128)(2,1)S(1)}, bf16[144,256]{1,0:T(8,128)(2,1)S(1)}, u32[]{:S(2)}, u32[]{:S(2)}) %collective-permute-start.4) | collective-permute-done | bytes 73760 | tf_op jit(solution)/shard_map/ppermute | solution.py:456
  26.3 2.3 %collective-permute-done.5.recv3_ref = bf16[144,256]{1,0:T(8,128)(2,1)S(1)} collective-permute-done((bf16[144,256]{1,0:T(8,128)(2,1)S(1)}, bf16[144,256]{1,0:T(8,128)(2,1)S(1)}, u32[]{:S(2)}, u32[]{:S(2)}) %collective-permute-start.5) | collective-permute-done | bytes 73760 | tf_op jit(solution)/shard_map/ppermute | solution.py:456
  29.7 2.2 %collective-permute-start.6 = (bf16[144,256]{1,0:T(8,128)(2,1)S(1)}, bf16[144,256]{1,0:T(8,128)(2,1)S(1)}, u32[]{:S(2)}, u32[]{:S(2)}) collective-permute-start(bf16[144,256]{1,0:T(8,128)(2,1)S(1)} %get-tuple-element.68), channel_id=1, source_target_pairs={{0,128},{4,132},{8,136},{12,140},{16,144},{20,148},{24,152},{28,15... | collective-permute-start | bytes 221192 | tf_op jit(solution)/shard_map/ppermute | solution.py:456
  38.9 2.0 %collective-permute-start.9 = (bf16[128,128]{1,0:T(8,128)(2,1)S(1)}, bf16[128,128]{1,0:T(8,128)(2,1)S(1)}, u32[]{:S(2)}, u32[]{:S(2)}) collective-permute-start(bf16[128,128]{1,0:T(8,128)(2,1)S(1)} %get-tuple-element.71), channel_id=1, source_target_pairs={{0,8},{4,12},{8,0},{12,4},{16,24},{20,28},{24,16},{28,20},{32,40},... | collective-permute-start | bytes 98312 | tf_op jit(solution)/shard_map/ppermute | solution.py:456
  44.1 3.5 %collective-permute-start.12 = (bf16[128,512]{1,0:T(8,128)(2,1)S(1)}, bf16[128,512]{1,0:T(8,128)(2,1)S(1)}, u32[]{:S(2)}, u32[]{:S(2)}) collective-permute-start(bf16[128,512]{1,0:T(8,128)(2,1)S(1)} %get-tuple-element.76), channel_id=1, source_target_pairs={{0,2},{1,3},{2,0},{3,1},{4,6},{5,7},{6,4},{7,5},{8,10},{9,11},{10,... | collective-permute-start | bytes 393224 | tf_op jit(solution)/shard_map/ppermute | solution.py:456
  48.6 3.3 %collective-permute-done.12.refs_0_ = bf16[128,512]{1,0:T(8,128)(2,1)S(1)} collective-permute-done((bf16[128,512]{1,0:T(8,128)(2,1)S(1)}, bf16[128,512]{1,0:T(8,128)(2,1)S(1)}, u32[]{:S(2)}, u32[]{:S(2)}) %collective-permute-start.12) | collective-permute-done | bytes 131104 | tf_op jit(solution)/shard_map/ppermute | solution.py:456
  52.0 1.9 %collective-permute-done.13.refs_1_ = bf16[128,512]{1,0:T(8,128)(2,1)S(1)} collective-permute-done((bf16[128,512]{1,0:T(8,128)(2,1)S(1)}, bf16[128,512]{1,0:T(8,128)(2,1)S(1)}, u32[]{:S(2)}, u32[]{:S(2)}) %collective-permute-start.13) | collective-permute-done | bytes 131104 | tf_op jit(solution)/shard_map/ppermute | solution.py:456
  54.5 2.4 %collective-permute-start.15 = (bf16[128,512]{1,0:T(8,128)(2,1)S(1)}, bf16[128,512]{1,0:T(8,128)(2,1)S(1)}, u32[]{:S(2)}, u32[]{:S(2)}) collective-permute-start(bf16[128,512]{1,0:T(8,128)(2,1)S(1)} %shard_map.103.hidden_ref), channel_id=1, source_target_pairs={{0,2},{1,3},{2,0},{3,1},{4,6},{5,7},{6,4},{7,5},{8,10},{9,11},{10,... | collective-permute-start | bytes 393224 | tf_op jit(solution)/shard_map/ppermute | solution.py:456
  59.6 2.1 %collective-permute-done.15.block2_ref = bf16[128,512]{1,0:T(8,128)(2,1)S(1)} collective-permute-done((bf16[128,512]{1,0:T(8,128)(2,1)S(1)}, bf16[128,512]{1,0:T(8,128)(2,1)S(1)}, u32[]{:S(2)}, u32[]{:S(2)}) %collective-permute-start.15) | collective-permute-done | bytes 131104 | tf_op jit(solution)/shard_map/ppermute | solution.py:456
  64.1 1.4 %shard_map.105 = (bf16[128,512]{1,0:T(8,128)(2,1)S(1)}, bf16[128,1024]{1,0:T(8,128)(2,1)S(1)}) custom-call(s32[5]{0:T(128)S(1)} %stack.23.place, bf16[2048,1536]{1,0:T(8,128)(2,1)S(1)} %get-tuple-element.79.w_ref, f32[128,1536]{1,0:T(8,128)S(1)} %shard_map.104.part_ref, bf16[128,512]{1,0:T(8,128)(2,1)S(1)} %shard_map.103.hidden_ref, ...), custom_call_target="tpu_custom_call" | custom-call | tf_op jit(solution)/shard_map/pallas_call | solution.py:436
  65.6 2.7 %collective-permute-start.18 = (bf16[128,1024]{1,0:T(8,128)(2,1)S(1)}, bf16[128,1024]{1,0:T(8,128)(2,1)S(1)}, u32[]{:S(2)}, u32[]{:S(2)}) collective-permute-start(bf16[128,1024]{1,0:T(8,128)(2,1)S(1)} %get-tuple-element.80.refs_0_), channel_id=1, source_target_pairs={{0,8},{4,12},{8,16},{12,20},{16,24},{20,28},{24,32},{28,36},{32,40... | collective-permute-start | bytes 786440 | tf_op jit(solution)/shard_map/ppermute | solution.py:450
  68.3 3.1 %collective-permute-start.19 = (bf16[128,512]{1,0:T(8,128)(2,1)S(1)}, bf16[128,512]{1,0:T(8,128)(2,1)S(1)}, u32[]{:S(2)}, u32[]{:S(2)}) collective-permute-start(bf16[128,512]{1,0:T(8,128)(2,1)S(1)} %get-tuple-element.81.q_ref), channel_id=1, source_target_pairs={{8,0},{12,4},{16,8},{20,12},{24,16},{28,20},{32,24},{36,28},{40,32... | collective-permute-start | bytes 393224 | tf_op jit(solution)/shard_map/ppermute | solution.py:450
  71.4 3.7 %collective-permute-done.19 = bf16[128,512]{1,0:T(8,128)(2,1)S(1)} collective-permute-done((bf16[128,512]{1,0:T(8,128)(2,1)S(1)}, bf16[128,512]{1,0:T(8,128)(2,1)S(1)}, u32[]{:S(2)}, u32[]{:S(2)}) %collective-permute-start.19) | collective-permute-done | bytes 131104 | tf_op jit(solution)/shard_map/ppermute | solution.py:450
  75.2 3.4 %collective-permute-start.20 = (bf16[128,1024]{1,0:T(8,128)(2,1)S(1)}, bf16[128,1024]{1,0:T(8,128)(2,1)S(1)}, u32[]{:S(2)}, u32[]{:S(2)}) collective-permute-start(bf16[128,1024]{1,0:T(8,128)(2,1)S(1)} %collective-permute-done.18.own_ref.refs_2_), channel_id=1, source_target_pairs={{0,8},{4,12},{8,16},{12,20},{16,24},{20,28},{24,32},{28,36},{32,40... | collective-permute-start | bytes 786440 | tf_op jit(solution)/shard_map/ppermute | solution.py:450
  78.6 2.9 %collective-permute-start.21 = (bf16[128,512]{1,0:T(8,128)(2,1)S(1)}, bf16[128,512]{1,0:T(8,128)(2,1)S(1)}, u32[]{:S(2)}, u32[]{:S(2)}) collective-permute-start(bf16[128,512]{1,0:T(8,128)(2,1)S(1)} %collective-permute-done.19), channel_id=1, source_target_pairs={{8,0},{12,4},{16,8},{20,12},{24,16},{28,20},{32,24},{36,28},{40,32... | collective-permute-start | bytes 393224 | tf_op jit(solution)/shard_map/ppermute | solution.py:450
  81.6 5.1 %collective-permute-done.21.q_ref = bf16[128,512]{1,0:T(8,128)(2,1)S(1)} collective-permute-done((bf16[128,512]{1,0:T(8,128)(2,1)S(1)}, bf16[128,512]{1,0:T(8,128)(2,1)S(1)}, u32[]{:S(2)}, u32[]{:S(2)}) %collective-permute-start.21) | collective-permute-done | bytes 131104 | tf_op jit(solution)/shard_map/ppermute | solution.py:450
  87.2 1.5 %shard_map.106 = (f32[128,1024]{1,0:T(8,128)S(1)}, bf16[128,512]{1,0:T(8,128)(2,1)}) custom-call(s32[5]{0:T(128)S(1)} %stack.23.place, bf16[128,512]{1,0:T(8,128)(2,1)S(1)} %shard_map.103.hidden_ref, bf16[128,512]{1,0:T(8,128)(2,1)S(1)} %collective-permute-done.21.q_ref, bf16[128,1024]{1,0:T(8,128)(2,1)S(1)} %collective-permute-done.18.own_ref.refs_2_, ...), custom_call_target="tpu_custom_call" | custom-call | tf_op jit(solution)/shard_map/pallas_call | solution.py:436
  89.7 4.6 %collective-permute-start.25 = (bf16[144,512]{1,0:T(8,128)(2,1)S(1)}, bf16[144,512]{1,0:T(8,128)(2,1)S(1)}, u32[]{:S(2)}, u32[]{:S(2)}) collective-permute-start(bf16[144,512]{1,0:T(8,128)(2,1)S(1)} %shard_map.108), channel_id=1, source_target_pairs={{0,16},{4,20},{8,24},{12,28},{16,32},{20,36},{24,40},{28,44},{32,4... | collective-permute-start | bytes 442376 | tf_op jit(solution)/shard_map/ppermute | solution.py:450
  94.3 1.6 %shard_map.107.sums_ref = f32[128,1024]{1,0:T(8,128)S(1)} custom-call(s32[5]{0:T(128)S(1)} %stack.23.place, bf16[128,512]{1,0:T(8,128)(2,1)S(1)} %get-tuple-element.81.q_ref, bf16[128,1024]{1,0:T(8,128)(2,1)S(1)} %get-tuple-element.80.refs_0_, bf16[128,1024]{1,0:T(8,128)(2,1)S(1)} %collective-permute-done.23.refs_1_, ...), custom_call_target="tpu_custom_call" | custom-call | tf_op jit(solution)/shard_map/pallas_call | solution.py:436
  95.9 8.3 %collective-permute-done.25.back_ref = bf16[144,512]{1,0:T(8,128)(2,1)S(1)} collective-permute-done((bf16[144,512]{1,0:T(8,128)(2,1)S(1)}, bf16[144,512]{1,0:T(8,128)(2,1)S(1)}, u32[]{:S(2)}, u32[]{:S(2)}) %collective-permute-start.25) | collective-permute-done | bytes 147488 | tf_op jit(solution)/shard_map/ppermute | solution.py:450
  (51 shorter events, 27.4 us)
Async XLA Ops:
  6.5 4.9 %collective-permute-start = (bf16[144,256]{1,0:T(8,128)(2,1)S(1)}, bf16[144,256]{1,0:T(8,128)(2,1)S(1)}, u32[]{:S(2)}, u32[]{:S(2)}) collective-permute-start(bf16[144,256]{1,0:T(8,128)(2,1)S(1)} %get-tuple-element.52), channel_id=1, source_target_pairs={{0,8},{4,12},{8,0},{12,4},{16,24},{20,28},{24,16},{28,20},{32,40},... | collective-permute-start | bytes 221192 | tf_op jit(solution)/shard_map/ppermute | solution.py:456
  6.7 4.7 %collective-permute-start.1 = (bf16[144,256]{1,0:T(8,128)(2,1)S(1)}, bf16[144,256]{1,0:T(8,128)(2,1)S(1)}, u32[]{:S(2)}, u32[]{:S(2)}) collective-permute-start(bf16[144,256]{1,0:T(8,128)(2,1)S(1)} %get-tuple-element.53), channel_id=1, source_target_pairs={{0,12},{4,8},{8,4},{12,0},{16,28},{20,24},{24,20},{28,16},{32,44},... | collective-permute-start | bytes 221192 | tf_op jit(solution)/shard_map/ppermute | solution.py:456
  7.8 3.6 %collective-permute-start.2 = (bf16[144,256]{1,0:T(8,128)(2,1)S(1)}, bf16[144,256]{1,0:T(8,128)(2,1)S(1)}, u32[]{:S(2)}, u32[]{:S(2)}) collective-permute-start(bf16[144,256]{1,0:T(8,128)(2,1)S(1)} %get-tuple-element.54), channel_id=1, source_target_pairs={{0,4},{4,0},{8,12},{12,8},{16,20},{20,16},{24,28},{28,24},{32,36},... | collective-permute-start | bytes 221192 | tf_op jit(solution)/shard_map/ppermute | solution.py:456
  12.5 11.3 %collective-permute-start.3 = (bf16[144,256]{1,0:T(8,128)(2,1)S(1)}, bf16[144,256]{1,0:T(8,128)(2,1)S(1)}, u32[]{:S(2)}, u32[]{:S(2)}) collective-permute-start(bf16[144,256]{1,0:T(8,128)(2,1)S(1)} %get-tuple-element.59), channel_id=1, source_target_pairs={{0,32},{4,36},{8,40},{12,44},{16,48},{20,52},{24,56},{28,60},{32,0... | collective-permute-start | bytes 221192 | tf_op jit(solution)/shard_map/ppermute | solution.py:456
  19.5 6.8 %collective-permute-start.4 = (bf16[144,256]{1,0:T(8,128)(2,1)S(1)}, bf16[144,256]{1,0:T(8,128)(2,1)S(1)}, u32[]{:S(2)}, u32[]{:S(2)}) collective-permute-start(bf16[144,256]{1,0:T(8,128)(2,1)S(1)} %get-tuple-element.59), channel_id=1, source_target_pairs={{0,16},{4,20},{8,24},{12,28},{16,0},{20,4},{24,8},{28,12},{32,48},... | collective-permute-start | bytes 221192 | tf_op jit(solution)/shard_map/ppermute | solution.py:456
  21.0 7.6 %collective-permute-start.5 = (bf16[144,256]{1,0:T(8,128)(2,1)S(1)}, bf16[144,256]{1,0:T(8,128)(2,1)S(1)}, u32[]{:S(2)}, u32[]{:S(2)}) collective-permute-start(bf16[144,256]{1,0:T(8,128)(2,1)S(1)} %get-tuple-element.59), channel_id=1, source_target_pairs={{0,48},{4,52},{8,56},{12,60},{16,32},{20,36},{24,40},{28,44},{32,1... | collective-permute-start | bytes 221192 | tf_op jit(solution)/shard_map/ppermute | solution.py:456
  29.7 5.9 %collective-permute-start.6 = (bf16[144,256]{1,0:T(8,128)(2,1)S(1)}, bf16[144,256]{1,0:T(8,128)(2,1)S(1)}, u32[]{:S(2)}, u32[]{:S(2)}) collective-permute-start(bf16[144,256]{1,0:T(8,128)(2,1)S(1)} %get-tuple-element.68), channel_id=1, source_target_pairs={{0,128},{4,132},{8,136},{12,140},{16,144},{20,148},{24,152},{28,15... | collective-permute-start | bytes 221192 | tf_op jit(solution)/shard_map/ppermute | solution.py:456
  31.9 4.6 %collective-permute-start.7 = (bf16[144,256]{1,0:T(8,128)(2,1)S(1)}, bf16[144,256]{1,0:T(8,128)(2,1)S(1)}, u32[]{:S(2)}, u32[]{:S(2)}) collective-permute-start(bf16[144,256]{1,0:T(8,128)(2,1)S(1)} %get-tuple-element.68), channel_id=1, source_target_pairs={{0,64},{4,68},{8,72},{12,76},{16,80},{20,84},{24,88},{28,92},{32,9... | collective-permute-start | bytes 221192 | tf_op jit(solution)/shard_map/ppermute | solution.py:456
  33.3 4.4 %collective-permute-start.8 = (bf16[144,256]{1,0:T(8,128)(2,1)S(1)}, bf16[144,256]{1,0:T(8,128)(2,1)S(1)}, u32[]{:S(2)}, u32[]{:S(2)}) collective-permute-start(bf16[144,256]{1,0:T(8,128)(2,1)S(1)} %get-tuple-element.68), channel_id=1, source_target_pairs={{0,192},{4,196},{8,200},{12,204},{16,208},{20,212},{24,216},{28,22... | collective-permute-start | bytes 221192 | tf_op jit(solution)/shard_map/ppermute | solution.py:456
  38.7 3.4 %collective-permute-start.10 = (bf16[128,128]{1,0:T(8,128)(2,1)S(1)}, bf16[128,128]{1,0:T(8,128)(2,1)S(1)}, u32[]{:S(2)}, u32[]{:S(2)}) collective-permute-start(bf16[128,128]{1,0:T(8,128)(2,1)S(1)} %get-tuple-element.72), channel_id=1, source_target_pairs={{0,12},{4,8},{8,4},{12,0},{16,28},{20,24},{24,20},{28,16},{32,44},... | collective-permute-start | bytes 98312 | tf_op jit(solution)/shard_map/ppermute | solution.py:456
  38.9 4.0 %collective-permute-start.9 = (bf16[128,128]{1,0:T(8,128)(2,1)S(1)}, bf16[128,128]{1,0:T(8,128)(2,1)S(1)}, u32[]{:S(2)}, u32[]{:S(2)}) collective-permute-start(bf16[128,128]{1,0:T(8,128)(2,1)S(1)} %get-tuple-element.71), channel_id=1, source_target_pairs={{0,8},{4,12},{8,0},{12,4},{16,24},{20,28},{24,16},{28,20},{32,40},... | collective-permute-start | bytes 98312 | tf_op jit(solution)/shard_map/ppermute | solution.py:456
  44.1 7.8 %collective-permute-start.12 = (bf16[128,512]{1,0:T(8,128)(2,1)S(1)}, bf16[128,512]{1,0:T(8,128)(2,1)S(1)}, u32[]{:S(2)}, u32[]{:S(2)}) collective-permute-start(bf16[128,512]{1,0:T(8,128)(2,1)S(1)} %get-tuple-element.76), channel_id=1, source_target_pairs={{0,2},{1,3},{2,0},{3,1},{4,6},{5,7},{6,4},{7,5},{8,10},{9,11},{10,... | collective-permute-start | bytes 393224 | tf_op jit(solution)/shard_map/ppermute | solution.py:456
  47.6 6.2 %collective-permute-start.13 = (bf16[128,512]{1,0:T(8,128)(2,1)S(1)}, bf16[128,512]{1,0:T(8,128)(2,1)S(1)}, u32[]{:S(2)}, u32[]{:S(2)}) collective-permute-start(bf16[128,512]{1,0:T(8,128)(2,1)S(1)} %get-tuple-element.77), channel_id=1, source_target_pairs={{0,1},{1,0},{2,3},{3,2},{4,5},{5,4},{6,7},{7,6},{8,9},{9,8},{10,11... | collective-permute-start | bytes 393224 | tf_op jit(solution)/shard_map/ppermute | solution.py:456
  48.3 6.2 %collective-permute-start.14 = (bf16[128,512]{1,0:T(8,128)(2,1)S(1)}, bf16[128,512]{1,0:T(8,128)(2,1)S(1)}, u32[]{:S(2)}, u32[]{:S(2)}) collective-permute-start(bf16[128,512]{1,0:T(8,128)(2,1)S(1)} %get-tuple-element.78), channel_id=1, source_target_pairs={{0,3},{1,2},{2,1},{3,0},{4,7},{5,6},{6,5},{7,4},{8,11},{9,10},{10,... | collective-permute-start | bytes 393224 | tf_op jit(solution)/shard_map/ppermute | solution.py:456
  54.5 7.2 %collective-permute-start.15 = (bf16[128,512]{1,0:T(8,128)(2,1)S(1)}, bf16[128,512]{1,0:T(8,128)(2,1)S(1)}, u32[]{:S(2)}, u32[]{:S(2)}) collective-permute-start(bf16[128,512]{1,0:T(8,128)(2,1)S(1)} %shard_map.103.hidden_ref), channel_id=1, source_target_pairs={{0,2},{1,3},{2,0},{3,1},{4,6},{5,7},{6,4},{7,5},{8,10},{9,11},{10,... | collective-permute-start | bytes 393224 | tf_op jit(solution)/shard_map/ppermute | solution.py:456
  56.9 6.2 %collective-permute-start.16 = (bf16[128,512]{1,0:T(8,128)(2,1)S(1)}, bf16[128,512]{1,0:T(8,128)(2,1)S(1)}, u32[]{:S(2)}, u32[]{:S(2)}) collective-permute-start(bf16[128,512]{1,0:T(8,128)(2,1)S(1)} %shard_map.103.hidden_ref), channel_id=1, source_target_pairs={{0,1},{1,0},{2,3},{3,2},{4,5},{5,4},{6,7},{7,6},{8,9},{9,8},{10,11... | collective-permute-start | bytes 393224 | tf_op jit(solution)/shard_map/ppermute | solution.py:456
  57.6 6.6 %collective-permute-start.17 = (bf16[128,512]{1,0:T(8,128)(2,1)S(1)}, bf16[128,512]{1,0:T(8,128)(2,1)S(1)}, u32[]{:S(2)}, u32[]{:S(2)}) collective-permute-start(bf16[128,512]{1,0:T(8,128)(2,1)S(1)} %shard_map.103.hidden_ref), channel_id=1, source_target_pairs={{0,3},{1,2},{2,1},{3,0},{4,7},{5,6},{6,5},{7,4},{8,11},{9,10},{10,... | collective-permute-start | bytes 393224 | tf_op jit(solution)/shard_map/ppermute | solution.py:456
  65.6 9.6 %collective-permute-start.18 = (bf16[128,1024]{1,0:T(8,128)(2,1)S(1)}, bf16[128,1024]{1,0:T(8,128)(2,1)S(1)}, u32[]{:S(2)}, u32[]{:S(2)}) collective-permute-start(bf16[128,1024]{1,0:T(8,128)(2,1)S(1)} %get-tuple-element.80.refs_0_), channel_id=1, source_target_pairs={{0,8},{4,12},{8,16},{12,20},{16,24},{20,28},{24,32},{28,36},{32,40... | collective-permute-start | bytes 786440 | tf_op jit(solution)/shard_map/ppermute | solution.py:450
  68.3 6.9 %collective-permute-start.19 = (bf16[128,512]{1,0:T(8,128)(2,1)S(1)}, bf16[128,512]{1,0:T(8,128)(2,1)S(1)}, u32[]{:S(2)}, u32[]{:S(2)}) collective-permute-start(bf16[128,512]{1,0:T(8,128)(2,1)S(1)} %get-tuple-element.81.q_ref), channel_id=1, source_target_pairs={{8,0},{12,4},{16,8},{20,12},{24,16},{28,20},{32,24},{36,28},{40,32... | collective-permute-start | bytes 393224 | tf_op jit(solution)/shard_map/ppermute | solution.py:450
  75.2 11.5 %collective-permute-start.20 = (bf16[128,1024]{1,0:T(8,128)(2,1)S(1)}, bf16[128,1024]{1,0:T(8,128)(2,1)S(1)}, u32[]{:S(2)}, u32[]{:S(2)}) collective-permute-start(bf16[128,1024]{1,0:T(8,128)(2,1)S(1)} %collective-permute-done.18.own_ref.refs_2_), channel_id=1, source_target_pairs={{0,8},{4,12},{8,16},{12,20},{16,24},{20,28},{24,32},{28,36},{32,40... | collective-permute-start | bytes 786440 | tf_op jit(solution)/shard_map/ppermute | solution.py:450
  78.6 8.1 %collective-permute-start.21 = (bf16[128,512]{1,0:T(8,128)(2,1)S(1)}, bf16[128,512]{1,0:T(8,128)(2,1)S(1)}, u32[]{:S(2)}, u32[]{:S(2)}) collective-permute-start(bf16[128,512]{1,0:T(8,128)(2,1)S(1)} %collective-permute-done.19), channel_id=1, source_target_pairs={{8,0},{12,4},{16,8},{20,12},{24,16},{28,20},{32,24},{36,28},{40,32... | collective-permute-start | bytes 393224 | tf_op jit(solution)/shard_map/ppermute | solution.py:450
  81.5 5.7 %collective-permute-start.22 = (bf16[128,1024]{1,0:T(8,128)(2,1)S(1)}, bf16[128,1024]{1,0:T(8,128)(2,1)S(1)}, u32[]{:S(2)}, u32[]{:S(2)}) collective-permute-start(bf16[128,1024]{1,0:T(8,128)(2,1)S(1)} %collective-permute-done.18.own_ref.refs_2_), channel_id=1, source_target_pairs={{0,4},{4,0},{8,12},{12,8},{16,20},{20,16},{24,28},{28,24},{32,36},... | collective-permute-start | bytes 786440 | tf_op jit(solution)/shard_map/ppermute | solution.py:456
  86.7 7.6 %collective-permute-start.23 = (bf16[128,1024]{1,0:T(8,128)(2,1)S(1)}, bf16[128,1024]{1,0:T(8,128)(2,1)S(1)}, u32[]{:S(2)}, u32[]{:S(2)}) collective-permute-start(bf16[128,1024]{1,0:T(8,128)(2,1)S(1)} %get-tuple-element.80.refs_0_), channel_id=1, source_target_pairs={{0,4},{4,0},{8,12},{12,8},{16,20},{20,16},{24,28},{28,24},{32,36},... | collective-permute-start | bytes 786440 | tf_op jit(solution)/shard_map/ppermute | solution.py:456
  89.7 14.5 %collective-permute-start.25 = (bf16[144,512]{1,0:T(8,128)(2,1)S(1)}, bf16[144,512]{1,0:T(8,128)(2,1)S(1)}, u32[]{:S(2)}, u32[]{:S(2)}) collective-permute-start(bf16[144,512]{1,0:T(8,128)(2,1)S(1)} %shard_map.108), channel_id=1, source_target_pairs={{0,16},{4,20},{8,24},{12,28},{16,32},{20,36},{24,40},{28,44},{32,4... | collective-permute-start | bytes 442376 | tf_op jit(solution)/shard_map/ppermute | solution.py:450
  (5 other events, 72.7 us)

commit v9 on v8

--- a/solution.py
+++ b/solution.py
@@ -253,7 +253,7 @@
         load.wait()
 
 
-def row_kernel(place, all_ref, recv2_ref, recv1_ref, recv3_ref, before_ref, pay_ref, pairs, starts):
+def row_kernel(place, all_ref, recv2_ref, recv3_ref, recv1_ref, before_ref, pay_ref, pairs, starts):
     group = place[3]
     pairs[group] = all_ref[...]
     for d, ref in ((1, recv1_ref), (2, recv2_ref), (3, recv3_ref)):
@@ -487,7 +487,7 @@
     before, everything, pay = call(
         group_kernel, [((3, WIDTH, 2 * WIDTH), F32), pair_shape, pay_shape], 1, [four_pairs]
     )(place, own, pay2, pay3, pay1)
-    row2, row1, row3 = [crossed(pay, 4 * d) for d in (2, 1, 3)]
+    row2, row3, row1 = [crossed(pay, 4 * d) for d in (2, 3, 1)]
     everything, w_qkv = lax.optimization_barrier((everything, w_qkv))
     w_qkv, everything = call(
         fetch_wide_kernel,
@@ -498,7 +498,7 @@
         FETCH_LIMIT,
     )(everything, w_qkv)
     before_row, pay = call(row_kernel, [pair_shape, pay_shape], 1, [four_pairs] * 2)(
-        place, everything, row2, row1, row3
+        place, everything, row2, row3, row1
     )
     row2, row1, row3 = [crossed(pay, 16 * d) for d in (2, 1, 3)]
     before_row, w_out, stream = lax.optimization_barrier((before_row, w_out, stream))

time: 105 us -> 104 us (level)
  transfers between devices with their start and end apart: 26 -> 26, of which waited for: 17 -> 16; matrix products, arithmetic and copies ran while one was open for 0% -> 0% of each run, Pallas kernels for 9% -> 9%
where the time goes in v9:
time: 104 us
  starting transfers between devices  42.8 us (41%)
  waiting for transfers between devices  37.2 us (36%)
  Pallas kernels  21.2 us (20%)
    ppermute x21, starting transfers between devices, crossed(): lax.ppermute(array, axis, [(i, i ^ mask) for i in range(lax.axis_size(axi...  26.5 us
    pallas_call x15, Pallas kernels, run(): pl.pallas_call(kernel, out_shape=[jax.ShapeDtypeStruct(shape, kind) for s...  21.2 us
    ppermute x21, waiting for transfers between devices, crossed(): lax.ppermute(array, axis, [(i, i ^ mask) for i in range(lax.axis_size(axi...  19.7 us
    ppermute x5, waiting for transfers between devices, moved(): lax.ppermute(array, axis, [(i, i + distance) for i in range(size) if 0 <=...  17.5 us
    ppermute x5, starting transfers between devices, moved(): lax.ppermute(array, axis, [(i, i + distance) for i in range(size) if 0 <=...  16.3 us
  transfers between devices with their start and end apart: 26, of which 16 were waited for; matrix products, arithmetic and copies ran while one was open for 0% of the time, Pallas kernels for 9%

profile of v9, /device:TPU:34, one launch (start us, length us, event | category | flops | bytes accessed | tf_op | source)
XLA Modules:
  0.0 103.9 jit_solution(8916136985647778189)
XLA Ops:
  1.6 4.9 %shard_map.95 = (bf16[128,512]{1,0:T(8,128)(2,1)S(1)}, bf16[4,128,128]{2,1,0:T(8,128)(2,1)S(1)}, bf16[4,128,128]{2,1,0:T(8,128)(2,1)S(1)}, f32[128,256]{1,0:T(8,...) custom-call(s32[5]{0:T(128)S(1)} %stack.23.place, ...), custom_call_target="tpu_custom_call" | custom-call | tf_op jit(solution)/shard_map/pallas_call | solution.py:436
  12.5 7.1 %collective-permute-start.3 = (bf16[144,256]{1,0:T(8,128)(2,1)S(1)}, bf16[144,256]{1,0:T(8,128)(2,1)S(1)}, u32[]{:S(2)}, u32[]{:S(2)}) collective-permute-start(bf16[144,256]{1,0:T(8,128)(2,1)S(1)} %get-tuple-element.59), channel_id=1, source_target_pairs={{0,32},{4,36},{8,40},{12,44},{16,48},{20,52},{24,56},{28,60},{32,0... | collective-permute-start | bytes 221192 | tf_op jit(solution)/shard_map/ppermute | solution.py:456
  19.5 1.5 %collective-permute-start.5 = (bf16[144,256]{1,0:T(8,128)(2,1)S(1)}, bf16[144,256]{1,0:T(8,128)(2,1)S(1)}, u32[]{:S(2)}, u32[]{:S(2)}) collective-permute-start(bf16[144,256]{1,0:T(8,128)(2,1)S(1)} %get-tuple-element.59), channel_id=1, source_target_pairs={{0,16},{4,20},{8,24},{12,28},{16,0},{20,4},{24,8},{28,12},{32,48},... | collective-permute-start | bytes 221192 | tf_op jit(solution)/shard_map/ppermute | solution.py:456
  21.0 2.8 %shard_map.98 = (bf16[2048,1536]{1,0:T(8,128)(2,1)S(1)}, f32[128,256]{1,0:T(8,128)S(1)}) custom-call(f32[128,256]{1,0:T(8,128)S(1)} %get-tuple-element.56.token_ref, bf16[2048,1536]{1,0:T(8,128)(2,1)} %source_ref), custom_call_target="tpu_custom_call" | custom-call | tf_op jit(solution)/shard_map/pallas_call | solution.py:436
  23.8 3.6 %collective-permute-done.4.recv3_ref = bf16[144,256]{1,0:T(8,128)(2,1)S(1)} collective-permute-done((bf16[144,256]{1,0:T(8,128)(2,1)S(1)}, bf16[144,256]{1,0:T(8,128)(2,1)S(1)}, u32[]{:S(2)}, u32[]{:S(2)}) %collective-permute-start.4) | collective-permute-done | bytes 73760 | tf_op jit(solution)/shard_map/ppermute | solution.py:456
  28.4 2.2 %collective-permute-start.6 = (bf16[144,256]{1,0:T(8,128)(2,1)S(1)}, bf16[144,256]{1,0:T(8,128)(2,1)S(1)}, u32[]{:S(2)}, u32[]{:S(2)}) collective-permute-start(bf16[144,256]{1,0:T(8,128)(2,1)S(1)} %get-tuple-element.68), channel_id=1, source_target_pairs={{0,128},{4,132},{8,136},{12,140},{16,144},{20,148},{24,152},{28,15... | collective-permute-start | bytes 221192 | tf_op jit(solution)/shard_map/ppermute | solution.py:456
  30.7 1.4 %collective-permute-start.7 = (bf16[144,256]{1,0:T(8,128)(2,1)S(1)}, bf16[144,256]{1,0:T(8,128)(2,1)S(1)}, u32[]{:S(2)}, u32[]{:S(2)}) collective-permute-start(bf16[144,256]{1,0:T(8,128)(2,1)S(1)} %get-tuple-element.68), channel_id=1, source_target_pairs={{0,64},{4,68},{8,72},{12,76},{16,80},{20,84},{24,88},{28,92},{32,9... | collective-permute-start | bytes 221192 | tf_op jit(solution)/shard_map/ppermute | solution.py:456
  41.0 1.8 %collective-permute-done.9.recv2_ref = bf16[128,128]{1,0:T(8,128)(2,1)S(1)} collective-permute-done((bf16[128,128]{1,0:T(8,128)(2,1)S(1)}, bf16[128,128]{1,0:T(8,128)(2,1)S(1)}, u32[]{:S(2)}, u32[]{:S(2)}) %collective-permute-start.9) | collective-permute-done | bytes 32800 | tf_op jit(solution)/shard_map/ppermute | solution.py:456
  44.0 3.5 %collective-permute-start.12 = (bf16[128,512]{1,0:T(8,128)(2,1)S(1)}, bf16[128,512]{1,0:T(8,128)(2,1)S(1)}, u32[]{:S(2)}, u32[]{:S(2)}) collective-permute-start(bf16[128,512]{1,0:T(8,128)(2,1)S(1)} %get-tuple-element.76), channel_id=1, source_target_pairs={{0,2},{1,3},{2,0},{3,1},{4,6},{5,7},{6,4},{7,5},{8,10},{9,11},{10,... | collective-permute-start | bytes 393224 | tf_op jit(solution)/shard_map/ppermute | solution.py:456
  48.5 3.5 %collective-permute-done.12.refs_0_ = bf16[128,512]{1,0:T(8,128)(2,1)S(1)} collective-permute-done((bf16[128,512]{1,0:T(8,128)(2,1)S(1)}, bf16[128,512]{1,0:T(8,128)(2,1)S(1)}, u32[]{:S(2)}, u32[]{:S(2)}) %collective-permute-start.12) | collective-permute-done | bytes 131104 | tf_op jit(solution)/shard_map/ppermute | solution.py:456
  54.4 1.8 %collective-permute-start.15 = (bf16[128,512]{1,0:T(8,128)(2,1)S(1)}, bf16[128,512]{1,0:T(8,128)(2,1)S(1)}, u32[]{:S(2)}, u32[]{:S(2)}) collective-permute-start(bf16[128,512]{1,0:T(8,128)(2,1)S(1)} %shard_map.103.hidden_ref), channel_id=1, source_target_pairs={{0,2},{1,3},{2,0},{3,1},{4,6},{5,7},{6,4},{7,5},{8,10},{9,11},{10,... | collective-permute-start | bytes 393224 | tf_op jit(solution)/shard_map/ppermute | solution.py:456
  56.8 1.7 %collective-permute-start.17 = (bf16[128,512]{1,0:T(8,128)(2,1)S(1)}, bf16[128,512]{1,0:T(8,128)(2,1)S(1)}, u32[]{:S(2)}, u32[]{:S(2)}) collective-permute-start(bf16[128,512]{1,0:T(8,128)(2,1)S(1)} %shard_map.103.hidden_ref), channel_id=1, source_target_pairs={{0,3},{1,2},{2,1},{3,0},{4,7},{5,6},{6,5},{7,4},{8,11},{9,10},{10,... | collective-permute-start | bytes 393224 | tf_op jit(solution)/shard_map/ppermute | solution.py:456
  59.5 1.6 %collective-permute-done.15.block2_ref = bf16[128,512]{1,0:T(8,128)(2,1)S(1)} collective-permute-done((bf16[128,512]{1,0:T(8,128)(2,1)S(1)}, bf16[128,512]{1,0:T(8,128)(2,1)S(1)}, u32[]{:S(2)}, u32[]{:S(2)}) %collective-permute-start.15) | collective-permute-done | bytes 131104 | tf_op jit(solution)/shard_map/ppermute | solution.py:456
  63.1 1.4 %shard_map.105 = (bf16[128,512]{1,0:T(8,128)(2,1)S(1)}, bf16[128,1024]{1,0:T(8,128)(2,1)S(1)}) custom-call(s32[5]{0:T(128)S(1)} %stack.23.place, bf16[2048,1536]{1,0:T(8,128)(2,1)S(1)} %get-tuple-element.79.w_ref, f32[128,1536]{1,0:T(8,128)S(1)} %shard_map.104.part_ref, bf16[128,512]{1,0:T(8,128)(2,1)S(1)} %shard_map.103.hidden_ref, ...), custom_call_target="tpu_custom_call" | custom-call | tf_op jit(solution)/shard_map/pallas_call | solution.py:436
  64.6 3.6 %collective-permute-start.18 = (bf16[128,1024]{1,0:T(8,128)(2,1)S(1)}, bf16[128,1024]{1,0:T(8,128)(2,1)S(1)}, u32[]{:S(2)}, u32[]{:S(2)}) collective-permute-start(bf16[128,1024]{1,0:T(8,128)(2,1)S(1)} %get-tuple-element.80.refs_0_), channel_id=1, source_target_pairs={{0,8},{4,12},{8,16},{12,20},{16,24},{20,28},{24,32},{28,36},{32,40... | collective-permute-start | bytes 786440 | tf_op jit(solution)/shard_map/ppermute | solution.py:450
  68.2 2.2 %collective-permute-start.19 = (bf16[128,512]{1,0:T(8,128)(2,1)S(1)}, bf16[128,512]{1,0:T(8,128)(2,1)S(1)}, u32[]{:S(2)}, u32[]{:S(2)}) collective-permute-start(bf16[128,512]{1,0:T(8,128)(2,1)S(1)} %get-tuple-element.81.q_ref), channel_id=1, source_target_pairs={{8,0},{12,4},{16,8},{20,12},{24,16},{28,20},{32,24},{36,28},{40,32... | collective-permute-start | bytes 393224 | tf_op jit(solution)/shard_map/ppermute | solution.py:450
  70.4 4.6 %collective-permute-done.19 = bf16[128,512]{1,0:T(8,128)(2,1)S(1)} collective-permute-done((bf16[128,512]{1,0:T(8,128)(2,1)S(1)}, bf16[128,512]{1,0:T(8,128)(2,1)S(1)}, u32[]{:S(2)}, u32[]{:S(2)}) %collective-permute-start.19) | collective-permute-done | bytes 131104 | tf_op jit(solution)/shard_map/ppermute | solution.py:450
  75.1 3.0 %collective-permute-start.20 = (bf16[128,1024]{1,0:T(8,128)(2,1)S(1)}, bf16[128,1024]{1,0:T(8,128)(2,1)S(1)}, u32[]{:S(2)}, u32[]{:S(2)}) collective-permute-start(bf16[128,1024]{1,0:T(8,128)(2,1)S(1)} %collective-permute-done.18.own_ref.refs_2_), channel_id=1, source_target_pairs={{0,8},{4,12},{8,16},{12,20},{16,24},{20,28},{24,32},{28,36},{32,40... | collective-permute-start | bytes 786440 | tf_op jit(solution)/shard_map/ppermute | solution.py:450
  78.1 2.8 %collective-permute-start.21 = (bf16[128,512]{1,0:T(8,128)(2,1)S(1)}, bf16[128,512]{1,0:T(8,128)(2,1)S(1)}, u32[]{:S(2)}, u32[]{:S(2)}) collective-permute-start(bf16[128,512]{1,0:T(8,128)(2,1)S(1)} %collective-permute-done.19), channel_id=1, source_target_pairs={{8,0},{12,4},{16,8},{20,12},{24,16},{28,20},{32,24},{36,28},{40,32... | collective-permute-start | bytes 393224 | tf_op jit(solution)/shard_map/ppermute | solution.py:450
  81.0 5.2 %collective-permute-done.21.q_ref = bf16[128,512]{1,0:T(8,128)(2,1)S(1)} collective-permute-done((bf16[128,512]{1,0:T(8,128)(2,1)S(1)}, bf16[128,512]{1,0:T(8,128)(2,1)S(1)}, u32[]{:S(2)}, u32[]{:S(2)}) %collective-permute-start.21) | collective-permute-done | bytes 131104 | tf_op jit(solution)/shard_map/ppermute | solution.py:450
  86.7 1.5 %shard_map.106 = (f32[128,1024]{1,0:T(8,128)S(1)}, bf16[128,512]{1,0:T(8,128)(2,1)}) custom-call(s32[5]{0:T(128)S(1)} %stack.23.place, bf16[128,512]{1,0:T(8,128)(2,1)S(1)} %shard_map.103.hidden_ref, bf16[128,512]{1,0:T(8,128)(2,1)S(1)} %collective-permute-done.21.q_ref, bf16[128,1024]{1,0:T(8,128)(2,1)S(1)} %collective-permute-done.18.own_ref.refs_2_, ...), custom_call_target="tpu_custom_call" | custom-call | tf_op jit(solution)/shard_map/pallas_call | solution.py:436
  89.2 4.6 %collective-permute-start.25 = (bf16[144,512]{1,0:T(8,128)(2,1)S(1)}, bf16[144,512]{1,0:T(8,128)(2,1)S(1)}, u32[]{:S(2)}, u32[]{:S(2)}) collective-permute-start(bf16[144,512]{1,0:T(8,128)(2,1)S(1)} %shard_map.108), channel_id=1, source_target_pairs={{0,16},{4,20},{8,24},{12,28},{16,32},{20,36},{24,40},{28,44},{32,4... | collective-permute-start | bytes 442376 | tf_op jit(solution)/shard_map/ppermute | solution.py:450
  93.9 1.6 %shard_map.107.sums_ref = f32[128,1024]{1,0:T(8,128)S(1)} custom-call(s32[5]{0:T(128)S(1)} %stack.23.place, bf16[128,512]{1,0:T(8,128)(2,1)S(1)} %get-tuple-element.81.q_ref, bf16[128,1024]{1,0:T(8,128)(2,1)S(1)} %get-tuple-element.80.refs_0_, bf16[128,1024]{1,0:T(8,128)(2,1)S(1)} %collective-permute-done.23.refs_1_, ...), custom_call_target="tpu_custom_call" | custom-call | tf_op jit(solution)/shard_map/pallas_call | solution.py:436
  95.4 7.7 %collective-permute-done.25.back_ref = bf16[144,512]{1,0:T(8,128)(2,1)S(1)} collective-permute-done((bf16[144,512]{1,0:T(8,128)(2,1)S(1)}, bf16[144,512]{1,0:T(8,128)(2,1)S(1)}, u32[]{:S(2)}, u32[]{:S(2)}) %collective-permute-start.25) | collective-permute-done | bytes 147488 | tf_op jit(solution)/shard_map/ppermute | solution.py:450
  (51 shorter events, 27.5 us)
Async XLA Ops:
  6.5 4.9 %collective-permute-start = (bf16[144,256]{1,0:T(8,128)(2,1)S(1)}, bf16[144,256]{1,0:T(8,128)(2,1)S(1)}, u32[]{:S(2)}, u32[]{:S(2)}) collective-permute-start(bf16[144,256]{1,0:T(8,128)(2,1)S(1)} %get-tuple-element.52), channel_id=1, source_target_pairs={{0,8},{4,12},{8,0},{12,4},{16,24},{20,28},{24,16},{28,20},{32,40},... | collective-permute-start | bytes 221192 | tf_op jit(solution)/shard_map/ppermute | solution.py:456
  6.7 4.7 %collective-permute-start.1 = (bf16[144,256]{1,0:T(8,128)(2,1)S(1)}, bf16[144,256]{1,0:T(8,128)(2,1)S(1)}, u32[]{:S(2)}, u32[]{:S(2)}) collective-permute-start(bf16[144,256]{1,0:T(8,128)(2,1)S(1)} %get-tuple-element.53), channel_id=1, source_target_pairs={{0,12},{4,8},{8,4},{12,0},{16,28},{20,24},{24,20},{28,16},{32,44},... | collective-permute-start | bytes 221192 | tf_op jit(solution)/shard_map/ppermute | solution.py:456
  7.8 3.6 %collective-permute-start.2 = (bf16[144,256]{1,0:T(8,128)(2,1)S(1)}, bf16[144,256]{1,0:T(8,128)(2,1)S(1)}, u32[]{:S(2)}, u32[]{:S(2)}) collective-permute-start(bf16[144,256]{1,0:T(8,128)(2,1)S(1)} %get-tuple-element.54), channel_id=1, source_target_pairs={{0,4},{4,0},{8,12},{12,8},{16,20},{20,16},{24,28},{28,24},{32,36},... | collective-permute-start | bytes 221192 | tf_op jit(solution)/shard_map/ppermute | solution.py:456
  12.5 11.3 %collective-permute-start.3 = (bf16[144,256]{1,0:T(8,128)(2,1)S(1)}, bf16[144,256]{1,0:T(8,128)(2,1)S(1)}, u32[]{:S(2)}, u32[]{:S(2)}) collective-permute-start(bf16[144,256]{1,0:T(8,128)(2,1)S(1)} %get-tuple-element.59), channel_id=1, source_target_pairs={{0,32},{4,36},{8,40},{12,44},{16,48},{20,52},{24,56},{28,60},{32,0... | collective-permute-start | bytes 221192 | tf_op jit(solution)/shard_map/ppermute | solution.py:456
  19.5 7.9 %collective-permute-start.4 = (bf16[144,256]{1,0:T(8,128)(2,1)S(1)}, bf16[144,256]{1,0:T(8,128)(2,1)S(1)}, u32[]{:S(2)}, u32[]{:S(2)}) collective-permute-start(bf16[144,256]{1,0:T(8,128)(2,1)S(1)} %get-tuple-element.59), channel_id=1, source_target_pairs={{0,48},{4,52},{8,56},{12,60},{16,32},{20,36},{24,40},{28,44},{32,1... | collective-permute-start | bytes 221192 | tf_op jit(solution)/shard_map/ppermute | solution.py:456
  19.5 7.9 %collective-permute-start.5 = (bf16[144,256]{1,0:T(8,128)(2,1)S(1)}, bf16[144,256]{1,0:T(8,128)(2,1)S(1)}, u32[]{:S(2)}, u32[]{:S(2)}) collective-permute-start(bf16[144,256]{1,0:T(8,128)(2,1)S(1)} %get-tuple-element.59), channel_id=1, source_target_pairs={{0,16},{4,20},{8,24},{12,28},{16,0},{20,4},{24,8},{28,12},{32,48},... | collective-permute-start | bytes 221192 | tf_op jit(solution)/shard_map/ppermute | solution.py:456
  28.4 6.2 %collective-permute-start.6 = (bf16[144,256]{1,0:T(8,128)(2,1)S(1)}, bf16[144,256]{1,0:T(8,128)(2,1)S(1)}, u32[]{:S(2)}, u32[]{:S(2)}) collective-permute-start(bf16[144,256]{1,0:T(8,128)(2,1)S(1)} %get-tuple-element.68), channel_id=1, source_target_pairs={{0,128},{4,132},{8,136},{12,140},{16,144},{20,148},{24,152},{28,15... | collective-permute-start | bytes 221192 | tf_op jit(solution)/shard_map/ppermute | solution.py:456
  30.7 4.7 %collective-permute-start.7 = (bf16[144,256]{1,0:T(8,128)(2,1)S(1)}, bf16[144,256]{1,0:T(8,128)(2,1)S(1)}, u32[]{:S(2)}, u32[]{:S(2)}) collective-permute-start(bf16[144,256]{1,0:T(8,128)(2,1)S(1)} %get-tuple-element.68), channel_id=1, source_target_pairs={{0,64},{4,68},{8,72},{12,76},{16,80},{20,84},{24,88},{28,92},{32,9... | collective-permute-start | bytes 221192 | tf_op jit(solution)/shard_map/ppermute | solution.py:456
  32.1 4.4 %collective-permute-start.8 = (bf16[144,256]{1,0:T(8,128)(2,1)S(1)}, bf16[144,256]{1,0:T(8,128)(2,1)S(1)}, u32[]{:S(2)}, u32[]{:S(2)}) collective-permute-start(bf16[144,256]{1,0:T(8,128)(2,1)S(1)} %get-tuple-element.68), channel_id=1, source_target_pairs={{0,192},{4,196},{8,200},{12,204},{16,208},{20,212},{24,216},{28,22... | collective-permute-start | bytes 221192 | tf_op jit(solution)/shard_map/ppermute | solution.py:456
  37.5 3.5 %collective-permute-start.10 = (bf16[128,128]{1,0:T(8,128)(2,1)S(1)}, bf16[128,128]{1,0:T(8,128)(2,1)S(1)}, u32[]{:S(2)}, u32[]{:S(2)}) collective-permute-start(bf16[128,128]{1,0:T(8,128)(2,1)S(1)} %get-tuple-element.72), channel_id=1, source_target_pairs={{0,12},{4,8},{8,4},{12,0},{16,28},{20,24},{24,20},{28,16},{32,44},... | collective-permute-start | bytes 98312 | tf_op jit(solution)/shard_map/ppermute | solution.py:456
  38.8 3.9 %collective-permute-start.9 = (bf16[128,128]{1,0:T(8,128)(2,1)S(1)}, bf16[128,128]{1,0:T(8,128)(2,1)S(1)}, u32[]{:S(2)}, u32[]{:S(2)}) collective-permute-start(bf16[128,128]{1,0:T(8,128)(2,1)S(1)} %get-tuple-element.71), channel_id=1, source_target_pairs={{0,8},{4,12},{8,0},{12,4},{16,24},{20,28},{24,16},{28,20},{32,40},... | collective-permute-start | bytes 98312 | tf_op jit(solution)/shard_map/ppermute | solution.py:456
  44.0 8.0 %collective-permute-start.12 = (bf16[128,512]{1,0:T(8,128)(2,1)S(1)}, bf16[128,512]{1,0:T(8,128)(2,1)S(1)}, u32[]{:S(2)}, u32[]{:S(2)}) collective-permute-start(bf16[128,512]{1,0:T(8,128)(2,1)S(1)} %get-tuple-element.76), channel_id=1, source_target_pairs={{0,2},{1,3},{2,0},{3,1},{4,6},{5,7},{6,4},{7,5},{8,10},{9,11},{10,... | collective-permute-start | bytes 393224 | tf_op jit(solution)/shard_map/ppermute | solution.py:456
  47.4 5.7 %collective-permute-start.13 = (bf16[128,512]{1,0:T(8,128)(2,1)S(1)}, bf16[128,512]{1,0:T(8,128)(2,1)S(1)}, u32[]{:S(2)}, u32[]{:S(2)}) collective-permute-start(bf16[128,512]{1,0:T(8,128)(2,1)S(1)} %get-tuple-element.77), channel_id=1, source_target_pairs={{0,1},{1,0},{2,3},{3,2},{4,5},{5,4},{6,7},{7,6},{8,9},{9,8},{10,11... | collective-permute-start | bytes 393224 | tf_op jit(solution)/shard_map/ppermute | solution.py:456
  48.1 6.2 %collective-permute-start.14 = (bf16[128,512]{1,0:T(8,128)(2,1)S(1)}, bf16[128,512]{1,0:T(8,128)(2,1)S(1)}, u32[]{:S(2)}, u32[]{:S(2)}) collective-permute-start(bf16[128,512]{1,0:T(8,128)(2,1)S(1)} %get-tuple-element.78), channel_id=1, source_target_pairs={{0,3},{1,2},{2,1},{3,0},{4,7},{5,6},{6,5},{7,4},{8,11},{9,10},{10,... | collective-permute-start | bytes 393224 | tf_op jit(solution)/shard_map/ppermute | solution.py:456
  54.4 6.7 %collective-permute-start.15 = (bf16[128,512]{1,0:T(8,128)(2,1)S(1)}, bf16[128,512]{1,0:T(8,128)(2,1)S(1)}, u32[]{:S(2)}, u32[]{:S(2)}) collective-permute-start(bf16[128,512]{1,0:T(8,128)(2,1)S(1)} %shard_map.103.hidden_ref), channel_id=1, source_target_pairs={{0,2},{1,3},{2,0},{3,1},{4,6},{5,7},{6,4},{7,5},{8,10},{9,11},{10,... | collective-permute-start | bytes 393224 | tf_op jit(solution)/shard_map/ppermute | solution.py:456
  56.2 5.7 %collective-permute-start.16 = (bf16[128,512]{1,0:T(8,128)(2,1)S(1)}, bf16[128,512]{1,0:T(8,128)(2,1)S(1)}, u32[]{:S(2)}, u32[]{:S(2)}) collective-permute-start(bf16[128,512]{1,0:T(8,128)(2,1)S(1)} %shard_map.103.hidden_ref), channel_id=1, source_target_pairs={{0,1},{1,0},{2,3},{3,2},{4,5},{5,4},{6,7},{7,6},{8,9},{9,8},{10,11... | collective-permute-start | bytes 393224 | tf_op jit(solution)/shard_map/ppermute | solution.py:456
  56.8 6.3 %collective-permute-start.17 = (bf16[128,512]{1,0:T(8,128)(2,1)S(1)}, bf16[128,512]{1,0:T(8,128)(2,1)S(1)}, u32[]{:S(2)}, u32[]{:S(2)}) collective-permute-start(bf16[128,512]{1,0:T(8,128)(2,1)S(1)} %shard_map.103.hidden_ref), channel_id=1, source_target_pairs={{0,3},{1,2},{2,1},{3,0},{4,7},{5,6},{6,5},{7,4},{8,11},{9,10},{10,... | collective-permute-start | bytes 393224 | tf_op jit(solution)/shard_map/ppermute | solution.py:456
  64.6 10.5 %collective-permute-start.18 = (bf16[128,1024]{1,0:T(8,128)(2,1)S(1)}, bf16[128,1024]{1,0:T(8,128)(2,1)S(1)}, u32[]{:S(2)}, u32[]{:S(2)}) collective-permute-start(bf16[128,1024]{1,0:T(8,128)(2,1)S(1)} %get-tuple-element.80.refs_0_), channel_id=1, source_target_pairs={{0,8},{4,12},{8,16},{12,20},{16,24},{20,28},{24,32},{28,36},{32,40... | collective-permute-start | bytes 786440 | tf_op jit(solution)/shard_map/ppermute | solution.py:450
  68.2 6.9 %collective-permute-start.19 = (bf16[128,512]{1,0:T(8,128)(2,1)S(1)}, bf16[128,512]{1,0:T(8,128)(2,1)S(1)}, u32[]{:S(2)}, u32[]{:S(2)}) collective-permute-start(bf16[128,512]{1,0:T(8,128)(2,1)S(1)} %get-tuple-element.81.q_ref), channel_id=1, source_target_pairs={{8,0},{12,4},{16,8},{20,12},{24,16},{28,20},{32,24},{36,28},{40,32... | collective-permute-start | bytes 393224 | tf_op jit(solution)/shard_map/ppermute | solution.py:450
  75.1 11.1 %collective-permute-start.20 = (bf16[128,1024]{1,0:T(8,128)(2,1)S(1)}, bf16[128,1024]{1,0:T(8,128)(2,1)S(1)}, u32[]{:S(2)}, u32[]{:S(2)}) collective-permute-start(bf16[128,1024]{1,0:T(8,128)(2,1)S(1)} %collective-permute-done.18.own_ref.refs_2_), channel_id=1, source_target_pairs={{0,8},{4,12},{8,16},{12,20},{16,24},{20,28},{24,32},{28,36},{32,40... | collective-permute-start | bytes 786440 | tf_op jit(solution)/shard_map/ppermute | solution.py:450
  78.1 8.1 %collective-permute-start.21 = (bf16[128,512]{1,0:T(8,128)(2,1)S(1)}, bf16[128,512]{1,0:T(8,128)(2,1)S(1)}, u32[]{:S(2)}, u32[]{:S(2)}) collective-permute-start(bf16[128,512]{1,0:T(8,128)(2,1)S(1)} %collective-permute-done.19), channel_id=1, source_target_pairs={{8,0},{12,4},{16,8},{20,12},{24,16},{28,20},{32,24},{36,28},{40,32... | collective-permute-start | bytes 393224 | tf_op jit(solution)/shard_map/ppermute | solution.py:450
  80.9 5.8 %collective-permute-start.22 = (bf16[128,1024]{1,0:T(8,128)(2,1)S(1)}, bf16[128,1024]{1,0:T(8,128)(2,1)S(1)}, u32[]{:S(2)}, u32[]{:S(2)}) collective-permute-start(bf16[128,1024]{1,0:T(8,128)(2,1)S(1)} %collective-permute-done.18.own_ref.refs_2_), channel_id=1, source_target_pairs={{0,4},{4,0},{8,12},{12,8},{16,20},{20,16},{24,28},{28,24},{32,36},... | collective-permute-start | bytes 786440 | tf_op jit(solution)/shard_map/ppermute | solution.py:456
  86.2 7.6 %collective-permute-start.23 = (bf16[128,1024]{1,0:T(8,128)(2,1)S(1)}, bf16[128,1024]{1,0:T(8,128)(2,1)S(1)}, u32[]{:S(2)}, u32[]{:S(2)}) collective-permute-start(bf16[128,1024]{1,0:T(8,128)(2,1)S(1)} %get-tuple-element.80.refs_0_), channel_id=1, source_target_pairs={{0,4},{4,0},{8,12},{12,8},{16,20},{20,16},{24,28},{28,24},{32,36},... | collective-permute-start | bytes 786440 | tf_op jit(solution)/shard_map/ppermute | solution.py:456
  89.2 13.9 %collective-permute-start.25 = (bf16[144,512]{1,0:T(8,128)(2,1)S(1)}, bf16[144,512]{1,0:T(8,128)(2,1)S(1)}, u32[]{:S(2)}, u32[]{:S(2)}) collective-permute-start(bf16[144,512]{1,0:T(8,128)(2,1)S(1)} %shard_map.108), channel_id=1, source_target_pairs={{0,16},{4,20},{8,24},{12,28},{16,32},{20,36},{24,40},{28,44},{32,4... | collective-permute-start | bytes 442376 | tf_op jit(solution)/shard_map/ppermute | solution.py:450
  (5 other events, 70.3 us)

commit v10 on v9

--- a/solution.py
+++ b/solution.py
@@ -535,9 +535,7 @@
     unit_queries, pack = call(project_kernel, [row_shape, ((rows, 2 * wide), BF16)], 1)(
         place, w_qkv, part, hidden, other2, other1, other3
     )
-    first, visitors = lax.optimization_barrier(
-        (moved(pack, "seq", 2), moved(unit_queries, "seq", -2))
-    )
+    first, visitors = moved(pack, "seq", 2), moved(unit_queries, "seq", -2)
     second, visitors = lax.optimization_barrier(
         (moved(first, "seq", 2), moved(visitors, "seq", -2))
     )

time: 104 us -> 105 us (level); the launches traced: 104 us -> 103 us
  waiting for transfers between devices: 37.2 us -> 33 us
  starting transfers between devices: 42.8 us -> 46.2 us
    ppermute x5, waiting for transfers between devices: 17.5 us -> 13.3 us  [moved(): lax.ppermute(array, axis, [(i, i + distance) for i in range(size) if 0 <=...]
    ppermute x5, starting transfers between devices: 16.3 us -> 19.7 us  [moved(): lax.ppermute(array, axis, [(i, i + distance) for i in range(size) if 0 <=...]
where the time goes in v10:
time: 105 us; the launch traced here: 103 us
  starting transfers between devices  46.2 us (44%)
  waiting for transfers between devices  33 us (31%)
  Pallas kernels  21.2 us (20%)
    ppermute x21, starting transfers between devices, crossed(): lax.ppermute(array, axis, [(i, i ^ mask) for i in range(lax.axis_size(axi...  26.5 us
    pallas_call x15, Pallas kernels, run(): pl.pallas_call(kernel, out_shape=[jax.ShapeDtypeStruct(shape, kind) for s...  21.2 us
    ppermute x5, starting transfers between devices, moved(): lax.ppermute(array, axis, [(i, i + distance) for i in range(size) if 0 <=...  19.7 us
    ppermute x21, waiting for transfers between devices, crossed(): lax.ppermute(array, axis, [(i, i ^ mask) for i in range(lax.axis_size(axi...  19.7 us
    ppermute x5, waiting for transfers between devices, moved(): lax.ppermute(array, axis, [(i, i + distance) for i in range(size) if 0 <=...  13.3 us
  transfers between devices with their start and end apart: 26, of which 16 were waited for; matrix products, arithmetic and copies ran while one was open for 0% of the time, Pallas kernels for 9%

profile of v10, /device:TPU:34, one launch (start us, length us, event | category | flops | bytes accessed | tf_op | source)
XLA Modules:
  0.0 103.1 jit_solution(12731722312014971823)
XLA Ops:
  1.6 4.9 %shard_map.95 = (bf16[128,512]{1,0:T(8,128)(2,1)S(1)}, bf16[4,128,128]{2,1,0:T(8,128)(2,1)S(1)}, bf16[4,128,128]{2,1,0:T(8,128)(2,1)S(1)}, f32[128,256]{1,0:T(8,...) custom-call(s32[5]{0:T(128)S(1)} %stack.23.place, ...), custom_call_target="tpu_custom_call" | custom-call | tf_op jit(solution)/shard_map/pallas_call | solution.py:436
  12.5 7.1 %collective-permute-start.3 = (bf16[144,256]{1,0:T(8,128)(2,1)S(1)}, bf16[144,256]{1,0:T(8,128)(2,1)S(1)}, u32[]{:S(2)}, u32[]{:S(2)}) collective-permute-start(bf16[144,256]{1,0:T(8,128)(2,1)S(1)} %get-tuple-element.57), channel_id=1, source_target_pairs={{0,32},{4,36},{8,40},{12,44},{16,48},{20,52},{24,56},{28,60},{32,0... | collective-permute-start | bytes 221192 | tf_op jit(solution)/shard_map/ppermute | solution.py:456
  19.5 1.5 %collective-permute-start.5 = (bf16[144,256]{1,0:T(8,128)(2,1)S(1)}, bf16[144,256]{1,0:T(8,128)(2,1)S(1)}, u32[]{:S(2)}, u32[]{:S(2)}) collective-permute-start(bf16[144,256]{1,0:T(8,128)(2,1)S(1)} %get-tuple-element.57), channel_id=1, source_target_pairs={{0,16},{4,20},{8,24},{12,28},{16,0},{20,4},{24,8},{28,12},{32,48},... | collective-permute-start | bytes 221192 | tf_op jit(solution)/shard_map/ppermute | solution.py:456
  21.0 2.8 %shard_map.98 = (bf16[2048,1536]{1,0:T(8,128)(2,1)S(1)}, f32[128,256]{1,0:T(8,128)S(1)}) custom-call(f32[128,256]{1,0:T(8,128)S(1)} %get-tuple-element.54.token_ref, bf16[2048,1536]{1,0:T(8,128)(2,1)} %source_ref), custom_call_target="tpu_custom_call" | custom-call | tf_op jit(solution)/shard_map/pallas_call | solution.py:436
  23.8 3.6 %collective-permute-done.4.recv3_ref = bf16[144,256]{1,0:T(8,128)(2,1)S(1)} collective-permute-done((bf16[144,256]{1,0:T(8,128)(2,1)S(1)}, bf16[144,256]{1,0:T(8,128)(2,1)S(1)}, u32[]{:S(2)}, u32[]{:S(2)}) %collective-permute-start.4) | collective-permute-done | bytes 73760 | tf_op jit(solution)/shard_map/ppermute | solution.py:456
  28.4 2.2 %collective-permute-start.6 = (bf16[144,256]{1,0:T(8,128)(2,1)S(1)}, bf16[144,256]{1,0:T(8,128)(2,1)S(1)}, u32[]{:S(2)}, u32[]{:S(2)}) collective-permute-start(bf16[144,256]{1,0:T(8,128)(2,1)S(1)} %get-tuple-element.66), channel_id=1, source_target_pairs={{0,128},{4,132},{8,136},{12,140},{16,144},{20,148},{24,152},{28,15... | collective-permute-start | bytes 221192 | tf_op jit(solution)/shard_map/ppermute | solution.py:456
  30.7 1.4 %collective-permute-start.7 = (bf16[144,256]{1,0:T(8,128)(2,1)S(1)}, bf16[144,256]{1,0:T(8,128)(2,1)S(1)}, u32[]{:S(2)}, u32[]{:S(2)}) collective-permute-start(bf16[144,256]{1,0:T(8,128)(2,1)S(1)} %get-tuple-element.66), channel_id=1, source_target_pairs={{0,64},{4,68},{8,72},{12,76},{16,80},{20,84},{24,88},{28,92},{32,9... | collective-permute-start | bytes 221192 | tf_op jit(solution)/shard_map/ppermute | solution.py:456
  41.0 1.8 %collective-permute-done.9.recv2_ref = bf16[128,128]{1,0:T(8,128)(2,1)S(1)} collective-permute-done((bf16[128,128]{1,0:T(8,128)(2,1)S(1)}, bf16[128,128]{1,0:T(8,128)(2,1)S(1)}, u32[]{:S(2)}, u32[]{:S(2)}) %collective-permute-start.9) | collective-permute-done | bytes 32800 | tf_op jit(solution)/shard_map/ppermute | solution.py:456
  44.0 3.5 %collective-permute-start.12 = (bf16[128,512]{1,0:T(8,128)(2,1)S(1)}, bf16[128,512]{1,0:T(8,128)(2,1)S(1)}, u32[]{:S(2)}, u32[]{:S(2)}) collective-permute-start(bf16[128,512]{1,0:T(8,128)(2,1)S(1)} %get-tuple-element.74), channel_id=1, source_target_pairs={{0,2},{1,3},{2,0},{3,1},{4,6},{5,7},{6,4},{7,5},{8,10},{9,11},{10,... | collective-permute-start | bytes 393224 | tf_op jit(solution)/shard_map/ppermute | solution.py:456
  48.5 3.5 %collective-permute-done.12.refs_0_ = bf16[128,512]{1,0:T(8,128)(2,1)S(1)} collective-permute-done((bf16[128,512]{1,0:T(8,128)(2,1)S(1)}, bf16[128,512]{1,0:T(8,128)(2,1)S(1)}, u32[]{:S(2)}, u32[]{:S(2)}) %collective-permute-start.12) | collective-permute-done | bytes 131104 | tf_op jit(solution)/shard_map/ppermute | solution.py:456
  54.4 1.8 %collective-permute-start.15 = (bf16[128,512]{1,0:T(8,128)(2,1)S(1)}, bf16[128,512]{1,0:T(8,128)(2,1)S(1)}, u32[]{:S(2)}, u32[]{:S(2)}) collective-permute-start(bf16[128,512]{1,0:T(8,128)(2,1)S(1)} %shard_map.103.hidden_ref), channel_id=1, source_target_pairs={{0,2},{1,3},{2,0},{3,1},{4,6},{5,7},{6,4},{7,5},{8,10},{9,11},{10,... | collective-permute-start | bytes 393224 | tf_op jit(solution)/shard_map/ppermute | solution.py:456
  56.8 1.7 %collective-permute-start.17 = (bf16[128,512]{1,0:T(8,128)(2,1)S(1)}, bf16[128,512]{1,0:T(8,128)(2,1)S(1)}, u32[]{:S(2)}, u32[]{:S(2)}) collective-permute-start(bf16[128,512]{1,0:T(8,128)(2,1)S(1)} %shard_map.103.hidden_ref), channel_id=1, source_target_pairs={{0,3},{1,2},{2,1},{3,0},{4,7},{5,6},{6,5},{7,4},{8,11},{9,10},{10,... | collective-permute-start | bytes 393224 | tf_op jit(solution)/shard_map/ppermute | solution.py:456
  59.5 1.6 %collective-permute-done.15.block2_ref = bf16[128,512]{1,0:T(8,128)(2,1)S(1)} collective-permute-done((bf16[128,512]{1,0:T(8,128)(2,1)S(1)}, bf16[128,512]{1,0:T(8,128)(2,1)S(1)}, u32[]{:S(2)}, u32[]{:S(2)}) %collective-permute-start.15) | collective-permute-done | bytes 131104 | tf_op jit(solution)/shard_map/ppermute | solution.py:456
  63.1 1.4 %shard_map.105 = (bf16[128,512]{1,0:T(8,128)(2,1)S(1)}, bf16[128,1024]{1,0:T(8,128)(2,1)S(1)}) custom-call(s32[5]{0:T(128)S(1)} %stack.23.place, bf16[2048,1536]{1,0:T(8,128)(2,1)S(1)} %get-tuple-element.77.w_ref, f32[128,1536]{1,0:T(8,128)S(1)} %shard_map.104.part_ref, bf16[128,512]{1,0:T(8,128)(2,1)S(1)} %shard_map.103.hidden_ref, ...), custom_call_target="tpu_custom_call" | custom-call | tf_op jit(solution)/shard_map/pallas_call | solution.py:436
  64.6 3.6 %collective-permute-start.18 = (bf16[128,1024]{1,0:T(8,128)(2,1)S(1)}, bf16[128,1024]{1,0:T(8,128)(2,1)S(1)}, u32[]{:S(2)}, u32[]{:S(2)}) collective-permute-start(bf16[128,1024]{1,0:T(8,128)(2,1)S(1)} %get-tuple-element.78.refs_0_), channel_id=1, source_target_pairs={{0,8},{4,12},{8,16},{12,20},{16,24},{20,28},{24,32},{28,36},{32,40... | collective-permute-start | bytes 786440 | tf_op jit(solution)/shard_map/ppermute | solution.py:450
  68.2 2.2 %collective-permute-start.20 = (bf16[128,512]{1,0:T(8,128)(2,1)S(1)}, bf16[128,512]{1,0:T(8,128)(2,1)S(1)}, u32[]{:S(2)}, u32[]{:S(2)}) collective-permute-start(bf16[128,512]{1,0:T(8,128)(2,1)S(1)} %get-tuple-element.79.q_ref), channel_id=1, source_target_pairs={{8,0},{12,4},{16,8},{20,12},{24,16},{28,20},{32,24},{36,28},{40,32... | collective-permute-start | bytes 393224 | tf_op jit(solution)/shard_map/ppermute | solution.py:450
  70.4 3.0 %collective-permute-done.18.own_ref.refs_2_ = bf16[128,1024]{1,0:T(8,128)(2,1)S(1)} collective-permute-done((bf16[128,1024]{1,0:T(8,128)(2,1)S(1)}, bf16[128,1024]{1,0:T(8,128)(2,1)S(1)}, u32[]{:S(2)}, u32[]{:S(2)}) %collective-permute-start.18) | collective-permute-done | bytes 262176 | tf_op jit(solution)/shard_map/ppermute | solution.py:450
  73.4 3.6 %collective-permute-start.19 = (bf16[128,1024]{1,0:T(8,128)(2,1)S(1)}, bf16[128,1024]{1,0:T(8,128)(2,1)S(1)}, u32[]{:S(2)}, u32[]{:S(2)}) collective-permute-start(bf16[128,1024]{1,0:T(8,128)(2,1)S(1)} %collective-permute-done.18.own_ref.refs_2_), channel_id=1, source_target_pairs={{0,8},{4,12},{8,16},{12,20},{16,24},{20,28},{24,32},{28,36},{32,40... | collective-permute-start | bytes 786440 | tf_op jit(solution)/shard_map/ppermute | solution.py:450
  77.1 3.4 %collective-permute-start.21 = (bf16[128,512]{1,0:T(8,128)(2,1)S(1)}, bf16[128,512]{1,0:T(8,128)(2,1)S(1)}, u32[]{:S(2)}, u32[]{:S(2)}) collective-permute-start(bf16[128,512]{1,0:T(8,128)(2,1)S(1)} %collective-permute-done.20), channel_id=1, source_target_pairs={{8,0},{12,4},{16,8},{20,12},{24,16},{28,20},{32,24},{36,28},{40,32... | collective-permute-start | bytes 393224 | tf_op jit(solution)/shard_map/ppermute | solution.py:450
  80.5 3.4 %collective-permute-done.21.q_ref = bf16[128,512]{1,0:T(8,128)(2,1)S(1)} collective-permute-done((bf16[128,512]{1,0:T(8,128)(2,1)S(1)}, bf16[128,512]{1,0:T(8,128)(2,1)S(1)}, u32[]{:S(2)}, u32[]{:S(2)}) %collective-permute-start.21) | collective-permute-done | bytes 131104 | tf_op jit(solution)/shard_map/ppermute | solution.py:450
  84.4 1.5 %shard_map.106 = (f32[128,1024]{1,0:T(8,128)S(1)}, bf16[128,512]{1,0:T(8,128)(2,1)}) custom-call(s32[5]{0:T(128)S(1)} %stack.23.place, bf16[128,512]{1,0:T(8,128)(2,1)S(1)} %shard_map.103.hidden_ref, bf16[128,512]{1,0:T(8,128)(2,1)S(1)} %collective-permute-done.21.q_ref, bf16[128,1024]{1,0:T(8,128)(2,1)S(1)} %collective-permute-done.18.own_ref.refs_2_, ...), custom_call_target="tpu_custom_call" | custom-call | tf_op jit(solution)/shard_map/pallas_call | solution.py:436
  86.9 6.9 %collective-permute-start.25 = (bf16[144,512]{1,0:T(8,128)(2,1)S(1)}, bf16[144,512]{1,0:T(8,128)(2,1)S(1)}, u32[]{:S(2)}, u32[]{:S(2)}) collective-permute-start(bf16[144,512]{1,0:T(8,128)(2,1)S(1)} %shard_map.108), channel_id=1, source_target_pairs={{0,16},{4,20},{8,24},{12,28},{16,32},{20,36},{24,40},{28,44},{32,4... | collective-permute-start | bytes 442376 | tf_op jit(solution)/shard_map/ppermute | solution.py:450
  93.9 1.6 %shard_map.107.sums_ref = f32[128,1024]{1,0:T(8,128)S(1)} custom-call(s32[5]{0:T(128)S(1)} %stack.23.place, bf16[128,512]{1,0:T(8,128)(2,1)S(1)} %get-tuple-element.79.q_ref, bf16[128,1024]{1,0:T(8,128)(2,1)S(1)} %get-tuple-element.78.refs_0_, bf16[128,1024]{1,0:T(8,128)(2,1)S(1)} %collective-permute-done.23.refs_1_, ...), custom_call_target="tpu_custom_call" | custom-call | tf_op jit(solution)/shard_map/pallas_call | solution.py:436
  95.4 6.9 %collective-permute-done.25.back_ref = bf16[144,512]{1,0:T(8,128)(2,1)S(1)} collective-permute-done((bf16[144,512]{1,0:T(8,128)(2,1)S(1)}, bf16[144,512]{1,0:T(8,128)(2,1)S(1)}, u32[]{:S(2)}, u32[]{:S(2)}) %collective-permute-start.25) | collective-permute-done | bytes 147488 | tf_op jit(solution)/shard_map/ppermute | solution.py:450
  (51 shorter events, 27.5 us)
Async XLA Ops:
  6.5 4.9 %collective-permute-start = (bf16[144,256]{1,0:T(8,128)(2,1)S(1)}, bf16[144,256]{1,0:T(8,128)(2,1)S(1)}, u32[]{:S(2)}, u32[]{:S(2)}) collective-permute-start(bf16[144,256]{1,0:T(8,128)(2,1)S(1)} %get-tuple-element.50), channel_id=1, source_target_pairs={{0,8},{4,12},{8,0},{12,4},{16,24},{20,28},{24,16},{28,20},{32,40},... | collective-permute-start | bytes 221192 | tf_op jit(solution)/shard_map/ppermute | solution.py:456
  6.7 4.7 %collective-permute-start.1 = (bf16[144,256]{1,0:T(8,128)(2,1)S(1)}, bf16[144,256]{1,0:T(8,128)(2,1)S(1)}, u32[]{:S(2)}, u32[]{:S(2)}) collective-permute-start(bf16[144,256]{1,0:T(8,128)(2,1)S(1)} %get-tuple-element.51), channel_id=1, source_target_pairs={{0,12},{4,8},{8,4},{12,0},{16,28},{20,24},{24,20},{28,16},{32,44},... | collective-permute-start | bytes 221192 | tf_op jit(solution)/shard_map/ppermute | solution.py:456
  7.8 3.6 %collective-permute-start.2 = (bf16[144,256]{1,0:T(8,128)(2,1)S(1)}, bf16[144,256]{1,0:T(8,128)(2,1)S(1)}, u32[]{:S(2)}, u32[]{:S(2)}) collective-permute-start(bf16[144,256]{1,0:T(8,128)(2,1)S(1)} %get-tuple-element.52), channel_id=1, source_target_pairs={{0,4},{4,0},{8,12},{12,8},{16,20},{20,16},{24,28},{28,24},{32,36},... | collective-permute-start | bytes 221192 | tf_op jit(solution)/shard_map/ppermute | solution.py:456
  12.5 11.3 %collective-permute-start.3 = (bf16[144,256]{1,0:T(8,128)(2,1)S(1)}, bf16[144,256]{1,0:T(8,128)(2,1)S(1)}, u32[]{:S(2)}, u32[]{:S(2)}) collective-permute-start(bf16[144,256]{1,0:T(8,128)(2,1)S(1)} %get-tuple-element.57), channel_id=1, source_target_pairs={{0,32},{4,36},{8,40},{12,44},{16,48},{20,52},{24,56},{28,60},{32,0... | collective-permute-start | bytes 221192 | tf_op jit(solution)/shard_map/ppermute | solution.py:456
  19.5 7.9 %collective-permute-start.4 = (bf16[144,256]{1,0:T(8,128)(2,1)S(1)}, bf16[144,256]{1,0:T(8,128)(2,1)S(1)}, u32[]{:S(2)}, u32[]{:S(2)}) collective-permute-start(bf16[144,256]{1,0:T(8,128)(2,1)S(1)} %get-tuple-element.57), channel_id=1, source_target_pairs={{0,48},{4,52},{8,56},{12,60},{16,32},{20,36},{24,40},{28,44},{32,1... | collective-permute-start | bytes 221192 | tf_op jit(solution)/shard_map/ppermute | solution.py:456
  19.5 7.9 %collective-permute-start.5 = (bf16[144,256]{1,0:T(8,128)(2,1)S(1)}, bf16[144,256]{1,0:T(8,128)(2,1)S(1)}, u32[]{:S(2)}, u32[]{:S(2)}) collective-permute-start(bf16[144,256]{1,0:T(8,128)(2,1)S(1)} %get-tuple-element.57), channel_id=1, source_target_pairs={{0,16},{4,20},{8,24},{12,28},{16,0},{20,4},{24,8},{28,12},{32,48},... | collective-permute-start | bytes 221192 | tf_op jit(solution)/shard_map/ppermute | solution.py:456
  28.4 6.2 %collective-permute-start.6 = (bf16[144,256]{1,0:T(8,128)(2,1)S(1)}, bf16[144,256]{1,0:T(8,128)(2,1)S(1)}, u32[]{:S(2)}, u32[]{:S(2)}) collective-permute-start(bf16[144,256]{1,0:T(8,128)(2,1)S(1)} %get-tuple-element.66), channel_id=1, source_target_pairs={{0,128},{4,132},{8,136},{12,140},{16,144},{20,148},{24,152},{28,15... | collective-permute-start | bytes 221192 | tf_op jit(solution)/shard_map/ppermute | solution.py:456
  30.7 4.7 %collective-permute-start.7 = (bf16[144,256]{1,0:T(8,128)(2,1)S(1)}, bf16[144,256]{1,0:T(8,128)(2,1)S(1)}, u32[]{:S(2)}, u32[]{:S(2)}) collective-permute-start(bf16[144,256]{1,0:T(8,128)(2,1)S(1)} %get-tuple-element.66), channel_id=1, source_target_pairs={{0,64},{4,68},{8,72},{12,76},{16,80},{20,84},{24,88},{28,92},{32,9... | collective-permute-start | bytes 221192 | tf_op jit(solution)/shard_map/ppermute | solution.py:456
  32.1 4.4 %collective-permute-start.8 = (bf16[144,256]{1,0:T(8,128)(2,1)S(1)}, bf16[144,256]{1,0:T(8,128)(2,1)S(1)}, u32[]{:S(2)}, u32[]{:S(2)}) collective-permute-start(bf16[144,256]{1,0:T(8,128)(2,1)S(1)} %get-tuple-element.66), channel_id=1, source_target_pairs={{0,192},{4,196},{8,200},{12,204},{16,208},{20,212},{24,216},{28,22... | collective-permute-start | bytes 221192 | tf_op jit(solution)/shard_map/ppermute | solution.py:456
  37.5 3.5 %collective-permute-start.10 = (bf16[128,128]{1,0:T(8,128)(2,1)S(1)}, bf16[128,128]{1,0:T(8,128)(2,1)S(1)}, u32[]{:S(2)}, u32[]{:S(2)}) collective-permute-start(bf16[128,128]{1,0:T(8,128)(2,1)S(1)} %get-tuple-element.70), channel_id=1, source_target_pairs={{0,12},{4,8},{8,4},{12,0},{16,28},{20,24},{24,20},{28,16},{32,44},... | collective-permute-start | bytes 98312 | tf_op jit(solution)/shard_map/ppermute | solution.py:456
  38.8 3.9 %collective-permute-start.9 = (bf16[128,128]{1,0:T(8,128)(2,1)S(1)}, bf16[128,128]{1,0:T(8,128)(2,1)S(1)}, u32[]{:S(2)}, u32[]{:S(2)}) collective-permute-start(bf16[128,128]{1,0:T(8,128)(2,1)S(1)} %get-tuple-element.69), channel_id=1, source_target_pairs={{0,8},{4,12},{8,0},{12,4},{16,24},{20,28},{24,16},{28,20},{32,40},... | collective-permute-start | bytes 98312 | tf_op jit(solution)/shard_map/ppermute | solution.py:456
  44.0 8.0 %collective-permute-start.12 = (bf16[128,512]{1,0:T(8,128)(2,1)S(1)}, bf16[128,512]{1,0:T(8,128)(2,1)S(1)}, u32[]{:S(2)}, u32[]{:S(2)}) collective-permute-start(bf16[128,512]{1,0:T(8,128)(2,1)S(1)} %get-tuple-element.74), channel_id=1, source_target_pairs={{0,2},{1,3},{2,0},{3,1},{4,6},{5,7},{6,4},{7,5},{8,10},{9,11},{10,... | collective-permute-start | bytes 393224 | tf_op jit(solution)/shard_map/ppermute | solution.py:456
  47.4 5.7 %collective-permute-start.13 = (bf16[128,512]{1,0:T(8,128)(2,1)S(1)}, bf16[128,512]{1,0:T(8,128)(2,1)S(1)}, u32[]{:S(2)}, u32[]{:S(2)}) collective-permute-start(bf16[128,512]{1,0:T(8,128)(2,1)S(1)} %get-tuple-element.75), channel_id=1, source_target_pairs={{0,1},{1,0},{2,3},{3,2},{4,5},{5,4},{6,7},{7,6},{8,9},{9,8},{10,11... | collective-permute-start | bytes 393224 | tf_op jit(solution)/shard_map/ppermute | solution.py:456
  48.1 6.2 %collective-permute-start.14 = (bf16[128,512]{1,0:T(8,128)(2,1)S(1)}, bf16[128,512]{1,0:T(8,128)(2,1)S(1)}, u32[]{:S(2)}, u32[]{:S(2)}) collective-permute-start(bf16[128,512]{1,0:T(8,128)(2,1)S(1)} %get-tuple-element.76), channel_id=1, source_target_pairs={{0,3},{1,2},{2,1},{3,0},{4,7},{5,6},{6,5},{7,4},{8,11},{9,10},{10,... | collective-permute-start | bytes 393224 | tf_op jit(solution)/shard_map/ppermute | solution.py:456
  54.4 6.7 %collective-permute-start.15 = (bf16[128,512]{1,0:T(8,128)(2,1)S(1)}, bf16[128,512]{1,0:T(8,128)(2,1)S(1)}, u32[]{:S(2)}, u32[]{:S(2)}) collective-permute-start(bf16[128,512]{1,0:T(8,128)(2,1)S(1)} %shard_map.103.hidden_ref), channel_id=1, source_target_pairs={{0,2},{1,3},{2,0},{3,1},{4,6},{5,7},{6,4},{7,5},{8,10},{9,11},{10,... | collective-permute-start | bytes 393224 | tf_op jit(solution)/shard_map/ppermute | solution.py:456
  56.2 5.7 %collective-permute-start.16 = (bf16[128,512]{1,0:T(8,128)(2,1)S(1)}, bf16[128,512]{1,0:T(8,128)(2,1)S(1)}, u32[]{:S(2)}, u32[]{:S(2)}) collective-permute-start(bf16[128,512]{1,0:T(8,128)(2,1)S(1)} %shard_map.103.hidden_ref), channel_id=1, source_target_pairs={{0,1},{1,0},{2,3},{3,2},{4,5},{5,4},{6,7},{7,6},{8,9},{9,8},{10,11... | collective-permute-start | bytes 393224 | tf_op jit(solution)/shard_map/ppermute | solution.py:456
  56.8 6.3 %collective-permute-start.17 = (bf16[128,512]{1,0:T(8,128)(2,1)S(1)}, bf16[128,512]{1,0:T(8,128)(2,1)S(1)}, u32[]{:S(2)}, u32[]{:S(2)}) collective-permute-start(bf16[128,512]{1,0:T(8,128)(2,1)S(1)} %shard_map.103.hidden_ref), channel_id=1, source_target_pairs={{0,3},{1,2},{2,1},{3,0},{4,7},{5,6},{6,5},{7,4},{8,11},{9,10},{10,... | collective-permute-start | bytes 393224 | tf_op jit(solution)/shard_map/ppermute | solution.py:456
  64.6 8.9 %collective-permute-start.18 = (bf16[128,1024]{1,0:T(8,128)(2,1)S(1)}, bf16[128,1024]{1,0:T(8,128)(2,1)S(1)}, u32[]{:S(2)}, u32[]{:S(2)}) collective-permute-start(bf16[128,1024]{1,0:T(8,128)(2,1)S(1)} %get-tuple-element.78.refs_0_), channel_id=1, source_target_pairs={{0,8},{4,12},{8,16},{12,20},{16,24},{20,28},{24,32},{28,36},{32,40... | collective-permute-start | bytes 786440 | tf_op jit(solution)/shard_map/ppermute | solution.py:450
  68.2 8.8 %collective-permute-start.20 = (bf16[128,512]{1,0:T(8,128)(2,1)S(1)}, bf16[128,512]{1,0:T(8,128)(2,1)S(1)}, u32[]{:S(2)}, u32[]{:S(2)}) collective-permute-start(bf16[128,512]{1,0:T(8,128)(2,1)S(1)} %get-tuple-element.79.q_ref), channel_id=1, source_target_pairs={{8,0},{12,4},{16,8},{20,12},{24,16},{28,20},{32,24},{36,28},{40,32... | collective-permute-start | bytes 393224 | tf_op jit(solution)/shard_map/ppermute | solution.py:450
  73.4 10.5 %collective-permute-start.19 = (bf16[128,1024]{1,0:T(8,128)(2,1)S(1)}, bf16[128,1024]{1,0:T(8,128)(2,1)S(1)}, u32[]{:S(2)}, u32[]{:S(2)}) collective-permute-start(bf16[128,1024]{1,0:T(8,128)(2,1)S(1)} %collective-permute-done.18.own_ref.refs_2_), channel_id=1, source_target_pairs={{0,8},{4,12},{8,16},{12,20},{16,24},{20,28},{24,32},{28,36},{32,40... | collective-permute-start | bytes 786440 | tf_op jit(solution)/shard_map/ppermute | solution.py:450
  77.1 6.9 %collective-permute-start.21 = (bf16[128,512]{1,0:T(8,128)(2,1)S(1)}, bf16[128,512]{1,0:T(8,128)(2,1)S(1)}, u32[]{:S(2)}, u32[]{:S(2)}) collective-permute-start(bf16[128,512]{1,0:T(8,128)(2,1)S(1)} %collective-permute-done.20), channel_id=1, source_target_pairs={{8,0},{12,4},{16,8},{20,12},{24,16},{28,20},{32,24},{36,28},{40,32... | collective-permute-start | bytes 393224 | tf_op jit(solution)/shard_map/ppermute | solution.py:450
  80.4 4.0 %collective-permute-start.22 = (bf16[128,1024]{1,0:T(8,128)(2,1)S(1)}, bf16[128,1024]{1,0:T(8,128)(2,1)S(1)}, u32[]{:S(2)}, u32[]{:S(2)}) collective-permute-start(bf16[128,1024]{1,0:T(8,128)(2,1)S(1)} %collective-permute-done.18.own_ref.refs_2_), channel_id=1, source_target_pairs={{0,4},{4,0},{8,12},{12,8},{16,20},{20,16},{24,28},{28,24},{32,36},... | collective-permute-start | bytes 786440 | tf_op jit(solution)/shard_map/ppermute | solution.py:456
  83.9 9.9 %collective-permute-start.23 = (bf16[128,1024]{1,0:T(8,128)(2,1)S(1)}, bf16[128,1024]{1,0:T(8,128)(2,1)S(1)}, u32[]{:S(2)}, u32[]{:S(2)}) collective-permute-start(bf16[128,1024]{1,0:T(8,128)(2,1)S(1)} %get-tuple-element.78.refs_0_), channel_id=1, source_target_pairs={{0,4},{4,0},{8,12},{12,8},{16,20},{20,16},{24,28},{28,24},{32,36},... | collective-permute-start | bytes 786440 | tf_op jit(solution)/shard_map/ppermute | solution.py:456
  86.9 15.4 %collective-permute-start.25 = (bf16[144,512]{1,0:T(8,128)(2,1)S(1)}, bf16[144,512]{1,0:T(8,128)(2,1)S(1)}, u32[]{:S(2)}, u32[]{:S(2)}) collective-permute-start(bf16[144,512]{1,0:T(8,128)(2,1)S(1)} %shard_map.108), channel_id=1, source_target_pairs={{0,16},{4,20},{8,24},{12,28},{16,32},{20,36},{24,40},{28,44},{32,4... | collective-permute-start | bytes 442376 | tf_op jit(solution)/shard_map/ppermute | solution.py:450
  (5 other events, 70.3 us)

commit v11 on v10

--- a/solution.py
+++ b/solution.py
@@ -286,7 +286,7 @@
 
 
 def out_kernel(
-    place, local_ref, through_ref, mine_ref, recv2_ref, recv3_ref, recv1_ref, w_ref, term_ref, *refs
+    place, local_ref, through_ref, mine_ref, recv1_ref, recv2_ref, recv3_ref, w_ref, term_ref, *refs
 ):
     part = place[1]
     me = place[2]
@@ -523,9 +523,9 @@
         local,
         through,
         mine,
+        crossed(out1, 1),
         crossed(out2, 2),
         crossed(out3, 3),
-        crossed(out1, 1),
         w_out,
     )
     received = [crossed(terms[r], r, "head") for r in (2, 1, 3)]

time: 105 us -> 108 us (1.029)
  the two profiles are of different devices: /device:TPU:34 before, /device:TPU:18 now
where the time goes in v11:
time: 108 us; the launch traced here: 107 us
  starting transfers between devices  43.6 us (40%)
  waiting for transfers between devices  39.9 us (37%)
  Pallas kernels  21.2 us (20%)
    ppermute x21, starting transfers between devices, crossed(): lax.ppermute(array, axis, [(i, i ^ mask) for i in range(lax.axis_size(axi...  25.8 us
    ppermute x21, waiting for transfers between devices, crossed(): lax.ppermute(array, axis, [(i, i ^ mask) for i in range(lax.axis_size(axi...  21.7 us
    pallas_call x15, Pallas kernels, run(): pl.pallas_call(kernel, out_shape=[jax.ShapeDtypeStruct(shape, kind) for s...  21.2 us
    ppermute x5, waiting for transfers between devices, moved(): lax.ppermute(array, axis, [(i, i + distance) for i in range(size) if 0 <=...  18.2 us
    ppermute x5, starting transfers between devices, moved(): lax.ppermute(array, axis, [(i, i + distance) for i in range(size) if 0 <=...  17.8 us
  transfers between devices with their start and end apart: 26, of which 19 were waited for; matrix products, arithmetic and copies ran while one was open for 0% of the time, Pallas kernels for 9%

profile of v11, /device:TPU:18, one launch (start us, length us, event | category | flops | bytes accessed | tf_op | source)
XLA Modules:
  0.0 107.4 jit_solution(2260196059861856945)
XLA Ops:
  1.6 4.9 %shard_map.95 = (bf16[128,512]{1,0:T(8,128)(2,1)S(1)}, bf16[4,128,128]{2,1,0:T(8,128)(2,1)S(1)}, bf16[4,128,128]{2,1,0:T(8,128)(2,1)S(1)}, f32[128,256]{1,0:T(8,...) custom-call(s32[5]{0:T(128)S(1)} %stack.23.place, ...), custom_call_target="tpu_custom_call" | custom-call | tf_op jit(solution)/shard_map/pallas_call | solution.py:436
  6.5 2.0 %collective-permute-start = (bf16[144,256]{1,0:T(8,128)(2,1)S(1)}, bf16[144,256]{1,0:T(8,128)(2,1)S(1)}, u32[]{:S(2)}, u32[]{:S(2)}) collective-permute-start(bf16[144,256]{1,0:T(8,128)(2,1)S(1)} %get-tuple-element.50), channel_id=1, source_target_pairs={{0,8},{4,12},{8,0},{12,4},{16,24},{20,28},{24,16},{28,20},{32,40},... | collective-permute-start | bytes 221192 | tf_op jit(solution)/shard_map/ppermute | solution.py:456
  10.9 1.9 %collective-permute-done.1.recv3_ref = bf16[144,256]{1,0:T(8,128)(2,1)S(1)} collective-permute-done((bf16[144,256]{1,0:T(8,128)(2,1)S(1)}, bf16[144,256]{1,0:T(8,128)(2,1)S(1)}, u32[]{:S(2)}, u32[]{:S(2)}) %collective-permute-start.1) | collective-permute-done | bytes 73760 | tf_op jit(solution)/shard_map/ppermute | solution.py:456
  13.9 6.6 %collective-permute-start.3 = (bf16[144,256]{1,0:T(8,128)(2,1)S(1)}, bf16[144,256]{1,0:T(8,128)(2,1)S(1)}, u32[]{:S(2)}, u32[]{:S(2)}) collective-permute-start(bf16[144,256]{1,0:T(8,128)(2,1)S(1)} %get-tuple-element.57), channel_id=1, source_target_pairs={{0,32},{4,36},{8,40},{12,44},{16,48},{20,52},{24,56},{28,60},{32,0... | collective-permute-start | bytes 221192 | tf_op jit(solution)/shard_map/ppermute | solution.py:456
  21.9 2.8 %shard_map.98 = (bf16[2048,1536]{1,0:T(8,128)(2,1)S(1)}, f32[128,256]{1,0:T(8,128)S(1)}) custom-call(f32[128,256]{1,0:T(8,128)S(1)} %get-tuple-element.54.token_ref, bf16[2048,1536]{1,0:T(8,128)(2,1)} %source_ref), custom_call_target="tpu_custom_call" | custom-call | tf_op jit(solution)/shard_map/pallas_call | solution.py:436
  24.7 2.2 %collective-permute-done.4.recv3_ref = bf16[144,256]{1,0:T(8,128)(2,1)S(1)} collective-permute-done((bf16[144,256]{1,0:T(8,128)(2,1)S(1)}, bf16[144,256]{1,0:T(8,128)(2,1)S(1)}, u32[]{:S(2)}, u32[]{:S(2)}) %collective-permute-start.4) | collective-permute-done | bytes 73760 | tf_op jit(solution)/shard_map/ppermute | solution.py:456
  29.5 2.2 %collective-permute-start.6 = (bf16[144,256]{1,0:T(8,128)(2,1)S(1)}, bf16[144,256]{1,0:T(8,128)(2,1)S(1)}, u32[]{:S(2)}, u32[]{:S(2)}) collective-permute-start(bf16[144,256]{1,0:T(8,128)(2,1)S(1)} %get-tuple-element.66), channel_id=1, source_target_pairs={{0,128},{4,132},{8,136},{12,140},{16,144},{20,148},{24,152},{28,15... | collective-permute-start | bytes 221192 | tf_op jit(solution)/shard_map/ppermute | solution.py:456
  40.8 1.8 %collective-permute-done.10.recv2_ref = bf16[128,128]{1,0:T(8,128)(2,1)S(1)} collective-permute-done((bf16[128,128]{1,0:T(8,128)(2,1)S(1)}, bf16[128,128]{1,0:T(8,128)(2,1)S(1)}, u32[]{:S(2)}, u32[]{:S(2)}) %collective-permute-start.10) | collective-permute-done | bytes 32800 | tf_op jit(solution)/shard_map/ppermute | solution.py:456
  45.0 2.2 %collective-permute-start.13 = (bf16[128,512]{1,0:T(8,128)(2,1)S(1)}, bf16[128,512]{1,0:T(8,128)(2,1)S(1)}, u32[]{:S(2)}, u32[]{:S(2)}) collective-permute-start(bf16[128,512]{1,0:T(8,128)(2,1)S(1)} %get-tuple-element.75), channel_id=1, source_target_pairs={{0,1},{1,0},{2,3},{3,2},{4,5},{5,4},{6,7},{7,6},{8,9},{9,8},{10,11... | collective-permute-start | bytes 393224 | tf_op jit(solution)/shard_map/ppermute | solution.py:456
  47.2 1.6 %collective-permute-start.14 = (bf16[128,512]{1,0:T(8,128)(2,1)S(1)}, bf16[128,512]{1,0:T(8,128)(2,1)S(1)}, u32[]{:S(2)}, u32[]{:S(2)}) collective-permute-start(bf16[128,512]{1,0:T(8,128)(2,1)S(1)} %get-tuple-element.76), channel_id=1, source_target_pairs={{0,3},{1,2},{2,1},{3,0},{4,7},{5,6},{6,5},{7,4},{8,11},{9,10},{10,... | collective-permute-start | bytes 393224 | tf_op jit(solution)/shard_map/ppermute | solution.py:456
  48.8 3.8 %collective-permute-done.12.refs_0_ = bf16[128,512]{1,0:T(8,128)(2,1)S(1)} collective-permute-done((bf16[128,512]{1,0:T(8,128)(2,1)S(1)}, bf16[128,512]{1,0:T(8,128)(2,1)S(1)}, u32[]{:S(2)}, u32[]{:S(2)}) %collective-permute-start.12) | collective-permute-done | bytes 131104 | tf_op jit(solution)/shard_map/ppermute | solution.py:456
  55.5 1.8 %collective-permute-start.16 = (bf16[128,512]{1,0:T(8,128)(2,1)S(1)}, bf16[128,512]{1,0:T(8,128)(2,1)S(1)}, u32[]{:S(2)}, u32[]{:S(2)}) collective-permute-start(bf16[128,512]{1,0:T(8,128)(2,1)S(1)} %shard_map.103.hidden_ref), channel_id=1, source_target_pairs={{0,1},{1,0},{2,3},{3,2},{4,5},{5,4},{6,7},{7,6},{8,9},{9,8},{10,11... | collective-permute-start | bytes 393224 | tf_op jit(solution)/shard_map/ppermute | solution.py:456
  59.7 2.9 %collective-permute-done.15.block2_ref = bf16[128,512]{1,0:T(8,128)(2,1)S(1)} collective-permute-done((bf16[128,512]{1,0:T(8,128)(2,1)S(1)}, bf16[128,512]{1,0:T(8,128)(2,1)S(1)}, u32[]{:S(2)}, u32[]{:S(2)}) %collective-permute-start.15) | collective-permute-done | bytes 131104 | tf_op jit(solution)/shard_map/ppermute | solution.py:456
  62.9 1.5 %collective-permute-done.17.block3_ref = bf16[128,512]{1,0:T(8,128)(2,1)S(1)} collective-permute-done((bf16[128,512]{1,0:T(8,128)(2,1)S(1)}, bf16[128,512]{1,0:T(8,128)(2,1)S(1)}, u32[]{:S(2)}, u32[]{:S(2)}) %collective-permute-start.17) | collective-permute-done | bytes 131104 | tf_op jit(solution)/shard_map/ppermute | solution.py:456
  65.9 2.7 %collective-permute-start.18 = (bf16[128,1024]{1,0:T(8,128)(2,1)S(1)}, bf16[128,1024]{1,0:T(8,128)(2,1)S(1)}, u32[]{:S(2)}, u32[]{:S(2)}) collective-permute-start(bf16[128,1024]{1,0:T(8,128)(2,1)S(1)} %get-tuple-element.78.refs_0_), channel_id=1, source_target_pairs={{0,8},{4,12},{8,16},{12,20},{16,24},{20,28},{24,32},{28,36},{32,40... | collective-permute-start | bytes 786440 | tf_op jit(solution)/shard_map/ppermute | solution.py:450
  68.5 5.3 %collective-permute-start.20 = (bf16[128,512]{1,0:T(8,128)(2,1)S(1)}, bf16[128,512]{1,0:T(8,128)(2,1)S(1)}, u32[]{:S(2)}, u32[]{:S(2)}) collective-permute-start(bf16[128,512]{1,0:T(8,128)(2,1)S(1)} %get-tuple-element.79.q_ref), channel_id=1, source_target_pairs={{8,0},{12,4},{16,8},{20,12},{24,16},{28,20},{32,24},{36,28},{40,32... | collective-permute-start | bytes 393224 | tf_op jit(solution)/shard_map/ppermute | solution.py:450
  73.8 4.4 %collective-permute-done.18.own_ref.refs_2_ = bf16[128,1024]{1,0:T(8,128)(2,1)S(1)} collective-permute-done((bf16[128,1024]{1,0:T(8,128)(2,1)S(1)}, bf16[128,1024]{1,0:T(8,128)(2,1)S(1)}, u32[]{:S(2)}, u32[]{:S(2)}) %collective-permute-start.18) | collective-permute-done | bytes 262176 | tf_op jit(solution)/shard_map/ppermute | solution.py:450
  78.2 1.9 %collective-permute-start.19 = (bf16[128,1024]{1,0:T(8,128)(2,1)S(1)}, bf16[128,1024]{1,0:T(8,128)(2,1)S(1)}, u32[]{:S(2)}, u32[]{:S(2)}) collective-permute-start(bf16[128,1024]{1,0:T(8,128)(2,1)S(1)} %collective-permute-done.18.own_ref.refs_2_), channel_id=1, source_target_pairs={{0,8},{4,12},{8,16},{12,20},{16,24},{20,28},{24,32},{28,36},{32,40... | collective-permute-start | bytes 786440 | tf_op jit(solution)/shard_map/ppermute | solution.py:450
  80.2 6.0 %collective-permute-start.21 = (bf16[128,512]{1,0:T(8,128)(2,1)S(1)}, bf16[128,512]{1,0:T(8,128)(2,1)S(1)}, u32[]{:S(2)}, u32[]{:S(2)}) collective-permute-start(bf16[128,512]{1,0:T(8,128)(2,1)S(1)} %collective-permute-done.20), channel_id=1, source_target_pairs={{8,0},{12,4},{16,8},{20,12},{24,16},{28,20},{32,24},{36,28},{40,32... | collective-permute-start | bytes 393224 | tf_op jit(solution)/shard_map/ppermute | solution.py:450
  86.3 2.4 %collective-permute-done.21.q_ref = bf16[128,512]{1,0:T(8,128)(2,1)S(1)} collective-permute-done((bf16[128,512]{1,0:T(8,128)(2,1)S(1)}, bf16[128,512]{1,0:T(8,128)(2,1)S(1)}, u32[]{:S(2)}, u32[]{:S(2)}) %collective-permute-start.21) | collective-permute-done | bytes 131104 | tf_op jit(solution)/shard_map/ppermute | solution.py:450
  90.3 1.5 %shard_map.106 = (f32[128,1024]{1,0:T(8,128)S(1)}, bf16[128,512]{1,0:T(8,128)(2,1)}) custom-call(s32[5]{0:T(128)S(1)} %stack.23.place, bf16[128,512]{1,0:T(8,128)(2,1)S(1)} %shard_map.103.hidden_ref, bf16[128,512]{1,0:T(8,128)(2,1)S(1)} %collective-permute-done.21.q_ref, bf16[128,1024]{1,0:T(8,128)(2,1)S(1)} %collective-permute-done.18.own_ref.refs_2_, ...), custom_call_target="tpu_custom_call" | custom-call | tf_op jit(solution)/shard_map/pallas_call | solution.py:436
  92.8 1.9 %collective-permute-start.25 = (bf16[144,512]{1,0:T(8,128)(2,1)S(1)}, bf16[144,512]{1,0:T(8,128)(2,1)S(1)}, u32[]{:S(2)}, u32[]{:S(2)}) collective-permute-start(bf16[144,512]{1,0:T(8,128)(2,1)S(1)} %shard_map.108), channel_id=1, source_target_pairs={{0,16},{4,20},{8,24},{12,28},{16,32},{20,36},{24,40},{28,44},{32,4... | collective-permute-start | bytes 442376 | tf_op jit(solution)/shard_map/ppermute | solution.py:450
  94.7 1.6 %shard_map.107.sums_ref = f32[128,1024]{1,0:T(8,128)S(1)} custom-call(s32[5]{0:T(128)S(1)} %stack.23.place, bf16[128,512]{1,0:T(8,128)(2,1)S(1)} %get-tuple-element.79.q_ref, bf16[128,1024]{1,0:T(8,128)(2,1)S(1)} %get-tuple-element.78.refs_0_, bf16[128,1024]{1,0:T(8,128)(2,1)S(1)} %collective-permute-done.23.refs_1_, ...), custom_call_target="tpu_custom_call" | custom-call | tf_op jit(solution)/shard_map/pallas_call | solution.py:436
  96.3 10.3 %collective-permute-done.25.back_ref = bf16[144,512]{1,0:T(8,128)(2,1)S(1)} collective-permute-done((bf16[144,512]{1,0:T(8,128)(2,1)S(1)}, bf16[144,512]{1,0:T(8,128)(2,1)S(1)}, u32[]{:S(2)}, u32[]{:S(2)}) %collective-permute-start.25) | collective-permute-done | bytes 147488 | tf_op jit(solution)/shard_map/ppermute | solution.py:450
  (51 shorter events, 30.5 us)
Async XLA Ops:
  6.5 4.4 %collective-permute-start = (bf16[144,256]{1,0:T(8,128)(2,1)S(1)}, bf16[144,256]{1,0:T(8,128)(2,1)S(1)}, u32[]{:S(2)}, u32[]{:S(2)}) collective-permute-start(bf16[144,256]{1,0:T(8,128)(2,1)S(1)} %get-tuple-element.50), channel_id=1, source_target_pairs={{0,8},{4,12},{8,0},{12,4},{16,24},{20,28},{24,16},{28,20},{32,40},... | collective-permute-start | bytes 221192 | tf_op jit(solution)/shard_map/ppermute | solution.py:456
  8.5 4.3 %collective-permute-start.1 = (bf16[144,256]{1,0:T(8,128)(2,1)S(1)}, bf16[144,256]{1,0:T(8,128)(2,1)S(1)}, u32[]{:S(2)}, u32[]{:S(2)}) collective-permute-start(bf16[144,256]{1,0:T(8,128)(2,1)S(1)} %get-tuple-element.51), channel_id=1, source_target_pairs={{0,12},{4,8},{8,4},{12,0},{16,28},{20,24},{24,20},{28,16},{32,44},... | collective-permute-start | bytes 221192 | tf_op jit(solution)/shard_map/ppermute | solution.py:456
  8.5 4.3 %collective-permute-start.2 = (bf16[144,256]{1,0:T(8,128)(2,1)S(1)}, bf16[144,256]{1,0:T(8,128)(2,1)S(1)}, u32[]{:S(2)}, u32[]{:S(2)}) collective-permute-start(bf16[144,256]{1,0:T(8,128)(2,1)S(1)} %get-tuple-element.52), channel_id=1, source_target_pairs={{0,4},{4,0},{8,12},{12,8},{16,20},{20,16},{24,28},{28,24},{32,36},... | collective-permute-start | bytes 221192 | tf_op jit(solution)/shard_map/ppermute | solution.py:456
  13.9 10.8 %collective-permute-start.3 = (bf16[144,256]{1,0:T(8,128)(2,1)S(1)}, bf16[144,256]{1,0:T(8,128)(2,1)S(1)}, u32[]{:S(2)}, u32[]{:S(2)}) collective-permute-start(bf16[144,256]{1,0:T(8,128)(2,1)S(1)} %get-tuple-element.57), channel_id=1, source_target_pairs={{0,32},{4,36},{8,40},{12,44},{16,48},{20,52},{24,56},{28,60},{32,0... | collective-permute-start | bytes 221192 | tf_op jit(solution)/shard_map/ppermute | solution.py:456
  20.4 6.5 %collective-permute-start.4 = (bf16[144,256]{1,0:T(8,128)(2,1)S(1)}, bf16[144,256]{1,0:T(8,128)(2,1)S(1)}, u32[]{:S(2)}, u32[]{:S(2)}) collective-permute-start(bf16[144,256]{1,0:T(8,128)(2,1)S(1)} %get-tuple-element.57), channel_id=1, source_target_pairs={{0,48},{4,52},{8,56},{12,60},{16,32},{20,36},{24,40},{28,44},{32,1... | collective-permute-start | bytes 221192 | tf_op jit(solution)/shard_map/ppermute | solution.py:456
  20.8 7.6 %collective-permute-start.5 = (bf16[144,256]{1,0:T(8,128)(2,1)S(1)}, bf16[144,256]{1,0:T(8,128)(2,1)S(1)}, u32[]{:S(2)}, u32[]{:S(2)}) collective-permute-start(bf16[144,256]{1,0:T(8,128)(2,1)S(1)} %get-tuple-element.57), channel_id=1, source_target_pairs={{0,16},{4,20},{8,24},{12,28},{16,0},{20,4},{24,8},{28,12},{32,48},... | collective-permute-start | bytes 221192 | tf_op jit(solution)/shard_map/ppermute | solution.py:456
  29.5 6.6 %collective-permute-start.6 = (bf16[144,256]{1,0:T(8,128)(2,1)S(1)}, bf16[144,256]{1,0:T(8,128)(2,1)S(1)}, u32[]{:S(2)}, u32[]{:S(2)}) collective-permute-start(bf16[144,256]{1,0:T(8,128)(2,1)S(1)} %get-tuple-element.66), channel_id=1, source_target_pairs={{0,128},{4,132},{8,136},{12,140},{16,144},{20,148},{24,152},{28,15... | collective-permute-start | bytes 221192 | tf_op jit(solution)/shard_map/ppermute | solution.py:456
  31.7 5.1 %collective-permute-start.7 = (bf16[144,256]{1,0:T(8,128)(2,1)S(1)}, bf16[144,256]{1,0:T(8,128)(2,1)S(1)}, u32[]{:S(2)}, u32[]{:S(2)}) collective-permute-start(bf16[144,256]{1,0:T(8,128)(2,1)S(1)} %get-tuple-element.66), channel_id=1, source_target_pairs={{0,64},{4,68},{8,72},{12,76},{16,80},{20,84},{24,88},{28,92},{32,9... | collective-permute-start | bytes 221192 | tf_op jit(solution)/shard_map/ppermute | solution.py:456
  33.1 4.4 %collective-permute-start.8 = (bf16[144,256]{1,0:T(8,128)(2,1)S(1)}, bf16[144,256]{1,0:T(8,128)(2,1)S(1)}, u32[]{:S(2)}, u32[]{:S(2)}) collective-permute-start(bf16[144,256]{1,0:T(8,128)(2,1)S(1)} %get-tuple-element.66), channel_id=1, source_target_pairs={{0,192},{4,196},{8,200},{12,204},{16,208},{20,212},{24,216},{28,22... | collective-permute-start | bytes 221192 | tf_op jit(solution)/shard_map/ppermute | solution.py:456
  38.5 4.0 %collective-permute-start.10 = (bf16[128,128]{1,0:T(8,128)(2,1)S(1)}, bf16[128,128]{1,0:T(8,128)(2,1)S(1)}, u32[]{:S(2)}, u32[]{:S(2)}) collective-permute-start(bf16[128,128]{1,0:T(8,128)(2,1)S(1)} %get-tuple-element.70), channel_id=1, source_target_pairs={{0,8},{4,12},{8,0},{12,4},{16,24},{20,28},{24,16},{28,20},{32,40},... | collective-permute-start | bytes 98312 | tf_op jit(solution)/shard_map/ppermute | solution.py:456
  39.5 3.7 %collective-permute-start.11 = (bf16[128,128]{1,0:T(8,128)(2,1)S(1)}, bf16[128,128]{1,0:T(8,128)(2,1)S(1)}, u32[]{:S(2)}, u32[]{:S(2)}) collective-permute-start(bf16[128,128]{1,0:T(8,128)(2,1)S(1)} %get-tuple-element.71), channel_id=1, source_target_pairs={{0,12},{4,8},{8,4},{12,0},{16,28},{20,24},{24,20},{28,16},{32,44},... | collective-permute-start | bytes 98312 | tf_op jit(solution)/shard_map/ppermute | solution.py:456
  44.4 8.1 %collective-permute-start.12 = (bf16[128,512]{1,0:T(8,128)(2,1)S(1)}, bf16[128,512]{1,0:T(8,128)(2,1)S(1)}, u32[]{:S(2)}, u32[]{:S(2)}) collective-permute-start(bf16[128,512]{1,0:T(8,128)(2,1)S(1)} %get-tuple-element.74), channel_id=1, source_target_pairs={{0,2},{1,3},{2,0},{3,1},{4,6},{5,7},{6,4},{7,5},{8,10},{9,11},{10,... | collective-permute-start | bytes 393224 | tf_op jit(solution)/shard_map/ppermute | solution.py:456
  45.0 8.5 %collective-permute-start.13 = (bf16[128,512]{1,0:T(8,128)(2,1)S(1)}, bf16[128,512]{1,0:T(8,128)(2,1)S(1)}, u32[]{:S(2)}, u32[]{:S(2)}) collective-permute-start(bf16[128,512]{1,0:T(8,128)(2,1)S(1)} %get-tuple-element.75), channel_id=1, source_target_pairs={{0,1},{1,0},{2,3},{3,2},{4,5},{5,4},{6,7},{7,6},{8,9},{9,8},{10,11... | collective-permute-start | bytes 393224 | tf_op jit(solution)/shard_map/ppermute | solution.py:456
  47.2 7.3 %collective-permute-start.14 = (bf16[128,512]{1,0:T(8,128)(2,1)S(1)}, bf16[128,512]{1,0:T(8,128)(2,1)S(1)}, u32[]{:S(2)}, u32[]{:S(2)}) collective-permute-start(bf16[128,512]{1,0:T(8,128)(2,1)S(1)} %get-tuple-element.76), channel_id=1, source_target_pairs={{0,3},{1,2},{2,1},{3,0},{4,7},{5,6},{6,5},{7,4},{8,11},{9,10},{10,... | collective-permute-start | bytes 393224 | tf_op jit(solution)/shard_map/ppermute | solution.py:456
  54.6 8.0 %collective-permute-start.15 = (bf16[128,512]{1,0:T(8,128)(2,1)S(1)}, bf16[128,512]{1,0:T(8,128)(2,1)S(1)}, u32[]{:S(2)}, u32[]{:S(2)}) collective-permute-start(bf16[128,512]{1,0:T(8,128)(2,1)S(1)} %shard_map.103.hidden_ref), channel_id=1, source_target_pairs={{0,2},{1,3},{2,0},{3,1},{4,6},{5,7},{6,4},{7,5},{8,10},{9,11},{10,... | collective-permute-start | bytes 393224 | tf_op jit(solution)/shard_map/ppermute | solution.py:456
  55.5 7.4 %collective-permute-start.16 = (bf16[128,512]{1,0:T(8,128)(2,1)S(1)}, bf16[128,512]{1,0:T(8,128)(2,1)S(1)}, u32[]{:S(2)}, u32[]{:S(2)}) collective-permute-start(bf16[128,512]{1,0:T(8,128)(2,1)S(1)} %shard_map.103.hidden_ref), channel_id=1, source_target_pairs={{0,1},{1,0},{2,3},{3,2},{4,5},{5,4},{6,7},{7,6},{8,9},{9,8},{10,11... | collective-permute-start | bytes 393224 | tf_op jit(solution)/shard_map/ppermute | solution.py:456
  57.3 7.1 %collective-permute-start.17 = (bf16[128,512]{1,0:T(8,128)(2,1)S(1)}, bf16[128,512]{1,0:T(8,128)(2,1)S(1)}, u32[]{:S(2)}, u32[]{:S(2)}) collective-permute-start(bf16[128,512]{1,0:T(8,128)(2,1)S(1)} %shard_map.103.hidden_ref), channel_id=1, source_target_pairs={{0,3},{1,2},{2,1},{3,0},{4,7},{5,6},{6,5},{7,4},{8,11},{9,10},{10,... | collective-permute-start | bytes 393224 | tf_op jit(solution)/shard_map/ppermute | solution.py:456
  65.9 12.4 %collective-permute-start.18 = (bf16[128,1024]{1,0:T(8,128)(2,1)S(1)}, bf16[128,1024]{1,0:T(8,128)(2,1)S(1)}, u32[]{:S(2)}, u32[]{:S(2)}) collective-permute-start(bf16[128,1024]{1,0:T(8,128)(2,1)S(1)} %get-tuple-element.78.refs_0_), channel_id=1, source_target_pairs={{0,8},{4,12},{8,16},{12,20},{16,24},{20,28},{24,32},{28,36},{32,40... | collective-permute-start | bytes 786440 | tf_op jit(solution)/shard_map/ppermute | solution.py:450
  68.5 11.6 %collective-permute-start.20 = (bf16[128,512]{1,0:T(8,128)(2,1)S(1)}, bf16[128,512]{1,0:T(8,128)(2,1)S(1)}, u32[]{:S(2)}, u32[]{:S(2)}) collective-permute-start(bf16[128,512]{1,0:T(8,128)(2,1)S(1)} %get-tuple-element.79.q_ref), channel_id=1, source_target_pairs={{8,0},{12,4},{16,8},{20,12},{24,16},{28,20},{32,24},{36,28},{40,32... | collective-permute-start | bytes 393224 | tf_op jit(solution)/shard_map/ppermute | solution.py:450
  78.2 11.5 %collective-permute-start.19 = (bf16[128,1024]{1,0:T(8,128)(2,1)S(1)}, bf16[128,1024]{1,0:T(8,128)(2,1)S(1)}, u32[]{:S(2)}, u32[]{:S(2)}) collective-permute-start(bf16[128,1024]{1,0:T(8,128)(2,1)S(1)} %collective-permute-done.18.own_ref.refs_2_), channel_id=1, source_target_pairs={{0,8},{4,12},{8,16},{12,20},{16,24},{20,28},{24,32},{28,36},{32,40... | collective-permute-start | bytes 786440 | tf_op jit(solution)/shard_map/ppermute | solution.py:450
  80.2 8.5 %collective-permute-start.21 = (bf16[128,512]{1,0:T(8,128)(2,1)S(1)}, bf16[128,512]{1,0:T(8,128)(2,1)S(1)}, u32[]{:S(2)}, u32[]{:S(2)}) collective-permute-start(bf16[128,512]{1,0:T(8,128)(2,1)S(1)} %collective-permute-done.20), channel_id=1, source_target_pairs={{8,0},{12,4},{16,8},{20,12},{24,16},{28,20},{32,24},{36,28},{40,32... | collective-permute-start | bytes 393224 | tf_op jit(solution)/shard_map/ppermute | solution.py:450
  86.2 4.1 %collective-permute-start.22 = (bf16[128,1024]{1,0:T(8,128)(2,1)S(1)}, bf16[128,1024]{1,0:T(8,128)(2,1)S(1)}, u32[]{:S(2)}, u32[]{:S(2)}) collective-permute-start(bf16[128,1024]{1,0:T(8,128)(2,1)S(1)} %collective-permute-done.18.own_ref.refs_2_), channel_id=1, source_target_pairs={{0,4},{4,0},{8,12},{12,8},{16,20},{20,16},{24,28},{28,24},{32,36},... | collective-permute-start | bytes 786440 | tf_op jit(solution)/shard_map/ppermute | solution.py:456
  89.8 4.9 %collective-permute-start.23 = (bf16[128,1024]{1,0:T(8,128)(2,1)S(1)}, bf16[128,1024]{1,0:T(8,128)(2,1)S(1)}, u32[]{:S(2)}, u32[]{:S(2)}) collective-permute-start(bf16[128,1024]{1,0:T(8,128)(2,1)S(1)} %get-tuple-element.78.refs_0_), channel_id=1, source_target_pairs={{0,4},{4,0},{8,12},{12,8},{16,20},{20,16},{24,28},{28,24},{32,36},... | collective-permute-start | bytes 786440 | tf_op jit(solution)/shard_map/ppermute | solution.py:456
  92.8 13.8 %collective-permute-start.25 = (bf16[144,512]{1,0:T(8,128)(2,1)S(1)}, bf16[144,512]{1,0:T(8,128)(2,1)S(1)}, u32[]{:S(2)}, u32[]{:S(2)}) collective-permute-start(bf16[144,512]{1,0:T(8,128)(2,1)S(1)} %shard_map.108), channel_id=1, source_target_pairs={{0,16},{4,20},{8,24},{12,28},{16,32},{20,36},{24,40},{28,44},{32,4... | collective-permute-start | bytes 442376 | tf_op jit(solution)/shard_map/ppermute | solution.py:450
  (5 other events, 72.7 us)

commit v12 on v9

--- a/solution.py
+++ b/solution.py
@@ -286,7 +286,7 @@
 
 
 def out_kernel(
-    place, local_ref, through_ref, mine_ref, recv2_ref, recv3_ref, recv1_ref, w_ref, term_ref, *refs
+    place, local_ref, through_ref, mine_ref, recv1_ref, recv3_ref, recv2_ref, w_ref, term_ref, *refs
 ):
     part = place[1]
     me = place[2]
@@ -523,9 +523,9 @@
         local,
         through,
         mine,
+        crossed(out1, 1),
+        crossed(out3, 3),
         crossed(out2, 2),
-        crossed(out3, 3),
-        crossed(out1, 1),
         w_out,
     )
     received = [crossed(terms[r], r, "head") for r in (2, 1, 3)]

time: 104 us -> 107 us (1.029); the launches traced: 104 us -> 105 us
  no operation moved by 1% of the time
where the time goes in v12:
time: 107 us; the launch traced here: 105 us
  starting transfers between devices  43.5 us (41%)
  waiting for transfers between devices  37.9 us (35%)
  Pallas kernels  21.3 us (20%)
    ppermute x21, starting transfers between devices, crossed(): lax.ppermute(array, axis, [(i, i ^ mask) for i in range(lax.axis_size(axi...  26.2 us
    pallas_call x15, Pallas kernels, run(): pl.pallas_call(kernel, out_shape=[jax.ShapeDtypeStruct(shape, kind) for s...  21.3 us
    ppermute x21, waiting for transfers between devices, crossed(): lax.ppermute(array, axis, [(i, i ^ mask) for i in range(lax.axis_size(axi...  20.7 us
    ppermute x5, starting transfers between devices, moved(): lax.ppermute(array, axis, [(i, i + distance) for i in range(size) if 0 <=...  17.3 us
    ppermute x5, waiting for transfers between devices, moved(): lax.ppermute(array, axis, [(i, i + distance) for i in range(size) if 0 <=...  17.2 us
  transfers between devices with their start and end apart: 26, of which 16 were waited for; matrix products, arithmetic and copies ran while one was open for 0% of the time, Pallas kernels for 9%

profile of v12, /device:TPU:34, one launch (start us, length us, event | category | flops | bytes accessed | tf_op | source)
XLA Modules:
  0.0 105.3 jit_solution(11751791108396158235)
XLA Ops:
  1.6 4.9 %shard_map.95 = (bf16[128,512]{1,0:T(8,128)(2,1)S(1)}, bf16[4,128,128]{2,1,0:T(8,128)(2,1)S(1)}, bf16[4,128,128]{2,1,0:T(8,128)(2,1)S(1)}, f32[128,256]{1,0:T(8,...) custom-call(s32[5]{0:T(128)S(1)} %stack.23.place, ...), custom_call_target="tpu_custom_call" | custom-call | tf_op jit(solution)/shard_map/pallas_call | solution.py:436
  12.5 7.1 %collective-permute-start.3 = (bf16[144,256]{1,0:T(8,128)(2,1)S(1)}, bf16[144,256]{1,0:T(8,128)(2,1)S(1)}, u32[]{:S(2)}, u32[]{:S(2)}) collective-permute-start(bf16[144,256]{1,0:T(8,128)(2,1)S(1)} %get-tuple-element.59), channel_id=1, source_target_pairs={{0,32},{4,36},{8,40},{12,44},{16,48},{20,52},{24,56},{28,60},{32,0... | collective-permute-start | bytes 221192 | tf_op jit(solution)/shard_map/ppermute | solution.py:456
  19.5 1.5 %collective-permute-start.5 = (bf16[144,256]{1,0:T(8,128)(2,1)S(1)}, bf16[144,256]{1,0:T(8,128)(2,1)S(1)}, u32[]{:S(2)}, u32[]{:S(2)}) collective-permute-start(bf16[144,256]{1,0:T(8,128)(2,1)S(1)} %get-tuple-element.59), channel_id=1, source_target_pairs={{0,16},{4,20},{8,24},{12,28},{16,0},{20,4},{24,8},{28,12},{32,48},... | collective-permute-start | bytes 221192 | tf_op jit(solution)/shard_map/ppermute | solution.py:456
  21.0 2.8 %shard_map.98 = (bf16[2048,1536]{1,0:T(8,128)(2,1)S(1)}, f32[128,256]{1,0:T(8,128)S(1)}) custom-call(f32[128,256]{1,0:T(8,128)S(1)} %get-tuple-element.56.token_ref, bf16[2048,1536]{1,0:T(8,128)(2,1)} %source_ref), custom_call_target="tpu_custom_call" | custom-call | tf_op jit(solution)/shard_map/pallas_call | solution.py:436
  23.8 3.6 %collective-permute-done.4.recv3_ref = bf16[144,256]{1,0:T(8,128)(2,1)S(1)} collective-permute-done((bf16[144,256]{1,0:T(8,128)(2,1)S(1)}, bf16[144,256]{1,0:T(8,128)(2,1)S(1)}, u32[]{:S(2)}, u32[]{:S(2)}) %collective-permute-start.4) | collective-permute-done | bytes 73760 | tf_op jit(solution)/shard_map/ppermute | solution.py:456
  28.4 2.2 %collective-permute-start.6 = (bf16[144,256]{1,0:T(8,128)(2,1)S(1)}, bf16[144,256]{1,0:T(8,128)(2,1)S(1)}, u32[]{:S(2)}, u32[]{:S(2)}) collective-permute-start(bf16[144,256]{1,0:T(8,128)(2,1)S(1)} %get-tuple-element.68), channel_id=1, source_target_pairs={{0,128},{4,132},{8,136},{12,140},{16,144},{20,148},{24,152},{28,15... | collective-permute-start | bytes 221192 | tf_op jit(solution)/shard_map/ppermute | solution.py:456
  39.4 1.5 %collective-permute-done.10.recv3_ref = bf16[128,128]{1,0:T(8,128)(2,1)S(1)} collective-permute-done((bf16[128,128]{1,0:T(8,128)(2,1)S(1)}, bf16[128,128]{1,0:T(8,128)(2,1)S(1)}, u32[]{:S(2)}, u32[]{:S(2)}) %collective-permute-start.10) | collective-permute-done | bytes 32800 | tf_op jit(solution)/shard_map/ppermute | solution.py:456
  43.0 3.5 %collective-permute-start.12 = (bf16[128,512]{1,0:T(8,128)(2,1)S(1)}, bf16[128,512]{1,0:T(8,128)(2,1)S(1)}, u32[]{:S(2)}, u32[]{:S(2)}) collective-permute-start(bf16[128,512]{1,0:T(8,128)(2,1)S(1)} %get-tuple-element.76), channel_id=1, source_target_pairs={{0,2},{1,3},{2,0},{3,1},{4,6},{5,7},{6,4},{7,5},{8,10},{9,11},{10,... | collective-permute-start | bytes 393224 | tf_op jit(solution)/shard_map/ppermute | solution.py:456
  47.5 3.6 %collective-permute-done.12.refs_0_ = bf16[128,512]{1,0:T(8,128)(2,1)S(1)} collective-permute-done((bf16[128,512]{1,0:T(8,128)(2,1)S(1)}, bf16[128,512]{1,0:T(8,128)(2,1)S(1)}, u32[]{:S(2)}, u32[]{:S(2)}) %collective-permute-start.12) | collective-permute-done | bytes 131104 | tf_op jit(solution)/shard_map/ppermute | solution.py:456
  51.1 2.3 %collective-permute-done.13.refs_1_ = bf16[128,512]{1,0:T(8,128)(2,1)S(1)} collective-permute-done((bf16[128,512]{1,0:T(8,128)(2,1)S(1)}, bf16[128,512]{1,0:T(8,128)(2,1)S(1)}, u32[]{:S(2)}, u32[]{:S(2)}) %collective-permute-start.13) | collective-permute-done | bytes 131104 | tf_op jit(solution)/shard_map/ppermute | solution.py:456
  53.7 2.8 %collective-permute-start.15 = (bf16[128,512]{1,0:T(8,128)(2,1)S(1)}, bf16[128,512]{1,0:T(8,128)(2,1)S(1)}, u32[]{:S(2)}, u32[]{:S(2)}) collective-permute-start(bf16[128,512]{1,0:T(8,128)(2,1)S(1)} %shard_map.103.hidden_ref), channel_id=1, source_target_pairs={{0,2},{1,3},{2,0},{3,1},{4,6},{5,7},{6,4},{7,5},{8,10},{9,11},{10,... | collective-permute-start | bytes 393224 | tf_op jit(solution)/shard_map/ppermute | solution.py:456
  58.8 2.9 %collective-permute-done.15.block2_ref = bf16[128,512]{1,0:T(8,128)(2,1)S(1)} collective-permute-done((bf16[128,512]{1,0:T(8,128)(2,1)S(1)}, bf16[128,512]{1,0:T(8,128)(2,1)S(1)}, u32[]{:S(2)}, u32[]{:S(2)}) %collective-permute-start.15) | collective-permute-done | bytes 131104 | tf_op jit(solution)/shard_map/ppermute | solution.py:456
  61.7 1.6 %collective-permute-done.16.block1_ref = bf16[128,512]{1,0:T(8,128)(2,1)S(1)} collective-permute-done((bf16[128,512]{1,0:T(8,128)(2,1)S(1)}, bf16[128,512]{1,0:T(8,128)(2,1)S(1)}, u32[]{:S(2)}, u32[]{:S(2)}) %collective-permute-start.16) | collective-permute-done | bytes 131104 | tf_op jit(solution)/shard_map/ppermute | solution.py:456
  63.8 1.4 %shard_map.105 = (bf16[128,512]{1,0:T(8,128)(2,1)S(1)}, bf16[128,1024]{1,0:T(8,128)(2,1)S(1)}) custom-call(s32[5]{0:T(128)S(1)} %stack.23.place, bf16[2048,1536]{1,0:T(8,128)(2,1)S(1)} %get-tuple-element.79.w_ref, f32[128,1536]{1,0:T(8,128)S(1)} %shard_map.104.part_ref, bf16[128,512]{1,0:T(8,128)(2,1)S(1)} %shard_map.103.hidden_ref, ...), custom_call_target="tpu_custom_call" | custom-call | tf_op jit(solution)/shard_map/pallas_call | solution.py:436
  65.3 3.3 %collective-permute-start.18 = (bf16[128,1024]{1,0:T(8,128)(2,1)S(1)}, bf16[128,1024]{1,0:T(8,128)(2,1)S(1)}, u32[]{:S(2)}, u32[]{:S(2)}) collective-permute-start(bf16[128,1024]{1,0:T(8,128)(2,1)S(1)} %get-tuple-element.80.refs_0_), channel_id=1, source_target_pairs={{0,8},{4,12},{8,16},{12,20},{16,24},{20,28},{24,32},{28,36},{32,40... | collective-permute-start | bytes 786440 | tf_op jit(solution)/shard_map/ppermute | solution.py:450
  68.5 2.6 %collective-permute-start.19 = (bf16[128,512]{1,0:T(8,128)(2,1)S(1)}, bf16[128,512]{1,0:T(8,128)(2,1)S(1)}, u32[]{:S(2)}, u32[]{:S(2)}) collective-permute-start(bf16[128,512]{1,0:T(8,128)(2,1)S(1)} %get-tuple-element.81.q_ref), channel_id=1, source_target_pairs={{8,0},{12,4},{16,8},{20,12},{24,16},{28,20},{32,24},{36,28},{40,32... | collective-permute-start | bytes 393224 | tf_op jit(solution)/shard_map/ppermute | solution.py:450
  71.1 4.3 %collective-permute-done.19 = bf16[128,512]{1,0:T(8,128)(2,1)S(1)} collective-permute-done((bf16[128,512]{1,0:T(8,128)(2,1)S(1)}, bf16[128,512]{1,0:T(8,128)(2,1)S(1)}, u32[]{:S(2)}, u32[]{:S(2)}) %collective-permute-start.19) | collective-permute-done | bytes 131104 | tf_op jit(solution)/shard_map/ppermute | solution.py:450
  75.4 3.4 %collective-permute-start.20 = (bf16[128,1024]{1,0:T(8,128)(2,1)S(1)}, bf16[128,1024]{1,0:T(8,128)(2,1)S(1)}, u32[]{:S(2)}, u32[]{:S(2)}) collective-permute-start(bf16[128,1024]{1,0:T(8,128)(2,1)S(1)} %collective-permute-done.18.own_ref.refs_2_), channel_id=1, source_target_pairs={{0,8},{4,12},{8,16},{12,20},{16,24},{20,28},{24,32},{28,36},{32,40... | collective-permute-start | bytes 786440 | tf_op jit(solution)/shard_map/ppermute | solution.py:450
  78.8 3.0 %collective-permute-start.21 = (bf16[128,512]{1,0:T(8,128)(2,1)S(1)}, bf16[128,512]{1,0:T(8,128)(2,1)S(1)}, u32[]{:S(2)}, u32[]{:S(2)}) collective-permute-start(bf16[128,512]{1,0:T(8,128)(2,1)S(1)} %collective-permute-done.19), channel_id=1, source_target_pairs={{8,0},{12,4},{16,8},{20,12},{24,16},{28,20},{32,24},{36,28},{40,32... | collective-permute-start | bytes 393224 | tf_op jit(solution)/shard_map/ppermute | solution.py:450
  81.9 5.0 %collective-permute-done.21.q_ref = bf16[128,512]{1,0:T(8,128)(2,1)S(1)} collective-permute-done((bf16[128,512]{1,0:T(8,128)(2,1)S(1)}, bf16[128,512]{1,0:T(8,128)(2,1)S(1)}, u32[]{:S(2)}, u32[]{:S(2)}) %collective-permute-start.21) | collective-permute-done | bytes 131104 | tf_op jit(solution)/shard_map/ppermute | solution.py:450
  87.4 1.5 %shard_map.106 = (f32[128,1024]{1,0:T(8,128)S(1)}, bf16[128,512]{1,0:T(8,128)(2,1)}) custom-call(s32[5]{0:T(128)S(1)} %stack.23.place, bf16[128,512]{1,0:T(8,128)(2,1)S(1)} %shard_map.103.hidden_ref, bf16[128,512]{1,0:T(8,128)(2,1)S(1)} %collective-permute-done.21.q_ref, bf16[128,1024]{1,0:T(8,128)(2,1)S(1)} %collective-permute-done.18.own_ref.refs_2_, ...), custom_call_target="tpu_custom_call" | custom-call | tf_op jit(solution)/shard_map/pallas_call | solution.py:436
  89.9 5.1 %collective-permute-start.25 = (bf16[144,512]{1,0:T(8,128)(2,1)S(1)}, bf16[144,512]{1,0:T(8,128)(2,1)S(1)}, u32[]{:S(2)}, u32[]{:S(2)}) collective-permute-start(bf16[144,512]{1,0:T(8,128)(2,1)S(1)} %shard_map.108), channel_id=1, source_target_pairs={{0,16},{4,20},{8,24},{12,28},{16,32},{20,36},{24,40},{28,44},{32,4... | collective-permute-start | bytes 442376 | tf_op jit(solution)/shard_map/ppermute | solution.py:450
  95.0 1.6 %shard_map.107.sums_ref = f32[128,1024]{1,0:T(8,128)S(1)} custom-call(s32[5]{0:T(128)S(1)} %stack.23.place, bf16[128,512]{1,0:T(8,128)(2,1)S(1)} %get-tuple-element.81.q_ref, bf16[128,1024]{1,0:T(8,128)(2,1)S(1)} %get-tuple-element.80.refs_0_, bf16[128,1024]{1,0:T(8,128)(2,1)S(1)} %collective-permute-done.23.refs_1_, ...), custom_call_target="tpu_custom_call" | custom-call | tf_op jit(solution)/shard_map/pallas_call | solution.py:436
  96.5 8.0 %collective-permute-done.25.back_ref = bf16[144,512]{1,0:T(8,128)(2,1)S(1)} collective-permute-done((bf16[144,512]{1,0:T(8,128)(2,1)S(1)}, bf16[144,512]{1,0:T(8,128)(2,1)S(1)}, u32[]{:S(2)}, u32[]{:S(2)}) %collective-permute-start.25) | collective-permute-done | bytes 147488 | tf_op jit(solution)/shard_map/ppermute | solution.py:450
  (51 shorter events, 25.2 us)
Async XLA Ops:
  6.5 4.9 %collective-permute-start = (bf16[144,256]{1,0:T(8,128)(2,1)S(1)}, bf16[144,256]{1,0:T(8,128)(2,1)S(1)}, u32[]{:S(2)}, u32[]{:S(2)}) collective-permute-start(bf16[144,256]{1,0:T(8,128)(2,1)S(1)} %get-tuple-element.52), channel_id=1, source_target_pairs={{0,8},{4,12},{8,0},{12,4},{16,24},{20,28},{24,16},{28,20},{32,40},... | collective-permute-start | bytes 221192 | tf_op jit(solution)/shard_map/ppermute | solution.py:456
  6.7 4.7 %collective-permute-start.1 = (bf16[144,256]{1,0:T(8,128)(2,1)S(1)}, bf16[144,256]{1,0:T(8,128)(2,1)S(1)}, u32[]{:S(2)}, u32[]{:S(2)}) collective-permute-start(bf16[144,256]{1,0:T(8,128)(2,1)S(1)} %get-tuple-element.53), channel_id=1, source_target_pairs={{0,12},{4,8},{8,4},{12,0},{16,28},{20,24},{24,20},{28,16},{32,44},... | collective-permute-start | bytes 221192 | tf_op jit(solution)/shard_map/ppermute | solution.py:456
  7.8 3.6 %collective-permute-start.2 = (bf16[144,256]{1,0:T(8,128)(2,1)S(1)}, bf16[144,256]{1,0:T(8,128)(2,1)S(1)}, u32[]{:S(2)}, u32[]{:S(2)}) collective-permute-start(bf16[144,256]{1,0:T(8,128)(2,1)S(1)} %get-tuple-element.54), channel_id=1, source_target_pairs={{0,4},{4,0},{8,12},{12,8},{16,20},{20,16},{24,28},{28,24},{32,36},... | collective-permute-start | bytes 221192 | tf_op jit(solution)/shard_map/ppermute | solution.py:456
  12.5 11.3 %collective-permute-start.3 = (bf16[144,256]{1,0:T(8,128)(2,1)S(1)}, bf16[144,256]{1,0:T(8,128)(2,1)S(1)}, u32[]{:S(2)}, u32[]{:S(2)}) collective-permute-start(bf16[144,256]{1,0:T(8,128)(2,1)S(1)} %get-tuple-element.59), channel_id=1, source_target_pairs={{0,32},{4,36},{8,40},{12,44},{16,48},{20,52},{24,56},{28,60},{32,0... | collective-permute-start | bytes 221192 | tf_op jit(solution)/shard_map/ppermute | solution.py:456
  19.5 7.9 %collective-permute-start.4 = (bf16[144,256]{1,0:T(8,128)(2,1)S(1)}, bf16[144,256]{1,0:T(8,128)(2,1)S(1)}, u32[]{:S(2)}, u32[]{:S(2)}) collective-permute-start(bf16[144,256]{1,0:T(8,128)(2,1)S(1)} %get-tuple-element.59), channel_id=1, source_target_pairs={{0,48},{4,52},{8,56},{12,60},{16,32},{20,36},{24,40},{28,44},{32,1... | collective-permute-start | bytes 221192 | tf_op jit(solution)/shard_map/ppermute | solution.py:456
  19.5 7.9 %collective-permute-start.5 = (bf16[144,256]{1,0:T(8,128)(2,1)S(1)}, bf16[144,256]{1,0:T(8,128)(2,1)S(1)}, u32[]{:S(2)}, u32[]{:S(2)}) collective-permute-start(bf16[144,256]{1,0:T(8,128)(2,1)S(1)} %get-tuple-element.59), channel_id=1, source_target_pairs={{0,16},{4,20},{8,24},{12,28},{16,0},{20,4},{24,8},{28,12},{32,48},... | collective-permute-start | bytes 221192 | tf_op jit(solution)/shard_map/ppermute | solution.py:456
  28.4 6.2 %collective-permute-start.6 = (bf16[144,256]{1,0:T(8,128)(2,1)S(1)}, bf16[144,256]{1,0:T(8,128)(2,1)S(1)}, u32[]{:S(2)}, u32[]{:S(2)}) collective-permute-start(bf16[144,256]{1,0:T(8,128)(2,1)S(1)} %get-tuple-element.68), channel_id=1, source_target_pairs={{0,128},{4,132},{8,136},{12,140},{16,144},{20,148},{24,152},{28,15... | collective-permute-start | bytes 221192 | tf_op jit(solution)/shard_map/ppermute | solution.py:456
  30.7 4.7 %collective-permute-start.7 = (bf16[144,256]{1,0:T(8,128)(2,1)S(1)}, bf16[144,256]{1,0:T(8,128)(2,1)S(1)}, u32[]{:S(2)}, u32[]{:S(2)}) collective-permute-start(bf16[144,256]{1,0:T(8,128)(2,1)S(1)} %get-tuple-element.68), channel_id=1, source_target_pairs={{0,64},{4,68},{8,72},{12,76},{16,80},{20,84},{24,88},{28,92},{32,9... | collective-permute-start | bytes 221192 | tf_op jit(solution)/shard_map/ppermute | solution.py:456
  32.1 4.4 %collective-permute-start.8 = (bf16[144,256]{1,0:T(8,128)(2,1)S(1)}, bf16[144,256]{1,0:T(8,128)(2,1)S(1)}, u32[]{:S(2)}, u32[]{:S(2)}) collective-permute-start(bf16[144,256]{1,0:T(8,128)(2,1)S(1)} %get-tuple-element.68), channel_id=1, source_target_pairs={{0,192},{4,196},{8,200},{12,204},{16,208},{20,212},{24,216},{28,22... | collective-permute-start | bytes 221192 | tf_op jit(solution)/shard_map/ppermute | solution.py:456
  37.5 3.5 %collective-permute-start.10 = (bf16[128,128]{1,0:T(8,128)(2,1)S(1)}, bf16[128,128]{1,0:T(8,128)(2,1)S(1)}, u32[]{:S(2)}, u32[]{:S(2)}) collective-permute-start(bf16[128,128]{1,0:T(8,128)(2,1)S(1)} %get-tuple-element.72), channel_id=1, source_target_pairs={{0,12},{4,8},{8,4},{12,0},{16,28},{20,24},{24,20},{28,16},{32,44},... | collective-permute-start | bytes 98312 | tf_op jit(solution)/shard_map/ppermute | solution.py:456
  37.6 4.2 %collective-permute-start.11 = (bf16[128,128]{1,0:T(8,128)(2,1)S(1)}, bf16[128,128]{1,0:T(8,128)(2,1)S(1)}, u32[]{:S(2)}, u32[]{:S(2)}) collective-permute-start(bf16[128,128]{1,0:T(8,128)(2,1)S(1)} %get-tuple-element.73), channel_id=1, source_target_pairs={{0,8},{4,12},{8,0},{12,4},{16,24},{20,28},{24,16},{28,20},{32,40},... | collective-permute-start | bytes 98312 | tf_op jit(solution)/shard_map/ppermute | solution.py:456
  43.0 8.1 %collective-permute-start.12 = (bf16[128,512]{1,0:T(8,128)(2,1)S(1)}, bf16[128,512]{1,0:T(8,128)(2,1)S(1)}, u32[]{:S(2)}, u32[]{:S(2)}) collective-permute-start(bf16[128,512]{1,0:T(8,128)(2,1)S(1)} %get-tuple-element.76), channel_id=1, source_target_pairs={{0,2},{1,3},{2,0},{3,1},{4,6},{5,7},{6,4},{7,5},{8,10},{9,11},{10,... | collective-permute-start | bytes 393224 | tf_op jit(solution)/shard_map/ppermute | solution.py:456
  46.4 7.0 %collective-permute-start.13 = (bf16[128,512]{1,0:T(8,128)(2,1)S(1)}, bf16[128,512]{1,0:T(8,128)(2,1)S(1)}, u32[]{:S(2)}, u32[]{:S(2)}) collective-permute-start(bf16[128,512]{1,0:T(8,128)(2,1)S(1)} %get-tuple-element.77), channel_id=1, source_target_pairs={{0,1},{1,0},{2,3},{3,2},{4,5},{5,4},{6,7},{7,6},{8,9},{9,8},{10,11... | collective-permute-start | bytes 393224 | tf_op jit(solution)/shard_map/ppermute | solution.py:456
  47.1 6.5 %collective-permute-start.14 = (bf16[128,512]{1,0:T(8,128)(2,1)S(1)}, bf16[128,512]{1,0:T(8,128)(2,1)S(1)}, u32[]{:S(2)}, u32[]{:S(2)}) collective-permute-start(bf16[128,512]{1,0:T(8,128)(2,1)S(1)} %get-tuple-element.78), channel_id=1, source_target_pairs={{0,3},{1,2},{2,1},{3,0},{4,7},{5,6},{6,5},{7,4},{8,11},{9,10},{10,... | collective-permute-start | bytes 393224 | tf_op jit(solution)/shard_map/ppermute | solution.py:456
  53.7 8.0 %collective-permute-start.15 = (bf16[128,512]{1,0:T(8,128)(2,1)S(1)}, bf16[128,512]{1,0:T(8,128)(2,1)S(1)}, u32[]{:S(2)}, u32[]{:S(2)}) collective-permute-start(bf16[128,512]{1,0:T(8,128)(2,1)S(1)} %shard_map.103.hidden_ref), channel_id=1, source_target_pairs={{0,2},{1,3},{2,0},{3,1},{4,6},{5,7},{6,4},{7,5},{8,10},{9,11},{10,... | collective-permute-start | bytes 393224 | tf_op jit(solution)/shard_map/ppermute | solution.py:456
  56.4 6.9 %collective-permute-start.16 = (bf16[128,512]{1,0:T(8,128)(2,1)S(1)}, bf16[128,512]{1,0:T(8,128)(2,1)S(1)}, u32[]{:S(2)}, u32[]{:S(2)}) collective-permute-start(bf16[128,512]{1,0:T(8,128)(2,1)S(1)} %shard_map.103.hidden_ref), channel_id=1, source_target_pairs={{0,1},{1,0},{2,3},{3,2},{4,5},{5,4},{6,7},{7,6},{8,9},{9,8},{10,11... | collective-permute-start | bytes 393224 | tf_op jit(solution)/shard_map/ppermute | solution.py:456
  57.1 6.7 %collective-permute-start.17 = (bf16[128,512]{1,0:T(8,128)(2,1)S(1)}, bf16[128,512]{1,0:T(8,128)(2,1)S(1)}, u32[]{:S(2)}, u32[]{:S(2)}) collective-permute-start(bf16[128,512]{1,0:T(8,128)(2,1)S(1)} %shard_map.103.hidden_ref), channel_id=1, source_target_pairs={{0,3},{1,2},{2,1},{3,0},{4,7},{5,6},{6,5},{7,4},{8,11},{9,10},{10,... | collective-permute-start | bytes 393224 | tf_op jit(solution)/shard_map/ppermute | solution.py:456
  65.3 10.1 %collective-permute-start.18 = (bf16[128,1024]{1,0:T(8,128)(2,1)S(1)}, bf16[128,1024]{1,0:T(8,128)(2,1)S(1)}, u32[]{:S(2)}, u32[]{:S(2)}) collective-permute-start(bf16[128,1024]{1,0:T(8,128)(2,1)S(1)} %get-tuple-element.80.refs_0_), channel_id=1, source_target_pairs={{0,8},{4,12},{8,16},{12,20},{16,24},{20,28},{24,32},{28,36},{32,40... | collective-permute-start | bytes 786440 | tf_op jit(solution)/shard_map/ppermute | solution.py:450
  68.5 6.9 %collective-permute-start.19 = (bf16[128,512]{1,0:T(8,128)(2,1)S(1)}, bf16[128,512]{1,0:T(8,128)(2,1)S(1)}, u32[]{:S(2)}, u32[]{:S(2)}) collective-permute-start(bf16[128,512]{1,0:T(8,128)(2,1)S(1)} %get-tuple-element.81.q_ref), channel_id=1, source_target_pairs={{8,0},{12,4},{16,8},{20,12},{24,16},{28,20},{32,24},{36,28},{40,32... | collective-permute-start | bytes 393224 | tf_op jit(solution)/shard_map/ppermute | solution.py:450
  75.4 11.5 %collective-permute-start.20 = (bf16[128,1024]{1,0:T(8,128)(2,1)S(1)}, bf16[128,1024]{1,0:T(8,128)(2,1)S(1)}, u32[]{:S(2)}, u32[]{:S(2)}) collective-permute-start(bf16[128,1024]{1,0:T(8,128)(2,1)S(1)} %collective-permute-done.18.own_ref.refs_2_), channel_id=1, source_target_pairs={{0,8},{4,12},{8,16},{12,20},{16,24},{20,28},{24,32},{28,36},{32,40... | collective-permute-start | bytes 786440 | tf_op jit(solution)/shard_map/ppermute | solution.py:450
  78.8 8.1 %collective-permute-start.21 = (bf16[128,512]{1,0:T(8,128)(2,1)S(1)}, bf16[128,512]{1,0:T(8,128)(2,1)S(1)}, u32[]{:S(2)}, u32[]{:S(2)}) collective-permute-start(bf16[128,512]{1,0:T(8,128)(2,1)S(1)} %collective-permute-done.19), channel_id=1, source_target_pairs={{8,0},{12,4},{16,8},{20,12},{24,16},{28,20},{32,24},{36,28},{40,32... | collective-permute-start | bytes 393224 | tf_op jit(solution)/shard_map/ppermute | solution.py:450
  81.8 5.6 %collective-permute-start.22 = (bf16[128,1024]{1,0:T(8,128)(2,1)S(1)}, bf16[128,1024]{1,0:T(8,128)(2,1)S(1)}, u32[]{:S(2)}, u32[]{:S(2)}) collective-permute-start(bf16[128,1024]{1,0:T(8,128)(2,1)S(1)} %collective-permute-done.18.own_ref.refs_2_), channel_id=1, source_target_pairs={{0,4},{4,0},{8,12},{12,8},{16,20},{20,16},{24,28},{28,24},{32,36},... | collective-permute-start | bytes 786440 | tf_op jit(solution)/shard_map/ppermute | solution.py:456
  86.9 8.1 %collective-permute-start.23 = (bf16[128,1024]{1,0:T(8,128)(2,1)S(1)}, bf16[128,1024]{1,0:T(8,128)(2,1)S(1)}, u32[]{:S(2)}, u32[]{:S(2)}) collective-permute-start(bf16[128,1024]{1,0:T(8,128)(2,1)S(1)} %get-tuple-element.80.refs_0_), channel_id=1, source_target_pairs={{0,4},{4,0},{8,12},{12,8},{16,20},{20,16},{24,28},{28,24},{32,36},... | collective-permute-start | bytes 786440 | tf_op jit(solution)/shard_map/ppermute | solution.py:456
  89.9 14.6 %collective-permute-start.25 = (bf16[144,512]{1,0:T(8,128)(2,1)S(1)}, bf16[144,512]{1,0:T(8,128)(2,1)S(1)}, u32[]{:S(2)}, u32[]{:S(2)}) collective-permute-start(bf16[144,512]{1,0:T(8,128)(2,1)S(1)} %shard_map.108), channel_id=1, source_target_pairs={{0,16},{4,20},{8,24},{12,28},{16,32},{20,36},{24,40},{28,44},{32,4... | collective-permute-start | bytes 442376 | tf_op jit(solution)/shard_map/ppermute | solution.py:450
  (5 other events, 69.8 us)

commit v13 on v9

--- a/solution.py
+++ b/solution.py
@@ -269,7 +269,7 @@
 
 
 def state_kernel(
-    place, recv2_ref, recv1_ref, recv3_ref, maps_ref, mine_ref, out1_ref, out2_ref, out3_ref, rows, states
+    place, recv2_ref, recv3_ref, recv1_ref, maps_ref, mine_ref, out1_ref, out2_ref, out3_ref, rows, states
 ):
     part, line = place[1], place[4]
     rows[line] = jnp.zeros(rows.shape[1:], F32)
@@ -500,7 +500,7 @@
     before_row, pay = call(row_kernel, [pair_shape, pay_shape], 1, [four_pairs] * 2)(
         place, everything, row2, row3, row1
     )
-    row2, row1, row3 = [crossed(pay, 16 * d) for d in (2, 1, 3)]
+    row2, row3, row1 = [crossed(pay, 16 * d) for d in (2, 3, 1)]
     before_row, w_out, stream = lax.optimization_barrier((before_row, w_out, stream))
     w_out, stream, maps = call(
         fetch_kernel,
@@ -511,7 +511,7 @@
         FETCH_LIMIT,
     )(place, before_row, before, w_out, stream)
     mine, out1, out2, out3 = call(state_kernel, [state_shape] * 4, 1, [four_pairs, four_states])(
-        place, row2, row1, row3, maps
+        place, row2, row3, row1, maps
     )
     terms = call(
         out_kernel,

time: 104 us -> 104 us (level)
    ppermute x21, waiting for transfers between devices: 19.7 us -> 18.5 us  [crossed(): lax.ppermute(array, axis, [(i, i ^ mask) for i in range(lax.axis_size(axi...]
where the time goes in v13:
time: 104 us
  starting transfers between devices  43.4 us (42%)
  waiting for transfers between devices  36.2 us (35%)
  Pallas kernels  21.2 us (20%)
    ppermute x21, starting transfers between devices, crossed(): lax.ppermute(array, axis, [(i, i ^ mask) for i in range(lax.axis_size(axi...  27.1 us
    pallas_call x15, Pallas kernels, run(): pl.pallas_call(kernel, out_shape=[jax.ShapeDtypeStruct(shape, kind) for s...  21.2 us
    ppermute x21, waiting for transfers between devices, crossed(): lax.ppermute(array, axis, [(i, i ^ mask) for i in range(lax.axis_size(axi...  18.5 us
    ppermute x5, waiting for transfers between devices, moved(): lax.ppermute(array, axis, [(i, i + distance) for i in range(size) if 0 <=...  17.8 us
    ppermute x5, starting transfers between devices, moved(): lax.ppermute(array, axis, [(i, i + distance) for i in range(size) if 0 <=...  16.3 us
  transfers between devices with their start and end apart: 26, of which 16 were waited for; matrix products, arithmetic and copies ran while one was open for 0% of the time, Pallas kernels for 9%

profile of v13, /device:TPU:34, one launch (start us, length us, event | category | flops | bytes accessed | tf_op | source)
XLA Modules:
  0.0 103.5 jit_solution(4893927808636998956)
XLA Ops:
  1.6 4.9 %shard_map.95 = (bf16[128,512]{1,0:T(8,128)(2,1)S(1)}, bf16[4,128,128]{2,1,0:T(8,128)(2,1)S(1)}, bf16[4,128,128]{2,1,0:T(8,128)(2,1)S(1)}, f32[128,256]{1,0:T(8,...) custom-call(s32[5]{0:T(128)S(1)} %stack.23.place, ...), custom_call_target="tpu_custom_call" | custom-call | tf_op jit(solution)/shard_map/pallas_call | solution.py:436
  12.5 7.1 %collective-permute-start.3 = (bf16[144,256]{1,0:T(8,128)(2,1)S(1)}, bf16[144,256]{1,0:T(8,128)(2,1)S(1)}, u32[]{:S(2)}, u32[]{:S(2)}) collective-permute-start(bf16[144,256]{1,0:T(8,128)(2,1)S(1)} %get-tuple-element.59), channel_id=1, source_target_pairs={{0,32},{4,36},{8,40},{12,44},{16,48},{20,52},{24,56},{28,60},{32,0... | collective-permute-start | bytes 221192 | tf_op jit(solution)/shard_map/ppermute | solution.py:456
  19.5 1.5 %collective-permute-start.5 = (bf16[144,256]{1,0:T(8,128)(2,1)S(1)}, bf16[144,256]{1,0:T(8,128)(2,1)S(1)}, u32[]{:S(2)}, u32[]{:S(2)}) collective-permute-start(bf16[144,256]{1,0:T(8,128)(2,1)S(1)} %get-tuple-element.59), channel_id=1, source_target_pairs={{0,16},{4,20},{8,24},{12,28},{16,0},{20,4},{24,8},{28,12},{32,48},... | collective-permute-start | bytes 221192 | tf_op jit(solution)/shard_map/ppermute | solution.py:456
  21.0 2.8 %shard_map.98 = (bf16[2048,1536]{1,0:T(8,128)(2,1)S(1)}, f32[128,256]{1,0:T(8,128)S(1)}) custom-call(f32[128,256]{1,0:T(8,128)S(1)} %get-tuple-element.56.token_ref, bf16[2048,1536]{1,0:T(8,128)(2,1)} %source_ref), custom_call_target="tpu_custom_call" | custom-call | tf_op jit(solution)/shard_map/pallas_call | solution.py:436
  23.8 3.6 %collective-permute-done.4.recv3_ref = bf16[144,256]{1,0:T(8,128)(2,1)S(1)} collective-permute-done((bf16[144,256]{1,0:T(8,128)(2,1)S(1)}, bf16[144,256]{1,0:T(8,128)(2,1)S(1)}, u32[]{:S(2)}, u32[]{:S(2)}) %collective-permute-start.4) | collective-permute-done | bytes 73760 | tf_op jit(solution)/shard_map/ppermute | solution.py:456
  28.4 2.2 %collective-permute-start.6 = (bf16[144,256]{1,0:T(8,128)(2,1)S(1)}, bf16[144,256]{1,0:T(8,128)(2,1)S(1)}, u32[]{:S(2)}, u32[]{:S(2)}) collective-permute-start(bf16[144,256]{1,0:T(8,128)(2,1)S(1)} %get-tuple-element.68), channel_id=1, source_target_pairs={{0,128},{4,132},{8,136},{12,140},{16,144},{20,148},{24,152},{28,15... | collective-permute-start | bytes 221192 | tf_op jit(solution)/shard_map/ppermute | solution.py:456
  30.7 2.6 %collective-permute-start.8 = (bf16[144,256]{1,0:T(8,128)(2,1)S(1)}, bf16[144,256]{1,0:T(8,128)(2,1)S(1)}, u32[]{:S(2)}, u32[]{:S(2)}) collective-permute-start(bf16[144,256]{1,0:T(8,128)(2,1)S(1)} %get-tuple-element.68), channel_id=1, source_target_pairs={{0,64},{4,68},{8,72},{12,76},{16,80},{20,84},{24,88},{28,92},{32,9... | collective-permute-start | bytes 221192 | tf_op jit(solution)/shard_map/ppermute | solution.py:456
  38.8 1.5 %collective-permute-done.10.recv3_ref = bf16[128,128]{1,0:T(8,128)(2,1)S(1)} collective-permute-done((bf16[128,128]{1,0:T(8,128)(2,1)S(1)}, bf16[128,128]{1,0:T(8,128)(2,1)S(1)}, u32[]{:S(2)}, u32[]{:S(2)}) %collective-permute-start.10) | collective-permute-done | bytes 32800 | tf_op jit(solution)/shard_map/ppermute | solution.py:456
  40.3 1.8 %collective-permute-done.9.recv2_ref = bf16[128,128]{1,0:T(8,128)(2,1)S(1)} collective-permute-done((bf16[128,128]{1,0:T(8,128)(2,1)S(1)}, bf16[128,128]{1,0:T(8,128)(2,1)S(1)}, u32[]{:S(2)}, u32[]{:S(2)}) %collective-permute-start.9) | collective-permute-done | bytes 32800 | tf_op jit(solution)/shard_map/ppermute | solution.py:456
  43.3 3.5 %collective-permute-start.12 = (bf16[128,512]{1,0:T(8,128)(2,1)S(1)}, bf16[128,512]{1,0:T(8,128)(2,1)S(1)}, u32[]{:S(2)}, u32[]{:S(2)}) collective-permute-start(bf16[128,512]{1,0:T(8,128)(2,1)S(1)} %get-tuple-element.76), channel_id=1, source_target_pairs={{0,2},{1,3},{2,0},{3,1},{4,6},{5,7},{6,4},{7,5},{8,10},{9,11},{10,... | collective-permute-start | bytes 393224 | tf_op jit(solution)/shard_map/ppermute | solution.py:456
  47.8 3.5 %collective-permute-done.12.refs_0_ = bf16[128,512]{1,0:T(8,128)(2,1)S(1)} collective-permute-done((bf16[128,512]{1,0:T(8,128)(2,1)S(1)}, bf16[128,512]{1,0:T(8,128)(2,1)S(1)}, u32[]{:S(2)}, u32[]{:S(2)}) %collective-permute-start.12) | collective-permute-done | bytes 131104 | tf_op jit(solution)/shard_map/ppermute | solution.py:456
  53.7 1.8 %collective-permute-start.15 = (bf16[128,512]{1,0:T(8,128)(2,1)S(1)}, bf16[128,512]{1,0:T(8,128)(2,1)S(1)}, u32[]{:S(2)}, u32[]{:S(2)}) collective-permute-start(bf16[128,512]{1,0:T(8,128)(2,1)S(1)} %shard_map.103.hidden_ref), channel_id=1, source_target_pairs={{0,2},{1,3},{2,0},{3,1},{4,6},{5,7},{6,4},{7,5},{8,10},{9,11},{10,... | collective-permute-start | bytes 393224 | tf_op jit(solution)/shard_map/ppermute | solution.py:456
  56.2 1.7 %collective-permute-start.17 = (bf16[128,512]{1,0:T(8,128)(2,1)S(1)}, bf16[128,512]{1,0:T(8,128)(2,1)S(1)}, u32[]{:S(2)}, u32[]{:S(2)}) collective-permute-start(bf16[128,512]{1,0:T(8,128)(2,1)S(1)} %shard_map.103.hidden_ref), channel_id=1, source_target_pairs={{0,3},{1,2},{2,1},{3,0},{4,7},{5,6},{6,5},{7,4},{8,11},{9,10},{10,... | collective-permute-start | bytes 393224 | tf_op jit(solution)/shard_map/ppermute | solution.py:456
  58.8 1.6 %collective-permute-done.15.block2_ref = bf16[128,512]{1,0:T(8,128)(2,1)S(1)} collective-permute-done((bf16[128,512]{1,0:T(8,128)(2,1)S(1)}, bf16[128,512]{1,0:T(8,128)(2,1)S(1)}, u32[]{:S(2)}, u32[]{:S(2)}) %collective-permute-start.15) | collective-permute-done | bytes 131104 | tf_op jit(solution)/shard_map/ppermute | solution.py:456
  63.9 3.8 %collective-permute-start.18 = (bf16[128,1024]{1,0:T(8,128)(2,1)S(1)}, bf16[128,1024]{1,0:T(8,128)(2,1)S(1)}, u32[]{:S(2)}, u32[]{:S(2)}) collective-permute-start(bf16[128,1024]{1,0:T(8,128)(2,1)S(1)} %get-tuple-element.80.refs_0_), channel_id=1, source_target_pairs={{0,8},{4,12},{8,16},{12,20},{16,24},{20,28},{24,32},{28,36},{32,40... | collective-permute-start | bytes 786440 | tf_op jit(solution)/shard_map/ppermute | solution.py:450
  67.7 2.1 %collective-permute-start.19 = (bf16[128,512]{1,0:T(8,128)(2,1)S(1)}, bf16[128,512]{1,0:T(8,128)(2,1)S(1)}, u32[]{:S(2)}, u32[]{:S(2)}) collective-permute-start(bf16[128,512]{1,0:T(8,128)(2,1)S(1)} %get-tuple-element.81.q_ref), channel_id=1, source_target_pairs={{8,0},{12,4},{16,8},{20,12},{24,16},{28,20},{32,24},{36,28},{40,32... | collective-permute-start | bytes 393224 | tf_op jit(solution)/shard_map/ppermute | solution.py:450
  69.8 4.8 %collective-permute-done.19 = bf16[128,512]{1,0:T(8,128)(2,1)S(1)} collective-permute-done((bf16[128,512]{1,0:T(8,128)(2,1)S(1)}, bf16[128,512]{1,0:T(8,128)(2,1)S(1)}, u32[]{:S(2)}, u32[]{:S(2)}) %collective-permute-start.19) | collective-permute-done | bytes 131104 | tf_op jit(solution)/shard_map/ppermute | solution.py:450
  74.6 3.7 %collective-permute-start.20 = (bf16[128,1024]{1,0:T(8,128)(2,1)S(1)}, bf16[128,1024]{1,0:T(8,128)(2,1)S(1)}, u32[]{:S(2)}, u32[]{:S(2)}) collective-permute-start(bf16[128,1024]{1,0:T(8,128)(2,1)S(1)} %collective-permute-done.18.own_ref.refs_2_), channel_id=1, source_target_pairs={{0,8},{4,12},{8,16},{12,20},{16,24},{20,28},{24,32},{28,36},{32,40... | collective-permute-start | bytes 786440 | tf_op jit(solution)/shard_map/ppermute | solution.py:450
  78.3 2.1 %collective-permute-start.21 = (bf16[128,512]{1,0:T(8,128)(2,1)S(1)}, bf16[128,512]{1,0:T(8,128)(2,1)S(1)}, u32[]{:S(2)}, u32[]{:S(2)}) collective-permute-start(bf16[128,512]{1,0:T(8,128)(2,1)S(1)} %collective-permute-done.19), channel_id=1, source_target_pairs={{8,0},{12,4},{16,8},{20,12},{24,16},{28,20},{32,24},{36,28},{40,32... | collective-permute-start | bytes 393224 | tf_op jit(solution)/shard_map/ppermute | solution.py:450
  80.5 4.8 %collective-permute-done.21.q_ref = bf16[128,512]{1,0:T(8,128)(2,1)S(1)} collective-permute-done((bf16[128,512]{1,0:T(8,128)(2,1)S(1)}, bf16[128,512]{1,0:T(8,128)(2,1)S(1)}, u32[]{:S(2)}, u32[]{:S(2)}) %collective-permute-start.21) | collective-permute-done | bytes 131104 | tf_op jit(solution)/shard_map/ppermute | solution.py:450
  85.8 1.5 %shard_map.106 = (f32[128,1024]{1,0:T(8,128)S(1)}, bf16[128,512]{1,0:T(8,128)(2,1)}) custom-call(s32[5]{0:T(128)S(1)} %stack.23.place, bf16[128,512]{1,0:T(8,128)(2,1)S(1)} %shard_map.103.hidden_ref, bf16[128,512]{1,0:T(8,128)(2,1)S(1)} %collective-permute-done.21.q_ref, bf16[128,1024]{1,0:T(8,128)(2,1)S(1)} %collective-permute-done.18.own_ref.refs_2_, ...), custom_call_target="tpu_custom_call" | custom-call | tf_op jit(solution)/shard_map/pallas_call | solution.py:436
  88.3 4.6 %collective-permute-start.25 = (bf16[144,512]{1,0:T(8,128)(2,1)S(1)}, bf16[144,512]{1,0:T(8,128)(2,1)S(1)}, u32[]{:S(2)}, u32[]{:S(2)}) collective-permute-start(bf16[144,512]{1,0:T(8,128)(2,1)S(1)} %shard_map.108), channel_id=1, source_target_pairs={{0,16},{4,20},{8,24},{12,28},{16,32},{20,36},{24,40},{28,44},{32,4... | collective-permute-start | bytes 442376 | tf_op jit(solution)/shard_map/ppermute | solution.py:450
  93.0 1.6 %shard_map.107.sums_ref = f32[128,1024]{1,0:T(8,128)S(1)} custom-call(s32[5]{0:T(128)S(1)} %stack.23.place, bf16[128,512]{1,0:T(8,128)(2,1)S(1)} %get-tuple-element.81.q_ref, bf16[128,1024]{1,0:T(8,128)(2,1)S(1)} %get-tuple-element.80.refs_0_, bf16[128,1024]{1,0:T(8,128)(2,1)S(1)} %collective-permute-done.23.refs_1_, ...), custom_call_target="tpu_custom_call" | custom-call | tf_op jit(solution)/shard_map/pallas_call | solution.py:436
  94.5 8.2 %collective-permute-done.25.back_ref = bf16[144,512]{1,0:T(8,128)(2,1)S(1)} collective-permute-done((bf16[144,512]{1,0:T(8,128)(2,1)S(1)}, bf16[144,512]{1,0:T(8,128)(2,1)S(1)}, u32[]{:S(2)}, u32[]{:S(2)}) %collective-permute-start.25) | collective-permute-done | bytes 147488 | tf_op jit(solution)/shard_map/ppermute | solution.py:450
  (51 shorter events, 25.7 us)
Async XLA Ops:
  6.5 4.9 %collective-permute-start = (bf16[144,256]{1,0:T(8,128)(2,1)S(1)}, bf16[144,256]{1,0:T(8,128)(2,1)S(1)}, u32[]{:S(2)}, u32[]{:S(2)}) collective-permute-start(bf16[144,256]{1,0:T(8,128)(2,1)S(1)} %get-tuple-element.52), channel_id=1, source_target_pairs={{0,8},{4,12},{8,0},{12,4},{16,24},{20,28},{24,16},{28,20},{32,40},... | collective-permute-start | bytes 221192 | tf_op jit(solution)/shard_map/ppermute | solution.py:456
  6.7 4.7 %collective-permute-start.1 = (bf16[144,256]{1,0:T(8,128)(2,1)S(1)}, bf16[144,256]{1,0:T(8,128)(2,1)S(1)}, u32[]{:S(2)}, u32[]{:S(2)}) collective-permute-start(bf16[144,256]{1,0:T(8,128)(2,1)S(1)} %get-tuple-element.53), channel_id=1, source_target_pairs={{0,12},{4,8},{8,4},{12,0},{16,28},{20,24},{24,20},{28,16},{32,44},... | collective-permute-start | bytes 221192 | tf_op jit(solution)/shard_map/ppermute | solution.py:456
  7.8 3.6 %collective-permute-start.2 = (bf16[144,256]{1,0:T(8,128)(2,1)S(1)}, bf16[144,256]{1,0:T(8,128)(2,1)S(1)}, u32[]{:S(2)}, u32[]{:S(2)}) collective-permute-start(bf16[144,256]{1,0:T(8,128)(2,1)S(1)} %get-tuple-element.54), channel_id=1, source_target_pairs={{0,4},{4,0},{8,12},{12,8},{16,20},{20,16},{24,28},{28,24},{32,36},... | collective-permute-start | bytes 221192 | tf_op jit(solution)/shard_map/ppermute | solution.py:456
  12.5 11.3 %collective-permute-start.3 = (bf16[144,256]{1,0:T(8,128)(2,1)S(1)}, bf16[144,256]{1,0:T(8,128)(2,1)S(1)}, u32[]{:S(2)}, u32[]{:S(2)}) collective-permute-start(bf16[144,256]{1,0:T(8,128)(2,1)S(1)} %get-tuple-element.59), channel_id=1, source_target_pairs={{0,32},{4,36},{8,40},{12,44},{16,48},{20,52},{24,56},{28,60},{32,0... | collective-permute-start | bytes 221192 | tf_op jit(solution)/shard_map/ppermute | solution.py:456
  19.5 7.9 %collective-permute-start.4 = (bf16[144,256]{1,0:T(8,128)(2,1)S(1)}, bf16[144,256]{1,0:T(8,128)(2,1)S(1)}, u32[]{:S(2)}, u32[]{:S(2)}) collective-permute-start(bf16[144,256]{1,0:T(8,128)(2,1)S(1)} %get-tuple-element.59), channel_id=1, source_target_pairs={{0,48},{4,52},{8,56},{12,60},{16,32},{20,36},{24,40},{28,44},{32,1... | collective-permute-start | bytes 221192 | tf_op jit(solution)/shard_map/ppermute | solution.py:456
  19.5 7.9 %collective-permute-start.5 = (bf16[144,256]{1,0:T(8,128)(2,1)S(1)}, bf16[144,256]{1,0:T(8,128)(2,1)S(1)}, u32[]{:S(2)}, u32[]{:S(2)}) collective-permute-start(bf16[144,256]{1,0:T(8,128)(2,1)S(1)} %get-tuple-element.59), channel_id=1, source_target_pairs={{0,16},{4,20},{8,24},{12,28},{16,0},{20,4},{24,8},{28,12},{32,48},... | collective-permute-start | bytes 221192 | tf_op jit(solution)/shard_map/ppermute | solution.py:456
  28.4 6.4 %collective-permute-start.6 = (bf16[144,256]{1,0:T(8,128)(2,1)S(1)}, bf16[144,256]{1,0:T(8,128)(2,1)S(1)}, u32[]{:S(2)}, u32[]{:S(2)}) collective-permute-start(bf16[144,256]{1,0:T(8,128)(2,1)S(1)} %get-tuple-element.68), channel_id=1, source_target_pairs={{0,128},{4,132},{8,136},{12,140},{16,144},{20,148},{24,152},{28,15... | collective-permute-start | bytes 221192 | tf_op jit(solution)/shard_map/ppermute | solution.py:456
  30.7 4.7 %collective-permute-start.7 = (bf16[144,256]{1,0:T(8,128)(2,1)S(1)}, bf16[144,256]{1,0:T(8,128)(2,1)S(1)}, u32[]{:S(2)}, u32[]{:S(2)}) collective-permute-start(bf16[144,256]{1,0:T(8,128)(2,1)S(1)} %get-tuple-element.68), channel_id=1, source_target_pairs={{0,192},{4,196},{8,200},{12,204},{16,208},{20,212},{24,216},{28,22... | collective-permute-start | bytes 221192 | tf_op jit(solution)/shard_map/ppermute | solution.py:456
  30.7 4.9 %collective-permute-start.8 = (bf16[144,256]{1,0:T(8,128)(2,1)S(1)}, bf16[144,256]{1,0:T(8,128)(2,1)S(1)}, u32[]{:S(2)}, u32[]{:S(2)}) collective-permute-start(bf16[144,256]{1,0:T(8,128)(2,1)S(1)} %get-tuple-element.68), channel_id=1, source_target_pairs={{0,64},{4,68},{8,72},{12,76},{16,80},{20,84},{24,88},{28,92},{32,9... | collective-permute-start | bytes 221192 | tf_op jit(solution)/shard_map/ppermute | solution.py:456
  36.6 3.7 %collective-permute-start.10 = (bf16[128,128]{1,0:T(8,128)(2,1)S(1)}, bf16[128,128]{1,0:T(8,128)(2,1)S(1)}, u32[]{:S(2)}, u32[]{:S(2)}) collective-permute-start(bf16[128,128]{1,0:T(8,128)(2,1)S(1)} %get-tuple-element.72), channel_id=1, source_target_pairs={{0,12},{4,8},{8,4},{12,0},{16,28},{20,24},{24,20},{28,16},{32,44},... | collective-permute-start | bytes 98312 | tf_op jit(solution)/shard_map/ppermute | solution.py:456
  38.2 3.9 %collective-permute-start.9 = (bf16[128,128]{1,0:T(8,128)(2,1)S(1)}, bf16[128,128]{1,0:T(8,128)(2,1)S(1)}, u32[]{:S(2)}, u32[]{:S(2)}) collective-permute-start(bf16[128,128]{1,0:T(8,128)(2,1)S(1)} %get-tuple-element.71), channel_id=1, source_target_pairs={{0,8},{4,12},{8,0},{12,4},{16,24},{20,28},{24,16},{28,20},{32,40},... | collective-permute-start | bytes 98312 | tf_op jit(solution)/shard_map/ppermute | solution.py:456
  43.3 8.0 %collective-permute-start.12 = (bf16[128,512]{1,0:T(8,128)(2,1)S(1)}, bf16[128,512]{1,0:T(8,128)(2,1)S(1)}, u32[]{:S(2)}, u32[]{:S(2)}) collective-permute-start(bf16[128,512]{1,0:T(8,128)(2,1)S(1)} %get-tuple-element.76), channel_id=1, source_target_pairs={{0,2},{1,3},{2,0},{3,1},{4,6},{5,7},{6,4},{7,5},{8,10},{9,11},{10,... | collective-permute-start | bytes 393224 | tf_op jit(solution)/shard_map/ppermute | solution.py:456
  46.8 5.7 %collective-permute-start.13 = (bf16[128,512]{1,0:T(8,128)(2,1)S(1)}, bf16[128,512]{1,0:T(8,128)(2,1)S(1)}, u32[]{:S(2)}, u32[]{:S(2)}) collective-permute-start(bf16[128,512]{1,0:T(8,128)(2,1)S(1)} %get-tuple-element.77), channel_id=1, source_target_pairs={{0,1},{1,0},{2,3},{3,2},{4,5},{5,4},{6,7},{7,6},{8,9},{9,8},{10,11... | collective-permute-start | bytes 393224 | tf_op jit(solution)/shard_map/ppermute | solution.py:456
  47.5 6.2 %collective-permute-start.14 = (bf16[128,512]{1,0:T(8,128)(2,1)S(1)}, bf16[128,512]{1,0:T(8,128)(2,1)S(1)}, u32[]{:S(2)}, u32[]{:S(2)}) collective-permute-start(bf16[128,512]{1,0:T(8,128)(2,1)S(1)} %get-tuple-element.78), channel_id=1, source_target_pairs={{0,3},{1,2},{2,1},{3,0},{4,7},{5,6},{6,5},{7,4},{8,11},{9,10},{10,... | collective-permute-start | bytes 393224 | tf_op jit(solution)/shard_map/ppermute | solution.py:456
  53.7 6.7 %collective-permute-start.15 = (bf16[128,512]{1,0:T(8,128)(2,1)S(1)}, bf16[128,512]{1,0:T(8,128)(2,1)S(1)}, u32[]{:S(2)}, u32[]{:S(2)}) collective-permute-start(bf16[128,512]{1,0:T(8,128)(2,1)S(1)} %shard_map.103.hidden_ref), channel_id=1, source_target_pairs={{0,2},{1,3},{2,0},{3,1},{4,6},{5,7},{6,4},{7,5},{8,10},{9,11},{10,... | collective-permute-start | bytes 393224 | tf_op jit(solution)/shard_map/ppermute | solution.py:456
  55.5 5.7 %collective-permute-start.16 = (bf16[128,512]{1,0:T(8,128)(2,1)S(1)}, bf16[128,512]{1,0:T(8,128)(2,1)S(1)}, u32[]{:S(2)}, u32[]{:S(2)}) collective-permute-start(bf16[128,512]{1,0:T(8,128)(2,1)S(1)} %shard_map.103.hidden_ref), channel_id=1, source_target_pairs={{0,1},{1,0},{2,3},{3,2},{4,5},{5,4},{6,7},{7,6},{8,9},{9,8},{10,11... | collective-permute-start | bytes 393224 | tf_op jit(solution)/shard_map/ppermute | solution.py:456
  56.2 6.3 %collective-permute-start.17 = (bf16[128,512]{1,0:T(8,128)(2,1)S(1)}, bf16[128,512]{1,0:T(8,128)(2,1)S(1)}, u32[]{:S(2)}, u32[]{:S(2)}) collective-permute-start(bf16[128,512]{1,0:T(8,128)(2,1)S(1)} %shard_map.103.hidden_ref), channel_id=1, source_target_pairs={{0,3},{1,2},{2,1},{3,0},{4,7},{5,6},{6,5},{7,4},{8,11},{9,10},{10,... | collective-permute-start | bytes 393224 | tf_op jit(solution)/shard_map/ppermute | solution.py:456
  63.9 10.6 %collective-permute-start.18 = (bf16[128,1024]{1,0:T(8,128)(2,1)S(1)}, bf16[128,1024]{1,0:T(8,128)(2,1)S(1)}, u32[]{:S(2)}, u32[]{:S(2)}) collective-permute-start(bf16[128,1024]{1,0:T(8,128)(2,1)S(1)} %get-tuple-element.80.refs_0_), channel_id=1, source_target_pairs={{0,8},{4,12},{8,16},{12,20},{16,24},{20,28},{24,32},{28,36},{32,40... | collective-permute-start | bytes 786440 | tf_op jit(solution)/shard_map/ppermute | solution.py:450
  67.7 6.9 %collective-permute-start.19 = (bf16[128,512]{1,0:T(8,128)(2,1)S(1)}, bf16[128,512]{1,0:T(8,128)(2,1)S(1)}, u32[]{:S(2)}, u32[]{:S(2)}) collective-permute-start(bf16[128,512]{1,0:T(8,128)(2,1)S(1)} %get-tuple-element.81.q_ref), channel_id=1, source_target_pairs={{8,0},{12,4},{16,8},{20,12},{24,16},{28,20},{32,24},{36,28},{40,32... | collective-permute-start | bytes 393224 | tf_op jit(solution)/shard_map/ppermute | solution.py:450
  74.6 10.8 %collective-permute-start.20 = (bf16[128,1024]{1,0:T(8,128)(2,1)S(1)}, bf16[128,1024]{1,0:T(8,128)(2,1)S(1)}, u32[]{:S(2)}, u32[]{:S(2)}) collective-permute-start(bf16[128,1024]{1,0:T(8,128)(2,1)S(1)} %collective-permute-done.18.own_ref.refs_2_), channel_id=1, source_target_pairs={{0,8},{4,12},{8,16},{12,20},{16,24},{20,28},{24,32},{28,36},{32,40... | collective-permute-start | bytes 786440 | tf_op jit(solution)/shard_map/ppermute | solution.py:450
  78.3 7.1 %collective-permute-start.21 = (bf16[128,512]{1,0:T(8,128)(2,1)S(1)}, bf16[128,512]{1,0:T(8,128)(2,1)S(1)}, u32[]{:S(2)}, u32[]{:S(2)}) collective-permute-start(bf16[128,512]{1,0:T(8,128)(2,1)S(1)} %collective-permute-done.19), channel_id=1, source_target_pairs={{8,0},{12,4},{16,8},{20,12},{24,16},{28,20},{32,24},{36,28},{40,32... | collective-permute-start | bytes 393224 | tf_op jit(solution)/shard_map/ppermute | solution.py:450
  80.4 5.4 %collective-permute-start.22 = (bf16[128,1024]{1,0:T(8,128)(2,1)S(1)}, bf16[128,1024]{1,0:T(8,128)(2,1)S(1)}, u32[]{:S(2)}, u32[]{:S(2)}) collective-permute-start(bf16[128,1024]{1,0:T(8,128)(2,1)S(1)} %collective-permute-done.18.own_ref.refs_2_), channel_id=1, source_target_pairs={{0,4},{4,0},{8,12},{12,8},{16,20},{20,16},{24,28},{28,24},{32,36},... | collective-permute-start | bytes 786440 | tf_op jit(solution)/shard_map/ppermute | solution.py:456
  85.3 7.6 %collective-permute-start.23 = (bf16[128,1024]{1,0:T(8,128)(2,1)S(1)}, bf16[128,1024]{1,0:T(8,128)(2,1)S(1)}, u32[]{:S(2)}, u32[]{:S(2)}) collective-permute-start(bf16[128,1024]{1,0:T(8,128)(2,1)S(1)} %get-tuple-element.80.refs_0_), channel_id=1, source_target_pairs={{0,4},{4,0},{8,12},{12,8},{16,20},{20,16},{24,28},{28,24},{32,36},... | collective-permute-start | bytes 786440 | tf_op jit(solution)/shard_map/ppermute | solution.py:456
  88.3 14.4 %collective-permute-start.25 = (bf16[144,512]{1,0:T(8,128)(2,1)S(1)}, bf16[144,512]{1,0:T(8,128)(2,1)S(1)}, u32[]{:S(2)}, u32[]{:S(2)}) collective-permute-start(bf16[144,512]{1,0:T(8,128)(2,1)S(1)} %shard_map.108), channel_id=1, source_target_pairs={{0,16},{4,20},{8,24},{12,28},{16,32},{20,36},{24,40},{28,44},{32,4... | collective-permute-start | bytes 442376 | tf_op jit(solution)/shard_map/ppermute | solution.py:450
  (5 other events, 71.1 us)
